TPU v7x, 32 devices: a whole 2x2x4 slice. The times are simulated.
32 devices in a mesh: dom: 8 (over z, x), sub: 4 (over y, core).
Axes of the slice: x: 2, y: 2, z: 4, core: 2. Of those that a mesh axis runs over, the one named last changes fastest.
Arguments:
- directions: bfloat16 [384, 64, 128], P(('dom', 'sub')), may hold values from -6 to 6
- tiles: bfloat16 [384, 27, 128, 128], P(('dom', 'sub')), may hold values from -0.109375 to 0.109375
- tile_cols: int32 [384, 27], P(('dom', 'sub')), may hold values from 0 to 79
- friction: float32 [384, 128], P(('dom', 'sub')), may hold values from 0.3 to 3
- neighbours: int32 [8, 4], P('dom'), may hold values from -1 to 7, as said below
- send_idx: int32 [32, 4, 2], P(('dom', 'sub')), may hold values from 0 to 11
- send_count: int32 [32, 4], P(('dom', 'sub')), may hold values from 1 to 2
- row_counts: int32 [32], P(('dom', 'sub')), may hold values from 6 to 12
Outputs:
- remainder: float32 [384, 64, 128], P(('dom', 'sub'))
- cross_gram: float32 [64, 64], replicated
Inputs may be any that keep to these rules, and one draw needn't show every extreme that they name: neighbours[p, c] is p + 1, p - 1, p + 2, p - 2 for c = 0, 1, 2, 3, or -1 where that partition is not a neighbour; slots 0 and 1 are filled wherever the partition exists; q is in p's list exactly when p is in q's.
All inputs are finite; a program needn't handle non-finite values.
Results may differ from a plain program's by a relative error of at most 0.0053.
Values may be sent and summed in bfloat16 or wider, within the bound.
No kernel may reach another device: no remote copies, remote signals or barrier semaphores. Data moves between devices by JAX's collectives and lax.ppermute only.
A program may use at most 128 MiB of HBM per device.

v0:
```python
import jax
import jax.numpy as jnp
from jax import lax
from jax.sharding import PartitionSpec as P

ITERS = 2


shift_offsets = (1, -1, 2, -2)


def from_behind(x, axis, by):
    peers = lax.axis_size(axis)
    pairs = [(i, i + by) for i in range(peers) if 0 <= i + by < peers]
    return lax.ppermute(x, axis, pairs)


def on_device(directions, tiles, tile_cols, friction, neighbours, send_idx, send_count, row_counts):
    sub_count = lax.axis_size("sub")
    blocks_here = directions.shape[0]
    dirs_count = directions.shape[1]
    tile_width = directions.shape[2]
    neigh_count = send_idx.shape[1]
    slot_count = send_idx.shape[2]
    own_columns = sub_count * blocks_here
    local_columns = own_columns + sub_count * neigh_count * slot_count
    high = lax.Precision.HIGHEST
    active = (jnp.arange(blocks_here) < row_counts[0]).astype(jnp.float32)
    linkage = neighbours[0]
    present = linkage >= 0
    send_mask = (
        present[:, None] & (jnp.arange(slot_count)[None, :] < send_count[0][:, None])
    ).astype(jnp.float32)
    flat_cols = tile_cols.reshape(-1)
    flat_sends = send_idx[0].reshape(-1)
    basis = directions * active[:, None, None].astype(jnp.bfloat16)
    remainder = jnp.zeros(directions.shape, jnp.float32)
    cross_total = jnp.zeros((dirs_count, dirs_count), jnp.float32)
    for step in range(ITERS):
        local_basis = jnp.einsum("rkb,rlb->kl", basis, basis, preferred_element_type=jnp.float32)
        own_rows = lax.all_gather(basis, "sub", axis=0, tiled=True)
        forward_outgoing = basis[send_idx[0]] * send_mask[:, :, None, None].astype(jnp.bfloat16)
        deliver_arrived = [forward_outgoing[0]] * neigh_count
        for deliver_colour in range(neigh_count):
            deliver_arrived[deliver_colour ^ 1] = from_behind(
                forward_outgoing[deliver_colour], "dom", shift_offsets[deliver_colour]
            )
        halo_rows = jnp.stack(deliver_arrived)
        halo_all = lax.all_gather(
            halo_rows.reshape(neigh_count * slot_count, dirs_count, tile_width),
            "sub",
            axis=0,
            tiled=True,
        )
        columns = jnp.concatenate([own_rows, halo_all], axis=0)
        picked = columns[tile_cols]
        state = jnp.einsum("rjkb,rjab->rka", picked, tiles, preferred_element_type=jnp.float32)
        weighted = (active[:, None, None] * friction[:, None, :] * state).astype(jnp.bfloat16)
        contrib = jnp.einsum("rka,rjab->rjkb", weighted, tiles, preferred_element_type=jnp.float32)
        summed = jax.ops.segment_sum(
            contrib.reshape(-1, dirs_count, tile_width), flat_cols, num_segments=local_columns
        )
        own_sum = lax.psum_scatter(summed[:own_columns], "sub", scatter_dimension=0, tiled=True)
        halo_sum = lax.psum_scatter(summed[own_columns:], "sub", scatter_dimension=0, tiled=True)
        returning = halo_sum.reshape(neigh_count, slot_count, dirs_count, tile_width)
        arrived = [returning[0]] * neigh_count
        for colour in range(neigh_count):
            arrived[colour ^ 1] = from_behind(returning[colour], "dom", shift_offsets[colour])
        returned = jnp.stack(arrived)
        returned = returned * send_mask[:, :, None, None]
        added = jax.ops.segment_sum(
            returned.reshape(-1, dirs_count, tile_width), flat_sends, num_segments=blocks_here
        )
        response = own_sum + added
        widened = basis.astype(jnp.float32)
        image = active[:, None, None] * (response + 1.0 * widened)
        local_cross = jnp.einsum("rkb,rlb->kl", widened, image, precision=high)
        basis_total, cross_total = lax.psum((local_basis, local_cross), ("dom", "sub"))
        factor = jnp.linalg.cholesky(basis_total)
        coupling = jax.scipy.linalg.cho_solve((factor, True), cross_total)
        remainder = image - jnp.einsum("rkb,kl->rlb", widened, coupling, precision=high)
        basis = remainder.astype(jnp.bfloat16)
    return (remainder, cross_total)


def solution(mesh):
    in_specs = (
        P(("dom", "sub"), None, None),
        P(("dom", "sub"), None, None, None),
        P(("dom", "sub"), None),
        P(("dom", "sub"), None),
        P("dom", None),
        P(("dom", "sub"), None, None),
        P(("dom", "sub"), None),
        P(("dom", "sub")),
    )
    out_specs = (P(("dom", "sub"), None, None), P())
    return jax.shard_map(
        on_device, mesh=mesh, in_specs=in_specs, out_specs=out_specs, check_vma=False
    )
```

profile of v0, /device:TPU:0, one launch (start us, length us, event | category | flops | bytes accessed | tf_op | source)
XLA Modules:
  0.0 436.9 jit_solution(6486566876765665189)
XLA Ops:
  7.9 0.7 compare_select_fusion.1
  8.7 0.7 compare_bitcast_fusion
  9.4 1.0 broadcast_multiply_fusion
  10.4 0.6 gather_fusion
  11.0 0.7 fusion.28
  11.8 1.3 collective-permute-start.2
  13.1 5.6 %collective-permute-start.3 = (bf16[2,64,128]{2,1,0:T(8,128)(2,1)S(1)}, bf16[2,64,128]{2,1,0:T(8,128)(2,1)S(1)}, u32[]{:S(2)}, u32[]{:S(2)}) collective-permute-start(bf16[2,64,128]{2,1,0:T(8,128)(2,1)S(1)} %get-tuple-element.21), channel_id=1, source_target_pairs={{0,8},{4,12},{8,16},{12,20},{16,24},{20,28},{1,9},{5,13},{9,17},{1... | collective-permute-start | bytes 98312 | tf_op jit(solution)/shard_map/ppermute | solution.py:15
  18.7 1.3 collective-permute-start
  20.0 4.5 %collective-permute-start.1 = (bf16[2,64,128]{2,1,0:T(8,128)(2,1)S(1)}, bf16[2,64,128]{2,1,0:T(8,128)(2,1)S(1)}, u32[]{:S(2)}, u32[]{:S(2)}) collective-permute-start(bf16[2,64,128]{2,1,0:T(8,128)(2,1)S(1)} %get-tuple-element.23), channel_id=1, source_target_pairs={{0,4},{4,8},{8,12},{12,16},{16,20},{20,24},{24,28},{1,5},{5,9},{9,... | collective-permute-start | bytes 98312 | tf_op jit(solution)/shard_map/ppermute | solution.py:15
  24.6 9.1 %all_gather.12 = bf16[48,64,128]{2,1,0:T(8,128)(2,1)S(1)} all-gather(bf16[12,64,128]{2,1,0:T(8,128)(2,1)S(1)} %broadcast_multiply_fusion), channel_id=1, replica_groups=mesh['dom'=8,'sub'=4] {'sub'}, dimensions={0}, use_global_device_ids=true | all-gather | bytes 983040 | tf_op jit(solution)/shard_map/all_gather | solution.py:41
  33.6 0.7 compare_select_fusion
  34.4 0.8 broadcast_multiply_fusion.3
  35.2 0.8 reshape.226
  36.0 7.3 %all_gather.13 = bf16[32,64,128]{2,1,0:T(8,128)(2,1)S(1)} all-gather(bf16[8,64,128]{2,1,0:T(8,128)(2,1)S(1)} %bitcast.160), channel_id=1, replica_groups=mesh['dom'=8,'sub'=4] {'sub'}, dimensions={0}, use_global_device_ids=true | all-gather | bytes 655360 | tf_op jit(solution)/shard_map/all_gather | solution.py:49
  43.5 13.3 %gather_fusion.1 = bf16[324,64,128]{2,1,0:T(8,128)(2,1)} fusion(bf16[80,64,128]{2,1,0:T(8,128)(2,1)S(1)} %pad_maximum_fusion, s32[1024]{0:T(1024)S(1)} %pad_clamp_fusion), kind=kCustom, calls=%fused_computation.1 | custom fusion | bytes 10618128 | tf_op jit(solution)/shard_map/gather | solution.py:56
  56.8 17.9 %fusion.10 = f32[12,64,27,128]{3,1,2,0:T(8,128)} fusion(bf16[12,27,128,128]{3,2,1,0:T(8,128)(2,1)} %param.12, bf16[12,27,64,128]{3,2,1,0:T(8,128)(2,1)} %bitcast.159, f32[12,128]{1,0:T(8,128)S(1)} %broadcast_multiply_fusion.3), kind=kOutput, calls=%fused_computation.24 | convolution fusion | flops 1359151104 | bytes 26548224 | tf_op jit(solution)/shard_map/rka,rjab->rjkb/dot_general | solution.py:59
  75.0 34.5 %scatter_fusion = f32[80,64,128]{2,1,0:T(8,128)S(1)} fusion(f32[80,64,128]{2,1,0:T(8,128)S(1)} %broadcast.141.clone, s32[324]{0:T(512)S(1)} %reshape.226, f32[324,64,128]{2,1,0:T(8,128)} %bitcast.157), kind=kCustom, calls=%fused_computation.4 | custom fusion | flops 2654208 | bytes 31851792 | tf_op jit(solution)/shard_map/scatter-add | solution.py:60
  109.5 1.0 slice.113
  110.6 1.3 slice.112
  111.9 23.9 %reduce-scatter.7.cloned.1.call-done = f32[8,64,128]{2,1,0:T(8,128)} async-done(((f32[32,64,128]{2,1,0:T(8,128)}), f32[8,64,128]{2,1,0:T(8,128)}) %reduce-scatter.7.cloned.1.call-update) | async-done | bytes 262160 | tf_op jit(solution)/shard_map/reduce_scatter | solution.py:64
  135.8 1.0 fusion.32
  136.8 1.3 collective-permute-start.4
  138.1 4.5 %collective-permute-start.5 = (f32[2,64,128]{2,1,0:T(8,128)S(1)}, f32[2,64,128]{2,1,0:T(8,128)S(1)}, u32[]{:S(2)}, u32[]{:S(2)}) collective-permute-start(f32[2,64,128]{2,1,0:T(8,128)S(1)} %get-tuple-element.15), channel_id=1, source_target_pairs={{0,4},{4,8},{8,12},{12,16},{16,20},{20,24},{24,28},{1,5},{5,9},{9,... | collective-permute-start | bytes 196616 | tf_op jit(solution)/shard_map/ppermute | solution.py:15
  142.6 1.3 collective-permute-start.6
  143.9 4.5 %collective-permute-start.7 = (f32[2,64,128]{2,1,0:T(8,128)S(1)}, f32[2,64,128]{2,1,0:T(8,128)S(1)}, u32[]{:S(2)}, u32[]{:S(2)}) collective-permute-start(f32[2,64,128]{2,1,0:T(8,128)S(1)} %get-tuple-element.13), channel_id=1, source_target_pairs={{0,8},{4,12},{8,16},{12,20},{16,24},{20,28},{1,9},{5,13},{9,17},{1... | collective-permute-start | bytes 196616 | tf_op jit(solution)/shard_map/ppermute | solution.py:15
  149.0 1.4 collective-permute-done.7
  150.5 16.2 %reduce-scatter.5.cloned.1.call-done = f32[12,64,128]{2,1,0:T(8,128)} async-done(((f32[48,64,128]{2,1,0:T(8,128)}), f32[12,64,128]{2,1,0:T(8,128)}) %reduce-scatter.5.cloned.1.call-update) | async-done | bytes 393232 | tf_op jit(solution)/shard_map/reduce_scatter | solution.py:63
  166.7 1.1 convert_add_fusion.1
  167.8 0.9 scatter_fusion.1
  168.7 0.4 convolution_bitcast_fusion.8
  169.1 40.0 %all-reduce.1 = (f32[64,64]{1,0:T(8,128)S(1)}, f32[64,64]{0,1:T(8,128)S(1)}) all-reduce(f32[64,64]{1,0:T(8,128)S(1)} %convolution_bitcast_fusion.8, f32[64,64]{0,1:T(8,128)S(1)} %convolution_bitcast_fusion.9), channel_id=1, replica_groups=mesh['dom'=8,'sub'=4] {'dom','sub'}, use_global_device_ids=true, to_apply=%region_7.9 | all-reduce | flops 8192 | bytes 65536 | tf_op jit(solution)/shard_map/psum | solution.py:78
  209.2 5.8 %cholesky.44 = f32[64,64]{1,0:T(8,128)S(1)} custom-call(f32[64,64]{1,0:T(8,128)S(1)} %fusion.26), custom_call_target="Cholesky" | custom-call | tf_op jit(solution)/shard_map/jit(cholesky)/cholesky | solution.py:79
  215.1 0.6 compare_reduce_fusion.1
  215.8 0.7 fusion.17
  216.4 4.9 %custom-call.8 = f32[1,64,64]{1,2,0:T(8,128)S(1)} custom-call(f32[1,64,64]{2,1,0:T(8,128)S(1)} %fusion.17), custom_call_target="InvertDiagBlocksLowerTriangular" | custom-call | tf_op jit(solution)/shard_map/jit(_cho_solve)/triangular_solve | solution.py:80
  222.2 0.6 gather_fusion.2
  222.8 1.3 collective-permute-start.8
  224.1 4.8 %collective-permute-start.9 = (bf16[2,64,128]{2,1,0:T(8,128)(2,1)S(1)}, bf16[2,64,128]{2,1,0:T(8,128)(2,1)S(1)}, u32[]{:S(2)}, u32[]{:S(2)}) collective-permute-start(bf16[2,64,128]{2,1,0:T(8,128)(2,1)S(1)} %get-tuple-element.19), channel_id=1, source_target_pairs={{0,4},{4,8},{8,12},{12,16},{16,20},{20,24},{24,28},{1,5},{5,9},{9,... | collective-permute-start | bytes 98312 | tf_op jit(solution)/shard_map/ppermute | solution.py:15
  228.9 1.3 collective-permute-start.10
  230.2 4.5 %collective-permute-start.11 = (bf16[2,64,128]{2,1,0:T(8,128)(2,1)S(1)}, bf16[2,64,128]{2,1,0:T(8,128)(2,1)S(1)}, u32[]{:S(2)}, u32[]{:S(2)}) collective-permute-start(bf16[2,64,128]{2,1,0:T(8,128)(2,1)S(1)} %get-tuple-element.17), channel_id=1, source_target_pairs={{0,8},{4,12},{8,16},{12,20},{16,24},{20,28},{1,9},{5,13},{9,17},{1... | collective-permute-start | bytes 98312 | tf_op jit(solution)/shard_map/ppermute | solution.py:15
  234.8 9.1 %all_gather.14 = bf16[48,64,128]{2,1,0:T(8,128)(2,1)S(1)} all-gather(bf16[12,64,128]{2,1,0:T(8,128)(2,1)S(1)} %fusion.4), channel_id=1, replica_groups=mesh['dom'=8,'sub'=4] {'sub'}, dimensions={0}, use_global_device_ids=true | all-gather | bytes 983040 | tf_op jit(solution)/shard_map/all_gather | solution.py:41
  244.0 7.3 %all_gather.15 = bf16[32,64,128]{2,1,0:T(8,128)(2,1)S(1)} all-gather(bf16[8,64,128]{2,1,0:T(8,128)(2,1)S(1)} %bitcast.161), channel_id=1, replica_groups=mesh['dom'=8,'sub'=4] {'sub'}, dimensions={0}, use_global_device_ids=true | all-gather | bytes 655360 | tf_op jit(solution)/shard_map/all_gather | solution.py:49
  251.4 13.3 %gather_fusion.3 = bf16[324,64,128]{2,1,0:T(8,128)(2,1)} fusion(bf16[80,64,128]{2,1,0:T(8,128)(2,1)S(1)} %pad_maximum_fusion.1, s32[1024]{0:T(1024)S(1)} %pad_clamp_fusion), kind=kCustom, calls=%fused_computation.3 | custom fusion | bytes 10618128 | tf_op jit(solution)/shard_map/gather | solution.py:56
  264.7 17.9 %fusion.8 = f32[12,64,27,128]{3,1,2,0:T(8,128)} fusion(bf16[12,27,128,128]{3,2,1,0:T(8,128)(2,1)} %param.12, bf16[12,27,64,128]{3,2,1,0:T(8,128)(2,1)} %bitcast.158, f32[12,128]{1,0:T(8,128)S(1)} %broadcast_multiply_fusion.3), kind=kOutput, calls=%fused_computation.22 | convolution fusion | flops 1359151104 | bytes 26548224 | tf_op jit(solution)/shard_map/rka,rjab->rjkb/dot_general | solution.py:59
  282.9 34.5 %scatter_fusion.2 = f32[80,64,128]{2,1,0:T(8,128)S(1)} fusion(f32[80,64,128]{2,1,0:T(8,128)S(1)} %broadcast.141, s32[324]{0:T(512)S(1)} %reshape.226, f32[324,64,128]{2,1,0:T(8,128)} %bitcast.156), kind=kCustom, calls=%fused_computation.6 | custom fusion | flops 2654208 | bytes 31851792 | tf_op jit(solution)/shard_map/scatter-add | solution.py:60
  317.4 1.0 slice.123
  318.5 1.3 slice.122
  319.8 23.6 %reduce-scatter.11.cloned.1.call-done = f32[8,64,128]{2,1,0:T(8,128)} async-done(((f32[32,64,128]{2,1,0:T(8,128)}), f32[8,64,128]{2,1,0:T(8,128)}) %reduce-scatter.11.cloned.1.call-update) | async-done | bytes 262160 | tf_op jit(solution)/shard_map/reduce_scatter | solution.py:64
  343.4 1.0 fusion.31
  344.4 1.3 collective-permute-start.12
  345.7 4.5 %collective-permute-start.13 = (f32[2,64,128]{2,1,0:T(8,128)S(1)}, f32[2,64,128]{2,1,0:T(8,128)S(1)}, u32[]{:S(2)}, u32[]{:S(2)}) collective-permute-start(f32[2,64,128]{2,1,0:T(8,128)S(1)} %get-tuple-element.11), channel_id=1, source_target_pairs={{0,4},{4,8},{8,12},{12,16},{16,20},{20,24},{24,28},{1,5},{5,9},{9,... | collective-permute-start | bytes 196616 | tf_op jit(solution)/shard_map/ppermute | solution.py:15
  350.2 1.3 collective-permute-start.14
  351.5 4.5 %collective-permute-start.15 = (f32[2,64,128]{2,1,0:T(8,128)S(1)}, f32[2,64,128]{2,1,0:T(8,128)S(1)}, u32[]{:S(2)}, u32[]{:S(2)}) collective-permute-start(f32[2,64,128]{2,1,0:T(8,128)S(1)} %get-tuple-element.9), channel_id=1, source_target_pairs={{0,8},{4,12},{8,16},{12,20},{16,24},{20,28},{1,9},{5,13},{9,17},{1... | collective-permute-start | bytes 196616 | tf_op jit(solution)/shard_map/ppermute | solution.py:15
  356.4 1.6 collective-permute-done.15
  358.1 16.1 %reduce-scatter.9.cloned.1.call-done = f32[12,64,128]{2,1,0:T(8,128)} async-done(((f32[48,64,128]{2,1,0:T(8,128)}), f32[12,64,128]{2,1,0:T(8,128)}) %reduce-scatter.9.cloned.1.call-update) | async-done | bytes 393232 | tf_op jit(solution)/shard_map/reduce_scatter | solution.py:63
  374.2 1.0 convert_add_fusion
  375.2 0.9 scatter_fusion.3
  376.1 0.4 convolution_bitcast_fusion.6
  376.6 40.1 %all-reduce = (f32[64,64]{1,0:T(8,128)S(1)}, f32[64,64]{0,1:T(8,128)S(1)}) all-reduce(f32[64,64]{1,0:T(8,128)S(1)} %convolution_bitcast_fusion.6, f32[64,64]{0,1:T(8,128)S(1)} %convolution_bitcast_fusion.7), channel_id=1, replica_groups=mesh['dom'=8,'sub'=4] {'dom','sub'}, use_global_device_ids=true, to_apply=%region_13.16 | all-reduce | flops 8192 | bytes 65536 | tf_op jit(solution)/shard_map/psum | solution.py:78
  416.7 5.8 %cholesky.55 = f32[64,64]{1,0:T(8,128)S(1)} custom-call(f32[64,64]{1,0:T(8,128)S(1)} %fusion.22), custom_call_target="Cholesky" | custom-call | tf_op jit(solution)/shard_map/jit(cholesky)/cholesky | solution.py:79
  422.6 0.6 compare_reduce_fusion
  423.3 0.7 fusion.18
  423.9 4.9 %custom-call.9 = f32[1,64,64]{1,2,0:T(8,128)S(1)} custom-call(f32[1,64,64]{2,1,0:T(8,128)S(1)} %fusion.18), custom_call_target="InvertDiagBlocksLowerTriangular" | custom-call | tf_op jit(solution)/shard_map/jit(_cho_solve)/triangular_solve | solution.py:80
  429.3 1.1 fusion
  (65 shorter events, 4.1 us)
Async XLA Ops:
  7.2 128.6 %reduce-scatter.7.cloned.1.call-start = ((), (), s32[]{:S(2)}) async-start(), calls=%async_computation.5 | async-start | bytes 1310720 | tf_op jit(solution)/shard_map/reduce_scatter | solution.py:64
  11.8 24.1 %collective-permute-start.2 = (bf16[2,64,128]{2,1,0:T(8,128)(2,1)S(1)}, bf16[2,64,128]{2,1,0:T(8,128)(2,1)S(1)}, u32[]{:S(2)}, u32[]{:S(2)}) collective-permute-start(bf16[2,64,128]{2,1,0:T(8,128)(2,1)S(1)} %get-tuple-element.22), channel_id=1, source_target_pairs={{8,0},{12,4},{16,8},{20,12},{24,16},{28,20},{9,1},{13,5},{17,9},{2... | collective-permute-start | bytes 98312 | tf_op jit(solution)/shard_map/ppermute | solution.py:15
  13.1 22.9 %collective-permute-start.3 = (bf16[2,64,128]{2,1,0:T(8,128)(2,1)S(1)}, bf16[2,64,128]{2,1,0:T(8,128)(2,1)S(1)}, u32[]{:S(2)}, u32[]{:S(2)}) collective-permute-start(bf16[2,64,128]{2,1,0:T(8,128)(2,1)S(1)} %get-tuple-element.21), channel_id=1, source_target_pairs={{0,8},{4,12},{8,16},{12,20},{16,24},{20,28},{1,9},{5,13},{9,17},{1... | collective-permute-start | bytes 98312 | tf_op jit(solution)/shard_map/ppermute | solution.py:15
  18.7 17.3 %collective-permute-start = (bf16[2,64,128]{2,1,0:T(8,128)(2,1)S(1)}, bf16[2,64,128]{2,1,0:T(8,128)(2,1)S(1)}, u32[]{:S(2)}, u32[]{:S(2)}) collective-permute-start(bf16[2,64,128]{2,1,0:T(8,128)(2,1)S(1)} %get-tuple-element.20), channel_id=1, source_target_pairs={{4,0},{8,4},{12,8},{16,12},{20,16},{24,20},{28,24},{5,1},{9,5},{13... | collective-permute-start | bytes 98312 | tf_op jit(solution)/shard_map/ppermute | solution.py:15
  20.0 16.0 %collective-permute-start.1 = (bf16[2,64,128]{2,1,0:T(8,128)(2,1)S(1)}, bf16[2,64,128]{2,1,0:T(8,128)(2,1)S(1)}, u32[]{:S(2)}, u32[]{:S(2)}) collective-permute-start(bf16[2,64,128]{2,1,0:T(8,128)(2,1)S(1)} %get-tuple-element.23), channel_id=1, source_target_pairs={{0,4},{4,8},{8,12},{12,16},{16,20},{20,24},{24,28},{1,5},{5,9},{9,... | collective-permute-start | bytes 98312 | tf_op jit(solution)/shard_map/ppermute | solution.py:15
  109.5 39.2 %copy-start.2 = (s32[1,4,2]{1,2,0:T(2,128)S(1)}, s32[1,4,2]{1,2,0:T(2,128)}, u32[]{:S(2)}) copy-start(s32[1,4,2]{1,2,0:T(2,128)} %param.16) | copy-start | bytes 100
  109.5 57.2 %copy-start = (bf16[12,64,128]{2,1,0:T(8,128)(2,1)S(1)}, bf16[12,64,128]{2,1,0:T(8,128)(2,1)}, u32[]{:S(2)}) copy-start(bf16[12,64,128]{2,1,0:T(8,128)(2,1)} %param.11) | copy-start | bytes 589828
  110.6 56.1 %reduce-scatter.5.cloned.1.call-start = ((), (), s32[]{:S(2)}) async-start(), calls=%async_computation.4 | async-start | bytes 1966080 | tf_op jit(solution)/shard_map/reduce_scatter | solution.py:63
  111.9 231.5 %reduce-scatter.11.cloned.1.call-start = ((), (), s32[]{:S(2)}) async-start(), calls=%async_computation.7 | async-start | bytes 1310720 | tf_op jit(solution)/shard_map/reduce_scatter | solution.py:64
  136.8 12.2 %collective-permute-start.4 = (f32[2,64,128]{2,1,0:T(8,128)S(1)}, f32[2,64,128]{2,1,0:T(8,128)S(1)}, u32[]{:S(2)}, u32[]{:S(2)}) collective-permute-start(f32[2,64,128]{2,1,0:T(8,128)S(1)} %get-tuple-element.12), channel_id=1, source_target_pairs={{4,0},{8,4},{12,8},{16,12},{20,16},{24,20},{28,24},{5,1},{9,5},{13... | collective-permute-start | bytes 196616 | tf_op jit(solution)/shard_map/ppermute | solution.py:15
  138.1 10.9 %collective-permute-start.5 = (f32[2,64,128]{2,1,0:T(8,128)S(1)}, f32[2,64,128]{2,1,0:T(8,128)S(1)}, u32[]{:S(2)}, u32[]{:S(2)}) collective-permute-start(f32[2,64,128]{2,1,0:T(8,128)S(1)} %get-tuple-element.15), channel_id=1, source_target_pairs={{0,4},{4,8},{8,12},{12,16},{16,20},{20,24},{24,28},{1,5},{5,9},{9,... | collective-permute-start | bytes 196616 | tf_op jit(solution)/shard_map/ppermute | solution.py:15
  142.6 6.3 %collective-permute-start.6 = (f32[2,64,128]{2,1,0:T(8,128)S(1)}, f32[2,64,128]{2,1,0:T(8,128)S(1)}, u32[]{:S(2)}, u32[]{:S(2)}) collective-permute-start(f32[2,64,128]{2,1,0:T(8,128)S(1)} %get-tuple-element.14), channel_id=1, source_target_pairs={{8,0},{12,4},{16,8},{20,12},{24,16},{28,20},{9,1},{13,5},{17,9},{2... | collective-permute-start | bytes 196616 | tf_op jit(solution)/shard_map/ppermute | solution.py:15
  143.9 6.4 %collective-permute-start.7 = (f32[2,64,128]{2,1,0:T(8,128)S(1)}, f32[2,64,128]{2,1,0:T(8,128)S(1)}, u32[]{:S(2)}, u32[]{:S(2)}) collective-permute-start(f32[2,64,128]{2,1,0:T(8,128)S(1)} %get-tuple-element.13), channel_id=1, source_target_pairs={{0,8},{4,12},{8,16},{12,20},{16,24},{20,28},{1,9},{5,13},{9,17},{1... | collective-permute-start | bytes 196616 | tf_op jit(solution)/shard_map/ppermute | solution.py:15
  222.8 21.1 %collective-permute-start.8 = (bf16[2,64,128]{2,1,0:T(8,128)(2,1)S(1)}, bf16[2,64,128]{2,1,0:T(8,128)(2,1)S(1)}, u32[]{:S(2)}, u32[]{:S(2)}) collective-permute-start(bf16[2,64,128]{2,1,0:T(8,128)(2,1)S(1)} %get-tuple-element.16), channel_id=1, source_target_pairs={{4,0},{8,4},{12,8},{16,12},{20,16},{24,20},{28,24},{5,1},{9,5},{13... | collective-permute-start | bytes 98312 | tf_op jit(solution)/shard_map/ppermute | solution.py:15
  224.1 19.8 %collective-permute-start.9 = (bf16[2,64,128]{2,1,0:T(8,128)(2,1)S(1)}, bf16[2,64,128]{2,1,0:T(8,128)(2,1)S(1)}, u32[]{:S(2)}, u32[]{:S(2)}) collective-permute-start(bf16[2,64,128]{2,1,0:T(8,128)(2,1)S(1)} %get-tuple-element.19), channel_id=1, source_target_pairs={{0,4},{4,8},{8,12},{12,16},{16,20},{20,24},{24,28},{1,5},{5,9},{9,... | collective-permute-start | bytes 98312 | tf_op jit(solution)/shard_map/ppermute | solution.py:15
  228.9 15.0 %collective-permute-start.10 = (bf16[2,64,128]{2,1,0:T(8,128)(2,1)S(1)}, bf16[2,64,128]{2,1,0:T(8,128)(2,1)S(1)}, u32[]{:S(2)}, u32[]{:S(2)}) collective-permute-start(bf16[2,64,128]{2,1,0:T(8,128)(2,1)S(1)} %get-tuple-element.18), channel_id=1, source_target_pairs={{8,0},{12,4},{16,8},{20,12},{24,16},{28,20},{9,1},{13,5},{17,9},{2... | collective-permute-start | bytes 98312 | tf_op jit(solution)/shard_map/ppermute | solution.py:15
  230.2 13.7 %collective-permute-start.11 = (bf16[2,64,128]{2,1,0:T(8,128)(2,1)S(1)}, bf16[2,64,128]{2,1,0:T(8,128)(2,1)S(1)}, u32[]{:S(2)}, u32[]{:S(2)}) collective-permute-start(bf16[2,64,128]{2,1,0:T(8,128)(2,1)S(1)} %get-tuple-element.17), channel_id=1, source_target_pairs={{0,8},{4,12},{8,16},{12,20},{16,24},{20,28},{1,9},{5,13},{9,17},{1... | collective-permute-start | bytes 98312 | tf_op jit(solution)/shard_map/ppermute | solution.py:15
  318.5 55.7 %reduce-scatter.9.cloned.1.call-start = ((), (), s32[]{:S(2)}) async-start(), calls=%async_computation.6 | async-start | bytes 1966080 | tf_op jit(solution)/shard_map/reduce_scatter | solution.py:63
  344.4 11.9 %collective-permute-start.12 = (f32[2,64,128]{2,1,0:T(8,128)S(1)}, f32[2,64,128]{2,1,0:T(8,128)S(1)}, u32[]{:S(2)}, u32[]{:S(2)}) collective-permute-start(f32[2,64,128]{2,1,0:T(8,128)S(1)} %get-tuple-element.8), channel_id=1, source_target_pairs={{4,0},{8,4},{12,8},{16,12},{20,16},{24,20},{28,24},{5,1},{9,5},{13... | collective-permute-start | bytes 196616 | tf_op jit(solution)/shard_map/ppermute | solution.py:15
  345.7 10.6 %collective-permute-start.13 = (f32[2,64,128]{2,1,0:T(8,128)S(1)}, f32[2,64,128]{2,1,0:T(8,128)S(1)}, u32[]{:S(2)}, u32[]{:S(2)}) collective-permute-start(f32[2,64,128]{2,1,0:T(8,128)S(1)} %get-tuple-element.11), channel_id=1, source_target_pairs={{0,4},{4,8},{8,12},{12,16},{16,20},{20,24},{24,28},{1,5},{5,9},{9,... | collective-permute-start | bytes 196616 | tf_op jit(solution)/shard_map/ppermute | solution.py:15
  350.2 6.2 %collective-permute-start.14 = (f32[2,64,128]{2,1,0:T(8,128)S(1)}, f32[2,64,128]{2,1,0:T(8,128)S(1)}, u32[]{:S(2)}, u32[]{:S(2)}) collective-permute-start(f32[2,64,128]{2,1,0:T(8,128)S(1)} %get-tuple-element.10), channel_id=1, source_target_pairs={{8,0},{12,4},{16,8},{20,12},{24,16},{28,20},{9,1},{13,5},{17,9},{2... | collective-permute-start | bytes 196616 | tf_op jit(solution)/shard_map/ppermute | solution.py:15
  351.5 6.4 %collective-permute-start.15 = (f32[2,64,128]{2,1,0:T(8,128)S(1)}, f32[2,64,128]{2,1,0:T(8,128)S(1)}, u32[]{:S(2)}, u32[]{:S(2)}) collective-permute-start(f32[2,64,128]{2,1,0:T(8,128)S(1)} %get-tuple-element.9), channel_id=1, source_target_pairs={{0,8},{4,12},{8,16},{12,20},{16,24},{20,28},{1,9},{5,13},{9,17},{1... | collective-permute-start | bytes 196616 | tf_op jit(solution)/shard_map/ppermute | solution.py:15
  416.6 13.8 %copy-start.1 = (f32[64,64]{1,0:T(8,128)}, f32[64,64]{1,0:T(8,128)S(1)}, u32[]{:S(2)}) copy-start(f32[64,64]{1,0:T(8,128)S(1)} %get-tuple-element.4) | copy-start | bytes 49156
Sparse Core Ops, SparseCore 0:
  110.7 25.0 reduce-scatter.6
  138.5 28.1 reduce-scatter.4
  318.6 24.7 reduce-scatter.10
  346.0 28.1 reduce-scatter.8
where the time goes:
time: 440 us; the launch traced here: 437 us
  blocking collectives  113 us (26%)
  other arithmetic  102 us (23%)
  waiting for transfers between devices  83 us (19%)
  starting transfers between devices  48.1 us (11%)
  matrix products  39.3 us (9%)
  local copies, waits for them, and re-layouts  36.4 us (8%)
  between operations  15 us (3%)
    psum x2, blocking collectives, on_device(): lax.psum((local_basis, local_cross), ('dom', 'sub'))  80.1 us
    scatter-add x2, other arithmetic, on_device(): jax.ops.segment_sum(contrib.reshape(-1, dirs_count, tile_width), flat_col...  69 us
    ppermute x16, starting transfers between devices, from_behind(): return lax.ppermute(x, axis, pairs)  48 us
    reduce_scatter x2, waiting for transfers between devices, on_device(): lax.psum_scatter(summed[own_columns:], 'sub', scatter_dimension=0, tiled=...  47.5 us
    dot_general x2, matrix products, on_device(): jnp.einsum('rka,rjab->rjkb', weighted, tiles, preferred_element_type=jnp....  35.7 us
    reduce_scatter x2, waiting for transfers between devices, on_device(): lax.psum_scatter(summed[:own_columns], 'sub', scatter_dimension=0, tiled=...  32.3 us
    gather x2, local copies, waits for them, and re-layouts, on_device(): picked = columns[tile_cols]  26.7 us
    all_gather x2, blocking collectives, on_device(): own_rows = lax.all_gather(basis, 'sub', axis=0, tiled=True)  18.2 us
  transfers between devices with their start and end apart: 20, of which 7 were waited for; matrix products, arithmetic and copies ran while one was open for 2% of the time, Pallas kernels for 0%

commit v1 on v0

v1 whole, which is shorter than its diff:
```python
import functools

import jax
import jax.numpy as jnp
from jax import lax
from jax.experimental import pallas as pl
from jax.experimental.pallas import tpu as pltpu
from jax.sharding import PartitionSpec as P

ITERS = 2
F32 = jnp.float32
BF16 = jnp.bfloat16
NT = (((1,), (1,)), ((), ()))
VMEM = pl.BlockSpec(memory_space=pltpu.VMEM)
SMEM = pl.BlockSpec(memory_space=pltpu.SMEM)


def bits_of(count):
    return [1 << b for b in reversed(range(count.bit_length() - 1))]


def swap(x, axis, bit):
    peers = lax.axis_size(axis)
    return lax.ppermute(x, axis, [(i, i ^ bit) for i in range(peers)])


def swap_pairs(x, by, lower):
    peers = lax.axis_size("dom")
    low = [p for p in range(peers - by) if lower(p)]
    return lax.ppermute(x, "dom", [(p, p + by) for p in low] + [(p + by, p) for p in low])


PAIRINGS = (
    (1, lambda p: p % 2 == 0),
    (1, lambda p: p % 2 == 1),
    (2, lambda p: p % 4 < 2),
    (2, lambda p: p % 4 >= 2),
)


def split_bf16(x, pieces):
    out = []
    for _ in range(pieces):
        out.append(x.astype(BF16))
        x = x - out[-1].astype(F32)
    return out


def forward_adjoint(n_parts, cols, tiles, weight, *refs):
    parts = refs[:n_parts]
    own_keep, own_send, halo_keep, halo_send, grams, columns, held, total = refs[n_parts:]
    blocks, tiles_row, width = tiles.shape[0], tiles.shape[1], tiles.shape[2]
    dirs = grams.shape[0]
    place = 0
    for part in parts:
        for i in range(part.shape[0]):
            columns[place + i] = part[i]
        place += part.shape[0]
    total[...] = jnp.zeros_like(total)
    mine = jnp.concatenate([parts[0][i] for i in range(blocks)], axis=1)
    basis_gram = lax.dot_general(mine, mine, NT, preferred_element_type=F32)
    grams[:, :dirs] = basis_gram
    grams[:, dirs:] = basis_gram

    def forward(row):
        picked = jnp.concatenate([columns[cols[row, j]] for j in range(tiles_row)], axis=1)
        wide = jnp.concatenate([tiles[row, j] for j in range(tiles_row)], axis=1)
        state = lax.dot_general(wide, picked, NT, preferred_element_type=F32).T
        weighted = (weight[pl.ds(row, 1), :] * state).astype(BF16)
        pieces = split_bf16(state, 2)
        grams[:, dirs:] += lax.dot_general(
            jnp.concatenate(pieces, axis=1),
            jnp.concatenate([weighted] * 2, axis=1),
            NT,
            preferred_element_type=F32,
        )
        return weighted

    def adjoint(row, weighted):
        for j in range(0, tiles_row, 2):
            pair = list(range(j, min(j + 2, tiles_row)))
            wide = jnp.concatenate([tiles[row, i] for i in pair], axis=1)
            product = jnp.dot(weighted, wide, preferred_element_type=F32)
            for k, i in enumerate(pair):
                total[cols[row, i]] += product[:, k * width : (k + 1) * width]

    held[0] = forward(0)

    def step(row, carry):
        adjoint(row, held[row % 2])
        held[(row + 1) % 2] = forward(row + 1)
        return carry

    lax.fori_loop(0, blocks - 1, step, 0)
    adjoint(blocks - 1, held[(blocks - 1) % 2])
    place = 0
    for out in (own_keep, own_send, halo_keep, halo_send):
        for i in range(out.shape[0]):
            out[i] = total[place + i]
        place += out.shape[0]


def call_forward_adjoint(cols, tiles, weight, parts):
    blocks, tiles_row, width = tiles.shape[0], tiles.shape[1], tiles.shape[2]
    dirs = parts[0].shape[1]
    n = len(parts)
    own = sum(p.shape[0] for p in parts[: n // 2])
    halo = sum(p.shape[0] for p in parts[n // 2 :])
    block = lambda count: jax.ShapeDtypeStruct((count, dirs, width), F32)
    return pl.pallas_call(
        functools.partial(forward_adjoint, n),
        in_specs=[SMEM] + [VMEM] * (2 + n),
        out_specs=[VMEM] * 5,
        out_shape=[
            block(own // 2),
            block(own // 2),
            block(halo // 2),
            block(halo // 2),
            jax.ShapeDtypeStruct((dirs, 2 * dirs), F32),
        ],
        scratch_shapes=[
            pltpu.VMEM((own + halo, dirs, width), BF16),
            pltpu.VMEM((2, dirs, width), BF16),
            pltpu.VMEM((own + halo, dirs, width), F32),
        ],
        compiler_params=pltpu.CompilerParams(vmem_limit_bytes=36 << 20),
        cost_estimate=pl.CostEstimate(
            flops=4 * blocks * tiles_row * width * width * dirs,
            bytes_accessed=blocks * tiles_row * width * width * 2,
            transcendentals=0,
        ),
        name="forward_adjoint",
    )(cols, tiles, weight, *parts)


def solve(grams, coupling):
    dirs = grams.shape[0]
    m = grams[...]
    rows = lax.broadcasted_iota(jnp.int32, m.shape, 0)
    for k in range(dirs):
        row = m[k : k + 1, :] / m[k : k + 1, k : k + 1]
        m = jnp.where(rows == k, row, m - m[:, k : k + 1] * row)
    turned = m[:, dirs:].T
    coupling[...] = jnp.concatenate(split_bf16(turned, 3), axis=1)


def call_solve(grams):
    dirs = grams.shape[0]
    return pl.pallas_call(
        solve,
        in_specs=[VMEM],
        out_specs=VMEM,
        out_shape=jax.ShapeDtypeStruct((dirs, 3 * dirs), BF16),
        cost_estimate=pl.CostEstimate(flops=4 * dirs**3, bytes_accessed=12 * dirs * dirs, transcendentals=dirs),
        name="solve",
    )(grams)


def project(sends, send_mask, live, coupling, basis, keep, core, far, *refs):
    returned = refs[:4]
    remainder, next_basis, outgoing = refs[4:]
    blocks = basis.shape[0]
    slots = returned[0].shape[0]
    for b in range(blocks):
        remainder[b] = keep[b] + core[b] + far[b].astype(F32)
    for i, pieces in enumerate(returned):
        for s in range(slots):
            remainder[sends[i, s]] += pieces[s] * send_mask[i, s]
    for b in range(blocks):
        block = basis[b]
        image = live[b] * (remainder[b] + 1.0 * block.astype(F32))
        tall = jnp.concatenate([block] * 3, axis=0)
        rest = image - jnp.dot(coupling[...], tall, preferred_element_type=F32)
        remainder[b] = rest
        next_basis[b] = rest.astype(BF16)
    for i in range(4):
        for s in range(slots):
            outgoing[i * slots + s] = next_basis[sends[i, s]] * send_mask[i, s].astype(BF16)


def call_project(sends, send_mask, live, coupling, basis, keep, core, far, returned):
    blocks, dirs, width = basis.shape
    slots = returned[0].shape[0]
    return pl.pallas_call(
        project,
        in_specs=[SMEM] * 3 + [VMEM] * (5 + 4),
        out_specs=[VMEM] * 3,
        out_shape=[
            jax.ShapeDtypeStruct((blocks, dirs, width), F32),
            jax.ShapeDtypeStruct((blocks, dirs, width), BF16),
            jax.ShapeDtypeStruct((4 * slots, dirs, width), BF16),
        ],
        cost_estimate=pl.CostEstimate(
            flops=6 * blocks * dirs * dirs * width, bytes_accessed=20 * blocks * dirs * width, transcendentals=0
        ),
        name="project",
    )(sends, send_mask, live, coupling, basis, keep, core, far, *returned)


def on_device(directions, tiles, tile_cols, friction, neighbours, send_idx, send_count, row_counts):
    dom_count, sub_count = lax.axis_size("dom"), lax.axis_size("sub")
    blocks, dirs, width = directions.shape
    slots = send_idx.shape[2]
    neigh = send_idx.shape[1]
    part, me = lax.axis_index("dom"), lax.axis_index("sub")
    sub_bits, dom_bits = bits_of(sub_count), bits_of(dom_count)

    live = (jnp.arange(blocks) < row_counts[0]).astype(F32)
    odd, upper = part % 2, (part // 2) % 2
    order = jnp.stack([odd, 1 - odd, 2 + upper, 3 - upper])
    sends = send_idx[0][order]
    held = (neighbours[0] >= 0)[:, None] & (jnp.arange(slots)[None, :] < send_count[0][:, None])
    send_mask = held.astype(F32)[order]

    def place_of(sub):
        relative = jnp.bitwise_xor(sub, me)
        place = 0
        for i, bit in enumerate(sub_bits):
            place = place + jnp.where(jnp.bitwise_and(relative, bit) != 0, 1 << i, 0)
        return place

    own_columns = sub_count * blocks
    h = tile_cols - own_columns
    colour = (h // slots) % neigh
    pairing = jnp.where(colour < 2, jnp.bitwise_xor(colour, odd), jnp.bitwise_xor(colour, upper))
    halo_place = own_columns + place_of(h // (neigh * slots)) * neigh * slots + pairing * slots + h % slots
    own_place = place_of(tile_cols // blocks) * blocks + tile_cols % blocks
    cols = jnp.where(h < 0, own_place, halo_place).astype(jnp.int32)
    weight = live[:, None] * friction

    basis = directions * live[:, None, None].astype(BF16)
    outgoing = basis[sends.reshape(-1)] * send_mask.reshape(-1)[:, None, None].astype(BF16)
    remainder = None
    cross = None
    for step in range(ITERS):
        halo = [
            swap_pairs(outgoing[i * slots : (i + 1) * slots], by, lower)
            for i, (by, lower) in enumerate(PAIRINGS)
        ]
        own_parts, halo_parts = [basis], [jnp.concatenate(halo, axis=0)]
        for bit in sub_bits:
            own_parts = own_parts + [swap(x, "sub", bit) for x in own_parts]
            halo_parts = halo_parts + [swap(x, "sub", bit) for x in halo_parts]
        own_keep, own_send, halo_keep, halo_send, grams = call_forward_adjoint(
            cols, tiles, weight, own_parts + halo_parts
        )
        own_got = swap(own_send, "sub", sub_bits[-1])
        halo_got = swap(halo_send, "sub", sub_bits[-1])
        per = neigh * slots
        halo_far = swap((halo_keep[per:] + halo_got[per:]).astype(BF16), "sub", sub_bits[0])
        own_far = swap((own_keep[blocks:] + own_got[blocks:]).astype(BF16), "sub", sub_bits[0])
        back = halo_keep[:per] + halo_got[:per] + halo_far.astype(F32)
        returned = [
            swap_pairs(back[i * slots : (i + 1) * slots], by, lower)
            for i, (by, lower) in enumerate(PAIRINGS)
        ]
        for bit in reversed(sub_bits):
            grams = grams + swap(grams, "sub", bit)
        for bit in reversed(dom_bits):
            grams = grams + swap(grams, "dom", bit)
        cross = grams[:, dirs:]
        coupling = call_solve(grams)
        remainder, basis, outgoing = call_project(
            sends, send_mask, live, coupling, basis, own_keep[:blocks], own_got[:blocks], own_far, returned
        )
    return (remainder, cross)


def solution(mesh):
    in_specs = (
        P(("dom", "sub"), None, None),
        P(("dom", "sub"), None, None, None),
        P(("dom", "sub"), None),
        P(("dom", "sub"), None),
        P("dom", None),
        P(("dom", "sub"), None, None),
        P(("dom", "sub"), None),
        P(("dom", "sub")),
    )
    out_specs = (P(("dom", "sub"), None, None), P())
    return jax.shard_map(
        on_device, mesh=mesh, in_specs=in_specs, out_specs=out_specs, check_vma=False
    )
```

time: 440 us -> 160 us (0.36)
  blocking collectives: 113 us -> 0 us
  other arithmetic: 102 us -> 6.95 us
  waiting for transfers between devices: 83 us -> 32.6 us
  Pallas kernels: 0 us -> 40.7 us
  matrix products: 39.3 us -> 0 us
  local copies, waits for them, and re-layouts: 36.4 us -> 14.6 us
  starting transfers between devices: 48.1 us -> 62.2 us
  between operations: 15 us -> 1.77 us
    psum x2 -> x0, blocking collectives: 80.1 us -> none  [on_device(): lax.psum((local_basis, local_cross), ('dom', 'sub'))]
    reduce_scatter x4 -> x0, waiting for transfers between devices: 79.8 us -> none  [the longest x2 47.5 us: on_device(): lax.psum_scatter(summed[own_columns:], 'sub', scatter_dimension=0, tiled=...]
    scatter-add x4 -> x0, other arithmetic: 70.8 us -> none  [the longest x2 69 us: on_device(): jax.ops.segment_sum(contrib.reshape(-1, dirs_count, tile_width), flat_col...]
    pallas_call x0 -> x6, Pallas kernels: none -> 40.7 us  [the longest x2 21.7 us: call_forward_adjoint(): pl.pallas_call(functools.partial(forward_adjoint, n), in_specs=[SMEM] + [...]
    dot_general x8 -> x0, matrix products: 38.3 us -> none  [the longest x2 35.7 us: on_device(): jnp.einsum('rka,rjab->rjkb', weighted, tiles, preferred_element_type=jnp....]
    all_gather x4 -> x0, blocking collectives: 32.8 us -> none  [the longest x2 18.2 us: on_device(): own_rows = lax.all_gather(basis, 'sub', axis=0, tiled=True)]
    ppermute x16 -> x46, waiting for transfers between devices: 3.1 us -> 32.6 us  [the longest x30 30.2 us: swap(): return lax.ppermute(x, axis, [(i, i ^ bit) for i in range(peers)])]
    another operation x16 -> x0, other arithmetic: 26.4 us -> none  [the longest x6 13 us: on_device(): factor = jnp.linalg.cholesky(basis_total)]
  transfers between devices with their start and end apart: 20 -> 46, of which waited for: 7 -> 17; matrix products, arithmetic and copies ran while one was open for 2% -> 6% of each run, Pallas kernels for 0% -> 9%
where the time goes in v1:
time: 160 us; the launch traced here: 159 us
  starting transfers between devices  62.2 us (39%)
  Pallas kernels  40.7 us (25%)
  waiting for transfers between devices  32.6 us (20%)
  local copies, waits for them, and re-layouts  14.6 us (9%)
  other arithmetic  6.95 us (4%)
  between operations  1.77 us (1%)
    ppermute x30, starting transfers between devices, swap(): return lax.ppermute(x, axis, [(i, i ^ bit) for i in range(peers)])  32.5 us
    ppermute x30, waiting for transfers between devices, swap(): return lax.ppermute(x, axis, [(i, i ^ bit) for i in range(peers)])  30.2 us
    ppermute x16, starting transfers between devices, swap_pairs(): lax.ppermute(x, 'dom', [(p, p + by) for p in low] + [(p + by, p) for p in...  29.7 us
    pallas_call x2, Pallas kernels, call_forward_adjoint(): pl.pallas_call(functools.partial(forward_adjoint, n), in_specs=[SMEM] + [...  21.7 us
    pallas_call x2, Pallas kernels, call_solve(): pl.pallas_call(solve, in_specs=[VMEM], out_specs=VMEM, out_shape=jax.Shap...  14 us
    unnamed x42, local copies, waits for them, and re-layouts  10.4 us
    pallas_call x2, Pallas kernels, call_project(): pl.pallas_call(project, in_specs=[SMEM] * 3 + [VMEM] * (5 + 4), out_specs...  5.04 us
  transfers between devices with their start and end apart: 46, of which 17 were waited for; matrix products, arithmetic and copies ran while one was open for 6% of the time, Pallas kernels for 9%

profile of v1, /device:TPU:0, one launch (start us, length us, event | category | flops | bytes accessed | tf_op | source)
XLA Modules:
  0.0 158.9 jit_solution(142806782406088645)
XLA Ops:
  1.3 1.0 broadcast_multiply_fusion.refs_0_.basis
  2.8 2.6 %collective-permute-start = (bf16[12,64,128]{2,1,0:T(8,128)(2,1)S(1)}, bf16[12,64,128]{2,1,0:T(8,128)(2,1)S(1)}, u32[]{:S(2)}, u32[]{:S(2)}) collective-permute-start(bf16[12,64,128]{2,1,0:T(8,128)(2,1)S(1)} %broadcast_multiply_fusion.refs_0_.basis), channel_id=1, source_target_pairs={{0,2},{1,3},{2,0},{3,1},{4,6},{5,7},{6,4},{7,5},{8,10},{9,11},{10,... | collective-permute-start | bytes 589832 | tf_op jit(solution)/shard_map/ppermute | solution.py:24
  5.4 0.7 compare_bitcast_fusion
  6.1 0.8 copy.11
  6.9 0.7 fusion.17
  8.2 0.6 gather_fusion
  9.0 0.6 gather_fusion.2
  9.7 0.7 collective-permute-start.6
  10.3 4.5 %collective-permute-start.5 = (bf16[2,64,128]{2,1,0:T(8,128)(2,1)S(1)}, bf16[2,64,128]{2,1,0:T(8,128)(2,1)S(1)}, u32[]{:S(2)}, u32[]{:S(2)}) collective-permute-start(bf16[2,64,128]{2,1,0:T(8,128)(2,1)S(1)} %get-tuple-element.47), channel_id=1, source_target_pairs={{0,8},{4,12},{16,24},{20,28},{8,0},{12,4},{24,16},{28,20},{1,9},{5... | collective-permute-start | bytes 98312 | tf_op jit(solution)/shard_map/ppermute | solution.py:30
  14.8 1.5 collective-permute-start.3
  16.3 2.4 %collective-permute-done.3 = bf16[2,64,128]{2,1,0:T(8,128)(2,1)S(1)} collective-permute-done((bf16[2,64,128]{2,1,0:T(8,128)(2,1)S(1)}, bf16[2,64,128]{2,1,0:T(8,128)(2,1)S(1)}, u32[]{:S(2)}, u32[]{:S(2)}) %collective-permute-start.3) | collective-permute-done | bytes 32800 | tf_op jit(solution)/shard_map/ppermute | solution.py:30
  18.7 0.7 collective-permute-start.4
  19.5 0.6 collective-permute-start.7
  20.0 0.8 broadcast_multiply_fusion.2.weight
  20.8 3.7 %collective-permute-done.7.refs_5_ = bf16[8,64,128]{2,1,0:T(8,128)(2,1)S(1)} collective-permute-done((bf16[8,64,128]{2,1,0:T(8,128)(2,1)S(1)}, bf16[8,64,128]{2,1,0:T(8,128)(2,1)S(1)}, u32[]{:S(2)}, u32[]{:S(2)}) %collective-permute-start.7) | collective-permute-done | bytes 131104 | tf_op jit(solution)/shard_map/ppermute | solution.py:24
  25.0 0.7 fusion.8.cols
  26.1 4.0 %copy-done = bf16[12,27,128,128]{3,2,1,0:T(8,128)(2,1)S(1)} copy-done((bf16[12,27,128,128]{3,2,1,0:T(8,128)(2,1)S(1)}, bf16[12,27,128,128]{3,2,1,0:T(8,128)(2,1)}, u32[]{:S(2)}) %copy-start) | copy-done | bytes 10616856
  30.2 10.8 %forward_adjoint.2 = (f32[24,64,128]{2,1,0:T(8,128)S(1)}, f32[24,64,128]{2,1,0:T(8,128)S(1)}, f32[16,64,128]{2,1,0:T(8,128)S(1)}, f32[16,64,128]{2,1,0:T(8,128)S(1)}, f32[64,128]{1,0:T(8,128)S(1)}) custom-call(s32[12,27]{1,0:T(8,128)S(1)} %fusion.8.cols, bf16[12,27,128,128]{3,2,1,0:T(8,128)(2,1)S(1)} %copy-done, ...), custom_call_target="tpu_custom_call" | custom-call | flops 1358954496 | bytes 10616832 | tf_op jit(solution)/shard_map/forward_adjoint/pallas_call | solution.py:110
  41.9 1.1 collective-permute-done.17
  43.0 0.6 collective-permute-start.18
  44.2 1.0 collective-permute-start.11
  45.2 4.3 %collective-permute-done.11 = f32[64,128]{1,0:T(8,128)S(1)} collective-permute-done((f32[64,128]{1,0:T(8,128)S(1)}, f32[64,128]{1,0:T(8,128)S(1)}, u32[]{:S(2)}, u32[]{:S(2)}) %collective-permute-start.11) | collective-permute-done | bytes 32800 | tf_op jit(solution)/shard_map/ppermute | solution.py:24
  49.5 7.5 %collective-permute-start.12 = (f32[64,128]{1,0:T(8,128)S(1)}, f32[64,128]{1,0:T(8,128)S(1)}, u32[]{:S(2)}, u32[]{:S(2)}) collective-permute-start(f32[64,128]{1,0:T(8,128)S(1)} %add.137), channel_id=1, source_target_pairs={{0,4},{4,0},{8,12},{12,8},{16,20},{20,16},{24,28},{28,24},{1,5},{5... | collective-permute-start | bytes 98312 | tf_op jit(solution)/shard_map/ppermute | solution.py:24
  57.0 1.9 %collective-permute-done.12 = f32[64,128]{1,0:T(8,128)S(1)} collective-permute-done((f32[64,128]{1,0:T(8,128)S(1)}, f32[64,128]{1,0:T(8,128)S(1)}, u32[]{:S(2)}, u32[]{:S(2)}) %collective-permute-start.12) | collective-permute-done | bytes 32800 | tf_op jit(solution)/shard_map/ppermute | solution.py:24
  58.9 0.6 collective-permute-start.13
  59.5 3.3 %collective-permute-done.13 = f32[64,128]{1,0:T(8,128)S(1)} collective-permute-done((f32[64,128]{1,0:T(8,128)S(1)}, f32[64,128]{1,0:T(8,128)S(1)}, u32[]{:S(2)}, u32[]{:S(2)}) %collective-permute-start.13) | collective-permute-done | bytes 32800 | tf_op jit(solution)/shard_map/ppermute | solution.py:24
  63.4 1.0 fusion.1
  64.9 0.7 collective-permute-start.22
  65.6 4.3 %collective-permute-start.21 = (f32[2,64,128]{2,1,0:T(8,128)S(1)}, f32[2,64,128]{2,1,0:T(8,128)S(1)}, u32[]{:S(2)}, u32[]{:S(2)}) collective-permute-start(f32[2,64,128]{2,1,0:T(8,128)S(1)} %get-tuple-element.39), channel_id=1, source_target_pairs={{0,8},{4,12},{16,24},{20,28},{8,0},{12,4},{24,16},{28,20},{1,9},{5... | collective-permute-start | bytes 196616 | tf_op jit(solution)/shard_map/ppermute | solution.py:30
  69.9 0.7 collective-permute-start.20
  70.6 3.3 %collective-permute-start.19 = (f32[2,64,128]{2,1,0:T(8,128)S(1)}, f32[2,64,128]{2,1,0:T(8,128)S(1)}, u32[]{:S(2)}, u32[]{:S(2)}) collective-permute-start(f32[2,64,128]{2,1,0:T(8,128)S(1)} %get-tuple-element.41), channel_id=1, source_target_pairs={{0,4},{8,12},{16,20},{24,28},{4,0},{12,8},{20,16},{28,24},{1,5},{9... | collective-permute-start | bytes 196616 | tf_op jit(solution)/shard_map/ppermute | solution.py:30
  73.9 0.6 add.140.grams
  74.5 7.0 %solve.2.coupling = bf16[64,192]{1,0:T(8,128)(2,1)} custom-call(f32[64,128]{1,0:T(8,128)} %add.140.grams), custom_call_target="tpu_custom_call" | custom-call | flops 1048576 | bytes 49152 | tf_op jit(solution)/shard_map/solve/pallas_call | solution.py:149
  82.3 2.5 %project.2 = (f32[12,64,128]{2,1,0:T(8,128)}, bf16[12,64,128]{2,1,0:T(8,128)(2,1)}, bf16[8,64,128]{2,1,0:T(8,128)(2,1)}) custom-call(s32[4,2]{1,0:T(4,128)} %copy-done.15, f32[4,2]{1,0:T(4,128)} %copy-done.16, f32[12]{0:T(128)} %copy-done.17, bf16[64,192]{1,0:T(8,128)(2,1)} %solve.2.coupling, bf16[12,64,128]{2,1,0:T(8,128)(2,1)} %copy-done.2, ...), custom_call_target="tpu_custom_call" | custom-call | flops 37748736 | bytes 1966080 | tf_op jit(solution)/shard_map/project/pallas_call | solution.py:184
  84.8 0.8 fusion.23
  85.7 0.7 collective-permute-start.29
  86.4 4.8 %collective-permute-start.28 = (bf16[2,64,128]{2,1,0:T(8,128)(2,1)S(1)}, bf16[2,64,128]{2,1,0:T(8,128)(2,1)S(1)}, u32[]{:S(2)}, u32[]{:S(2)}) collective-permute-start(bf16[2,64,128]{2,1,0:T(8,128)(2,1)S(1)} %get-tuple-element.43), channel_id=1, source_target_pairs={{0,8},{4,12},{16,24},{20,28},{8,0},{12,4},{24,16},{28,20},{1,9},{5... | collective-permute-start | bytes 98312 | tf_op jit(solution)/shard_map/ppermute | solution.py:30
  91.2 0.7 collective-permute-start.27
  91.9 1.6 %collective-permute-start.23 = (bf16[12,64,128]{2,1,0:T(8,128)(2,1)}, bf16[12,64,128]{2,1,0:T(8,128)(2,1)S(1)}, u32[]{:S(2)}, u32[]{:S(2)}) collective-permute-start(bf16[12,64,128]{2,1,0:T(8,128)(2,1)} %get-tuple-element.20.refs_0_.basis), channel_id=1, source_target_pairs={{0,2},{1,3},{2,0},{3,1},{4,6},{5,7},{6,4},{7,5},{8,10},{9,11},{10,... | collective-permute-start | bytes 589832 | tf_op jit(solution)/shard_map/ppermute | solution.py:24
  93.5 1.2 collective-permute-start.30
  94.7 3.1 %collective-permute-done.23.refs_1_ = bf16[12,64,128]{2,1,0:T(8,128)(2,1)S(1)} collective-permute-done((bf16[12,64,128]{2,1,0:T(8,128)(2,1)}, bf16[12,64,128]{2,1,0:T(8,128)(2,1)S(1)}, u32[]{:S(2)}, u32[]{:S(2)}) %collective-permute-start.23) | collective-permute-done | bytes 196640 | tf_op jit(solution)/shard_map/ppermute | solution.py:24
  98.3 0.9 collective-permute-done.30.refs_5_
  99.4 1.1 collective-permute-done.32.refs_7_
  100.6 4.0 %copy-done.1 = bf16[12,27,128,128]{3,2,1,0:T(8,128)(2,1)S(1)} copy-done((bf16[12,27,128,128]{3,2,1,0:T(8,128)(2,1)S(1)}, bf16[12,27,128,128]{3,2,1,0:T(8,128)(2,1)}, u32[]{:S(2)}) %copy-start.1) | copy-done | bytes 10616856
  104.6 0.9 copy-done.3
  105.5 10.9 %forward_adjoint.3 = (f32[24,64,128]{2,1,0:T(8,128)S(1)}, f32[24,64,128]{2,1,0:T(8,128)S(1)}, f32[16,64,128]{2,1,0:T(8,128)S(1)}, f32[16,64,128]{2,1,0:T(8,128)S(1)}, f32[64,128]{1,0:T(8,128)S(1)}) custom-call(s32[12,27]{1,0:T(8,128)S(1)} %fusion.8.cols, bf16[12,27,128,128]{3,2,1,0:T(8,128)(2,1)S(1)} %copy-done.1, ...), custom_call_target="tpu_custom_call" | custom-call | flops 1358954496 | bytes 10616832 | tf_op jit(solution)/shard_map/forward_adjoint/pallas_call | solution.py:110
  117.1 1.3 collective-permute-done.40
  118.4 1.6 collective-permute-start.41
  120.0 1.1 collective-permute-start.34
  121.0 3.6 %collective-permute-done.34 = f32[64,128]{1,0:T(8,128)S(1)} collective-permute-done((f32[64,128]{1,0:T(8,128)S(1)}, f32[64,128]{1,0:T(8,128)S(1)}, u32[]{:S(2)}, u32[]{:S(2)}) %collective-permute-start.34) | collective-permute-done | bytes 32800 | tf_op jit(solution)/shard_map/ppermute | solution.py:24
  124.7 4.7 %collective-permute-start.35 = (f32[64,128]{1,0:T(8,128)S(1)}, f32[64,128]{1,0:T(8,128)S(1)}, u32[]{:S(2)}, u32[]{:S(2)}) collective-permute-start(f32[64,128]{1,0:T(8,128)S(1)} %add.146), channel_id=1, source_target_pairs={{0,4},{4,0},{8,12},{12,8},{16,20},{20,16},{24,28},{28,24},{1,5},{5... | collective-permute-start | bytes 98312 | tf_op jit(solution)/shard_map/ppermute | solution.py:24
  129.4 1.9 %collective-permute-done.35 = f32[64,128]{1,0:T(8,128)S(1)} collective-permute-done((f32[64,128]{1,0:T(8,128)S(1)}, f32[64,128]{1,0:T(8,128)S(1)}, u32[]{:S(2)}, u32[]{:S(2)}) %collective-permute-start.35) | collective-permute-done | bytes 32800 | tf_op jit(solution)/shard_map/ppermute | solution.py:24
  131.3 1.1 collective-permute-start.36
  132.4 2.8 %collective-permute-done.36 = f32[64,128]{1,0:T(8,128)S(1)} collective-permute-done((f32[64,128]{1,0:T(8,128)S(1)}, f32[64,128]{1,0:T(8,128)S(1)}, u32[]{:S(2)}, u32[]{:S(2)}) %collective-permute-start.36) | collective-permute-done | bytes 32800 | tf_op jit(solution)/shard_map/ppermute | solution.py:24
  135.2 2.6 %collective-permute-start.37 = (f32[64,128]{1,0:T(8,128)S(1)}, f32[64,128]{1,0:T(8,128)S(1)}, u32[]{:S(2)}, u32[]{:S(2)}) collective-permute-start(f32[64,128]{1,0:T(8,128)S(1)} %add.148), channel_id=1, source_target_pairs={{0,16},{4,20},{8,24},{12,28},{16,0},{20,4},{24,8},{28,12},{1,17},{... | collective-permute-start | bytes 98312 | tf_op jit(solution)/shard_map/ppermute | solution.py:24
  137.9 1.0 fusion
  139.0 1.5 collective-permute-start.39
  140.5 0.7 collective-permute-start.45
  141.2 3.2 %collective-permute-start.44 = (f32[2,64,128]{2,1,0:T(8,128)S(1)}, f32[2,64,128]{2,1,0:T(8,128)S(1)}, u32[]{:S(2)}, u32[]{:S(2)}) collective-permute-start(f32[2,64,128]{2,1,0:T(8,128)S(1)} %get-tuple-element.35), channel_id=1, source_target_pairs={{0,8},{4,12},{16,24},{20,28},{8,0},{12,4},{24,16},{28,20},{1,9},{5... | collective-permute-start | bytes 196616 | tf_op jit(solution)/shard_map/ppermute | solution.py:30
  144.4 0.7 collective-permute-start.43
  145.1 2.8 %collective-permute-start.42 = (f32[2,64,128]{2,1,0:T(8,128)S(1)}, f32[2,64,128]{2,1,0:T(8,128)S(1)}, u32[]{:S(2)}, u32[]{:S(2)}) collective-permute-start(f32[2,64,128]{2,1,0:T(8,128)S(1)} %get-tuple-element.37), channel_id=1, source_target_pairs={{0,4},{8,12},{16,20},{24,28},{4,0},{12,8},{20,16},{28,24},{1,5},{9... | collective-permute-start | bytes 196616 | tf_op jit(solution)/shard_map/ppermute | solution.py:30
  147.9 0.7 slice.158
  148.6 7.0 %solve.3.coupling = bf16[64,192]{1,0:T(8,128)(2,1)} custom-call(f32[64,128]{1,0:T(8,128)} %copy-done.4), custom_call_target="tpu_custom_call" | custom-call | flops 1048576 | bytes 49152 | tf_op jit(solution)/shard_map/solve/pallas_call | solution.py:149
  156.4 2.5 %project.3 = (f32[12,64,128]{2,1,0:T(8,128)}, bf16[12,64,128]{2,1,0:T(8,128)(2,1)}, bf16[8,64,128]{2,1,0:T(8,128)(2,1)}) custom-call(s32[4,2]{1,0:T(4,128)} %copy-done.15, f32[4,2]{1,0:T(4,128)} %copy-done.16, f32[12]{0:T(128)} %copy-done.17, bf16[64,192]{1,0:T(8,128)(2,1)} %solve.3.coupling, bf16[12,64,128]{2,1,0:T(8,128)(2,1)} %get-tuple-element.20.refs_0_.basis, ...), custom_call_target="tpu_custom_call" | custom-call | flops 37748736 | bytes 1966080 | tf_op jit(solution)/shard_map/project/pallas_call | solution.py:184
  (118 shorter events, 8.1 us)
Async XLA Ops:
  2.3 79.3 %copy-start.2 = (bf16[12,64,128]{2,1,0:T(8,128)(2,1)}, bf16[12,64,128]{2,1,0:T(8,128)(2,1)S(1)}, u32[]{:S(2)}) copy-start(bf16[12,64,128]{2,1,0:T(8,128)(2,1)S(1)} %broadcast_multiply_fusion.refs_0_.basis) | copy-start | bytes 589828
  2.3 23.5 %collective-permute-start.1 = (bf16[12,64,128]{2,1,0:T(8,128)(2,1)S(1)}, bf16[12,64,128]{2,1,0:T(8,128)(2,1)S(1)}, u32[]{:S(2)}, u32[]{:S(2)}) collective-permute-start(bf16[12,64,128]{2,1,0:T(8,128)(2,1)S(1)} %broadcast_multiply_fusion.refs_0_.basis), channel_id=1, source_target_pairs={{0,1},{1,0},{2,3},{3,2},{4,5},{5,4},{6,7},{7,6},{8,9},{9,8},{10,11... | collective-permute-start | bytes 589832 | tf_op jit(solution)/shard_map/ppermute | solution.py:24
  2.8 21.7 %collective-permute-start = (bf16[12,64,128]{2,1,0:T(8,128)(2,1)S(1)}, bf16[12,64,128]{2,1,0:T(8,128)(2,1)S(1)}, u32[]{:S(2)}, u32[]{:S(2)}) collective-permute-start(bf16[12,64,128]{2,1,0:T(8,128)(2,1)S(1)} %broadcast_multiply_fusion.refs_0_.basis), channel_id=1, source_target_pairs={{0,2},{1,3},{2,0},{3,1},{4,6},{5,7},{6,4},{7,5},{8,10},{9,11},{10,... | collective-permute-start | bytes 589832 | tf_op jit(solution)/shard_map/ppermute | solution.py:24
  8.2 73.4 %copy-start.16 = (f32[4,2]{1,0:T(4,128)}, f32[4,2]{1,0:T(4,128)S(1)}, u32[]{:S(2)}) copy-start(f32[4,2]{1,0:T(4,128)S(1)} %gather_fusion.1) | copy-start | bytes 100
  8.8 72.8 %copy-start.15 = (s32[4,2]{1,0:T(4,128)}, s32[4,2]{1,0:T(4,128)S(1)}, u32[]{:S(2)}) copy-start(s32[4,2]{1,0:T(4,128)S(1)} %gather_fusion) | copy-start | bytes 100
  9.7 9.8 %collective-permute-start.6 = (bf16[2,64,128]{2,1,0:T(8,128)(2,1)S(1)}, bf16[2,64,128]{2,1,0:T(8,128)(2,1)S(1)}, u32[]{:S(2)}, u32[]{:S(2)}) collective-permute-start(bf16[2,64,128]{2,1,0:T(8,128)(2,1)S(1)} %get-tuple-element.46), channel_id=1, source_target_pairs={{8,16},{12,20},{16,8},{20,12},{9,17},{13,21},{17,9},{21,13},{10,18... | collective-permute-start | bytes 98312 | tf_op jit(solution)/shard_map/ppermute | solution.py:30
  10.3 9.1 %collective-permute-start.5 = (bf16[2,64,128]{2,1,0:T(8,128)(2,1)S(1)}, bf16[2,64,128]{2,1,0:T(8,128)(2,1)S(1)}, u32[]{:S(2)}, u32[]{:S(2)}) collective-permute-start(bf16[2,64,128]{2,1,0:T(8,128)(2,1)S(1)} %get-tuple-element.47), channel_id=1, source_target_pairs={{0,8},{4,12},{16,24},{20,28},{8,0},{12,4},{24,16},{28,20},{1,9},{5... | collective-permute-start | bytes 98312 | tf_op jit(solution)/shard_map/ppermute | solution.py:30
  14.8 3.9 %collective-permute-start.3 = (bf16[2,64,128]{2,1,0:T(8,128)(2,1)S(1)}, bf16[2,64,128]{2,1,0:T(8,128)(2,1)S(1)}, u32[]{:S(2)}, u32[]{:S(2)}) collective-permute-start(bf16[2,64,128]{2,1,0:T(8,128)(2,1)S(1)} %get-tuple-element.49), channel_id=1, source_target_pairs={{0,4},{8,12},{16,20},{24,28},{4,0},{12,8},{20,16},{28,24},{1,5},{9... | collective-permute-start | bytes 98312 | tf_op jit(solution)/shard_map/ppermute | solution.py:30
  16.3 65.3 %copy-start.17 = (f32[12]{0:T(128)}, f32[12]{0:T(128)S(1)}, u32[]{:S(2)}) copy-start(f32[12]{0:T(128)S(1)} %compare_convert_fusion.live) | copy-start | bytes 148
  18.7 0.7 collective-permute-start.4
  19.5 5.0 %collective-permute-start.7 = (bf16[8,64,128]{2,1,0:T(8,128)(2,1)S(1)}, bf16[8,64,128]{2,1,0:T(8,128)(2,1)S(1)}, u32[]{:S(2)}, u32[]{:S(2)}) collective-permute-start(bf16[8,64,128]{2,1,0:T(8,128)(2,1)S(1)} %constant_dynamic-update-slice_fusion.refs_4_), channel_id=1, source_target_pairs={{0,2},{1,3},{2,0},{3,1},{4,6},{5,7},{6,4},{7,5},{8,10},{9,11},{10,... | collective-permute-start | bytes 393224 | tf_op jit(solution)/shard_map/ppermute | solution.py:24
  20.8 4.9 %collective-permute-start.8 = (bf16[8,64,128]{2,1,0:T(8,128)(2,1)S(1)}, bf16[8,64,128]{2,1,0:T(8,128)(2,1)S(1)}, u32[]{:S(2)}, u32[]{:S(2)}) collective-permute-start(bf16[8,64,128]{2,1,0:T(8,128)(2,1)S(1)} %constant_dynamic-update-slice_fusion.refs_4_), channel_id=1, source_target_pairs={{0,1},{1,0},{2,3},{3,2},{4,5},{5,4},{6,7},{7,6},{8,9},{9,8},{10,11... | collective-permute-start | bytes 393224 | tf_op jit(solution)/shard_map/ppermute | solution.py:24
  24.5 1.3 collective-permute-start.9
  24.5 1.6 %collective-permute-start.2 = (bf16[12,64,128]{2,1,0:T(8,128)(2,1)S(1)}, bf16[12,64,128]{2,1,0:T(8,128)(2,1)S(1)}, u32[]{:S(2)}, u32[]{:S(2)}) collective-permute-start(bf16[12,64,128]{2,1,0:T(8,128)(2,1)S(1)} %collective-permute-done.refs_1_), channel_id=1, source_target_pairs={{0,1},{1,0},{2,3},{3,2},{4,5},{5,4},{6,7},{7,6},{8,9},{9,8},{10,11... | collective-permute-start | bytes 589832 | tf_op jit(solution)/shard_map/ppermute | solution.py:24
  26.1 4.0 %copy-start = (bf16[12,27,128,128]{3,2,1,0:T(8,128)(2,1)S(1)}, bf16[12,27,128,128]{3,2,1,0:T(8,128)(2,1)}, u32[]{:S(2)}) copy-start(bf16[12,27,128,128]{3,2,1,0:T(8,128)(2,1)} %tiles.3) | copy-start | bytes 31850500
  41.0 2.0 %collective-permute-start.17 = (f32[16,64,128]{2,1,0:T(8,128)S(1)}, f32[16,64,128]{2,1,0:T(8,128)S(1)}, u32[]{:S(2)}, u32[]{:S(2)}) collective-permute-start(f32[16,64,128]{2,1,0:T(8,128)S(1)} %get-tuple-element.19), channel_id=1, source_target_pairs={{0,1},{1,0},{2,3},{3,2},{4,5},{5,4},{6,7},{7,6},{8,9},{9,8},{10,11... | collective-permute-start | bytes 1572872 | tf_op jit(solution)/shard_map/ppermute | solution.py:24
  41.4 22.0 %collective-permute-start.15 = (f32[24,64,128]{2,1,0:T(8,128)S(1)}, f32[24,64,128]{2,1,0:T(8,128)S(1)}, u32[]{:S(2)}, u32[]{:S(2)}) collective-permute-start(f32[24,64,128]{2,1,0:T(8,128)S(1)} %get-tuple-element.17), channel_id=1, source_target_pairs={{0,1},{1,0},{2,3},{3,2},{4,5},{5,4},{6,7},{7,6},{8,9},{9,8},{10,11... | collective-permute-start | bytes 2359304 | tf_op jit(solution)/shard_map/ppermute | solution.py:24
  41.6 2.6 %collective-permute-start.10 = (f32[64,128]{1,0:T(8,128)S(1)}, f32[64,128]{1,0:T(8,128)S(1)}, u32[]{:S(2)}, u32[]{:S(2)}) collective-permute-start(f32[64,128]{1,0:T(8,128)S(1)} %get-tuple-element.15), channel_id=1, source_target_pairs={{0,1},{1,0},{2,3},{3,2},{4,5},{5,4},{6,7},{7,6},{8,9},{9,8},{10,11... | collective-permute-start | bytes 98312 | tf_op jit(solution)/shard_map/ppermute | solution.py:24
  43.0 20.3 %collective-permute-start.18 = (bf16[8,64,128]{2,1,0:T(8,128)(2,1)S(1)}, bf16[8,64,128]{2,1,0:T(8,128)(2,1)S(1)}, u32[]{:S(2)}, u32[]{:S(2)}) collective-permute-start(bf16[8,64,128]{2,1,0:T(8,128)(2,1)S(1)} %fusion.4), channel_id=1, source_target_pairs={{0,2},{1,3},{2,0},{3,1},{4,6},{5,7},{6,4},{7,5},{8,10},{9,11},{10,... | collective-permute-start | bytes 393224 | tf_op jit(solution)/shard_map/ppermute | solution.py:24
  44.2 5.4 %collective-permute-start.11 = (f32[64,128]{1,0:T(8,128)S(1)}, f32[64,128]{1,0:T(8,128)S(1)}, u32[]{:S(2)}, u32[]{:S(2)}) collective-permute-start(f32[64,128]{1,0:T(8,128)S(1)} %add.136), channel_id=1, source_target_pairs={{0,2},{1,3},{2,0},{3,1},{4,6},{5,7},{6,4},{7,5},{8,10},{9,11},{10,... | collective-permute-start | bytes 98312 | tf_op jit(solution)/shard_map/ppermute | solution.py:24
  49.5 9.4 %collective-permute-start.12 = (f32[64,128]{1,0:T(8,128)S(1)}, f32[64,128]{1,0:T(8,128)S(1)}, u32[]{:S(2)}, u32[]{:S(2)}) collective-permute-start(f32[64,128]{1,0:T(8,128)S(1)} %add.137), channel_id=1, source_target_pairs={{0,4},{4,0},{8,12},{12,8},{16,20},{20,16},{24,28},{28,24},{1,5},{5... | collective-permute-start | bytes 98312 | tf_op jit(solution)/shard_map/ppermute | solution.py:24
  58.9 3.9 %collective-permute-start.13 = (f32[64,128]{1,0:T(8,128)S(1)}, f32[64,128]{1,0:T(8,128)S(1)}, u32[]{:S(2)}, u32[]{:S(2)}) collective-permute-start(f32[64,128]{1,0:T(8,128)S(1)} %add.138), channel_id=1, source_target_pairs={{0,8},{4,12},{8,0},{12,4},{16,24},{20,28},{24,16},{28,20},{1,9},{5... | collective-permute-start | bytes 98312 | tf_op jit(solution)/shard_map/ppermute | solution.py:24
  62.9 7.7 %collective-permute-start.14 = (f32[64,128]{1,0:T(8,128)S(1)}, f32[64,128]{1,0:T(8,128)S(1)}, u32[]{:S(2)}, u32[]{:S(2)}) collective-permute-start(f32[64,128]{1,0:T(8,128)S(1)} %add.139), channel_id=1, source_target_pairs={{0,16},{4,20},{8,24},{12,28},{16,0},{20,4},{24,8},{28,12},{1,17},{... | collective-permute-start | bytes 98312 | tf_op jit(solution)/shard_map/ppermute | solution.py:24
  64.4 17.2 %collective-permute-start.16 = (bf16[12,64,128]{2,1,0:T(8,128)(2,1)S(1)}, bf16[12,64,128]{2,1,0:T(8,128)(2,1)S(1)}, u32[]{:S(2)}, u32[]{:S(2)}) collective-permute-start(bf16[12,64,128]{2,1,0:T(8,128)(2,1)S(1)} %get-tuple-element.31), channel_id=1, source_target_pairs={{0,2},{1,3},{2,0},{3,1},{4,6},{5,7},{6,4},{7,5},{8,10},{9,11},{10,... | collective-permute-start | bytes 589832 | tf_op jit(solution)/shard_map/ppermute | solution.py:24
  64.9 16.6 %collective-permute-start.22 = (f32[2,64,128]{2,1,0:T(8,128)S(1)}, f32[2,64,128]{2,1,0:T(8,128)S(1)}, u32[]{:S(2)}, u32[]{:S(2)}) collective-permute-start(f32[2,64,128]{2,1,0:T(8,128)S(1)} %get-tuple-element.38), channel_id=1, source_target_pairs={{8,16},{12,20},{16,8},{20,12},{9,17},{13,21},{17,9},{21,13},{10,18... | collective-permute-start | bytes 196616 | tf_op jit(solution)/shard_map/ppermute | solution.py:30
  65.6 15.9 %collective-permute-start.21 = (f32[2,64,128]{2,1,0:T(8,128)S(1)}, f32[2,64,128]{2,1,0:T(8,128)S(1)}, u32[]{:S(2)}, u32[]{:S(2)}) collective-permute-start(f32[2,64,128]{2,1,0:T(8,128)S(1)} %get-tuple-element.39), channel_id=1, source_target_pairs={{0,8},{4,12},{16,24},{20,28},{8,0},{12,4},{24,16},{28,20},{1,9},{5... | collective-permute-start | bytes 196616 | tf_op jit(solution)/shard_map/ppermute | solution.py:30
  69.9 11.6 %collective-permute-start.20 = (f32[2,64,128]{2,1,0:T(8,128)S(1)}, f32[2,64,128]{2,1,0:T(8,128)S(1)}, u32[]{:S(2)}, u32[]{:S(2)}) collective-permute-start(f32[2,64,128]{2,1,0:T(8,128)S(1)} %get-tuple-element.40), channel_id=1, source_target_pairs={{4,8},{12,16},{20,24},{8,4},{16,12},{24,20},{5,9},{13,17},{21,25},... | collective-permute-start | bytes 196616 | tf_op jit(solution)/shard_map/ppermute | solution.py:30
  70.6 11.0 %collective-permute-start.19 = (f32[2,64,128]{2,1,0:T(8,128)S(1)}, f32[2,64,128]{2,1,0:T(8,128)S(1)}, u32[]{:S(2)}, u32[]{:S(2)}) collective-permute-start(f32[2,64,128]{2,1,0:T(8,128)S(1)} %get-tuple-element.41), channel_id=1, source_target_pairs={{0,4},{8,12},{16,20},{24,28},{4,0},{12,8},{20,16},{28,24},{1,5},{9... | collective-permute-start | bytes 196616 | tf_op jit(solution)/shard_map/ppermute | solution.py:30
  81.5 0.6 copy-start.9
  81.5 0.6 copy-start.11
  81.5 0.7 copy-start.12
  81.6 0.7 copy-start.14
  81.6 0.7 copy-start.6
  85.7 7.8 %collective-permute-start.26 = (bf16[2,64,128]{2,1,0:T(8,128)(2,1)S(1)}, bf16[2,64,128]{2,1,0:T(8,128)(2,1)S(1)}, u32[]{:S(2)}, u32[]{:S(2)}) collective-permute-start(bf16[2,64,128]{2,1,0:T(8,128)(2,1)S(1)} %get-tuple-element.45), channel_id=1, source_target_pairs={{0,4},{8,12},{16,20},{24,28},{4,0},{12,8},{20,16},{28,24},{1,5},{9... | collective-permute-start | bytes 98312 | tf_op jit(solution)/shard_map/ppermute | solution.py:30
  85.7 7.8 %collective-permute-start.29 = (bf16[2,64,128]{2,1,0:T(8,128)(2,1)S(1)}, bf16[2,64,128]{2,1,0:T(8,128)(2,1)S(1)}, u32[]{:S(2)}, u32[]{:S(2)}) collective-permute-start(bf16[2,64,128]{2,1,0:T(8,128)(2,1)S(1)} %get-tuple-element.42), channel_id=1, source_target_pairs={{8,16},{12,20},{16,8},{20,12},{9,17},{13,21},{17,9},{21,13},{10,18... | collective-permute-start | bytes 98312 | tf_op jit(solution)/shard_map/ppermute | solution.py:30
  86.4 7.1 %collective-permute-start.28 = (bf16[2,64,128]{2,1,0:T(8,128)(2,1)S(1)}, bf16[2,64,128]{2,1,0:T(8,128)(2,1)S(1)}, u32[]{:S(2)}, u32[]{:S(2)}) collective-permute-start(bf16[2,64,128]{2,1,0:T(8,128)(2,1)S(1)} %get-tuple-element.43), channel_id=1, source_target_pairs={{0,8},{4,12},{16,24},{20,28},{8,0},{12,4},{24,16},{28,20},{1,9},{5... | collective-permute-start | bytes 98312 | tf_op jit(solution)/shard_map/ppermute | solution.py:30
  91.2 2.3 %collective-permute-start.27 = (bf16[2,64,128]{2,1,0:T(8,128)(2,1)S(1)}, bf16[2,64,128]{2,1,0:T(8,128)(2,1)S(1)}, u32[]{:S(2)}, u32[]{:S(2)}) collective-permute-start(bf16[2,64,128]{2,1,0:T(8,128)(2,1)S(1)} %get-tuple-element.44), channel_id=1, source_target_pairs={{4,8},{12,16},{20,24},{8,4},{16,12},{24,20},{5,9},{13,17},{21,25},... | collective-permute-start | bytes 98312 | tf_op jit(solution)/shard_map/ppermute | solution.py:30
  91.9 5.9 %collective-permute-start.23 = (bf16[12,64,128]{2,1,0:T(8,128)(2,1)}, bf16[12,64,128]{2,1,0:T(8,128)(2,1)S(1)}, u32[]{:S(2)}, u32[]{:S(2)}) collective-permute-start(bf16[12,64,128]{2,1,0:T(8,128)(2,1)} %get-tuple-element.20.refs_0_.basis), channel_id=1, source_target_pairs={{0,2},{1,3},{2,0},{3,1},{4,6},{5,7},{6,4},{7,5},{8,10},{9,11},{10,... | collective-permute-start | bytes 589832 | tf_op jit(solution)/shard_map/ppermute | solution.py:24
  93.5 5.7 %collective-permute-start.30 = (bf16[8,64,128]{2,1,0:T(8,128)(2,1)S(1)}, bf16[8,64,128]{2,1,0:T(8,128)(2,1)S(1)}, u32[]{:S(2)}, u32[]{:S(2)}) collective-permute-start(bf16[8,64,128]{2,1,0:T(8,128)(2,1)S(1)} %constant_dynamic-update-slice_fusion.4.refs_4_), channel_id=1, source_target_pairs={{0,2},{1,3},{2,0},{3,1},{4,6},{5,7},{6,4},{7,5},{8,10},{9,11},{10,... | collective-permute-start | bytes 393224 | tf_op jit(solution)/shard_map/ppermute | solution.py:24
  94.7 4.7 %collective-permute-start.24 = (bf16[12,64,128]{2,1,0:T(8,128)(2,1)}, bf16[12,64,128]{2,1,0:T(8,128)(2,1)S(1)}, u32[]{:S(2)}, u32[]{:S(2)}) collective-permute-start(bf16[12,64,128]{2,1,0:T(8,128)(2,1)} %get-tuple-element.20.refs_0_.basis), channel_id=1, source_target_pairs={{0,1},{1,0},{2,3},{3,2},{4,5},{5,4},{6,7},{7,6},{8,9},{9,8},{10,11... | collective-permute-start | bytes 589832 | tf_op jit(solution)/shard_map/ppermute | solution.py:24
  97.8 2.8 %collective-permute-start.25 = (bf16[12,64,128]{2,1,0:T(8,128)(2,1)S(1)}, bf16[12,64,128]{2,1,0:T(8,128)(2,1)S(1)}, u32[]{:S(2)}, u32[]{:S(2)}) collective-permute-start(bf16[12,64,128]{2,1,0:T(8,128)(2,1)S(1)} %collective-permute-done.23.refs_1_), channel_id=1, source_target_pairs={{0,1},{1,0},{2,3},{3,2},{4,5},{5,4},{6,7},{7,6},{8,9},{9,8},{10,11... | collective-permute-start | bytes 589832 | tf_op jit(solution)/shard_map/ppermute | solution.py:24
  97.8 1.6 %collective-permute-start.31 = (bf16[8,64,128]{2,1,0:T(8,128)(2,1)S(1)}, bf16[8,64,128]{2,1,0:T(8,128)(2,1)S(1)}, u32[]{:S(2)}, u32[]{:S(2)}) collective-permute-start(bf16[8,64,128]{2,1,0:T(8,128)(2,1)S(1)} %constant_dynamic-update-slice_fusion.4.refs_4_), channel_id=1, source_target_pairs={{0,1},{1,0},{2,3},{3,2},{4,5},{5,4},{6,7},{7,6},{8,9},{9,8},{10,11... | collective-permute-start | bytes 393224 | tf_op jit(solution)/shard_map/ppermute | solution.py:24
  99.2 1.3 collective-permute-start.32
  100.6 4.0 %copy-start.1 = (bf16[12,27,128,128]{3,2,1,0:T(8,128)(2,1)S(1)}, bf16[12,27,128,128]{3,2,1,0:T(8,128)(2,1)}, u32[]{:S(2)}) copy-start(bf16[12,27,128,128]{3,2,1,0:T(8,128)(2,1)} %tiles.3) | copy-start | bytes 31850500
  104.6 0.9 copy-start.3
  116.4 2.0 %collective-permute-start.40 = (f32[16,64,128]{2,1,0:T(8,128)S(1)}, f32[16,64,128]{2,1,0:T(8,128)S(1)}, u32[]{:S(2)}, u32[]{:S(2)}) collective-permute-start(f32[16,64,128]{2,1,0:T(8,128)S(1)} %get-tuple-element.26), channel_id=1, source_target_pairs={{0,1},{1,0},{2,3},{3,2},{4,5},{5,4},{6,7},{7,6},{8,9},{9,8},{10,11... | collective-permute-start | bytes 1572872 | tf_op jit(solution)/shard_map/ppermute | solution.py:24
  116.6 21.4 %collective-permute-start.38 = (f32[24,64,128]{2,1,0:T(8,128)S(1)}, f32[24,64,128]{2,1,0:T(8,128)S(1)}, u32[]{:S(2)}, u32[]{:S(2)}) collective-permute-start(f32[24,64,128]{2,1,0:T(8,128)S(1)} %get-tuple-element.24), channel_id=1, source_target_pairs={{0,1},{1,0},{2,3},{3,2},{4,5},{5,4},{6,7},{7,6},{8,9},{9,8},{10,11... | collective-permute-start | bytes 2359304 | tf_op jit(solution)/shard_map/ppermute | solution.py:24
  116.9 3.0 %collective-permute-start.33 = (f32[64,128]{1,0:T(8,128)S(1)}, f32[64,128]{1,0:T(8,128)S(1)}, u32[]{:S(2)}, u32[]{:S(2)}) collective-permute-start(f32[64,128]{1,0:T(8,128)S(1)} %get-tuple-element.22), channel_id=1, source_target_pairs={{0,1},{1,0},{2,3},{3,2},{4,5},{5,4},{6,7},{7,6},{8,9},{9,8},{10,11... | collective-permute-start | bytes 98312 | tf_op jit(solution)/shard_map/ppermute | solution.py:24
  118.4 19.5 %collective-permute-start.41 = (bf16[8,64,128]{2,1,0:T(8,128)(2,1)S(1)}, bf16[8,64,128]{2,1,0:T(8,128)(2,1)S(1)}, u32[]{:S(2)}, u32[]{:S(2)}) collective-permute-start(bf16[8,64,128]{2,1,0:T(8,128)(2,1)S(1)} %fusion.2), channel_id=1, source_target_pairs={{0,2},{1,3},{2,0},{3,1},{4,6},{5,7},{6,4},{7,5},{8,10},{9,11},{10,... | collective-permute-start | bytes 393224 | tf_op jit(solution)/shard_map/ppermute | solution.py:24
  120.0 4.7 %collective-permute-start.34 = (f32[64,128]{1,0:T(8,128)S(1)}, f32[64,128]{1,0:T(8,128)S(1)}, u32[]{:S(2)}, u32[]{:S(2)}) collective-permute-start(f32[64,128]{1,0:T(8,128)S(1)} %add.145), channel_id=1, source_target_pairs={{0,2},{1,3},{2,0},{3,1},{4,6},{5,7},{6,4},{7,5},{8,10},{9,11},{10,... | collective-permute-start | bytes 98312 | tf_op jit(solution)/shard_map/ppermute | solution.py:24
  124.7 6.6 %collective-permute-start.35 = (f32[64,128]{1,0:T(8,128)S(1)}, f32[64,128]{1,0:T(8,128)S(1)}, u32[]{:S(2)}, u32[]{:S(2)}) collective-permute-start(f32[64,128]{1,0:T(8,128)S(1)} %add.146), channel_id=1, source_target_pairs={{0,4},{4,0},{8,12},{12,8},{16,20},{20,16},{24,28},{28,24},{1,5},{5... | collective-permute-start | bytes 98312 | tf_op jit(solution)/shard_map/ppermute | solution.py:24
  131.3 3.9 %collective-permute-start.36 = (f32[64,128]{1,0:T(8,128)S(1)}, f32[64,128]{1,0:T(8,128)S(1)}, u32[]{:S(2)}, u32[]{:S(2)}) collective-permute-start(f32[64,128]{1,0:T(8,128)S(1)} %add.147), channel_id=1, source_target_pairs={{0,8},{4,12},{8,0},{12,4},{16,24},{20,28},{24,16},{28,20},{1,9},{5... | collective-permute-start | bytes 98312 | tf_op jit(solution)/shard_map/ppermute | solution.py:24
  135.2 9.8 %collective-permute-start.37 = (f32[64,128]{1,0:T(8,128)S(1)}, f32[64,128]{1,0:T(8,128)S(1)}, u32[]{:S(2)}, u32[]{:S(2)}) collective-permute-start(f32[64,128]{1,0:T(8,128)S(1)} %add.148), channel_id=1, source_target_pairs={{0,16},{4,20},{8,24},{12,28},{16,0},{20,4},{24,8},{28,12},{1,17},{... | collective-permute-start | bytes 98312 | tf_op jit(solution)/shard_map/ppermute | solution.py:24
  139.0 16.6 %collective-permute-start.39 = (bf16[12,64,128]{2,1,0:T(8,128)(2,1)S(1)}, bf16[12,64,128]{2,1,0:T(8,128)(2,1)S(1)}, u32[]{:S(2)}, u32[]{:S(2)}) collective-permute-start(bf16[12,64,128]{2,1,0:T(8,128)(2,1)S(1)} %get-tuple-element.28), channel_id=1, source_target_pairs={{0,2},{1,3},{2,0},{3,1},{4,6},{5,7},{6,4},{7,5},{8,10},{9,11},{10,... | collective-permute-start | bytes 589832 | tf_op jit(solution)/shard_map/ppermute | solution.py:24
  140.5 15.0 %collective-permute-start.45 = (f32[2,64,128]{2,1,0:T(8,128)S(1)}, f32[2,64,128]{2,1,0:T(8,128)S(1)}, u32[]{:S(2)}, u32[]{:S(2)}) collective-permute-start(f32[2,64,128]{2,1,0:T(8,128)S(1)} %get-tuple-element.34), channel_id=1, source_target_pairs={{8,16},{12,20},{16,8},{20,12},{9,17},{13,21},{17,9},{21,13},{10,18... | collective-permute-start | bytes 196616 | tf_op jit(solution)/shard_map/ppermute | solution.py:30
  141.2 14.4 %collective-permute-start.44 = (f32[2,64,128]{2,1,0:T(8,128)S(1)}, f32[2,64,128]{2,1,0:T(8,128)S(1)}, u32[]{:S(2)}, u32[]{:S(2)}) collective-permute-start(f32[2,64,128]{2,1,0:T(8,128)S(1)} %get-tuple-element.35), channel_id=1, source_target_pairs={{0,8},{4,12},{16,24},{20,28},{8,0},{12,4},{24,16},{28,20},{1,9},{5... | collective-permute-start | bytes 196616 | tf_op jit(solution)/shard_map/ppermute | solution.py:30
  144.4 11.2 %collective-permute-start.43 = (f32[2,64,128]{2,1,0:T(8,128)S(1)}, f32[2,64,128]{2,1,0:T(8,128)S(1)}, u32[]{:S(2)}, u32[]{:S(2)}) collective-permute-start(f32[2,64,128]{2,1,0:T(8,128)S(1)} %get-tuple-element.36), channel_id=1, source_target_pairs={{4,8},{12,16},{20,24},{8,4},{16,12},{24,20},{5,9},{13,17},{21,25},... | collective-permute-start | bytes 196616 | tf_op jit(solution)/shard_map/ppermute | solution.py:30
  145.1 10.5 %collective-permute-start.42 = (f32[2,64,128]{2,1,0:T(8,128)S(1)}, f32[2,64,128]{2,1,0:T(8,128)S(1)}, u32[]{:S(2)}, u32[]{:S(2)}) collective-permute-start(f32[2,64,128]{2,1,0:T(8,128)S(1)} %get-tuple-element.37), channel_id=1, source_target_pairs={{0,4},{8,12},{16,20},{24,28},{4,0},{12,8},{20,16},{28,24},{1,5},{9... | collective-permute-start | bytes 196616 | tf_op jit(solution)/shard_map/ppermute | solution.py:30
  147.9 0.7 copy-start.4
  155.6 0.6 copy-start.7
  155.6 0.6 copy-start.8
  155.6 0.7 copy-start.10
  155.6 0.7 copy-start.13
  155.6 0.7 copy-start.5

commit v2 on v0

v2 whole, which is shorter than its diff:
```python
import functools

import jax
import jax.numpy as jnp
from jax import lax
from jax.experimental import pallas as pl
from jax.experimental.pallas import tpu as pltpu
from jax.sharding import PartitionSpec as P

ITERS = 2
F32 = jnp.float32
BF16 = jnp.bfloat16
NT = (((1,), (1,)), ((), ()))
VMEM = pl.BlockSpec(memory_space=pltpu.VMEM)
SMEM = pl.BlockSpec(memory_space=pltpu.SMEM)
SMALL = pltpu.CompilerParams(vmem_limit_bytes=8 << 20)

PAIRINGS = (
    (1, lambda p: p % 2 == 0),
    (1, lambda p: p % 2 == 1),
    (2, lambda p: p % 4 < 2),
    (2, lambda p: p % 4 >= 2),
)


def bits_of(count):
    return [1 << b for b in range(count.bit_length() - 1)]


def swap(x, axis, bit):
    peers = lax.axis_size(axis)
    return lax.ppermute(x, axis, [(i, i ^ bit) for i in range(peers)])


def pair_up(x, pairing):
    by, lower = PAIRINGS[pairing]
    low = [p for p in range(lax.axis_size("dom") - by) if lower(p)]
    return lax.ppermute(x, "dom", [(p, p + by) for p in low] + [(p + by, p) for p in low])


def split_bf16(x, pieces):
    out = []
    for _ in range(pieces):
        out.append(x.astype(BF16))
        x = x - out[-1].astype(F32)
    return out


class Facts:
    def __init__(self, ref, neigh, slots):
        self.ref, self.neigh, self.slots = ref, neigh, slots

    def part(self):
        return self.ref[0]

    def sub(self):
        return self.ref[1]

    def live_rows(self):
        return self.ref[2]

    def live(self, block):
        return (block < self.live_rows()).astype(F32)

    def colour(self, pairing):
        odd, upper = self.part() % 2, (self.part() // 2) % 2
        return (odd, 1 - odd, 2 + upper, 3 - upper)[pairing]

    def send(self, pairing, slot):
        colour = self.colour(pairing)
        sent = (self.ref[3 + colour] >= 0) & (slot < self.ref[3 + self.neigh + colour])
        return self.ref[3 + 2 * self.neigh + colour * self.slots + slot], sent.astype(F32)


def pack_facts(neighbours, send_idx, send_count, row_counts):
    place = jnp.stack([lax.axis_index("dom"), lax.axis_index("sub")]).astype(jnp.int32)
    return jnp.concatenate(
        [place, row_counts, neighbours.reshape(-1), send_count.reshape(-1), send_idx.reshape(-1)]
    )


def write_outgoing(facts, basis, outgoing):
    for pairing, out in enumerate(outgoing):
        for slot in range(facts.slots):
            block, sent = facts.send(pairing, slot)
            out[slot] = basis[block] * sent.astype(BF16)


def prepare(shape, facts, directions, basis, *outgoing):
    facts = Facts(facts, *shape)
    for b in range(basis.shape[0]):
        basis[b] = directions[b] * facts.live(b).astype(BF16)
    write_outgoing(facts, basis, outgoing)


def call_prepare(shape, facts, directions):
    out = jax.ShapeDtypeStruct((shape[1],) + directions.shape[1:], BF16)
    return pl.pallas_call(
        functools.partial(prepare, shape),
        in_specs=[SMEM, VMEM],
        out_specs=[VMEM] * 5,
        out_shape=[jax.ShapeDtypeStruct(directions.shape, BF16)] + [out] * 4,
        compiler_params=SMALL,
        name="prepare",
    )(facts, directions)


def forward_adjoint(shape, relatives, facts, cols, tiles, friction, *refs):
    neigh, slots = shape
    count = len(relatives)
    own_parts, halo_parts = refs[:count], refs[count : 2 * count]
    keep, send, columns, total, held = refs[2 * count :]
    facts = Facts(facts, neigh, slots)
    blocks, tiles_row, width = tiles.shape[0], tiles.shape[1], tiles.shape[2]
    dirs = keep.shape[1]
    live_rows = facts.live_rows()

    own_base = [jnp.bitwise_xor(facts.sub(), r) * blocks for r in relatives]
    halo_base = [
        [
            count * blocks + (jnp.bitwise_xor(facts.sub(), r) * neigh + facts.colour(i)) * slots
            for i in range(neigh)
        ]
        for r in relatives
    ]
    for part, base in zip(own_parts, own_base):
        for i in range(blocks):
            columns[base + i] = part[i]
    for part, bases in zip(halo_parts, halo_base):
        for i in range(neigh):
            for s in range(slots):
                columns[bases[i] + s] = part[i * slots + s]
    total[...] = jnp.zeros_like(total)
    mine = jnp.concatenate([own_parts[0][i] for i in range(blocks)], axis=1)
    basis_gram = lax.dot_general(mine, mine, NT, preferred_element_type=F32)
    grams = send.at[send.shape[0] - 1]
    grams[:, :dirs] = basis_gram
    grams[:, dirs:] = basis_gram

    def forward(row):
        picked = jnp.concatenate([columns[cols[row, j]] for j in range(tiles_row)], axis=1)
        wide = jnp.concatenate([tiles[row, j] for j in range(tiles_row)], axis=1)
        state = lax.dot_general(wide, picked, NT, preferred_element_type=F32).T
        weighted = (friction[pl.ds(row, 1), :] * state).astype(BF16)
        grams[:, dirs:] += lax.dot_general(
            jnp.concatenate(split_bf16(state, 2), axis=1),
            jnp.concatenate([weighted] * 2, axis=1),
            NT,
            preferred_element_type=F32,
        )
        return weighted

    def adjoint(row, weighted):
        for j in range(0, tiles_row, 2):
            pair = list(range(j, min(j + 2, tiles_row)))
            wide = jnp.concatenate([tiles[row, i] for i in pair], axis=1)
            product = jnp.dot(weighted, wide, preferred_element_type=F32)
            for k, i in enumerate(pair):
                total[cols[row, i]] += product[:, k * width : (k + 1) * width]

    def step(row, carry):
        adjoint(row, held[row % 2])
        held[(row + 1) % 2] = forward(row + 1)
        return carry

    held[0] = forward(0)
    lax.fori_loop(0, live_rows - 1, step, 0)
    adjoint(live_rows - 1, held[(live_rows - 1) % 2])

    half = count // 2
    for out, chosen in ((keep, range(half)), (send, range(half, count))):
        place = 0
        for k in chosen:
            for i in range(blocks):
                out[place + i] = total[own_base[k] + i]
            place += blocks
        for k in chosen:
            for i in range(neigh):
                for s in range(slots):
                    out[place + i * slots + s] = total[halo_base[k][i] + s]
            place += neigh * slots


def call_forward_adjoint(shape, relatives, facts, cols, tiles, friction, own_parts, halo_parts):
    blocks, tiles_row, width = tiles.shape[0], tiles.shape[1], tiles.shape[2]
    dirs = own_parts[0].shape[1]
    count = len(relatives)
    local = count * (blocks + shape[0] * shape[1])
    return pl.pallas_call(
        functools.partial(forward_adjoint, shape, relatives),
        in_specs=[SMEM, SMEM, VMEM, VMEM] + [VMEM] * (2 * count),
        out_specs=[VMEM] * 2,
        out_shape=[
            jax.ShapeDtypeStruct((local // 2, dirs, width), F32),
            jax.ShapeDtypeStruct((local // 2 + 1, dirs, width), F32),
        ],
        scratch_shapes=[
            pltpu.VMEM((local, dirs, width), BF16),
            pltpu.VMEM((local, dirs, width), F32),
            pltpu.VMEM((2, dirs, width), BF16),
        ],
        compiler_params=pltpu.CompilerParams(vmem_limit_bytes=24 << 20),
        cost_estimate=pl.CostEstimate(
            flops=4 * blocks * tiles_row * width * width * dirs,
            bytes_accessed=blocks * tiles_row * width * width * 2,
            transcendentals=0,
        ),
        name="forward_adjoint",
    )(facts, cols, tiles, friction, *own_parts, *halo_parts)


def join(blocks, halo, keep, send, got, near_own, near_halo, far_own, far_halo):
    for b in range(blocks):
        near_own[b] = keep[b] + got[b]
        far_own[b] = (keep[blocks + b] + got[blocks + b]).astype(BF16)
    for h in range(halo):
        near_halo[h] = keep[2 * blocks + h] + got[2 * blocks + h]
        far_halo[h] = (keep[2 * blocks + halo + h] + got[2 * blocks + halo + h]).astype(BF16)
    last = send.shape[0] - 1
    for i, piece in enumerate(split_bf16(send[last] + got[last], 3)):
        far_halo[halo + i] = piece


def call_join(blocks, halo, keep, send, got):
    tail = keep.shape[1:]
    return pl.pallas_call(
        functools.partial(join, blocks, halo),
        in_specs=[VMEM] * 3,
        out_specs=[VMEM] * 4,
        out_shape=[
            jax.ShapeDtypeStruct((blocks,) + tail, F32),
            jax.ShapeDtypeStruct((halo,) + tail, F32),
            jax.ShapeDtypeStruct((blocks,) + tail, BF16),
            jax.ShapeDtypeStruct((halo + 3,) + tail, BF16),
        ],
        compiler_params=SMALL,
        name="join",
    )(keep, send, got)


def hand_back(slots, near_halo, sent, got, *outs):
    halo = near_halo.shape[0]
    grams = [sum(x[halo + i].astype(F32) for i in reversed(range(3))) for x in (sent, got)]
    for pairing, out in enumerate(outs):
        for s in range(slots):
            out[s] = near_halo[pairing * slots + s] + got[pairing * slots + s].astype(F32)
    outs[0][slots] = grams[0] + grams[1]


def call_hand_back(slots, near_halo, sent, got):
    tail = near_halo.shape[1:]
    out = lambda n: jax.ShapeDtypeStruct((n,) + tail, F32)
    return pl.pallas_call(
        functools.partial(hand_back, slots),
        in_specs=[VMEM] * 3,
        out_specs=[VMEM] * 4,
        out_shape=[out(slots + 1), out(slots), out(slots), out(slots)],
        compiler_params=SMALL,
        name="hand_back",
    )(near_halo, sent, got)


def eliminate(grams, dirs):
    wide = grams.shape[1]
    panels = [grams[8 * i : 8 * i + 8, :] for i in range(dirs // 8)]
    rows = lax.broadcasted_iota(jnp.int32, (8, wide), 0)

    def spread(x, column):
        return jnp.broadcast_to(x[:, column : column + 1], (8, wide))

    for k in range(dirs // 8):
        pivot = panels[k]
        lead = [spread(pivot, 8 * k + j) for j in range(8)]
        for t in range(8):
            inverse = 1.0 / lead[t][t : t + 1, :]
            row = pivot[t : t + 1, :] * inverse
            pivot = jnp.where(rows == t, row, pivot - lead[t] * row)
            for j in range(t + 1, 8):
                other = lead[j][t : t + 1, :] * inverse
                lead[j] = jnp.where(rows == t, other, lead[j] - lead[t] * other)
        for i in range(dirs // 8):
            if i != k:
                old = panels[i]
                new = old
                for j in range(8):
                    new = new - spread(old, 8 * k + j) * pivot[j : j + 1, :]
                panels[i] = new
        panels[k] = pivot
    return jnp.concatenate(panels, axis=0)[:, dirs:]


def project(shape, last, facts, grams_here, grams_there, basis, near_own, far_own, *refs):
    slots = shape[1]
    facts = Facts(facts, *shape)
    returned, outs, image = refs[:4], refs[4:-1], refs[-1]
    blocks, dirs = basis.shape[0], basis.shape[1]
    for b in range(blocks):
        image[b] = near_own[b] + far_own[b].astype(F32)
    for pairing, back in enumerate(returned):
        for s in range(slots):
            block, sent = facts.send(pairing, s)
            image[block] += back[s] * sent
    grams = grams_here[...] + grams_there[...]
    coupling = eliminate(grams, dirs)
    turned = jnp.concatenate(split_bf16(coupling.T, 3), axis=1)
    if last:
        outs[1][...] = grams[:, dirs:]
    for b in range(blocks):
        block = basis[b]
        wanted = facts.live(b) * (image[b] + 1.0 * block.astype(F32))
        tall = jnp.concatenate([block] * 3, axis=0)
        rest = wanted - jnp.dot(turned, tall, preferred_element_type=F32)
        outs[0][b] = rest.astype(outs[0].dtype)
    if not last:
        write_outgoing(facts, outs[0], outs[1:])


def call_project(shape, last, facts, grams_here, grams_there, basis, near_own, far_own, returned):
    blocks, dirs, width = basis.shape
    if last:
        out_shape = [jax.ShapeDtypeStruct(basis.shape, F32), jax.ShapeDtypeStruct((dirs, dirs), F32)]
    else:
        out_shape = [jax.ShapeDtypeStruct(basis.shape, BF16)]
        out_shape += [jax.ShapeDtypeStruct((shape[1], dirs, width), BF16)] * 4
    return pl.pallas_call(
        functools.partial(project, shape, last),
        in_specs=[SMEM] + [VMEM] * 9,
        out_specs=[VMEM] * len(out_shape),
        out_shape=out_shape,
        scratch_shapes=[pltpu.VMEM((blocks, dirs, width), F32)],
        cost_estimate=pl.CostEstimate(
            flops=6 * blocks * dirs * dirs * width, bytes_accessed=20 * blocks * dirs * width, transcendentals=0
        ),
        compiler_params=SMALL,
        name="project",
    )(facts, grams_here, grams_there, basis, near_own, far_own, *returned)


def on_device(directions, tiles, tile_cols, friction, neighbours, send_idx, send_count, row_counts):
    near, far = bits_of(lax.axis_size("sub"))
    dom_bits = bits_of(lax.axis_size("dom"))
    blocks = directions.shape[0]
    neigh, slots = send_idx.shape[1:]
    shape = (neigh, slots)
    relatives = (0, far, near, near | far)
    facts = pack_facts(neighbours, send_idx, send_count, row_counts)
    basis, *outgoing = call_prepare(shape, facts, directions)
    for step in range(ITERS):
        own_far = swap(basis, "sub", far)
        halo = jnp.concatenate([pair_up(x, i) for i, x in enumerate(outgoing)], axis=0)
        halo_far = swap(halo, "sub", far)
        own_parts = [basis, own_far, swap(basis, "sub", near), swap(own_far, "sub", near)]
        halo_parts = [halo, halo_far, swap(halo, "sub", near), swap(halo_far, "sub", near)]
        keep, send = call_forward_adjoint(
            shape, relatives, facts, tile_cols, tiles, friction, own_parts, halo_parts
        )
        got = swap(send, "sub", near)
        near_own, near_halo, far_own, far_halo = call_join(blocks, neigh * slots, keep, send, got)
        far_halo_got = swap(far_halo, "sub", far)
        far_own_got = swap(far_own, "sub", far)
        back = call_hand_back(slots, near_halo, far_halo, far_halo_got)
        first = pair_up(back[0], 0)
        third = jnp.concatenate([back[2], back[0][slots:] + first[slots:]], axis=0)
        third_got = pair_up(third, 2)
        returned = [first, pair_up(back[1], 1), third_got, pair_up(back[3], 3)]
        here, there = third[slots], third_got[slots]
        for bit in dom_bits[2:]:
            here = here + there
            there = swap(here, "dom", bit)
        last = step == ITERS - 1
        basis, *outgoing = call_project(
            shape, last, facts, here, there, basis, near_own, far_own_got, returned
        )
    remainder, cross = basis, outgoing[0]
    return (remainder, cross)


def solution(mesh):
    in_specs = (
        P(("dom", "sub"), None, None),
        P(("dom", "sub"), None, None, None),
        P(("dom", "sub"), None),
        P(("dom", "sub"), None),
        P("dom", None),
        P(("dom", "sub"), None, None),
        P(("dom", "sub"), None),
        P(("dom", "sub")),
    )
    out_specs = (P(("dom", "sub"), None, None), P())
    return jax.shard_map(
        on_device, mesh=mesh, in_specs=in_specs, out_specs=out_specs, check_vma=False
    )
```

time: 440 us -> 132 us (0.30)
  blocking collectives: 113 us -> 0 us
  other arithmetic: 102 us -> 0.04 us
  waiting for transfers between devices: 83 us -> 38.2 us
  matrix products: 39.3 us -> 0 us
  local copies, waits for them, and re-layouts: 36.4 us -> 8.03 us
  Pallas kernels: 0 us -> 22.1 us
  between operations: 15 us -> 1.52 us
  starting transfers between devices: 48.1 us -> 61.5 us
    psum x2 -> x0, blocking collectives: 80.1 us -> none  [on_device(): lax.psum((local_basis, local_cross), ('dom', 'sub'))]
    reduce_scatter x4 -> x0, waiting for transfers between devices: 79.8 us -> none  [the longest x2 47.5 us: on_device(): lax.psum_scatter(summed[own_columns:], 'sub', scatter_dimension=0, tiled=...]
    scatter-add x4 -> x0, other arithmetic: 70.8 us -> none  [the longest x2 69 us: on_device(): jax.ops.segment_sum(contrib.reshape(-1, dirs_count, tile_width), flat_col...]
    dot_general x8 -> x0, matrix products: 38.3 us -> none  [the longest x2 35.7 us: on_device(): jnp.einsum('rka,rjab->rjkb', weighted, tiles, preferred_element_type=jnp....]
    ppermute x16 -> x36, waiting for transfers between devices: 3.1 us -> 38.2 us  [the longest x20 31.4 us: swap(): return lax.ppermute(x, axis, [(i, i ^ bit) for i in range(peers)])]
    all_gather x4 -> x0, blocking collectives: 32.8 us -> none  [the longest x2 18.2 us: on_device(): own_rows = lax.all_gather(basis, 'sub', axis=0, tiled=True)]
    gather x4 -> x0, local copies, waits for them, and re-layouts: 27.8 us -> none  [the longest x2 26.7 us: on_device(): picked = columns[tile_cols]]
    another operation x16 -> x0, other arithmetic: 26.4 us -> none  [the longest x6 13 us: on_device(): factor = jnp.linalg.cholesky(basis_total)]
  transfers between devices with their start and end apart: 20 -> 36, of which waited for: 7 -> 18; matrix products, arithmetic and copies ran while one was open for 2% -> 0% of each run, Pallas kernels for 0% -> 0%
where the time goes in v2:
time: 132 us; the launch traced here: 131 us
  starting transfers between devices  61.5 us (47%)
  waiting for transfers between devices  38.2 us (29%)
  Pallas kernels  22.1 us (17%)
  local copies, waits for them, and re-layouts  8.03 us (6%)
  between operations  1.52 us (1%)
    ppermute x20, starting transfers between devices, swap(): return lax.ppermute(x, axis, [(i, i ^ bit) for i in range(peers)])  33.7 us
    ppermute x20, waiting for transfers between devices, swap(): return lax.ppermute(x, axis, [(i, i ^ bit) for i in range(peers)])  31.4 us
    ppermute x16, starting transfers between devices, pair_up(): lax.ppermute(x, 'dom', [(p, p + by) for p in low] + [(p + by, p) for p in...  27.8 us
    pallas_call x2, Pallas kernels, call_forward_adjoint(): pl.pallas_call(functools.partial(forward_adjoint, shape, relatives), in_s...  13.9 us
    pallas_call x2, Pallas kernels, call_project(): pl.pallas_call(functools.partial(project, shape, last), in_specs=[SMEM] +...  7.21 us
    unnamed x21, local copies, waits for them, and re-layouts  7.17 us
    ppermute x16, waiting for transfers between devices, pair_up(): lax.ppermute(x, 'dom', [(p, p + by) for p in low] + [(p + by, p) for p in...  6.87 us
  transfers between devices with their start and end apart: 36, of which 18 were waited for; matrix products, arithmetic and copies ran while one was open for 0% of the time, Pallas kernels for 0%

profile of v2, /device:TPU:0, one launch (start us, length us, event | category | flops | bytes accessed | tf_op | source)
XLA Modules:
  0.0 131.4 jit_solution(16151540644216720165)
XLA Ops:
  1.3 0.8 copy.11
  2.0 0.1 reshape.17
  2.1 0.7 concatenate.15.facts
  2.9 0.9 copy-done.2
  3.8 0.7 prepare.1
  4.5 3.0 %collective-permute-start.3 = (bf16[2,64,128]{2,1,0:T(8,128)(2,1)S(1)}, bf16[2,64,128]{2,1,0:T(8,128)(2,1)S(1)}, u32[]{:S(2)}, u32[]{:S(2)}) collective-permute-start(bf16[2,64,128]{2,1,0:T(8,128)(2,1)S(1)} %get-tuple-element.33), channel_id=1, source_target_pairs={{0,4},{8,12},{16,20},{24,28},{4,0},{12,8},{20,16},{28,24},{1,5},{9... | collective-permute-start | bytes 98312 | tf_op jit(solution)/shard_map/ppermute | solution.py:38
  7.5 0.7 collective-permute-start.4
  8.2 2.9 %collective-permute-start.5 = (bf16[2,64,128]{2,1,0:T(8,128)(2,1)S(1)}, bf16[2,64,128]{2,1,0:T(8,128)(2,1)S(1)}, u32[]{:S(2)}, u32[]{:S(2)}) collective-permute-start(bf16[2,64,128]{2,1,0:T(8,128)(2,1)S(1)} %get-tuple-element.35), channel_id=1, source_target_pairs={{0,8},{4,12},{16,24},{20,28},{8,0},{12,4},{24,16},{28,20},{1,9},{5... | collective-permute-start | bytes 98312 | tf_op jit(solution)/shard_map/ppermute | solution.py:38
  11.1 0.7 collective-permute-start.6
  11.7 2.0 %collective-permute-start = (bf16[12,64,128]{2,1,0:T(8,128)(2,1)S(1)}, bf16[12,64,128]{2,1,0:T(8,128)(2,1)S(1)}, u32[]{:S(2)}, u32[]{:S(2)}) collective-permute-start(bf16[12,64,128]{2,1,0:T(8,128)(2,1)S(1)} %get-tuple-element.32.refs_0_.basis), channel_id=1, source_target_pairs={{0,2},{1,3},{2,0},{3,1},{4,6},{5,7},{6,4},{7,5},{8,10},{9,11},{10,... | collective-permute-start | bytes 589832 | tf_op jit(solution)/shard_map/ppermute | solution.py:32
  13.8 1.4 %collective-permute-start.7 = (bf16[8,64,128]{2,1,0:T(8,128)(2,1)S(1)}, bf16[8,64,128]{2,1,0:T(8,128)(2,1)S(1)}, u32[]{:S(2)}, u32[]{:S(2)}) collective-permute-start(bf16[8,64,128]{2,1,0:T(8,128)(2,1)S(1)} %constant_dynamic-update-slice_fusion.refs_4_), channel_id=1, source_target_pairs={{0,2},{1,3},{2,0},{3,1},{4,6},{5,7},{6,4},{7,5},{8,10},{9,11},{10,... | collective-permute-start | bytes 393224 | tf_op jit(solution)/shard_map/ppermute | solution.py:32
  15.2 4.0 %collective-permute-done.refs_1_ = bf16[12,64,128]{2,1,0:T(8,128)(2,1)S(1)} collective-permute-done((bf16[12,64,128]{2,1,0:T(8,128)(2,1)S(1)}, bf16[12,64,128]{2,1,0:T(8,128)(2,1)S(1)}, u32[]{:S(2)}, u32[]{:S(2)}) %collective-permute-start) | collective-permute-done | bytes 196640 | tf_op jit(solution)/shard_map/ppermute | solution.py:32
  19.3 0.5 collective-permute-start.8
  19.8 0.9 collective-permute-done.7.refs_5_
  20.7 0.2 collective-permute-done.8.refs_6_
  20.9 1.1 collective-permute-done.9.refs_7_
  22.0 4.0 %copy-done = bf16[12,27,128,128]{3,2,1,0:T(8,128)(2,1)S(1)} copy-done((bf16[12,27,128,128]{3,2,1,0:T(8,128)(2,1)S(1)}, bf16[12,27,128,128]{3,2,1,0:T(8,128)(2,1)}, u32[]{:S(2)}) %copy-start) | copy-done | bytes 10616856
  26.0 0.7 copy-done.3
  26.7 0.7 copy-done.5
  27.4 7.0 %forward_adjoint.2 = (f32[40,64,128]{2,1,0:T(8,128)S(1)}, f32[41,64,128]{2,1,0:T(8,128)S(1)}) custom-call(s32[19]{0:T(128)S(1)} %concatenate.15.facts, s32[12,27]{1,0:T(8,128)S(1)} %copy-done.3, bf16[12,27,128,128]{3,2,1,0:T(8,128)(2,1)S(1)} %copy-done, f32[12,128]{1,0:T(8,128)S(1)} %copy-done.5, bf16[12,64,128]{2,1,0:T(8,128)(2,1)S(1)} %get-tuple-element.32.refs_0_.basis, ...), custom_call_target="tpu_custom_call" | custom-call | flops 1358954496 | bytes 10616832 | tf_op jit(solution)/shard_map/forward_adjoint/pallas_call | solution.py:189
  34.4 2.6 %collective-permute-start.10 = (f32[41,64,128]{2,1,0:T(8,128)S(1)}, f32[41,64,128]{2,1,0:T(8,128)S(1)}, u32[]{:S(2)}, u32[]{:S(2)}) collective-permute-start(f32[41,64,128]{2,1,0:T(8,128)S(1)} %get-tuple-element.38.send), channel_id=1, source_target_pairs={{0,1},{1,0},{2,3},{3,2},{4,5},{5,4},{6,7},{7,6},{8,9},{9,8},{10,11... | collective-permute-start | bytes 4030472 | tf_op jit(solution)/shard_map/ppermute | solution.py:32
  37.1 2.7 %collective-permute-done.10.got = f32[41,64,128]{2,1,0:T(8,128)S(1)} collective-permute-done((f32[41,64,128]{2,1,0:T(8,128)S(1)}, f32[41,64,128]{2,1,0:T(8,128)S(1)}, u32[]{:S(2)}, u32[]{:S(2)}) %collective-permute-start.10) | collective-permute-done | bytes 1343520 | tf_op jit(solution)/shard_map/ppermute | solution.py:32
  39.8 0.1 join.2
  39.9 0.0 copy-start.4
  39.9 3.5 %collective-permute-start.11 = (bf16[11,64,128]{2,1,0:T(8,128)(2,1)S(1)}, bf16[11,64,128]{2,1,0:T(8,128)(2,1)S(1)}, u32[]{:S(2)}, u32[]{:S(2)}) collective-permute-start(bf16[11,64,128]{2,1,0:T(8,128)(2,1)S(1)} %get-tuple-element.40.sent), channel_id=1, source_target_pairs={{0,2},{1,3},{2,0},{3,1},{4,6},{5,7},{6,4},{7,5},{8,10},{9,11},{10,... | collective-permute-start | bytes 540680 | tf_op jit(solution)/shard_map/ppermute | solution.py:32
  43.4 4.9 %collective-permute-done.11.got = bf16[11,64,128]{2,1,0:T(8,128)(2,1)S(1)} collective-permute-done((bf16[11,64,128]{2,1,0:T(8,128)(2,1)S(1)}, bf16[11,64,128]{2,1,0:T(8,128)(2,1)S(1)}, u32[]{:S(2)}, u32[]{:S(2)}) %collective-permute-start.11) | collective-permute-done | bytes 180256 | tf_op jit(solution)/shard_map/ppermute | solution.py:32
  48.3 3.0 %collective-permute-start.12 = (f32[3,64,128]{2,1,0:T(8,128)S(1)}, f32[3,64,128]{2,1,0:T(8,128)S(1)}, u32[]{:S(2)}, u32[]{:S(2)}) collective-permute-start(f32[3,64,128]{2,1,0:T(8,128)S(1)} %get-tuple-element.41), channel_id=1, source_target_pairs={{0,4},{8,12},{16,20},{24,28},{4,0},{12,8},{20,16},{28,24},{1,5},{9... | collective-permute-start | bytes 294920 | tf_op jit(solution)/shard_map/ppermute | solution.py:38
  51.3 2.6 %collective-permute-done.12.refs_0_ = f32[3,64,128]{2,1,0:T(8,128)S(1)} collective-permute-done((f32[3,64,128]{2,1,0:T(8,128)S(1)}, f32[3,64,128]{2,1,0:T(8,128)S(1)}, u32[]{:S(2)}, u32[]{:S(2)}) %collective-permute-start.12) | collective-permute-done | bytes 98336 | tf_op jit(solution)/shard_map/ppermute | solution.py:38
  53.9 2.9 %collective-permute-start.13 = (f32[3,64,128]{2,1,0:T(8,128)S(1)}, f32[3,64,128]{2,1,0:T(8,128)S(1)}, u32[]{:S(2)}, u32[]{:S(2)}) collective-permute-start(f32[3,64,128]{2,1,0:T(8,128)S(1)} %pad_maximum_fusion), channel_id=1, source_target_pairs={{0,8},{4,12},{16,24},{20,28},{8,0},{12,4},{24,16},{28,20},{1,9},{5... | collective-permute-start | bytes 294920 | tf_op jit(solution)/shard_map/ppermute | solution.py:38
  56.8 0.7 collective-permute-start.15
  57.5 0.7 collective-permute-start.16
  58.2 0.7 collective-permute-start.17
  58.8 0.6 collective-permute-done.13.refs_2_
  59.4 6.9 %collective-permute-start.14 = (f32[64,128]{1,0:T(8,128)S(1)}, f32[64,128]{1,0:T(8,128)S(1)}, u32[]{:S(2)}, u32[]{:S(2)}) collective-permute-start(f32[64,128]{1,0:T(8,128)S(1)} %fusion.1.grams_here), channel_id=1, source_target_pairs={{0,16},{4,20},{8,24},{12,28},{16,0},{20,4},{24,8},{28,12},{1,17},{... | collective-permute-start | bytes 98312 | tf_op jit(solution)/shard_map/ppermute | solution.py:32
  66.4 2.5 %collective-permute-done.14.grams_there = f32[64,128]{1,0:T(8,128)S(1)} collective-permute-done((f32[64,128]{1,0:T(8,128)S(1)}, f32[64,128]{1,0:T(8,128)S(1)}, u32[]{:S(2)}, u32[]{:S(2)}) %collective-permute-start.14) | collective-permute-done | bytes 32800 | tf_op jit(solution)/shard_map/ppermute | solution.py:32
  68.8 3.2 %project.2 = (bf16[12,64,128]{2,1,0:T(8,128)(2,1)S(1)}, bf16[2,64,128]{2,1,0:T(8,128)(2,1)S(1)}, bf16[2,64,128]{2,1,0:T(8,128)(2,1)S(1)}, bf16[2,64,128]{2,1,0:T(8,128)(2,1)S(1)}, bf16[2,64,128]{2,1,0:T(8,128)(2,1)S(1)}) custom-call(s32[19]{0:T(128)S(1)} %concatenate.15.facts, f32[64,128]{1,0:T(8,128)S(1)} %fusion.1.grams_here, ...), custom_call_target="tpu_custom_call" | custom-call | flops 37748736 | bytes 1966080 | tf_op jit(solution)/shard_map/project/pallas_call | solution.py:325
  72.1 0.1 collective-permute-start.21
  72.1 0.7 collective-permute-start.22
  72.8 4.8 %collective-permute-start.23 = (bf16[2,64,128]{2,1,0:T(8,128)(2,1)S(1)}, bf16[2,64,128]{2,1,0:T(8,128)(2,1)S(1)}, u32[]{:S(2)}, u32[]{:S(2)}) collective-permute-start(bf16[2,64,128]{2,1,0:T(8,128)(2,1)S(1)} %get-tuple-element.50), channel_id=1, source_target_pairs={{0,8},{4,12},{16,24},{20,28},{8,0},{12,4},{24,16},{28,20},{1,9},{5... | collective-permute-start | bytes 98312 | tf_op jit(solution)/shard_map/ppermute | solution.py:38
  77.6 0.7 collective-permute-start.24
  78.2 1.4 %collective-permute-start.18 = (bf16[12,64,128]{2,1,0:T(8,128)(2,1)S(1)}, bf16[12,64,128]{2,1,0:T(8,128)(2,1)S(1)}, u32[]{:S(2)}, u32[]{:S(2)}) collective-permute-start(bf16[12,64,128]{2,1,0:T(8,128)(2,1)S(1)} %get-tuple-element.47.refs_0_.basis), channel_id=1, source_target_pairs={{0,2},{1,3},{2,0},{3,1},{4,6},{5,7},{6,4},{7,5},{8,10},{9,11},{10,... | collective-permute-start | bytes 589832 | tf_op jit(solution)/shard_map/ppermute | solution.py:32
  79.7 0.0 collective-permute-done.23
  79.8 1.4 %collective-permute-start.25 = (bf16[8,64,128]{2,1,0:T(8,128)(2,1)S(1)}, bf16[8,64,128]{2,1,0:T(8,128)(2,1)S(1)}, u32[]{:S(2)}, u32[]{:S(2)}) collective-permute-start(bf16[8,64,128]{2,1,0:T(8,128)(2,1)S(1)} %constant_dynamic-update-slice_fusion.4.refs_4_), channel_id=1, source_target_pairs={{0,2},{1,3},{2,0},{3,1},{4,6},{5,7},{6,4},{7,5},{8,10},{9,11},{10,... | collective-permute-start | bytes 393224 | tf_op jit(solution)/shard_map/ppermute | solution.py:32
  81.2 2.8 %collective-permute-done.18.refs_1_ = bf16[12,64,128]{2,1,0:T(8,128)(2,1)S(1)} collective-permute-done((bf16[12,64,128]{2,1,0:T(8,128)(2,1)S(1)}, bf16[12,64,128]{2,1,0:T(8,128)(2,1)S(1)}, u32[]{:S(2)}, u32[]{:S(2)}) %collective-permute-start.18) | collective-permute-done | bytes 196640 | tf_op jit(solution)/shard_map/ppermute | solution.py:32
  84.0 0.5 collective-permute-start.26
  84.5 0.9 collective-permute-done.25.refs_5_
  85.4 0.2 collective-permute-done.26.refs_6_
  85.6 1.1 collective-permute-done.27.refs_7_
  86.8 6.9 %forward_adjoint.3 = (f32[40,64,128]{2,1,0:T(8,128)S(1)}, f32[41,64,128]{2,1,0:T(8,128)S(1)}) custom-call(s32[19]{0:T(128)S(1)} %concatenate.15.facts, s32[12,27]{1,0:T(8,128)S(1)} %copy-done.4, bf16[12,27,128,128]{3,2,1,0:T(8,128)(2,1)S(1)} %copy-done.1, f32[12,128]{1,0:T(8,128)S(1)} %copy-done.6, bf16[12,64,128]{2,1,0:T(8,128)(2,1)S(1)} %get-tuple-element.47.refs_0_.basis, ...), custom_call_target="tpu_custom_call" | custom-call | flops 1358954496 | bytes 10616832 | tf_op jit(solution)/shard_map/forward_adjoint/pallas_call | solution.py:189
  93.7 2.6 %collective-permute-start.28 = (f32[41,64,128]{2,1,0:T(8,128)S(1)}, f32[41,64,128]{2,1,0:T(8,128)S(1)}, u32[]{:S(2)}, u32[]{:S(2)}) collective-permute-start(f32[41,64,128]{2,1,0:T(8,128)S(1)} %get-tuple-element.53.send), channel_id=1, source_target_pairs={{0,1},{1,0},{2,3},{3,2},{4,5},{5,4},{6,7},{7,6},{8,9},{9,8},{10,11... | collective-permute-start | bytes 4030472 | tf_op jit(solution)/shard_map/ppermute | solution.py:32
  96.2 2.7 %collective-permute-done.28.got = f32[41,64,128]{2,1,0:T(8,128)S(1)} collective-permute-done((f32[41,64,128]{2,1,0:T(8,128)S(1)}, f32[41,64,128]{2,1,0:T(8,128)S(1)}, u32[]{:S(2)}, u32[]{:S(2)}) %collective-permute-start.28) | collective-permute-done | bytes 1343520 | tf_op jit(solution)/shard_map/ppermute | solution.py:32
  98.9 0.1 join.3
  99.1 3.3 %collective-permute-start.29 = (bf16[11,64,128]{2,1,0:T(8,128)(2,1)S(1)}, bf16[11,64,128]{2,1,0:T(8,128)(2,1)S(1)}, u32[]{:S(2)}, u32[]{:S(2)}) collective-permute-start(bf16[11,64,128]{2,1,0:T(8,128)(2,1)S(1)} %get-tuple-element.55.sent), channel_id=1, source_target_pairs={{0,2},{1,3},{2,0},{3,1},{4,6},{5,7},{6,4},{7,5},{8,10},{9,11},{10,... | collective-permute-start | bytes 540680 | tf_op jit(solution)/shard_map/ppermute | solution.py:32
  102.3 4.9 %collective-permute-done.29.got = bf16[11,64,128]{2,1,0:T(8,128)(2,1)S(1)} collective-permute-done((bf16[11,64,128]{2,1,0:T(8,128)(2,1)S(1)}, bf16[11,64,128]{2,1,0:T(8,128)(2,1)S(1)}, u32[]{:S(2)}, u32[]{:S(2)}) %collective-permute-start.29) | collective-permute-done | bytes 180256 | tf_op jit(solution)/shard_map/ppermute | solution.py:32
  107.2 2.0 %collective-permute-start.30 = (f32[3,64,128]{2,1,0:T(8,128)S(1)}, f32[3,64,128]{2,1,0:T(8,128)S(1)}, u32[]{:S(2)}, u32[]{:S(2)}) collective-permute-start(f32[3,64,128]{2,1,0:T(8,128)S(1)} %get-tuple-element.56), channel_id=1, source_target_pairs={{0,4},{8,12},{16,20},{24,28},{4,0},{12,8},{20,16},{28,24},{1,5},{9... | collective-permute-start | bytes 294920 | tf_op jit(solution)/shard_map/ppermute | solution.py:38
  109.3 2.6 %collective-permute-done.30.refs_0_ = f32[3,64,128]{2,1,0:T(8,128)S(1)} collective-permute-done((f32[3,64,128]{2,1,0:T(8,128)S(1)}, f32[3,64,128]{2,1,0:T(8,128)S(1)}, u32[]{:S(2)}, u32[]{:S(2)}) %collective-permute-start.30) | collective-permute-done | bytes 98336 | tf_op jit(solution)/shard_map/ppermute | solution.py:38
  111.9 3.8 %collective-permute-start.31 = (f32[3,64,128]{2,1,0:T(8,128)S(1)}, f32[3,64,128]{2,1,0:T(8,128)S(1)}, u32[]{:S(2)}, u32[]{:S(2)}) collective-permute-start(f32[3,64,128]{2,1,0:T(8,128)S(1)} %pad_maximum_fusion.1), channel_id=1, source_target_pairs={{0,8},{4,12},{16,24},{20,28},{8,0},{12,4},{24,16},{28,20},{1,9},{5... | collective-permute-start | bytes 294920 | tf_op jit(solution)/shard_map/ppermute | solution.py:38
  115.8 0.3 collective-permute-start.33
  116.1 0.7 collective-permute-start.34
  116.7 0.7 collective-permute-start.35
  117.4 1.0 collective-permute-done.31.refs_2_
  118.4 6.5 %collective-permute-start.32 = (f32[64,128]{1,0:T(8,128)S(1)}, f32[64,128]{1,0:T(8,128)S(1)}, u32[]{:S(2)}, u32[]{:S(2)}) collective-permute-start(f32[64,128]{1,0:T(8,128)S(1)} %fusion.grams_here), channel_id=1, source_target_pairs={{0,16},{4,20},{8,24},{12,28},{16,0},{20,4},{24,8},{28,12},{1,17},{... | collective-permute-start | bytes 98312 | tf_op jit(solution)/shard_map/ppermute | solution.py:32
  124.9 2.5 %collective-permute-done.32.grams_there = f32[64,128]{1,0:T(8,128)S(1)} collective-permute-done((f32[64,128]{1,0:T(8,128)S(1)}, f32[64,128]{1,0:T(8,128)S(1)}, u32[]{:S(2)}, u32[]{:S(2)}) %collective-permute-start.32) | collective-permute-done | bytes 32800 | tf_op jit(solution)/shard_map/ppermute | solution.py:32
  127.4 4.0 %project.3 = (f32[12,64,128]{2,1,0:T(8,128)}, f32[64,64]{1,0:T(8,128)}) custom-call(s32[19]{0:T(128)S(1)} %concatenate.15.facts, f32[64,128]{1,0:T(8,128)S(1)} %fusion.grams_here, f32[64,128]{1,0:T(8,128)S(1)} %collective-permute-done.32.grams_there, bf16[12,64,128]{2,1,0:T(8,128)(2,1)S(1)} %get-tuple-element.47.refs_0_.basis, ...), custom_call_target="tpu_custom_call" | custom-call | flops 37748736 | bytes 1966080 | tf_op jit(solution)/shard_map/project/pallas_call | solution.py:325
  (48 shorter events, 0.3 us)
Async XLA Ops:
  2.9 0.9 copy-start.2
  4.5 9.2 %collective-permute-start.3 = (bf16[2,64,128]{2,1,0:T(8,128)(2,1)S(1)}, bf16[2,64,128]{2,1,0:T(8,128)(2,1)S(1)}, u32[]{:S(2)}, u32[]{:S(2)}) collective-permute-start(bf16[2,64,128]{2,1,0:T(8,128)(2,1)S(1)} %get-tuple-element.33), channel_id=1, source_target_pairs={{0,4},{8,12},{16,20},{24,28},{4,0},{12,8},{20,16},{28,24},{1,5},{9... | collective-permute-start | bytes 98312 | tf_op jit(solution)/shard_map/ppermute | solution.py:38
  7.5 6.2 %collective-permute-start.4 = (bf16[2,64,128]{2,1,0:T(8,128)(2,1)S(1)}, bf16[2,64,128]{2,1,0:T(8,128)(2,1)S(1)}, u32[]{:S(2)}, u32[]{:S(2)}) collective-permute-start(bf16[2,64,128]{2,1,0:T(8,128)(2,1)S(1)} %get-tuple-element.34), channel_id=1, source_target_pairs={{4,8},{12,16},{20,24},{8,4},{16,12},{24,20},{5,9},{13,17},{21,25},... | collective-permute-start | bytes 98312 | tf_op jit(solution)/shard_map/ppermute | solution.py:38
  8.2 5.6 %collective-permute-start.5 = (bf16[2,64,128]{2,1,0:T(8,128)(2,1)S(1)}, bf16[2,64,128]{2,1,0:T(8,128)(2,1)S(1)}, u32[]{:S(2)}, u32[]{:S(2)}) collective-permute-start(bf16[2,64,128]{2,1,0:T(8,128)(2,1)S(1)} %get-tuple-element.35), channel_id=1, source_target_pairs={{0,8},{4,12},{16,24},{20,28},{8,0},{12,4},{24,16},{28,20},{1,9},{5... | collective-permute-start | bytes 98312 | tf_op jit(solution)/shard_map/ppermute | solution.py:38
  11.1 2.7 %collective-permute-start.6 = (bf16[2,64,128]{2,1,0:T(8,128)(2,1)S(1)}, bf16[2,64,128]{2,1,0:T(8,128)(2,1)S(1)}, u32[]{:S(2)}, u32[]{:S(2)}) collective-permute-start(bf16[2,64,128]{2,1,0:T(8,128)(2,1)S(1)} %get-tuple-element.36), channel_id=1, source_target_pairs={{8,16},{12,20},{16,8},{20,12},{9,17},{13,21},{17,9},{21,13},{10,18... | collective-permute-start | bytes 98312 | tf_op jit(solution)/shard_map/ppermute | solution.py:38
  11.7 7.6 %collective-permute-start = (bf16[12,64,128]{2,1,0:T(8,128)(2,1)S(1)}, bf16[12,64,128]{2,1,0:T(8,128)(2,1)S(1)}, u32[]{:S(2)}, u32[]{:S(2)}) collective-permute-start(bf16[12,64,128]{2,1,0:T(8,128)(2,1)S(1)} %get-tuple-element.32.refs_0_.basis), channel_id=1, source_target_pairs={{0,2},{1,3},{2,0},{3,1},{4,6},{5,7},{6,4},{7,5},{8,10},{9,11},{10,... | collective-permute-start | bytes 589832 | tf_op jit(solution)/shard_map/ppermute | solution.py:32
  13.8 6.9 %collective-permute-start.7 = (bf16[8,64,128]{2,1,0:T(8,128)(2,1)S(1)}, bf16[8,64,128]{2,1,0:T(8,128)(2,1)S(1)}, u32[]{:S(2)}, u32[]{:S(2)}) collective-permute-start(bf16[8,64,128]{2,1,0:T(8,128)(2,1)S(1)} %constant_dynamic-update-slice_fusion.refs_4_), channel_id=1, source_target_pairs={{0,2},{1,3},{2,0},{3,1},{4,6},{5,7},{6,4},{7,5},{8,10},{9,11},{10,... | collective-permute-start | bytes 393224 | tf_op jit(solution)/shard_map/ppermute | solution.py:32
  15.2 5.7 %collective-permute-start.1 = (bf16[12,64,128]{2,1,0:T(8,128)(2,1)S(1)}, bf16[12,64,128]{2,1,0:T(8,128)(2,1)S(1)}, u32[]{:S(2)}, u32[]{:S(2)}) collective-permute-start(bf16[12,64,128]{2,1,0:T(8,128)(2,1)S(1)} %get-tuple-element.32.refs_0_.basis), channel_id=1, source_target_pairs={{0,1},{1,0},{2,3},{3,2},{4,5},{5,4},{6,7},{7,6},{8,9},{9,8},{10,11... | collective-permute-start | bytes 589832 | tf_op jit(solution)/shard_map/ppermute | solution.py:32
  19.3 2.8 %collective-permute-start.2 = (bf16[12,64,128]{2,1,0:T(8,128)(2,1)S(1)}, bf16[12,64,128]{2,1,0:T(8,128)(2,1)S(1)}, u32[]{:S(2)}, u32[]{:S(2)}) collective-permute-start(bf16[12,64,128]{2,1,0:T(8,128)(2,1)S(1)} %collective-permute-done.refs_1_), channel_id=1, source_target_pairs={{0,1},{1,0},{2,3},{3,2},{4,5},{5,4},{6,7},{7,6},{8,9},{9,8},{10,11... | collective-permute-start | bytes 589832 | tf_op jit(solution)/shard_map/ppermute | solution.py:32
  19.3 1.6 %collective-permute-start.8 = (bf16[8,64,128]{2,1,0:T(8,128)(2,1)S(1)}, bf16[8,64,128]{2,1,0:T(8,128)(2,1)S(1)}, u32[]{:S(2)}, u32[]{:S(2)}) collective-permute-start(bf16[8,64,128]{2,1,0:T(8,128)(2,1)S(1)} %constant_dynamic-update-slice_fusion.refs_4_), channel_id=1, source_target_pairs={{0,1},{1,0},{2,3},{3,2},{4,5},{5,4},{6,7},{7,6},{8,9},{9,8},{10,11... | collective-permute-start | bytes 393224 | tf_op jit(solution)/shard_map/ppermute | solution.py:32
  20.7 1.3 %collective-permute-start.9 = (bf16[8,64,128]{2,1,0:T(8,128)(2,1)S(1)}, bf16[8,64,128]{2,1,0:T(8,128)(2,1)S(1)}, u32[]{:S(2)}, u32[]{:S(2)}) collective-permute-start(bf16[8,64,128]{2,1,0:T(8,128)(2,1)S(1)} %collective-permute-done.7.refs_5_), channel_id=1, source_target_pairs={{0,1},{1,0},{2,3},{3,2},{4,5},{5,4},{6,7},{7,6},{8,9},{9,8},{10,11... | collective-permute-start | bytes 393224 | tf_op jit(solution)/shard_map/ppermute | solution.py:32
  22.0 4.0 %copy-start = (bf16[12,27,128,128]{3,2,1,0:T(8,128)(2,1)S(1)}, bf16[12,27,128,128]{3,2,1,0:T(8,128)(2,1)}, u32[]{:S(2)}) copy-start(bf16[12,27,128,128]{3,2,1,0:T(8,128)(2,1)} %tiles.3) | copy-start | bytes 31850500
  26.0 0.7 copy-start.3
  26.7 0.7 copy-start.5
  27.4 59.3 %copy-start.1 = (bf16[12,27,128,128]{3,2,1,0:T(8,128)(2,1)S(1)}, bf16[12,27,128,128]{3,2,1,0:T(8,128)(2,1)}, u32[]{:S(2)}) copy-start(bf16[12,27,128,128]{3,2,1,0:T(8,128)(2,1)} %tiles.3) | copy-start | bytes 31850500
  34.4 5.3 %collective-permute-start.10 = (f32[41,64,128]{2,1,0:T(8,128)S(1)}, f32[41,64,128]{2,1,0:T(8,128)S(1)}, u32[]{:S(2)}, u32[]{:S(2)}) collective-permute-start(f32[41,64,128]{2,1,0:T(8,128)S(1)} %get-tuple-element.38.send), channel_id=1, source_target_pairs={{0,1},{1,0},{2,3},{3,2},{4,5},{5,4},{6,7},{7,6},{8,9},{9,8},{10,11... | collective-permute-start | bytes 4030472 | tf_op jit(solution)/shard_map/ppermute | solution.py:32
  39.9 46.8 %copy-start.4 = (s32[12,27]{1,0:T(8,128)S(1)}, s32[12,27]{1,0:T(8,128)}, u32[]{:S(2)}) copy-start(s32[12,27]{1,0:T(8,128)} %cols.3) | copy-start | bytes 3892
  39.9 46.8 %copy-start.6 = (f32[12,128]{1,0:T(8,128)S(1)}, f32[12,128]{1,0:T(8,128)}, u32[]{:S(2)}) copy-start(f32[12,128]{1,0:T(8,128)} %friction.3) | copy-start | bytes 18436
  39.9 8.3 %collective-permute-start.11 = (bf16[11,64,128]{2,1,0:T(8,128)(2,1)S(1)}, bf16[11,64,128]{2,1,0:T(8,128)(2,1)S(1)}, u32[]{:S(2)}, u32[]{:S(2)}) collective-permute-start(bf16[11,64,128]{2,1,0:T(8,128)(2,1)S(1)} %get-tuple-element.40.sent), channel_id=1, source_target_pairs={{0,2},{1,3},{2,0},{3,1},{4,6},{5,7},{6,4},{7,5},{8,10},{9,11},{10,... | collective-permute-start | bytes 540680 | tf_op jit(solution)/shard_map/ppermute | solution.py:32
  48.3 5.6 %collective-permute-start.12 = (f32[3,64,128]{2,1,0:T(8,128)S(1)}, f32[3,64,128]{2,1,0:T(8,128)S(1)}, u32[]{:S(2)}, u32[]{:S(2)}) collective-permute-start(f32[3,64,128]{2,1,0:T(8,128)S(1)} %get-tuple-element.41), channel_id=1, source_target_pairs={{0,4},{8,12},{16,20},{24,28},{4,0},{12,8},{20,16},{28,24},{1,5},{9... | collective-permute-start | bytes 294920 | tf_op jit(solution)/shard_map/ppermute | solution.py:38
  53.9 5.5 %collective-permute-start.13 = (f32[3,64,128]{2,1,0:T(8,128)S(1)}, f32[3,64,128]{2,1,0:T(8,128)S(1)}, u32[]{:S(2)}, u32[]{:S(2)}) collective-permute-start(f32[3,64,128]{2,1,0:T(8,128)S(1)} %pad_maximum_fusion), channel_id=1, source_target_pairs={{0,8},{4,12},{16,24},{20,28},{8,0},{12,4},{24,16},{28,20},{1,9},{5... | collective-permute-start | bytes 294920 | tf_op jit(solution)/shard_map/ppermute | solution.py:38
  56.8 9.5 %collective-permute-start.15 = (bf16[12,64,128]{2,1,0:T(8,128)(2,1)S(1)}, bf16[12,64,128]{2,1,0:T(8,128)(2,1)S(1)}, u32[]{:S(2)}, u32[]{:S(2)}) collective-permute-start(bf16[12,64,128]{2,1,0:T(8,128)(2,1)S(1)} %get-tuple-element.44), channel_id=1, source_target_pairs={{0,2},{1,3},{2,0},{3,1},{4,6},{5,7},{6,4},{7,5},{8,10},{9,11},{10,... | collective-permute-start | bytes 589832 | tf_op jit(solution)/shard_map/ppermute | solution.py:32
  57.5 8.9 %collective-permute-start.16 = (f32[2,64,128]{2,1,0:T(8,128)S(1)}, f32[2,64,128]{2,1,0:T(8,128)S(1)}, u32[]{:S(2)}, u32[]{:S(2)}) collective-permute-start(f32[2,64,128]{2,1,0:T(8,128)S(1)} %get-tuple-element.45), channel_id=1, source_target_pairs={{4,8},{12,16},{20,24},{8,4},{16,12},{24,20},{5,9},{13,17},{21,25},... | collective-permute-start | bytes 196616 | tf_op jit(solution)/shard_map/ppermute | solution.py:38
  58.2 8.2 %collective-permute-start.17 = (f32[2,64,128]{2,1,0:T(8,128)S(1)}, f32[2,64,128]{2,1,0:T(8,128)S(1)}, u32[]{:S(2)}, u32[]{:S(2)}) collective-permute-start(f32[2,64,128]{2,1,0:T(8,128)S(1)} %get-tuple-element.46), channel_id=1, source_target_pairs={{8,16},{12,20},{16,8},{20,12},{9,17},{13,21},{17,9},{21,13},{10,18... | collective-permute-start | bytes 196616 | tf_op jit(solution)/shard_map/ppermute | solution.py:38
  59.4 9.4 %collective-permute-start.14 = (f32[64,128]{1,0:T(8,128)S(1)}, f32[64,128]{1,0:T(8,128)S(1)}, u32[]{:S(2)}, u32[]{:S(2)}) collective-permute-start(f32[64,128]{1,0:T(8,128)S(1)} %fusion.1.grams_here), channel_id=1, source_target_pairs={{0,16},{4,20},{8,24},{12,28},{16,0},{20,4},{24,8},{28,12},{1,17},{... | collective-permute-start | bytes 98312 | tf_op jit(solution)/shard_map/ppermute | solution.py:32
  72.1 7.6 %collective-permute-start.21 = (bf16[2,64,128]{2,1,0:T(8,128)(2,1)S(1)}, bf16[2,64,128]{2,1,0:T(8,128)(2,1)S(1)}, u32[]{:S(2)}, u32[]{:S(2)}) collective-permute-start(bf16[2,64,128]{2,1,0:T(8,128)(2,1)S(1)} %get-tuple-element.48), channel_id=1, source_target_pairs={{0,4},{8,12},{16,20},{24,28},{4,0},{12,8},{20,16},{28,24},{1,5},{9... | collective-permute-start | bytes 98312 | tf_op jit(solution)/shard_map/ppermute | solution.py:38
  72.1 7.5 %collective-permute-start.22 = (bf16[2,64,128]{2,1,0:T(8,128)(2,1)S(1)}, bf16[2,64,128]{2,1,0:T(8,128)(2,1)S(1)}, u32[]{:S(2)}, u32[]{:S(2)}) collective-permute-start(bf16[2,64,128]{2,1,0:T(8,128)(2,1)S(1)} %get-tuple-element.49), channel_id=1, source_target_pairs={{4,8},{12,16},{20,24},{8,4},{16,12},{24,20},{5,9},{13,17},{21,25},... | collective-permute-start | bytes 98312 | tf_op jit(solution)/shard_map/ppermute | solution.py:38
  72.8 6.9 %collective-permute-start.23 = (bf16[2,64,128]{2,1,0:T(8,128)(2,1)S(1)}, bf16[2,64,128]{2,1,0:T(8,128)(2,1)S(1)}, u32[]{:S(2)}, u32[]{:S(2)}) collective-permute-start(bf16[2,64,128]{2,1,0:T(8,128)(2,1)S(1)} %get-tuple-element.50), channel_id=1, source_target_pairs={{0,8},{4,12},{16,24},{20,28},{8,0},{12,4},{24,16},{28,20},{1,9},{5... | collective-permute-start | bytes 98312 | tf_op jit(solution)/shard_map/ppermute | solution.py:38
  77.6 2.2 %collective-permute-start.24 = (bf16[2,64,128]{2,1,0:T(8,128)(2,1)S(1)}, bf16[2,64,128]{2,1,0:T(8,128)(2,1)S(1)}, u32[]{:S(2)}, u32[]{:S(2)}) collective-permute-start(bf16[2,64,128]{2,1,0:T(8,128)(2,1)S(1)} %get-tuple-element.51), channel_id=1, source_target_pairs={{8,16},{12,20},{16,8},{20,12},{9,17},{13,21},{17,9},{21,13},{10,18... | collective-permute-start | bytes 98312 | tf_op jit(solution)/shard_map/ppermute | solution.py:38
  78.2 5.7 %collective-permute-start.18 = (bf16[12,64,128]{2,1,0:T(8,128)(2,1)S(1)}, bf16[12,64,128]{2,1,0:T(8,128)(2,1)S(1)}, u32[]{:S(2)}, u32[]{:S(2)}) collective-permute-start(bf16[12,64,128]{2,1,0:T(8,128)(2,1)S(1)} %get-tuple-element.47.refs_0_.basis), channel_id=1, source_target_pairs={{0,2},{1,3},{2,0},{3,1},{4,6},{5,7},{6,4},{7,5},{8,10},{9,11},{10,... | collective-permute-start | bytes 589832 | tf_op jit(solution)/shard_map/ppermute | solution.py:32
  79.8 5.6 %collective-permute-start.25 = (bf16[8,64,128]{2,1,0:T(8,128)(2,1)S(1)}, bf16[8,64,128]{2,1,0:T(8,128)(2,1)S(1)}, u32[]{:S(2)}, u32[]{:S(2)}) collective-permute-start(bf16[8,64,128]{2,1,0:T(8,128)(2,1)S(1)} %constant_dynamic-update-slice_fusion.4.refs_4_), channel_id=1, source_target_pairs={{0,2},{1,3},{2,0},{3,1},{4,6},{5,7},{6,4},{7,5},{8,10},{9,11},{10,... | collective-permute-start | bytes 393224 | tf_op jit(solution)/shard_map/ppermute | solution.py:32
  81.2 4.4 %collective-permute-start.19 = (bf16[12,64,128]{2,1,0:T(8,128)(2,1)S(1)}, bf16[12,64,128]{2,1,0:T(8,128)(2,1)S(1)}, u32[]{:S(2)}, u32[]{:S(2)}) collective-permute-start(bf16[12,64,128]{2,1,0:T(8,128)(2,1)S(1)} %get-tuple-element.47.refs_0_.basis), channel_id=1, source_target_pairs={{0,1},{1,0},{2,3},{3,2},{4,5},{5,4},{6,7},{7,6},{8,9},{9,8},{10,11... | collective-permute-start | bytes 589832 | tf_op jit(solution)/shard_map/ppermute | solution.py:32
  84.0 2.8 %collective-permute-start.20 = (bf16[12,64,128]{2,1,0:T(8,128)(2,1)S(1)}, bf16[12,64,128]{2,1,0:T(8,128)(2,1)S(1)}, u32[]{:S(2)}, u32[]{:S(2)}) collective-permute-start(bf16[12,64,128]{2,1,0:T(8,128)(2,1)S(1)} %collective-permute-done.18.refs_1_), channel_id=1, source_target_pairs={{0,1},{1,0},{2,3},{3,2},{4,5},{5,4},{6,7},{7,6},{8,9},{9,8},{10,11... | collective-permute-start | bytes 589832 | tf_op jit(solution)/shard_map/ppermute | solution.py:32
  84.0 1.6 %collective-permute-start.26 = (bf16[8,64,128]{2,1,0:T(8,128)(2,1)S(1)}, bf16[8,64,128]{2,1,0:T(8,128)(2,1)S(1)}, u32[]{:S(2)}, u32[]{:S(2)}) collective-permute-start(bf16[8,64,128]{2,1,0:T(8,128)(2,1)S(1)} %constant_dynamic-update-slice_fusion.4.refs_4_), channel_id=1, source_target_pairs={{0,1},{1,0},{2,3},{3,2},{4,5},{5,4},{6,7},{7,6},{8,9},{9,8},{10,11... | collective-permute-start | bytes 393224 | tf_op jit(solution)/shard_map/ppermute | solution.py:32
  85.4 1.3 %collective-permute-start.27 = (bf16[8,64,128]{2,1,0:T(8,128)(2,1)S(1)}, bf16[8,64,128]{2,1,0:T(8,128)(2,1)S(1)}, u32[]{:S(2)}, u32[]{:S(2)}) collective-permute-start(bf16[8,64,128]{2,1,0:T(8,128)(2,1)S(1)} %collective-permute-done.25.refs_5_), channel_id=1, source_target_pairs={{0,1},{1,0},{2,3},{3,2},{4,5},{5,4},{6,7},{7,6},{8,9},{9,8},{10,11... | collective-permute-start | bytes 393224 | tf_op jit(solution)/shard_map/ppermute | solution.py:32
  93.7 5.3 %collective-permute-start.28 = (f32[41,64,128]{2,1,0:T(8,128)S(1)}, f32[41,64,128]{2,1,0:T(8,128)S(1)}, u32[]{:S(2)}, u32[]{:S(2)}) collective-permute-start(f32[41,64,128]{2,1,0:T(8,128)S(1)} %get-tuple-element.53.send), channel_id=1, source_target_pairs={{0,1},{1,0},{2,3},{3,2},{4,5},{5,4},{6,7},{7,6},{8,9},{9,8},{10,11... | collective-permute-start | bytes 4030472 | tf_op jit(solution)/shard_map/ppermute | solution.py:32
  99.1 8.1 %collective-permute-start.29 = (bf16[11,64,128]{2,1,0:T(8,128)(2,1)S(1)}, bf16[11,64,128]{2,1,0:T(8,128)(2,1)S(1)}, u32[]{:S(2)}, u32[]{:S(2)}) collective-permute-start(bf16[11,64,128]{2,1,0:T(8,128)(2,1)S(1)} %get-tuple-element.55.sent), channel_id=1, source_target_pairs={{0,2},{1,3},{2,0},{3,1},{4,6},{5,7},{6,4},{7,5},{8,10},{9,11},{10,... | collective-permute-start | bytes 540680 | tf_op jit(solution)/shard_map/ppermute | solution.py:32
  107.2 4.7 %collective-permute-start.30 = (f32[3,64,128]{2,1,0:T(8,128)S(1)}, f32[3,64,128]{2,1,0:T(8,128)S(1)}, u32[]{:S(2)}, u32[]{:S(2)}) collective-permute-start(f32[3,64,128]{2,1,0:T(8,128)S(1)} %get-tuple-element.56), channel_id=1, source_target_pairs={{0,4},{8,12},{16,20},{24,28},{4,0},{12,8},{20,16},{28,24},{1,5},{9... | collective-permute-start | bytes 294920 | tf_op jit(solution)/shard_map/ppermute | solution.py:38
  111.9 6.4 %collective-permute-start.31 = (f32[3,64,128]{2,1,0:T(8,128)S(1)}, f32[3,64,128]{2,1,0:T(8,128)S(1)}, u32[]{:S(2)}, u32[]{:S(2)}) collective-permute-start(f32[3,64,128]{2,1,0:T(8,128)S(1)} %pad_maximum_fusion.1), channel_id=1, source_target_pairs={{0,8},{4,12},{16,24},{20,28},{8,0},{12,4},{24,16},{28,20},{1,9},{5... | collective-permute-start | bytes 294920 | tf_op jit(solution)/shard_map/ppermute | solution.py:38
  115.8 9.1 %collective-permute-start.33 = (bf16[12,64,128]{2,1,0:T(8,128)(2,1)S(1)}, bf16[12,64,128]{2,1,0:T(8,128)(2,1)S(1)}, u32[]{:S(2)}, u32[]{:S(2)}) collective-permute-start(bf16[12,64,128]{2,1,0:T(8,128)(2,1)S(1)} %get-tuple-element.59), channel_id=1, source_target_pairs={{0,2},{1,3},{2,0},{3,1},{4,6},{5,7},{6,4},{7,5},{8,10},{9,11},{10,... | collective-permute-start | bytes 589832 | tf_op jit(solution)/shard_map/ppermute | solution.py:32
  116.1 8.9 %collective-permute-start.34 = (f32[2,64,128]{2,1,0:T(8,128)S(1)}, f32[2,64,128]{2,1,0:T(8,128)S(1)}, u32[]{:S(2)}, u32[]{:S(2)}) collective-permute-start(f32[2,64,128]{2,1,0:T(8,128)S(1)} %get-tuple-element.60), channel_id=1, source_target_pairs={{4,8},{12,16},{20,24},{8,4},{16,12},{24,20},{5,9},{13,17},{21,25},... | collective-permute-start | bytes 196616 | tf_op jit(solution)/shard_map/ppermute | solution.py:38
  116.7 8.2 %collective-permute-start.35 = (f32[2,64,128]{2,1,0:T(8,128)S(1)}, f32[2,64,128]{2,1,0:T(8,128)S(1)}, u32[]{:S(2)}, u32[]{:S(2)}) collective-permute-start(f32[2,64,128]{2,1,0:T(8,128)S(1)} %get-tuple-element.61), channel_id=1, source_target_pairs={{8,16},{12,20},{16,8},{20,12},{9,17},{13,21},{17,9},{21,13},{10,18... | collective-permute-start | bytes 196616 | tf_op jit(solution)/shard_map/ppermute | solution.py:38
  118.4 9.0 %collective-permute-start.32 = (f32[64,128]{1,0:T(8,128)S(1)}, f32[64,128]{1,0:T(8,128)S(1)}, u32[]{:S(2)}, u32[]{:S(2)}) collective-permute-start(f32[64,128]{1,0:T(8,128)S(1)} %fusion.grams_here), channel_id=1, source_target_pairs={{0,16},{4,20},{8,24},{12,28},{16,0},{20,4},{24,8},{28,12},{1,17},{... | collective-permute-start | bytes 98312 | tf_op jit(solution)/shard_map/ppermute | solution.py:32

commit v3 on v2

v3 whole, which is shorter than its diff:
```python
import functools

import jax
import jax.numpy as jnp
from jax import lax
from jax.experimental import pallas as pl
from jax.experimental.pallas import tpu as pltpu
from jax.sharding import PartitionSpec as P

ITERS = 2
F32 = jnp.float32
BF16 = jnp.bfloat16
NT = (((1,), (1,)), ((), ()))
VMEM = pl.BlockSpec(memory_space=pltpu.VMEM)
SMEM = pl.BlockSpec(memory_space=pltpu.SMEM)
ANY = pl.BlockSpec(memory_space=pl.ANY)
SMALL = pltpu.CompilerParams(vmem_limit_bytes=8 << 20)

PAIRINGS = (lambda p: p % 4 < 2, lambda p: p % 4 >= 2)


def bits_of(count):
    return [1 << b for b in range(count.bit_length() - 1)]


def swap(x, axis, bit):
    peers = lax.axis_size(axis)
    return lax.ppermute(x, axis, [(i, i ^ bit) for i in range(peers)])


def pair_up(x, pairing):
    low = [p for p in range(lax.axis_size("dom") - 2) if PAIRINGS[pairing](p)]
    return lax.ppermute(x, "dom", [(p, p + 2) for p in low] + [(p + 2, p) for p in low])


def split_bf16(x, pieces):
    out = []
    for _ in range(pieces):
        out.append(x.astype(BF16))
        x = x - out[-1].astype(F32)
    return out


def joined(ref, start):
    return ref[start + 2].astype(F32) + ref[start + 1].astype(F32) + ref[start].astype(F32)


class Facts:
    def __init__(self, ref, neigh, slots):
        self.ref, self.neigh, self.slots = ref, neigh, slots

    def odd(self):
        return self.ref[0, 0] % 2

    def upper(self):
        return (self.ref[0, 0] // 2) % 2

    def sub(self):
        return self.ref[0, 1]

    def live_rows(self):
        return self.ref[0, 2]

    def live(self, block):
        return (block < self.live_rows()).astype(F32)

    def colour(self, role):
        return (self.odd(), 1 - self.odd(), 2 + self.upper(), 3 - self.upper())[role]

    def relays(self, pairing, out):
        down = self.upper() if pairing == 0 else 1 - self.upper()
        return (down != self.odd() if out else down == self.odd()).astype(F32)

    def send(self, role, slot):
        colour = self.colour(role)
        sent = (self.ref[1, colour] >= 0) & (slot < self.ref[2, colour])
        return self.ref[3 + slot, colour], sent.astype(F32)


def pack_facts(neighbours, send_idx, send_count, row_counts):
    place = jnp.stack([lax.axis_index("dom"), lax.axis_index("sub")]).astype(jnp.int32)
    first = jnp.pad(jnp.concatenate([place, row_counts]), (0, neighbours.shape[1] - 3))
    return jnp.concatenate([first[None, :], neighbours, send_count, jnp.swapaxes(send_idx[0], 0, 1)])


def write_outgoing(facts, basis, flip, first, second):
    for slot in range(facts.slots):
        block, sent = facts.send(0, slot)
        flip[slot] = basis[block] * sent.astype(BF16)
        block, sent = facts.send(1, slot)
        far = basis[block] * sent.astype(BF16)
        for pairing, out in enumerate((first, second)):
            block, sent = facts.send(2 + pairing, slot)
            out[slot] = basis[block] * sent.astype(BF16)
            out[facts.slots + slot] = far * facts.relays(pairing, True).astype(BF16)


def outgoing_shapes(slots, dirs, width):
    return [jax.ShapeDtypeStruct((n * slots, dirs, width), BF16) for n in (1, 2, 2)]


def prepare(shape, facts, directions, basis, ways, *outgoing):
    facts = Facts(facts, *shape)
    for pairing in range(2):
        ways[pairing] = jnp.full(ways.shape[1:], facts.relays(pairing, False), F32).astype(BF16)
    for b in range(basis.shape[0]):
        basis[b] = directions[b] * facts.live(b).astype(BF16)
    write_outgoing(facts, basis, *outgoing)


def call_prepare(shape, facts, directions):
    return pl.pallas_call(
        functools.partial(prepare, shape),
        in_specs=[SMEM, VMEM],
        out_specs=[VMEM] * 5,
        out_shape=[
            jax.ShapeDtypeStruct(directions.shape, BF16),
            jax.ShapeDtypeStruct((2, 16, directions.shape[2]), BF16),
        ]
        + outgoing_shapes(shape[1], *directions.shape[1:]),
        compiler_params=SMALL,
        cost_estimate=pl.CostEstimate(flops=8 << 30, bytes_accessed=64 << 20, transcendentals=0),
        name="prepare",
    )(facts, directions)


def pass_on(slots, ways, flip, first, second, out):
    for s in range(slots):
        out[s] = flip[s]
        out[slots + s] = first[slots + s] * ways[0, :1] + second[slots + s] * ways[1, :1]


def call_pass_on(slots, ways, flip, first, second):
    return pl.pallas_call(
        functools.partial(pass_on, slots),
        in_specs=[VMEM] * 4,
        out_specs=VMEM,
        out_shape=jax.ShapeDtypeStruct(first.shape, BF16),
        compiler_params=SMALL,
        name="pass_on",
    )(ways, flip, first, second)


def stack(slots, flip, first, second, *refs):
    out = refs[-1]
    for s in range(2 * slots):
        out[s] = flip[s]
    for s in range(slots):
        out[2 * slots + s] = first[s]
        out[3 * slots + s] = second[s]


def call_stack(slots, flip, first, second, after):
    return pl.pallas_call(
        functools.partial(stack, slots),
        in_specs=[VMEM] * 3 + [ANY] * len(after),
        out_specs=VMEM,
        out_shape=jax.ShapeDtypeStruct((4 * slots,) + flip.shape[1:], BF16),
        compiler_params=SMALL,
        name="stack",
    )(flip, first, second, *after)


def forward_adjoint(shape, relatives, facts, cols, tiles, friction, *refs):
    neigh, slots = shape
    count = len(relatives)
    own_parts, halo_parts, refs = refs[:count], refs[count : 2 * count], refs[2 * count :]
    keep, send, grams = refs[:3]
    facts = Facts(facts, neigh, slots)
    blocks, tiles_row, width = tiles.shape[0], tiles.shape[1], tiles.shape[2]
    dirs = grams.shape[0]
    live_rows = facts.live_rows()
    columns, total, weights, pieces = refs[3:]

    own_base = [jnp.bitwise_xor(facts.sub(), r) * blocks for r in relatives]
    halo_base = [
        [
            count * blocks + (jnp.bitwise_xor(facts.sub(), r) * neigh + facts.colour(i)) * slots
            for i in range(neigh)
        ]
        for r in relatives
    ]
    for part, base in zip(own_parts, own_base):
        for i in range(blocks):
            columns[base + i] = part[i]
    for part, bases in zip(halo_parts, halo_base):
        for i in range(neigh):
            for s in range(slots):
                columns[bases[i] + s] = part[i * slots + s]
    total[...] = jnp.zeros_like(total)
    weights[...] = jnp.zeros_like(weights)
    pieces[...] = jnp.zeros_like(pieces)

    def forward(row):
        picked = jnp.concatenate([columns[cols[row, j]] for j in range(tiles_row)], axis=1)
        wide = jnp.concatenate([tiles[row, j] for j in range(tiles_row)], axis=1)
        state = lax.dot_general(wide, picked, NT, preferred_element_type=F32).T
        weights[row] = (friction[pl.ds(row, 1), :] * state).astype(BF16)
        pieces[row] = jnp.concatenate(split_bf16(state, 2), axis=1)

    def adjoint(row):
        weighted = weights[row]
        for j in range(0, tiles_row, 2):
            pair = list(range(j, min(j + 2, tiles_row)))
            wide = jnp.concatenate([tiles[row, i] for i in pair], axis=1)
            product = jnp.dot(weighted, wide, preferred_element_type=F32)
            for k, i in enumerate(pair):
                total[cols[row, i]] += product[:, k * width : (k + 1) * width]

    def step(row, carry):
        adjoint(row)
        forward(row + 1)
        return carry

    forward(0)
    lax.fori_loop(0, live_rows - 1, step, 0)
    adjoint(live_rows - 1)

    mine = jnp.concatenate([own_parts[0][i] for i in range(blocks)], axis=1)
    basis_gram = lax.dot_general(mine, mine, NT, preferred_element_type=F32)
    cross_gram = lax.dot_general(
        jnp.concatenate([pieces[i] for i in range(blocks)], axis=1),
        jnp.concatenate([weights[i // 2] for i in range(2 * blocks)], axis=1),
        NT,
        preferred_element_type=F32,
    )
    grams[:, :dirs] = basis_gram
    grams[:, dirs:] = basis_gram + cross_gram

    half = count // 2
    for out, chosen in ((keep, range(half)), (send, range(half, count))):
        place = 0
        for k in chosen:
            for i in range(blocks):
                out[place + i] = total[own_base[k] + i]
            place += blocks
        for k in chosen:
            for i in range(neigh):
                for s in range(slots):
                    out[place + i * slots + s] = total[halo_base[k][i] + s]
            place += neigh * slots


def call_forward_adjoint(shape, relatives, facts, cols, tiles, friction, own_parts, halo_parts):
    blocks, tiles_row, width = tiles.shape[0], tiles.shape[1], tiles.shape[2]
    dirs = own_parts[0].shape[1]
    count = len(relatives)
    own, halo = count * blocks, count * shape[0] * shape[1]
    out = lambda n: jax.ShapeDtypeStruct((n, dirs, width), F32)
    out_shape = [out((own + halo) // 2)] * 2 + [jax.ShapeDtypeStruct((dirs, 2 * dirs), F32)]
    scratch_shapes = [
        pltpu.VMEM((own + halo, dirs, width), BF16),
        pltpu.VMEM((own + halo, dirs, width), F32),
        pltpu.VMEM((blocks, dirs, width), BF16),
        pltpu.VMEM((blocks, dirs, 2 * width), BF16),
    ]
    return pl.pallas_call(
        functools.partial(forward_adjoint, shape, relatives),
        in_specs=[SMEM, SMEM, VMEM, VMEM] + [VMEM] * (2 * count),
        out_specs=[VMEM] * len(out_shape),
        out_shape=out_shape,
        scratch_shapes=scratch_shapes,
        compiler_params=pltpu.CompilerParams(vmem_limit_bytes=24 << 20),
        cost_estimate=pl.CostEstimate(
            flops=4 * blocks * tiles_row * width * width * dirs,
            bytes_accessed=blocks * tiles_row * width * width * 2,
            transcendentals=0,
        ),
        name="forward_adjoint",
    )(facts, cols, tiles, friction, *own_parts, *halo_parts)


def join(start, keep, got, *refs):
    near, far = refs[-2:]
    count = near.shape[0]
    for i in range(count):
        near[i] = keep[start + i] + got[start + i]
        far[i] = (keep[start + count + i] + got[start + count + i]).astype(BF16)


def call_join(start, count, keep, got, after):
    shape = (count,) + keep.shape[1:]
    return pl.pallas_call(
        functools.partial(join, start),
        in_specs=[VMEM] * 2 + [ANY] * len(after),
        out_specs=[VMEM] * 2,
        out_shape=[jax.ShapeDtypeStruct(shape, F32), jax.ShapeDtypeStruct(shape, BF16)],
        compiler_params=SMALL,
        name="join",
    )(keep, got, *after)


def hand_back(slots, near_halo, far_halo, here, there, flip, first, second):
    sums = [(near_halo[i] + far_halo[i].astype(F32)).astype(BF16) for i in range(near_halo.shape[0])]
    for s in range(2 * slots):
        flip[s] = sums[s]
    for s in range(slots):
        first[s] = sums[2 * slots + s]
        second[s] = sums[3 * slots + s]
    for i, piece in enumerate(split_bf16(here[...] + there[...], 3)):
        flip[2 * slots + i] = piece


def call_hand_back(slots, near_halo, far_halo, here, there):
    tail = near_halo.shape[1:]
    out = lambda n: jax.ShapeDtypeStruct((n,) + tail, BF16)
    return pl.pallas_call(
        functools.partial(hand_back, slots),
        in_specs=[VMEM] * 4,
        out_specs=[VMEM] * 3,
        out_shape=[out(2 * slots + 3), out(slots), out(slots)],
        compiler_params=SMALL,
        name="hand_back",
    )(near_halo, far_halo, here, there)


def pass_back(slots, ways, flip, got, first, second, first_out, second_out):
    for s in range(slots):
        first_out[s] = first[s]
        second_out[s] = second[s]
        first_out[slots + s] = got[slots + s] * ways[0, :1]
        second_out[slots + s] = got[slots + s] * ways[1, :1]
    for i, piece in enumerate(split_bf16(joined(flip, 2 * slots) + joined(got, 2 * slots), 3)):
        first_out[2 * slots + i] = piece


def call_pass_back(slots, ways, flip, got, first, second):
    tail = flip.shape[1:]
    out = lambda n: jax.ShapeDtypeStruct((n,) + tail, BF16)
    return pl.pallas_call(
        functools.partial(pass_back, slots),
        in_specs=[VMEM] * 5,
        out_specs=[VMEM] * 2,
        out_shape=[out(2 * slots + 3), out(2 * slots)],
        compiler_params=SMALL,
        name="pass_back",
    )(ways, flip, got, first, second)


def eliminate(grams, dirs):
    wide = grams.shape[1]
    panels = [grams[8 * i : 8 * i + 8, :] for i in range(dirs // 8)]
    rows = lax.broadcasted_iota(jnp.int32, (8, wide), 0)

    def spread(x, column):
        return jnp.broadcast_to(x[:, column : column + 1], (8, wide))

    for k in range(dirs // 8):
        pivot = panels[k]
        lead = [spread(pivot, 8 * k + j) for j in range(8)]
        for t in range(8):
            inverse = 1.0 / lead[t][t : t + 1, :]
            row = pivot[t : t + 1, :] * inverse
            pivot = jnp.where(rows == t, row, pivot - lead[t] * row)
            for j in range(t + 1, 8):
                other = lead[j][t : t + 1, :] * inverse
                lead[j] = jnp.where(rows == t, other, lead[j] - lead[t] * other)
        for i in range(dirs // 8):
            if i != k:
                old = panels[i]
                new = old
                for j in range(8):
                    new = new - spread(old, 8 * k + j) * pivot[j : j + 1, :]
                panels[i] = new
        panels[k] = pivot
    return jnp.concatenate(panels, axis=0)[:, dirs:]


def project(shape, last, facts, passed, basis, near_own, far_own, *refs):
    slots = shape[1]
    facts = Facts(facts, *shape)
    flip, pairs, outs, image = refs[0], refs[1:3], refs[3:-1], refs[-1]
    blocks, dirs = basis.shape[0], basis.shape[1]
    for b in range(blocks):
        image[b] = near_own[b] + far_own[b].astype(F32)
    for s in range(slots):
        relayed = sum(x[slots + s].astype(F32) * facts.relays(i, True) for i, x in enumerate(pairs))
        for role, back in enumerate((flip[s], relayed, pairs[0][s], pairs[1][s])):
            block, sent = facts.send(role, s)
            image[block] += back.astype(F32) * sent
    grams = joined(passed, 2 * slots) + joined(pairs[0], 2 * slots)
    coupling = eliminate(grams, dirs)
    turned = jnp.concatenate(split_bf16(coupling.T, 3), axis=1)
    if last:
        outs[1][...] = grams[:, dirs:]
    for b in range(blocks):
        block = basis[b]
        wanted = facts.live(b) * (image[b] + 1.0 * block.astype(F32))
        tall = jnp.concatenate([block] * 3, axis=0)
        rest = wanted - jnp.dot(turned, tall, preferred_element_type=F32)
        outs[0][b] = rest.astype(outs[0].dtype)
    if not last:
        write_outgoing(facts, outs[0], *outs[1:])


def call_project(shape, last, facts, sent, basis, near_own, far_own, returned):
    blocks, dirs, width = basis.shape
    if last:
        out_shape = [jax.ShapeDtypeStruct(basis.shape, F32), jax.ShapeDtypeStruct((dirs, dirs), F32)]
    else:
        out_shape = [jax.ShapeDtypeStruct(basis.shape, BF16)]
        out_shape += outgoing_shapes(shape[1], dirs, width)
    return pl.pallas_call(
        functools.partial(project, shape, last),
        in_specs=[SMEM] + [VMEM] * 7,
        out_specs=[VMEM] * len(out_shape),
        out_shape=out_shape,
        scratch_shapes=[pltpu.VMEM((blocks, dirs, width), F32)],
        cost_estimate=pl.CostEstimate(
            flops=6 * blocks * dirs * dirs * width, bytes_accessed=20 * blocks * dirs * width, transcendentals=0
        ),
        compiler_params=SMALL,
        name="project",
    )(facts, sent, basis, near_own, far_own, *returned)


def on_device(directions, tiles, tile_cols, friction, neighbours, send_idx, send_count, row_counts):
    near, far = bits_of(lax.axis_size("sub"))
    dom_bits = bits_of(lax.axis_size("dom"))
    blocks = directions.shape[0]
    neigh, slots = send_idx.shape[1:]
    shape = (neigh, slots)
    relatives = (0, far, near, near | far)
    facts = pack_facts(neighbours, send_idx, send_count, row_counts)
    basis, ways, *outgoing = call_prepare(shape, facts, directions)
    for step in range(ITERS):
        own_far, own_near = swap(basis, "sub", far), swap(basis, "sub", near)
        pairs = [pair_up(x, i) for i, x in enumerate(outgoing[1:])]
        flip = swap(call_pass_on(slots, ways, outgoing[0], *pairs), "dom", dom_bits[0])
        halo = call_stack(slots, flip, *pairs, [own_far, own_near])
        halo_far = swap(halo, "sub", far)
        own_parts = [basis, own_far, own_near, swap(own_far, "sub", near)]
        halo_parts = [halo, halo_far, swap(halo, "sub", near), swap(halo_far, "sub", near)]
        keep, send, grams = call_forward_adjoint(
            shape, relatives, facts, tile_cols, tiles, friction, own_parts, halo_parts
        )
        for bit in dom_bits[2:]:
            grams = grams + swap(grams, "dom", bit)
        got = swap(send, "sub", near)
        near_halo, far_halo = call_join(2 * blocks, neigh * slots, keep, got, [grams])
        far_halo = swap(far_halo, "sub", far)
        grams = grams + swap(grams, "sub", near)
        grams_got = swap(grams, "sub", far)
        near_own, far_own = call_join(0, blocks, keep, got, [grams_got])
        far_own_got = swap(far_own, "sub", far)
        flip, *back = call_hand_back(slots, near_halo, far_halo, grams, grams_got)
        flip_got = swap(flip, "dom", dom_bits[0])
        back = call_pass_back(slots, ways, flip, flip_got, *back)
        returned = [flip_got] + [pair_up(x, i) for i, x in enumerate(back)]
        last = step == ITERS - 1
        basis, *outgoing = call_project(
            shape, last, facts, back[0], basis, near_own, far_own_got, returned
        )
    remainder, cross = basis, outgoing[0]
    return (remainder, cross)


def solution(mesh):
    in_specs = (
        P(("dom", "sub"), None, None),
        P(("dom", "sub"), None, None, None),
        P(("dom", "sub"), None),
        P(("dom", "sub"), None),
        P("dom", None),
        P(("dom", "sub"), None, None),
        P(("dom", "sub"), None),
        P(("dom", "sub")),
    )
    out_specs = (P(("dom", "sub"), None, None), P())
    return jax.shard_map(
        on_device, mesh=mesh, in_specs=in_specs, out_specs=out_specs, check_vma=False
    )
```

time: 132 us -> 113 us (0.86)
  starting transfers between devices: 61.5 us -> 37 us
  waiting for transfers between devices: 38.2 us -> 48.7 us
  local copies, waits for them, and re-layouts: 8.03 us -> 1.13 us
    ppermute x16 -> x8, starting transfers between devices: 27.8 us -> 7.74 us  [pair_up(): lax.ppermute(x, 'dom', [(p, p + 2) for p in low] + [(p + 2, p) for p in l...]
    ppermute x20 -> x28, waiting for transfers between devices: 31.4 us -> 37.5 us  [swap(): return lax.ppermute(x, axis, [(i, i ^ bit) for i in range(peers)])]
    unnamed x21 -> x12, local copies, waits for them, and re-layouts: 7.17 us -> 1.12 us
    ppermute x20 -> x28, starting transfers between devices: 33.7 us -> 29.2 us  [swap(): return lax.ppermute(x, axis, [(i, i ^ bit) for i in range(peers)])]
    ppermute x16 -> x8, waiting for transfers between devices: 6.87 us -> 11.3 us  [pair_up(): lax.ppermute(x, 'dom', [(p, p + 2) for p in low] + [(p + 2, p) for p in l...]
  transfers between devices with their start and end apart: 36 -> 36, of which waited for: 18 -> 20; matrix products, arithmetic and copies ran while one was open for 0% -> 0% of each run, Pallas kernels for 0% -> 0%
where the time goes in v3:
time: 113 us; the launch traced here: 112 us
  waiting for transfers between devices  48.7 us (43%)
  starting transfers between devices  37 us (33%)
  Pallas kernels  22.5 us (20%)
  between operations  1.53 us (1%)
    ppermute x28, waiting for transfers between devices, swap(): return lax.ppermute(x, axis, [(i, i ^ bit) for i in range(peers)])  37.5 us
    ppermute x28, starting transfers between devices, swap(): return lax.ppermute(x, axis, [(i, i ^ bit) for i in range(peers)])  29.2 us
    pallas_call x2, Pallas kernels, call_forward_adjoint(): pl.pallas_call(functools.partial(forward_adjoint, shape, relatives), in_s...  13.9 us
    ppermute x8, waiting for transfers between devices, pair_up(): lax.ppermute(x, 'dom', [(p, p + 2) for p in low] + [(p + 2, p) for p in l...  11.3 us
    ppermute x8, starting transfers between devices, pair_up(): lax.ppermute(x, 'dom', [(p, p + 2) for p in low] + [(p + 2, p) for p in l...  7.74 us
    pallas_call x2, Pallas kernels, call_project(): pl.pallas_call(functools.partial(project, shape, last), in_specs=[SMEM] +...  7.37 us
  transfers between devices with their start and end apart: 36, of which 20 were waited for; matrix products, arithmetic and copies ran while one was open for 0% of the time, Pallas kernels for 0%

profile of v3, /device:TPU:0, one launch (start us, length us, event | category | flops | bytes accessed | tf_op | source)
XLA Modules:
  0.0 111.8 jit_solution(13969525727773531522)
XLA Ops:
  1.3 0.1 pad_add_fusion.1
  1.4 0.9 pad_add_fusion.facts
  2.2 0.0 copy-start.2
  2.2 1.1 copy-done.2
  3.3 0.8 prepare.1
  4.1 3.0 %collective-permute-start = (bf16[12,64,128]{2,1,0:T(8,128)(2,1)S(1)}, bf16[12,64,128]{2,1,0:T(8,128)(2,1)S(1)}, u32[]{:S(2)}, u32[]{:S(2)}) collective-permute-start(bf16[12,64,128]{2,1,0:T(8,128)(2,1)S(1)} %get-tuple-element.36.refs_0_.basis), channel_id=1, source_target_pairs={{0,2},{1,3},{2,0},{3,1},{4,6},{5,7},{6,4},{7,5},{8,10},{9,11},{10,... | collective-permute-start | bytes 589832 | tf_op jit(solution)/shard_map/ppermute | solution.py:28
  7.2 1.6 %collective-permute-start.3 = (bf16[4,64,128]{2,1,0:T(8,128)(2,1)S(1)}, bf16[4,64,128]{2,1,0:T(8,128)(2,1)S(1)}, u32[]{:S(2)}, u32[]{:S(2)}) collective-permute-start(bf16[4,64,128]{2,1,0:T(8,128)(2,1)S(1)} %get-tuple-element.38), channel_id=1, source_target_pairs={{0,8},{4,12},{16,24},{20,28},{8,0},{12,4},{24,16},{28,20},{1,9},{5... | collective-permute-start | bytes 196616 | tf_op jit(solution)/shard_map/ppermute | solution.py:33
  8.7 0.7 collective-permute-start.4
  9.4 2.3 %collective-permute-done.3.first = bf16[4,64,128]{2,1,0:T(8,128)(2,1)S(1)} collective-permute-done((bf16[4,64,128]{2,1,0:T(8,128)(2,1)S(1)}, bf16[4,64,128]{2,1,0:T(8,128)(2,1)S(1)}, u32[]{:S(2)}, u32[]{:S(2)}) %collective-permute-start.3) | collective-permute-done | bytes 65568 | tf_op jit(solution)/shard_map/ppermute | solution.py:33
  11.7 0.0 collective-permute-done.4.second
  11.7 1.6 %collective-permute-start.5 = (bf16[4,64,128]{2,1,0:T(8,128)(2,1)S(1)}, bf16[4,64,128]{2,1,0:T(8,128)(2,1)S(1)}, u32[]{:S(2)}, u32[]{:S(2)}) collective-permute-start(bf16[4,64,128]{2,1,0:T(8,128)(2,1)S(1)} %pass_on.2), channel_id=1, source_target_pairs={{0,4},{4,0},{8,12},{12,8},{16,20},{20,16},{24,28},{28,24},{1,5},{5... | collective-permute-start | bytes 196616 | tf_op jit(solution)/shard_map/ppermute | solution.py:28
  13.2 2.8 %collective-permute-done.5.flip = bf16[4,64,128]{2,1,0:T(8,128)(2,1)S(1)} collective-permute-done((bf16[4,64,128]{2,1,0:T(8,128)(2,1)S(1)}, bf16[4,64,128]{2,1,0:T(8,128)(2,1)S(1)}, u32[]{:S(2)}, u32[]{:S(2)}) %collective-permute-start.5) | collective-permute-done | bytes 65568 | tf_op jit(solution)/shard_map/ppermute | solution.py:28
  16.0 0.0 collective-permute-done.refs_0_.refs_1_
  16.0 0.4 collective-permute-start.6
  16.4 0.5 collective-permute-start.7
  17.0 4.1 %collective-permute-done.6.refs_5_ = bf16[8,64,128]{2,1,0:T(8,128)(2,1)S(1)} collective-permute-done((bf16[8,64,128]{2,1,0:T(8,128)(2,1)S(1)}, bf16[8,64,128]{2,1,0:T(8,128)(2,1)S(1)}, u32[]{:S(2)}, u32[]{:S(2)}) %collective-permute-start.6) | collective-permute-done | bytes 131104 | tf_op jit(solution)/shard_map/ppermute | solution.py:28
  21.1 1.3 %collective-permute-done.8.refs_7_ = bf16[8,64,128]{2,1,0:T(8,128)(2,1)S(1)} collective-permute-done((bf16[8,64,128]{2,1,0:T(8,128)(2,1)S(1)}, bf16[8,64,128]{2,1,0:T(8,128)(2,1)S(1)}, u32[]{:S(2)}, u32[]{:S(2)}) %collective-permute-start.8) | collective-permute-done | bytes 131104 | tf_op jit(solution)/shard_map/ppermute | solution.py:28
  22.5 7.0 %forward_adjoint.2 = (f32[40,64,128]{2,1,0:T(8,128)S(1)}, f32[40,64,128]{2,1,0:T(8,128)S(1)}, f32[64,128]{1,0:T(8,128)S(1)}) custom-call(s32[5,4]{1,0:T(8,128)S(1)} %pad_add_fusion.facts, s32[12,27]{1,0:T(8,128)S(1)} %copy-done, bf16[12,27,128,128]{3,2,1,0:T(8,128)(2,1)S(1)} %bitcast.8, f32[12,128]{1,0:T(8,128)S(1)} %copy-done.1, ...), custom_call_target="tpu_custom_call" | custom-call | flops 1358954496 | bytes 10616832 | tf_op jit(solution)/shard_map/forward_adjoint/pallas_call | solution.py:257
  29.4 0.1 collective-permute-start.9
  29.5 7.7 %collective-permute-start.10 = (f32[64,128]{1,0:T(8,128)S(1)}, f32[64,128]{1,0:T(8,128)S(1)}, u32[]{:S(2)}, u32[]{:S(2)}) collective-permute-start(f32[64,128]{1,0:T(8,128)S(1)} %get-tuple-element.42), channel_id=1, source_target_pairs={{0,16},{4,20},{8,24},{12,28},{16,0},{20,4},{24,8},{28,12},{1,17},{... | collective-permute-start | bytes 98312 | tf_op jit(solution)/shard_map/ppermute | solution.py:28
  37.1 2.0 %collective-permute-done.10 = f32[64,128]{1,0:T(8,128)S(1)} collective-permute-done((f32[64,128]{1,0:T(8,128)S(1)}, f32[64,128]{1,0:T(8,128)S(1)}, u32[]{:S(2)}, u32[]{:S(2)}) %collective-permute-start.10) | collective-permute-done | bytes 32800 | tf_op jit(solution)/shard_map/ppermute | solution.py:28
  39.1 0.1 join.4
  39.2 0.1 collective-permute-start.11
  39.3 0.1 collective-permute-start.12
  39.4 1.2 %collective-permute-done.12 = f32[64,128]{1,0:T(8,128)S(1)} collective-permute-done((f32[64,128]{1,0:T(8,128)S(1)}, f32[64,128]{1,0:T(8,128)S(1)}, u32[]{:S(2)}, u32[]{:S(2)}) %collective-permute-start.12) | collective-permute-done | bytes 32800 | tf_op jit(solution)/shard_map/ppermute | solution.py:28
  40.6 1.9 %collective-permute-start.13 = (f32[64,128]{1,0:T(8,128)S(1)}, f32[64,128]{1,0:T(8,128)S(1)}, u32[]{:S(2)}, u32[]{:S(2)}) collective-permute-start(f32[64,128]{1,0:T(8,128)S(1)} %add.15.here), channel_id=1, source_target_pairs={{0,2},{1,3},{2,0},{3,1},{4,6},{5,7},{6,4},{7,5},{8,10},{9,11},{10,... | collective-permute-start | bytes 98312 | tf_op jit(solution)/shard_map/ppermute | solution.py:28
  42.5 2.7 %collective-permute-done.13.there.refs_0_ = f32[64,128]{1,0:T(8,128)S(1)} collective-permute-done((f32[64,128]{1,0:T(8,128)S(1)}, f32[64,128]{1,0:T(8,128)S(1)}, u32[]{:S(2)}, u32[]{:S(2)}) %collective-permute-start.13) | collective-permute-done | bytes 32800 | tf_op jit(solution)/shard_map/ppermute | solution.py:28
  45.3 0.6 collective-permute-start.14
  45.9 0.1 join.5
  46.0 0.7 collective-permute-start.15
  46.7 3.4 %collective-permute-done.14.got.refs_0_ = bf16[7,64,128]{2,1,0:T(8,128)(2,1)S(1)} collective-permute-done((bf16[7,64,128]{2,1,0:T(8,128)(2,1)S(1)}, bf16[7,64,128]{2,1,0:T(8,128)(2,1)S(1)}, u32[]{:S(2)}, u32[]{:S(2)}) %collective-permute-start.14) | collective-permute-done | bytes 114720 | tf_op jit(solution)/shard_map/ppermute | solution.py:28
  50.2 0.1 collective-permute-start.16
  50.2 0.7 collective-permute-start.17
  50.9 0.8 collective-permute-done.15.far_own
  51.7 3.3 %collective-permute-done.16.refs_1_ = bf16[7,64,128]{2,1,0:T(8,128)(2,1)S(1)} collective-permute-done((bf16[7,64,128]{2,1,0:T(8,128)(2,1)S(1)}, bf16[7,64,128]{2,1,0:T(8,128)(2,1)S(1)}, u32[]{:S(2)}, u32[]{:S(2)}) %collective-permute-start.16) | collective-permute-done | bytes 114720 | tf_op jit(solution)/shard_map/ppermute | solution.py:33
  55.0 3.3 %project.2 = (bf16[12,64,128]{2,1,0:T(8,128)(2,1)S(1)}, bf16[2,64,128]{2,1,0:T(8,128)(2,1)S(1)}, bf16[4,64,128]{2,1,0:T(8,128)(2,1)S(1)}, bf16[4,64,128]{2,1,0:T(8,128)(2,1)S(1)}) custom-call(s32[5,4]{1,0:T(8,128)S(1)} %pad_add_fusion.facts, bf16[7,64,128]{2,1,0:T(8,128)(2,1)S(1)} %get-tuple-element.48.passed, ...), custom_call_target="tpu_custom_call" | custom-call | flops 37748736 | bytes 1966080 | tf_op jit(solution)/shard_map/project/pallas_call | solution.py:403
  58.4 1.3 %collective-permute-start.18 = (bf16[12,64,128]{2,1,0:T(8,128)(2,1)S(1)}, bf16[12,64,128]{2,1,0:T(8,128)(2,1)S(1)}, u32[]{:S(2)}, u32[]{:S(2)}) collective-permute-start(bf16[12,64,128]{2,1,0:T(8,128)(2,1)S(1)} %get-tuple-element.52.refs_0_.basis), channel_id=1, source_target_pairs={{0,2},{1,3},{2,0},{3,1},{4,6},{5,7},{6,4},{7,5},{8,10},{9,11},{10,... | collective-permute-start | bytes 589832 | tf_op jit(solution)/shard_map/ppermute | solution.py:28
  59.6 3.4 %collective-permute-start.21 = (bf16[4,64,128]{2,1,0:T(8,128)(2,1)S(1)}, bf16[4,64,128]{2,1,0:T(8,128)(2,1)S(1)}, u32[]{:S(2)}, u32[]{:S(2)}) collective-permute-start(bf16[4,64,128]{2,1,0:T(8,128)(2,1)S(1)} %get-tuple-element.54), channel_id=1, source_target_pairs={{0,8},{4,12},{16,24},{20,28},{8,0},{12,4},{24,16},{28,20},{1,9},{5... | collective-permute-start | bytes 196616 | tf_op jit(solution)/shard_map/ppermute | solution.py:33
  63.0 0.7 collective-permute-start.22
  63.7 2.1 %collective-permute-done.21.first = bf16[4,64,128]{2,1,0:T(8,128)(2,1)S(1)} collective-permute-done((bf16[4,64,128]{2,1,0:T(8,128)(2,1)S(1)}, bf16[4,64,128]{2,1,0:T(8,128)(2,1)S(1)}, u32[]{:S(2)}, u32[]{:S(2)}) %collective-permute-start.21) | collective-permute-done | bytes 65568 | tf_op jit(solution)/shard_map/ppermute | solution.py:33
  65.8 0.1 collective-permute-start.23
  65.9 4.3 %collective-permute-done.23.flip = bf16[4,64,128]{2,1,0:T(8,128)(2,1)S(1)} collective-permute-done((bf16[4,64,128]{2,1,0:T(8,128)(2,1)S(1)}, bf16[4,64,128]{2,1,0:T(8,128)(2,1)S(1)}, u32[]{:S(2)}, u32[]{:S(2)}) %collective-permute-start.23) | collective-permute-done | bytes 65568 | tf_op jit(solution)/shard_map/ppermute | solution.py:28
  70.2 0.9 collective-permute-start.24
  71.1 0.5 collective-permute-start.25
  71.6 3.6 %collective-permute-done.24.refs_5_ = bf16[8,64,128]{2,1,0:T(8,128)(2,1)S(1)} collective-permute-done((bf16[8,64,128]{2,1,0:T(8,128)(2,1)S(1)}, bf16[8,64,128]{2,1,0:T(8,128)(2,1)S(1)}, u32[]{:S(2)}, u32[]{:S(2)}) %collective-permute-start.24) | collective-permute-done | bytes 131104 | tf_op jit(solution)/shard_map/ppermute | solution.py:28
  75.2 1.3 %collective-permute-done.26.refs_7_ = bf16[8,64,128]{2,1,0:T(8,128)(2,1)S(1)} collective-permute-done((bf16[8,64,128]{2,1,0:T(8,128)(2,1)S(1)}, bf16[8,64,128]{2,1,0:T(8,128)(2,1)S(1)}, u32[]{:S(2)}, u32[]{:S(2)}) %collective-permute-start.26) | collective-permute-done | bytes 131104 | tf_op jit(solution)/shard_map/ppermute | solution.py:28
  76.5 6.9 %forward_adjoint.3 = (f32[40,64,128]{2,1,0:T(8,128)S(1)}, f32[40,64,128]{2,1,0:T(8,128)S(1)}, f32[64,128]{1,0:T(8,128)S(1)}) custom-call(s32[5,4]{1,0:T(8,128)S(1)} %pad_add_fusion.facts, s32[12,27]{1,0:T(8,128)S(1)} %copy-done, bf16[12,27,128,128]{3,2,1,0:T(8,128)(2,1)S(1)} %bitcast.8, f32[12,128]{1,0:T(8,128)S(1)} %copy-done.1, ...), custom_call_target="tpu_custom_call" | custom-call | flops 1358954496 | bytes 10616832 | tf_op jit(solution)/shard_map/forward_adjoint/pallas_call | solution.py:257
  83.5 0.1 collective-permute-start.27
  83.6 6.3 %collective-permute-start.28 = (f32[64,128]{1,0:T(8,128)S(1)}, f32[64,128]{1,0:T(8,128)S(1)}, u32[]{:S(2)}, u32[]{:S(2)}) collective-permute-start(f32[64,128]{1,0:T(8,128)S(1)} %get-tuple-element.58), channel_id=1, source_target_pairs={{0,16},{4,20},{8,24},{12,28},{16,0},{20,4},{24,8},{28,12},{1,17},{... | collective-permute-start | bytes 98312 | tf_op jit(solution)/shard_map/ppermute | solution.py:28
  89.9 2.0 %collective-permute-done.28 = f32[64,128]{1,0:T(8,128)S(1)} collective-permute-done((f32[64,128]{1,0:T(8,128)S(1)}, f32[64,128]{1,0:T(8,128)S(1)}, u32[]{:S(2)}, u32[]{:S(2)}) %collective-permute-start.28) | collective-permute-done | bytes 32800 | tf_op jit(solution)/shard_map/ppermute | solution.py:28
  91.9 0.1 join.6
  91.9 0.4 collective-permute-start.29
  92.4 1.2 %collective-permute-done.30 = f32[64,128]{1,0:T(8,128)S(1)} collective-permute-done((f32[64,128]{1,0:T(8,128)S(1)}, f32[64,128]{1,0:T(8,128)S(1)}, u32[]{:S(2)}, u32[]{:S(2)}) %collective-permute-start.30) | collective-permute-done | bytes 32800 | tf_op jit(solution)/shard_map/ppermute | solution.py:28
  93.6 1.7 %collective-permute-start.31 = (f32[64,128]{1,0:T(8,128)S(1)}, f32[64,128]{1,0:T(8,128)S(1)}, u32[]{:S(2)}, u32[]{:S(2)}) collective-permute-start(f32[64,128]{1,0:T(8,128)S(1)} %add.17.here), channel_id=1, source_target_pairs={{0,2},{1,3},{2,0},{3,1},{4,6},{5,7},{6,4},{7,5},{8,10},{9,11},{10,... | collective-permute-start | bytes 98312 | tf_op jit(solution)/shard_map/ppermute | solution.py:28
  95.2 2.7 %collective-permute-done.31.there.refs_0_ = f32[64,128]{1,0:T(8,128)S(1)} collective-permute-done((f32[64,128]{1,0:T(8,128)S(1)}, f32[64,128]{1,0:T(8,128)S(1)}, u32[]{:S(2)}, u32[]{:S(2)}) %collective-permute-start.31) | collective-permute-done | bytes 32800 | tf_op jit(solution)/shard_map/ppermute | solution.py:28
  98.0 0.1 collective-permute-start.32
  98.1 0.1 join.7
  98.2 1.3 %collective-permute-start.33 = (bf16[12,64,128]{2,1,0:T(8,128)(2,1)S(1)}, bf16[12,64,128]{2,1,0:T(8,128)(2,1)S(1)}, u32[]{:S(2)}, u32[]{:S(2)}) collective-permute-start(bf16[12,64,128]{2,1,0:T(8,128)(2,1)S(1)} %get-tuple-element.66), channel_id=1, source_target_pairs={{0,2},{1,3},{2,0},{3,1},{4,6},{5,7},{6,4},{7,5},{8,10},{9,11},{10,... | collective-permute-start | bytes 589832 | tf_op jit(solution)/shard_map/ppermute | solution.py:28
  99.4 3.4 %collective-permute-done.32.got.refs_0_ = bf16[7,64,128]{2,1,0:T(8,128)(2,1)S(1)} collective-permute-done((bf16[7,64,128]{2,1,0:T(8,128)(2,1)S(1)}, bf16[7,64,128]{2,1,0:T(8,128)(2,1)S(1)}, u32[]{:S(2)}, u32[]{:S(2)}) %collective-permute-start.32) | collective-permute-done | bytes 114720 | tf_op jit(solution)/shard_map/ppermute | solution.py:28
  102.9 0.1 collective-permute-start.34
  103.0 0.7 collective-permute-start.35
  103.6 0.5 collective-permute-done.33.far_own
  104.2 3.6 %collective-permute-done.34.refs_1_ = bf16[7,64,128]{2,1,0:T(8,128)(2,1)S(1)} collective-permute-done((bf16[7,64,128]{2,1,0:T(8,128)(2,1)S(1)}, bf16[7,64,128]{2,1,0:T(8,128)(2,1)S(1)}, u32[]{:S(2)}, u32[]{:S(2)}) %collective-permute-start.34) | collective-permute-done | bytes 114720 | tf_op jit(solution)/shard_map/ppermute | solution.py:33
  107.7 4.0 %project.3 = (f32[12,64,128]{2,1,0:T(8,128)}, f32[64,64]{1,0:T(8,128)}) custom-call(s32[5,4]{1,0:T(8,128)S(1)} %pad_add_fusion.facts, bf16[7,64,128]{2,1,0:T(8,128)(2,1)S(1)} %get-tuple-element.64.passed, bf16[12,64,128]{2,1,0:T(8,128)(2,1)S(1)} %get-tuple-element.52.refs_0_.basis, f32[12,64,128]{2,1,0:T(8,128)S(1)} %get-tuple-element.65.near_own, ...), custom_call_target="tpu_custom_call" | custom-call | flops 37748736 | bytes 1966080 | tf_op jit(solution)/shard_map/project/pallas_call | solution.py:403
  (45 shorter events, 0.3 us)
Async XLA Ops:
  1.4 21.1 %slice-start = ((s8[10616832]{0:T(1024)(128)(4,1)}), s8[4194304]{0:T(1024)(128)(4,1)S(1)}, s32[]{:S(2)}) async-start(s8[10616832]{0:T(1024)(128)(4,1)} %bitcast.7), calls=%async_computation | async-start | bytes 8388608
  2.2 1.1 copy-start.2
  3.3 19.1 %slice-start.1 = ((s8[10616832]{0:T(1024)(128)(4,1)}), s8[4194304]{0:T(1024)(128)(4,1)S(1)}, s32[]{:S(2)}) async-start(s8[10616832]{0:T(1024)(128)(4,1)} %bitcast.7), calls=%async_computation.1 | async-start | bytes 8388608
  3.3 19.1 %slice-start.2 = ((s8[10616832]{0:T(1024)(128)(4,1)}), s8[2228224]{0:T(1024)(128)(4,1)S(1)}, s32[]{:S(2)}) async-start(s8[10616832]{0:T(1024)(128)(4,1)} %bitcast.7), calls=%async_computation.2 | async-start | bytes 4456448
  3.3 19.1 %copy-start = (s32[12,27]{1,0:T(8,128)S(1)}, s32[12,27]{1,0:T(8,128)}, u32[]{:S(2)}) copy-start(s32[12,27]{1,0:T(8,128)} %cols.3) | copy-start | bytes 3892
  3.3 19.1 %copy-start.1 = (f32[12,128]{1,0:T(8,128)S(1)}, f32[12,128]{1,0:T(8,128)}, u32[]{:S(2)}) copy-start(f32[12,128]{1,0:T(8,128)} %friction.3) | copy-start | bytes 18436
  4.1 11.9 %collective-permute-start = (bf16[12,64,128]{2,1,0:T(8,128)(2,1)S(1)}, bf16[12,64,128]{2,1,0:T(8,128)(2,1)S(1)}, u32[]{:S(2)}, u32[]{:S(2)}) collective-permute-start(bf16[12,64,128]{2,1,0:T(8,128)(2,1)S(1)} %get-tuple-element.36.refs_0_.basis), channel_id=1, source_target_pairs={{0,2},{1,3},{2,0},{3,1},{4,6},{5,7},{6,4},{7,5},{8,10},{9,11},{10,... | collective-permute-start | bytes 589832 | tf_op jit(solution)/shard_map/ppermute | solution.py:28
  7.2 8.9 %collective-permute-start.1 = (bf16[12,64,128]{2,1,0:T(8,128)(2,1)S(1)}, bf16[12,64,128]{2,1,0:T(8,128)(2,1)S(1)}, u32[]{:S(2)}, u32[]{:S(2)}) collective-permute-start(bf16[12,64,128]{2,1,0:T(8,128)(2,1)S(1)} %get-tuple-element.36.refs_0_.basis), channel_id=1, source_target_pairs={{0,1},{1,0},{2,3},{3,2},{4,5},{5,4},{6,7},{7,6},{8,9},{9,8},{10,11... | collective-permute-start | bytes 589832 | tf_op jit(solution)/shard_map/ppermute | solution.py:28
  7.2 4.5 %collective-permute-start.3 = (bf16[4,64,128]{2,1,0:T(8,128)(2,1)S(1)}, bf16[4,64,128]{2,1,0:T(8,128)(2,1)S(1)}, u32[]{:S(2)}, u32[]{:S(2)}) collective-permute-start(bf16[4,64,128]{2,1,0:T(8,128)(2,1)S(1)} %get-tuple-element.38), channel_id=1, source_target_pairs={{0,8},{4,12},{16,24},{20,28},{8,0},{12,4},{24,16},{28,20},{1,9},{5... | collective-permute-start | bytes 196616 | tf_op jit(solution)/shard_map/ppermute | solution.py:33
  8.7 2.9 %collective-permute-start.4 = (bf16[4,64,128]{2,1,0:T(8,128)(2,1)S(1)}, bf16[4,64,128]{2,1,0:T(8,128)(2,1)S(1)}, u32[]{:S(2)}, u32[]{:S(2)}) collective-permute-start(bf16[4,64,128]{2,1,0:T(8,128)(2,1)S(1)} %get-tuple-element.39), channel_id=1, source_target_pairs={{8,16},{12,20},{16,8},{20,12},{9,17},{13,21},{17,9},{21,13},{10,18... | collective-permute-start | bytes 196616 | tf_op jit(solution)/shard_map/ppermute | solution.py:33
  11.7 4.3 %collective-permute-start.5 = (bf16[4,64,128]{2,1,0:T(8,128)(2,1)S(1)}, bf16[4,64,128]{2,1,0:T(8,128)(2,1)S(1)}, u32[]{:S(2)}, u32[]{:S(2)}) collective-permute-start(bf16[4,64,128]{2,1,0:T(8,128)(2,1)S(1)} %pass_on.2), channel_id=1, source_target_pairs={{0,4},{4,0},{8,12},{12,8},{16,20},{20,16},{24,28},{28,24},{1,5},{5... | collective-permute-start | bytes 196616 | tf_op jit(solution)/shard_map/ppermute | solution.py:28
  16.0 5.0 %collective-permute-start.6 = (bf16[8,64,128]{2,1,0:T(8,128)(2,1)S(1)}, bf16[8,64,128]{2,1,0:T(8,128)(2,1)S(1)}, u32[]{:S(2)}, u32[]{:S(2)}) collective-permute-start(bf16[8,64,128]{2,1,0:T(8,128)(2,1)S(1)} %stack.10.refs_4_), channel_id=1, source_target_pairs={{0,2},{1,3},{2,0},{3,1},{4,6},{5,7},{6,4},{7,5},{8,10},{9,11},{10,... | collective-permute-start | bytes 393224 | tf_op jit(solution)/shard_map/ppermute | solution.py:28
  16.4 4.6 %collective-permute-start.2 = (bf16[12,64,128]{2,1,0:T(8,128)(2,1)S(1)}, bf16[12,64,128]{2,1,0:T(8,128)(2,1)S(1)}, u32[]{:S(2)}, u32[]{:S(2)}) collective-permute-start(bf16[12,64,128]{2,1,0:T(8,128)(2,1)S(1)} %collective-permute-done.refs_0_.refs_1_), channel_id=1, source_target_pairs={{0,1},{1,0},{2,3},{3,2},{4,5},{5,4},{6,7},{7,6},{8,9},{9,8},{10,11... | collective-permute-start | bytes 589832 | tf_op jit(solution)/shard_map/ppermute | solution.py:28
  16.4 4.6 %collective-permute-start.7 = (bf16[8,64,128]{2,1,0:T(8,128)(2,1)S(1)}, bf16[8,64,128]{2,1,0:T(8,128)(2,1)S(1)}, u32[]{:S(2)}, u32[]{:S(2)}) collective-permute-start(bf16[8,64,128]{2,1,0:T(8,128)(2,1)S(1)} %stack.10.refs_4_), channel_id=1, source_target_pairs={{0,1},{1,0},{2,3},{3,2},{4,5},{5,4},{6,7},{7,6},{8,9},{9,8},{10,11... | collective-permute-start | bytes 393224 | tf_op jit(solution)/shard_map/ppermute | solution.py:28
  21.1 1.3 %collective-permute-start.8 = (bf16[8,64,128]{2,1,0:T(8,128)(2,1)S(1)}, bf16[8,64,128]{2,1,0:T(8,128)(2,1)S(1)}, u32[]{:S(2)}, u32[]{:S(2)}) collective-permute-start(bf16[8,64,128]{2,1,0:T(8,128)(2,1)S(1)} %collective-permute-done.6.refs_5_), channel_id=1, source_target_pairs={{0,1},{1,0},{2,3},{3,2},{4,5},{5,4},{6,7},{7,6},{8,9},{9,8},{10,11... | collective-permute-start | bytes 393224 | tf_op jit(solution)/shard_map/ppermute | solution.py:28
  29.4 9.7 %collective-permute-start.9 = (f32[40,64,128]{2,1,0:T(8,128)S(1)}, f32[40,64,128]{2,1,0:T(8,128)S(1)}, u32[]{:S(2)}, u32[]{:S(2)}) collective-permute-start(f32[40,64,128]{2,1,0:T(8,128)S(1)} %get-tuple-element.41), channel_id=1, source_target_pairs={{0,1},{1,0},{2,3},{3,2},{4,5},{5,4},{6,7},{7,6},{8,9},{9,8},{10,11... | collective-permute-start | bytes 3932168 | tf_op jit(solution)/shard_map/ppermute | solution.py:28
  29.5 9.6 %collective-permute-start.10 = (f32[64,128]{1,0:T(8,128)S(1)}, f32[64,128]{1,0:T(8,128)S(1)}, u32[]{:S(2)}, u32[]{:S(2)}) collective-permute-start(f32[64,128]{1,0:T(8,128)S(1)} %get-tuple-element.42), channel_id=1, source_target_pairs={{0,16},{4,20},{8,24},{12,28},{16,0},{20,4},{24,8},{28,12},{1,17},{... | collective-permute-start | bytes 98312 | tf_op jit(solution)/shard_map/ppermute | solution.py:28
  39.2 6.0 %collective-permute-start.11 = (bf16[8,64,128]{2,1,0:T(8,128)(2,1)S(1)}, bf16[8,64,128]{2,1,0:T(8,128)(2,1)S(1)}, u32[]{:S(2)}, u32[]{:S(2)}) collective-permute-start(bf16[8,64,128]{2,1,0:T(8,128)(2,1)S(1)} %get-tuple-element.44), channel_id=1, source_target_pairs={{0,2},{1,3},{2,0},{3,1},{4,6},{5,7},{6,4},{7,5},{8,10},{9,11},{10,... | collective-permute-start | bytes 393224 | tf_op jit(solution)/shard_map/ppermute | solution.py:28
  39.3 1.3 %collective-permute-start.12 = (f32[64,128]{1,0:T(8,128)S(1)}, f32[64,128]{1,0:T(8,128)S(1)}, u32[]{:S(2)}, u32[]{:S(2)}) collective-permute-start(f32[64,128]{1,0:T(8,128)S(1)} %add.14.refs_0_), channel_id=1, source_target_pairs={{0,1},{1,0},{2,3},{3,2},{4,5},{5,4},{6,7},{7,6},{8,9},{9,8},{10,11... | collective-permute-start | bytes 98312 | tf_op jit(solution)/shard_map/ppermute | solution.py:28
  40.6 4.7 %collective-permute-start.13 = (f32[64,128]{1,0:T(8,128)S(1)}, f32[64,128]{1,0:T(8,128)S(1)}, u32[]{:S(2)}, u32[]{:S(2)}) collective-permute-start(f32[64,128]{1,0:T(8,128)S(1)} %add.15.here), channel_id=1, source_target_pairs={{0,2},{1,3},{2,0},{3,1},{4,6},{5,7},{6,4},{7,5},{8,10},{9,11},{10,... | collective-permute-start | bytes 98312 | tf_op jit(solution)/shard_map/ppermute | solution.py:28
  45.3 4.9 %collective-permute-start.14 = (bf16[7,64,128]{2,1,0:T(8,128)(2,1)S(1)}, bf16[7,64,128]{2,1,0:T(8,128)(2,1)S(1)}, u32[]{:S(2)}, u32[]{:S(2)}) collective-permute-start(bf16[7,64,128]{2,1,0:T(8,128)(2,1)S(1)} %get-tuple-element.45.flip), channel_id=1, source_target_pairs={{0,4},{4,0},{8,12},{12,8},{16,20},{20,16},{24,28},{28,24},{1,5},{5... | collective-permute-start | bytes 344072 | tf_op jit(solution)/shard_map/ppermute | solution.py:28
  46.0 5.7 %collective-permute-start.15 = (bf16[12,64,128]{2,1,0:T(8,128)(2,1)S(1)}, bf16[12,64,128]{2,1,0:T(8,128)(2,1)S(1)}, u32[]{:S(2)}, u32[]{:S(2)}) collective-permute-start(bf16[12,64,128]{2,1,0:T(8,128)(2,1)S(1)} %get-tuple-element.50), channel_id=1, source_target_pairs={{0,2},{1,3},{2,0},{3,1},{4,6},{5,7},{6,4},{7,5},{8,10},{9,11},{10,... | collective-permute-start | bytes 589832 | tf_op jit(solution)/shard_map/ppermute | solution.py:28
  50.2 4.9 %collective-permute-start.16 = (bf16[7,64,128]{2,1,0:T(8,128)(2,1)S(1)}, bf16[7,64,128]{2,1,0:T(8,128)(2,1)S(1)}, u32[]{:S(2)}, u32[]{:S(2)}) collective-permute-start(bf16[7,64,128]{2,1,0:T(8,128)(2,1)S(1)} %get-tuple-element.48.passed), channel_id=1, source_target_pairs={{0,8},{4,12},{16,24},{20,28},{8,0},{12,4},{24,16},{28,20},{1,9},{5... | collective-permute-start | bytes 344072 | tf_op jit(solution)/shard_map/ppermute | solution.py:33
  50.2 1.5 %collective-permute-start.17 = (bf16[4,64,128]{2,1,0:T(8,128)(2,1)S(1)}, bf16[4,64,128]{2,1,0:T(8,128)(2,1)S(1)}, u32[]{:S(2)}, u32[]{:S(2)}) collective-permute-start(bf16[4,64,128]{2,1,0:T(8,128)(2,1)S(1)} %get-tuple-element.51), channel_id=1, source_target_pairs={{8,16},{12,20},{16,8},{20,12},{9,17},{13,21},{17,9},{21,13},{10,18... | collective-permute-start | bytes 196616 | tf_op jit(solution)/shard_map/ppermute | solution.py:33
  58.4 11.8 %collective-permute-start.18 = (bf16[12,64,128]{2,1,0:T(8,128)(2,1)S(1)}, bf16[12,64,128]{2,1,0:T(8,128)(2,1)S(1)}, u32[]{:S(2)}, u32[]{:S(2)}) collective-permute-start(bf16[12,64,128]{2,1,0:T(8,128)(2,1)S(1)} %get-tuple-element.52.refs_0_.basis), channel_id=1, source_target_pairs={{0,2},{1,3},{2,0},{3,1},{4,6},{5,7},{6,4},{7,5},{8,10},{9,11},{10,... | collective-permute-start | bytes 589832 | tf_op jit(solution)/shard_map/ppermute | solution.py:28
  59.6 10.5 %collective-permute-start.19 = (bf16[12,64,128]{2,1,0:T(8,128)(2,1)S(1)}, bf16[12,64,128]{2,1,0:T(8,128)(2,1)S(1)}, u32[]{:S(2)}, u32[]{:S(2)}) collective-permute-start(bf16[12,64,128]{2,1,0:T(8,128)(2,1)S(1)} %get-tuple-element.52.refs_0_.basis), channel_id=1, source_target_pairs={{0,1},{1,0},{2,3},{3,2},{4,5},{5,4},{6,7},{7,6},{8,9},{9,8},{10,11... | collective-permute-start | bytes 589832 | tf_op jit(solution)/shard_map/ppermute | solution.py:28
  59.6 6.1 %collective-permute-start.21 = (bf16[4,64,128]{2,1,0:T(8,128)(2,1)S(1)}, bf16[4,64,128]{2,1,0:T(8,128)(2,1)S(1)}, u32[]{:S(2)}, u32[]{:S(2)}) collective-permute-start(bf16[4,64,128]{2,1,0:T(8,128)(2,1)S(1)} %get-tuple-element.54), channel_id=1, source_target_pairs={{0,8},{4,12},{16,24},{20,28},{8,0},{12,4},{24,16},{28,20},{1,9},{5... | collective-permute-start | bytes 196616 | tf_op jit(solution)/shard_map/ppermute | solution.py:33
  63.0 2.8 %collective-permute-start.22 = (bf16[4,64,128]{2,1,0:T(8,128)(2,1)S(1)}, bf16[4,64,128]{2,1,0:T(8,128)(2,1)S(1)}, u32[]{:S(2)}, u32[]{:S(2)}) collective-permute-start(bf16[4,64,128]{2,1,0:T(8,128)(2,1)S(1)} %get-tuple-element.55), channel_id=1, source_target_pairs={{8,16},{12,20},{16,8},{20,12},{9,17},{13,21},{17,9},{21,13},{10,18... | collective-permute-start | bytes 196616 | tf_op jit(solution)/shard_map/ppermute | solution.py:33
  65.8 4.3 %collective-permute-start.23 = (bf16[4,64,128]{2,1,0:T(8,128)(2,1)S(1)}, bf16[4,64,128]{2,1,0:T(8,128)(2,1)S(1)}, u32[]{:S(2)}, u32[]{:S(2)}) collective-permute-start(bf16[4,64,128]{2,1,0:T(8,128)(2,1)S(1)} %pass_on.3), channel_id=1, source_target_pairs={{0,4},{4,0},{8,12},{12,8},{16,20},{20,16},{24,28},{28,24},{1,5},{5... | collective-permute-start | bytes 196616 | tf_op jit(solution)/shard_map/ppermute | solution.py:28
  70.2 5.0 %collective-permute-start.24 = (bf16[8,64,128]{2,1,0:T(8,128)(2,1)S(1)}, bf16[8,64,128]{2,1,0:T(8,128)(2,1)S(1)}, u32[]{:S(2)}, u32[]{:S(2)}) collective-permute-start(bf16[8,64,128]{2,1,0:T(8,128)(2,1)S(1)} %stack.11.refs_4_), channel_id=1, source_target_pairs={{0,2},{1,3},{2,0},{3,1},{4,6},{5,7},{6,4},{7,5},{8,10},{9,11},{10,... | collective-permute-start | bytes 393224 | tf_op jit(solution)/shard_map/ppermute | solution.py:28
  71.0 4.1 %collective-permute-start.20 = (bf16[12,64,128]{2,1,0:T(8,128)(2,1)S(1)}, bf16[12,64,128]{2,1,0:T(8,128)(2,1)S(1)}, u32[]{:S(2)}, u32[]{:S(2)}) collective-permute-start(bf16[12,64,128]{2,1,0:T(8,128)(2,1)S(1)} %collective-permute-done.18.refs_0_.refs_1_), channel_id=1, source_target_pairs={{0,1},{1,0},{2,3},{3,2},{4,5},{5,4},{6,7},{7,6},{8,9},{9,8},{10,11... | collective-permute-start | bytes 589832 | tf_op jit(solution)/shard_map/ppermute | solution.py:28
  71.1 4.1 %collective-permute-start.25 = (bf16[8,64,128]{2,1,0:T(8,128)(2,1)S(1)}, bf16[8,64,128]{2,1,0:T(8,128)(2,1)S(1)}, u32[]{:S(2)}, u32[]{:S(2)}) collective-permute-start(bf16[8,64,128]{2,1,0:T(8,128)(2,1)S(1)} %stack.11.refs_4_), channel_id=1, source_target_pairs={{0,1},{1,0},{2,3},{3,2},{4,5},{5,4},{6,7},{7,6},{8,9},{9,8},{10,11... | collective-permute-start | bytes 393224 | tf_op jit(solution)/shard_map/ppermute | solution.py:28
  75.2 1.3 %collective-permute-start.26 = (bf16[8,64,128]{2,1,0:T(8,128)(2,1)S(1)}, bf16[8,64,128]{2,1,0:T(8,128)(2,1)S(1)}, u32[]{:S(2)}, u32[]{:S(2)}) collective-permute-start(bf16[8,64,128]{2,1,0:T(8,128)(2,1)S(1)} %collective-permute-done.24.refs_5_), channel_id=1, source_target_pairs={{0,1},{1,0},{2,3},{3,2},{4,5},{5,4},{6,7},{7,6},{8,9},{9,8},{10,11... | collective-permute-start | bytes 393224 | tf_op jit(solution)/shard_map/ppermute | solution.py:28
  83.5 8.4 %collective-permute-start.27 = (f32[40,64,128]{2,1,0:T(8,128)S(1)}, f32[40,64,128]{2,1,0:T(8,128)S(1)}, u32[]{:S(2)}, u32[]{:S(2)}) collective-permute-start(f32[40,64,128]{2,1,0:T(8,128)S(1)} %get-tuple-element.57), channel_id=1, source_target_pairs={{0,1},{1,0},{2,3},{3,2},{4,5},{5,4},{6,7},{7,6},{8,9},{9,8},{10,11... | collective-permute-start | bytes 3932168 | tf_op jit(solution)/shard_map/ppermute | solution.py:28
  83.6 8.3 %collective-permute-start.28 = (f32[64,128]{1,0:T(8,128)S(1)}, f32[64,128]{1,0:T(8,128)S(1)}, u32[]{:S(2)}, u32[]{:S(2)}) collective-permute-start(f32[64,128]{1,0:T(8,128)S(1)} %get-tuple-element.58), channel_id=1, source_target_pairs={{0,16},{4,20},{8,24},{12,28},{16,0},{20,4},{24,8},{28,12},{1,17},{... | collective-permute-start | bytes 98312 | tf_op jit(solution)/shard_map/ppermute | solution.py:28
  91.9 6.0 %collective-permute-start.29 = (bf16[8,64,128]{2,1,0:T(8,128)(2,1)S(1)}, bf16[8,64,128]{2,1,0:T(8,128)(2,1)S(1)}, u32[]{:S(2)}, u32[]{:S(2)}) collective-permute-start(bf16[8,64,128]{2,1,0:T(8,128)(2,1)S(1)} %get-tuple-element.60), channel_id=1, source_target_pairs={{0,2},{1,3},{2,0},{3,1},{4,6},{5,7},{6,4},{7,5},{8,10},{9,11},{10,... | collective-permute-start | bytes 393224 | tf_op jit(solution)/shard_map/ppermute | solution.py:28
  92.4 1.2 %collective-permute-start.30 = (f32[64,128]{1,0:T(8,128)S(1)}, f32[64,128]{1,0:T(8,128)S(1)}, u32[]{:S(2)}, u32[]{:S(2)}) collective-permute-start(f32[64,128]{1,0:T(8,128)S(1)} %add.16.refs_0_), channel_id=1, source_target_pairs={{0,1},{1,0},{2,3},{3,2},{4,5},{5,4},{6,7},{7,6},{8,9},{9,8},{10,11... | collective-permute-start | bytes 98312 | tf_op jit(solution)/shard_map/ppermute | solution.py:28
  93.6 4.4 %collective-permute-start.31 = (f32[64,128]{1,0:T(8,128)S(1)}, f32[64,128]{1,0:T(8,128)S(1)}, u32[]{:S(2)}, u32[]{:S(2)}) collective-permute-start(f32[64,128]{1,0:T(8,128)S(1)} %add.17.here), channel_id=1, source_target_pairs={{0,2},{1,3},{2,0},{3,1},{4,6},{5,7},{6,4},{7,5},{8,10},{9,11},{10,... | collective-permute-start | bytes 98312 | tf_op jit(solution)/shard_map/ppermute | solution.py:28
  98.0 4.9 %collective-permute-start.32 = (bf16[7,64,128]{2,1,0:T(8,128)(2,1)S(1)}, bf16[7,64,128]{2,1,0:T(8,128)(2,1)S(1)}, u32[]{:S(2)}, u32[]{:S(2)}) collective-permute-start(bf16[7,64,128]{2,1,0:T(8,128)(2,1)S(1)} %get-tuple-element.61.flip), channel_id=1, source_target_pairs={{0,4},{4,0},{8,12},{12,8},{16,20},{20,16},{24,28},{28,24},{1,5},{5... | collective-permute-start | bytes 344072 | tf_op jit(solution)/shard_map/ppermute | solution.py:28
  98.2 6.0 %collective-permute-start.33 = (bf16[12,64,128]{2,1,0:T(8,128)(2,1)S(1)}, bf16[12,64,128]{2,1,0:T(8,128)(2,1)S(1)}, u32[]{:S(2)}, u32[]{:S(2)}) collective-permute-start(bf16[12,64,128]{2,1,0:T(8,128)(2,1)S(1)} %get-tuple-element.66), channel_id=1, source_target_pairs={{0,2},{1,3},{2,0},{3,1},{4,6},{5,7},{6,4},{7,5},{8,10},{9,11},{10,... | collective-permute-start | bytes 589832 | tf_op jit(solution)/shard_map/ppermute | solution.py:28
  102.9 4.9 %collective-permute-start.34 = (bf16[7,64,128]{2,1,0:T(8,128)(2,1)S(1)}, bf16[7,64,128]{2,1,0:T(8,128)(2,1)S(1)}, u32[]{:S(2)}, u32[]{:S(2)}) collective-permute-start(bf16[7,64,128]{2,1,0:T(8,128)(2,1)S(1)} %get-tuple-element.64.passed), channel_id=1, source_target_pairs={{0,8},{4,12},{16,24},{20,28},{8,0},{12,4},{24,16},{28,20},{1,9},{5... | collective-permute-start | bytes 344072 | tf_op jit(solution)/shard_map/ppermute | solution.py:33
  103.0 1.2 %collective-permute-start.35 = (bf16[4,64,128]{2,1,0:T(8,128)(2,1)S(1)}, bf16[4,64,128]{2,1,0:T(8,128)(2,1)S(1)}, u32[]{:S(2)}, u32[]{:S(2)}) collective-permute-start(bf16[4,64,128]{2,1,0:T(8,128)(2,1)S(1)} %get-tuple-element.67), channel_id=1, source_target_pairs={{8,16},{12,20},{16,8},{20,12},{9,17},{13,21},{17,9},{21,13},{10,18... | collective-permute-start | bytes 196616 | tf_op jit(solution)/shard_map/ppermute | solution.py:33

commit v4 on v3

--- a/solution.py
+++ b/solution.py
@@ -8,6 +8,7 @@
 from jax.sharding import PartitionSpec as P
 
 ITERS = 2
+STREAMED = 8
 F32 = jnp.float32
 BF16 = jnp.bfloat16
 NT = (((1,), (1,)), ((), ()))
@@ -28,6 +29,13 @@
     return lax.ppermute(x, axis, [(i, i ^ bit) for i in range(peers)])
 
 
+def swap_both(x, dom_bit, sub_bit):
+    subs = lax.axis_size("sub")
+    peers = [(p, s) for p in range(lax.axis_size("dom")) for s in range(subs)]
+    pairs = [(p * subs + s, (p ^ dom_bit) * subs + (s ^ sub_bit)) for p, s in peers]
+    return lax.ppermute(x, ("dom", "sub"), pairs)
+
+
 def pair_up(x, pairing):
     low = [p for p in range(lax.axis_size("dom") - 2) if PAIRINGS[pairing](p)]
     return lax.ppermute(x, "dom", [(p, p + 2) for p in low] + [(p + 2, p) for p in low])
@@ -42,7 +50,7 @@
 
 
 def joined(ref, start):
-    return ref[start + 2].astype(F32) + ref[start + 1].astype(F32) + ref[start].astype(F32)
+    return ref[start + 1].astype(F32) + ref[start].astype(F32)
 
 
 class Facts:
@@ -141,30 +149,30 @@
     )(ways, flip, first, second)
 
 
-def stack(slots, flip, first, second, *refs):
-    out = refs[-1]
-    for s in range(2 * slots):
-        out[s] = flip[s]
-    for s in range(slots):
-        out[2 * slots + s] = first[s]
-        out[3 * slots + s] = second[s]
-
-
-def call_stack(slots, flip, first, second, after):
-    return pl.pallas_call(
-        functools.partial(stack, slots),
-        in_specs=[VMEM] * 3 + [ANY] * len(after),
+def stack(counts, *refs):
+    out, place = refs[-1], 0
+    for ref, count in zip(refs, counts):
+        for i in range(count):
+            out[place + i] = ref[i]
+        place += count
+
+
+def call_stack(pieces, counts, after=()):
+    return pl.pallas_call(
+        functools.partial(stack, counts),
+        in_specs=[VMEM] * len(pieces) + [ANY] * len(after),
         out_specs=VMEM,
-        out_shape=jax.ShapeDtypeStruct((4 * slots,) + flip.shape[1:], BF16),
+        out_shape=jax.ShapeDtypeStruct((sum(counts),) + pieces[0].shape[1:], pieces[0].dtype),
         compiler_params=SMALL,
         name="stack",
-    )(flip, first, second, *after)
-
-
-def forward_adjoint(shape, relatives, facts, cols, tiles, friction, *refs):
+    )(*pieces, *after)
+
+
+def forward_adjoint(shape, relatives, sources, facts, cols, tiles, friction, *refs):
     neigh, slots = shape
     count = len(relatives)
-    own_parts, halo_parts, refs = refs[:count], refs[count : 2 * count], refs[2 * count :]
+    inputs = 1 + max(ref for places in sources for ref, _ in places)
+    parts, refs = refs[:inputs], refs[inputs:]
     keep, send, grams = refs[:3]
     facts = Facts(facts, neigh, slots)
     blocks, tiles_row, width = tiles.shape[0], tiles.shape[1], tiles.shape[2]
@@ -180,13 +188,13 @@
         ]
         for r in relatives
     ]
-    for part, base in zip(own_parts, own_base):
+    for (own, first, second), base, bases in zip(sources, own_base, halo_base):
         for i in range(blocks):
-            columns[base + i] = part[i]
-    for part, bases in zip(halo_parts, halo_base):
+            columns[base + i] = parts[own[0]][own[1] + i]
         for i in range(neigh):
+            part, place = (first, second)[i // 2]
             for s in range(slots):
-                columns[bases[i] + s] = part[i * slots + s]
+                columns[bases[i] + s] = parts[part][place + i % 2 * slots + s]
     total[...] = jnp.zeros_like(total)
     weights[...] = jnp.zeros_like(weights)
     pieces[...] = jnp.zeros_like(pieces)
@@ -194,7 +202,9 @@
     def forward(row):
         picked = jnp.concatenate([columns[cols[row, j]] for j in range(tiles_row)], axis=1)
         wide = jnp.concatenate([tiles[row, j] for j in range(tiles_row)], axis=1)
-        state = lax.dot_general(wide, picked, NT, preferred_element_type=F32).T
+        cut = STREAMED * width
+        state = lax.dot_general(wide[:, :cut], picked[:, :cut], NT, preferred_element_type=F32).T
+        state += lax.dot_general(picked[:, cut:], wide[:, cut:], NT, preferred_element_type=F32)
         weights[row] = (friction[pl.ds(row, 1), :] * state).astype(BF16)
         pieces[row] = jnp.concatenate(split_bf16(state, 2), axis=1)
 
@@ -216,7 +226,7 @@
     lax.fori_loop(0, live_rows - 1, step, 0)
     adjoint(live_rows - 1)
 
-    mine = jnp.concatenate([own_parts[0][i] for i in range(blocks)], axis=1)
+    mine = jnp.concatenate([parts[0][i] for i in range(blocks)], axis=1)
     basis_gram = lax.dot_general(mine, mine, NT, preferred_element_type=F32)
     cross_gram = lax.dot_general(
         jnp.concatenate([pieces[i] for i in range(blocks)], axis=1),
@@ -241,9 +251,9 @@
             place += neigh * slots
 
 
-def call_forward_adjoint(shape, relatives, facts, cols, tiles, friction, own_parts, halo_parts):
+def call_forward_adjoint(shape, relatives, sources, facts, cols, tiles, friction, parts):
     blocks, tiles_row, width = tiles.shape[0], tiles.shape[1], tiles.shape[2]
-    dirs = own_parts[0].shape[1]
+    dirs = parts[0].shape[1]
     count = len(relatives)
     own, halo = count * blocks, count * shape[0] * shape[1]
     out = lambda n: jax.ShapeDtypeStruct((n, dirs, width), F32)
@@ -255,8 +265,8 @@
         pltpu.VMEM((blocks, dirs, 2 * width), BF16),
     ]
     return pl.pallas_call(
-        functools.partial(forward_adjoint, shape, relatives),
-        in_specs=[SMEM, SMEM, VMEM, VMEM] + [VMEM] * (2 * count),
+        functools.partial(forward_adjoint, shape, relatives, sources),
+        in_specs=[SMEM, SMEM, VMEM, VMEM] + [VMEM] * len(parts),
         out_specs=[VMEM] * len(out_shape),
         out_shape=out_shape,
         scratch_shapes=scratch_shapes,
@@ -267,7 +277,7 @@
             transcendentals=0,
         ),
         name="forward_adjoint",
-    )(facts, cols, tiles, friction, *own_parts, *halo_parts)
+    )(facts, cols, tiles, friction, *parts)
 
 
 def join(start, keep, got, *refs):
@@ -290,51 +300,58 @@
     )(keep, got, *after)
 
 
-def hand_back(slots, near_halo, far_halo, here, there, flip, first, second):
-    sums = [(near_halo[i] + far_halo[i].astype(F32)).astype(BF16) for i in range(near_halo.shape[0])]
-    for s in range(2 * slots):
-        flip[s] = sums[s]
+def hand_back(slots, blocks, keep, got, here, there, near_flip, far_flip, far_pairs, near_pairs):
+    pair = 2 * slots
+    near = [keep[2 * blocks + i] + got[2 * blocks + i] for i in range(2 * pair)]
+    far = [keep[2 * blocks + 2 * pair + i] + got[2 * blocks + 2 * pair + i] for i in range(2 * pair)]
+    for i in range(pair):
+        near_flip[i] = near[i].astype(BF16)
+        far_flip[i] = far[i].astype(BF16)
+        far_pairs[i] = far[pair + i].astype(BF16)
+        near_pairs[i] = near[pair + i]
+    for i, piece in enumerate(split_bf16(here[...] + there[...], 2)):
+        for out in (near_flip, far_flip, far_pairs):
+            out[pair + i] = piece
+
+
+def call_hand_back(slots, blocks, keep, got, here, there):
+    pair, tail = 2 * slots, keep.shape[1:]
+    out = jax.ShapeDtypeStruct((pair + 2,) + tail, BF16)
+    return pl.pallas_call(
+        functools.partial(hand_back, slots, blocks),
+        in_specs=[VMEM] * 4,
+        out_specs=[VMEM] * 4,
+        out_shape=[out, out, out, jax.ShapeDtypeStruct((pair,) + tail, F32)],
+        compiler_params=SMALL,
+        name="hand_back",
+    )(keep, got, here, there)
+
+
+def pass_back(slots, ways, sent, flip, flip_far, far, near_pairs, first, second, own):
+    pair = 2 * slots
     for s in range(slots):
-        first[s] = sums[2 * slots + s]
-        second[s] = sums[3 * slots + s]
-    for i, piece in enumerate(split_bf16(here[...] + there[...], 3)):
-        flip[2 * slots + i] = piece
-
-
-def call_hand_back(slots, near_halo, far_halo, here, there):
-    tail = near_halo.shape[1:]
-    out = lambda n: jax.ShapeDtypeStruct((n,) + tail, BF16)
-    return pl.pallas_call(
-        functools.partial(hand_back, slots),
-        in_specs=[VMEM] * 4,
+        own[s] = flip[s].astype(F32) + flip_far[s].astype(F32)
+        relayed = (flip[slots + s].astype(F32) + flip_far[slots + s].astype(F32)).astype(BF16)
+        for pairing, out in enumerate((first, second)):
+            i = pairing * slots + s
+            out[s] = (near_pairs[i] + far[i].astype(F32)).astype(BF16)
+            out[slots + s] = relayed * ways[pairing, :1]
+    grams = (joined(sent, pair) + joined(far, pair)) + (joined(flip, pair) + joined(flip_far, pair))
+    for i, piece in enumerate(split_bf16(grams, 2)):
+        first[pair + i] = piece
+
+
+def call_pass_back(slots, ways, sent, flip, flip_far, far, near_pairs):
+    pair, tail = 2 * slots, flip.shape[1:]
+    out = lambda n, t: jax.ShapeDtypeStruct((n,) + tail, t)
+    return pl.pallas_call(
+        functools.partial(pass_back, slots),
+        in_specs=[VMEM] * 6,
         out_specs=[VMEM] * 3,
-        out_shape=[out(2 * slots + 3), out(slots), out(slots)],
-        compiler_params=SMALL,
-        name="hand_back",
-    )(near_halo, far_halo, here, there)
-
-
-def pass_back(slots, ways, flip, got, first, second, first_out, second_out):
-    for s in range(slots):
-        first_out[s] = first[s]
-        second_out[s] = second[s]
-        first_out[slots + s] = got[slots + s] * ways[0, :1]
-        second_out[slots + s] = got[slots + s] * ways[1, :1]
-    for i, piece in enumerate(split_bf16(joined(flip, 2 * slots) + joined(got, 2 * slots), 3)):
-        first_out[2 * slots + i] = piece
-
-
-def call_pass_back(slots, ways, flip, got, first, second):
-    tail = flip.shape[1:]
-    out = lambda n: jax.ShapeDtypeStruct((n,) + tail, BF16)
-    return pl.pallas_call(
-        functools.partial(pass_back, slots),
-        in_specs=[VMEM] * 5,
-        out_specs=[VMEM] * 2,
-        out_shape=[out(2 * slots + 3), out(2 * slots)],
+        out_shape=[out(pair + 2, BF16), out(pair, BF16), out(slots, F32)],
         compiler_params=SMALL,
         name="pass_back",
-    )(ways, flip, got, first, second)
+    )(ways, sent, flip, flip_far, far, near_pairs)
 
 
 def eliminate(grams, dirs):
@@ -426,27 +443,33 @@
     for step in range(ITERS):
         own_far, own_near = swap(basis, "sub", far), swap(basis, "sub", near)
         pairs = [pair_up(x, i) for i, x in enumerate(outgoing[1:])]
-        flip = swap(call_pass_on(slots, ways, outgoing[0], *pairs), "dom", dom_bits[0])
-        halo = call_stack(slots, flip, *pairs, [own_far, own_near])
-        halo_far = swap(halo, "sub", far)
-        own_parts = [basis, own_far, own_near, swap(own_far, "sub", near)]
-        halo_parts = [halo, halo_far, swap(halo, "sub", near), swap(halo_far, "sub", near)]
+        pair = 2 * slots
+        onward = call_pass_on(slots, ways, outgoing[0], *pairs)
+        flip, far01 = swap(onward, "dom", dom_bits[0]), swap_both(onward, dom_bits[0], far)
+        halo23 = call_stack(pairs, (slots, slots), [own_near, own_far])
+        far23 = swap(halo23, "sub", far)
+        rest = swap(call_stack([flip, halo23, far01, far23], (pair,) * 4), "sub", near)
+        parts = [basis, own_near, own_far, swap(own_far, "sub", near)]
+        parts += [flip, halo23, far01, far23, rest]
+        sources = (
+            ((0, 0), (4, 0), (5, 0)),
+            ((2, 0), (6, 0), (7, 0)),
+            ((1, 0), (8, 0), (8, pair)),
+            ((3, 0), (8, 2 * pair), (8, 3 * pair)),
+        )
         keep, send, grams = call_forward_adjoint(
-            shape, relatives, facts, tile_cols, tiles, friction, own_parts, halo_parts
+            shape, relatives, sources, facts, tile_cols, tiles, friction, parts
         )
         for bit in dom_bits[2:]:
             grams = grams + swap(grams, "dom", bit)
-        got = swap(send, "sub", near)
-        near_halo, far_halo = call_join(2 * blocks, neigh * slots, keep, got, [grams])
-        far_halo = swap(far_halo, "sub", far)
-        grams = grams + swap(grams, "sub", near)
-        grams_got = swap(grams, "sub", far)
-        near_own, far_own = call_join(0, blocks, keep, got, [grams_got])
+        got, grams_got = swap(send, "sub", near), swap(grams, "sub", near)
+        near_flip, far_flip, far_pairs, near_pairs = call_hand_back(slots, blocks, keep, got, grams, grams_got)
+        flip, flip_far = swap(near_flip, "dom", dom_bits[0]), swap_both(far_flip, dom_bits[0], far)
+        pairs_got = swap(far_pairs, "sub", far)
+        near_own, far_own = call_join(0, blocks, keep, got, [pairs_got])
         far_own_got = swap(far_own, "sub", far)
-        flip, *back = call_hand_back(slots, near_halo, far_halo, grams, grams_got)
-        flip_got = swap(flip, "dom", dom_bits[0])
-        back = call_pass_back(slots, ways, flip, flip_got, *back)
-        returned = [flip_got] + [pair_up(x, i) for i, x in enumerate(back)]
+        *back, flip = call_pass_back(slots, ways, near_flip, flip, flip_far, pairs_got, near_pairs)
+        returned = [flip] + [pair_up(x, i) for i, x in enumerate(back)]
         last = step == ITERS - 1
         basis, *outgoing = call_project(
             shape, last, facts, back[0], basis, near_own, far_own_got, returned

time: 113 us -> 105 us (0.929)
  waiting for transfers between devices: 48.7 us -> 31.2 us
  starting transfers between devices: 37 us -> 48.2 us
  Pallas kernels: 22.5 us -> 20.5 us
    ppermute x28 -> x24, waiting for transfers between devices: 37.5 us -> 15.5 us  [swap(): return lax.ppermute(x, axis, [(i, i ^ bit) for i in range(peers)])]
    ppermute x0 -> x4, waiting for transfers between devices: none -> 8.02 us  [swap_both(): return lax.ppermute(x, ('dom', 'sub'), pairs)]
    ppermute x8, starting transfers between devices: 7.74 us -> 13.9 us  [pair_up(): lax.ppermute(x, 'dom', [(p, p + 2) for p in low] + [(p + 2, p) for p in l...]
    ppermute x0 -> x4, starting transfers between devices: none -> 3.78 us  [swap_both(): return lax.ppermute(x, ('dom', 'sub'), pairs)]
    ppermute x8, waiting for transfers between devices: 11.3 us -> 7.65 us  [pair_up(): lax.ppermute(x, 'dom', [(p, p + 2) for p in low] + [(p + 2, p) for p in l...]
    pallas_call x8 -> x10, Pallas kernels: 14.1 us -> 12.1 us  [the longest x2 11.8 us: call_forward_adjoint(): pl.pallas_call(functools.partial(forward_adjoint, shape, relatives, sourc...]
    ppermute x28 -> x24, starting transfers between devices: 29.2 us -> 30.5 us  [swap(): return lax.ppermute(x, axis, [(i, i ^ bit) for i in range(peers)])]
  transfers between devices with their start and end apart: 36 -> 36, of which waited for: 20 -> 21; matrix products, arithmetic and copies ran while one was open for 0% -> 0% of each run, Pallas kernels for 0% -> 0%
where the time goes in v4:
time: 105 us; the launch traced here: 103 us
  starting transfers between devices  48.2 us (46%)
  waiting for transfers between devices  31.2 us (30%)
  Pallas kernels  20.5 us (20%)
  between operations  1.52 us (1%)
  local copies, waits for them, and re-layouts  1.13 us (1%)
    ppermute x24, starting transfers between devices, swap(): return lax.ppermute(x, axis, [(i, i ^ bit) for i in range(peers)])  30.5 us
    ppermute x24, waiting for transfers between devices, swap(): return lax.ppermute(x, axis, [(i, i ^ bit) for i in range(peers)])  15.5 us
    ppermute x8, starting transfers between devices, pair_up(): lax.ppermute(x, 'dom', [(p, p + 2) for p in low] + [(p + 2, p) for p in l...  13.9 us
    pallas_call x2, Pallas kernels, call_forward_adjoint(): pl.pallas_call(functools.partial(forward_adjoint, shape, relatives, sourc...  11.8 us
    ppermute x4, waiting for transfers between devices, swap_both(): return lax.ppermute(x, ('dom', 'sub'), pairs)  8.02 us
    ppermute x8, waiting for transfers between devices, pair_up(): lax.ppermute(x, 'dom', [(p, p + 2) for p in low] + [(p + 2, p) for p in l...  7.65 us
    pallas_call x2, Pallas kernels, call_project(): pl.pallas_call(functools.partial(project, shape, last), in_specs=[SMEM] +...  7.36 us
    ppermute x4, starting transfers between devices, swap_both(): return lax.ppermute(x, ('dom', 'sub'), pairs)  3.78 us
  transfers between devices with their start and end apart: 36, of which 21 were waited for; matrix products, arithmetic and copies ran while one was open for 0% of the time, Pallas kernels for 0%

profile of v4, /device:TPU:0, one launch (start us, length us, event | category | flops | bytes accessed | tf_op | source)
XLA Modules:
  0.0 103.4 jit_solution(5479723477659757402)
XLA Ops:
  1.3 0.1 pad_add_fusion.1
  1.4 0.9 pad_add_fusion.facts
  2.2 1.1 %copy-done.2 = bf16[12,64,128]{2,1,0:T(8,128)(2,1)S(1)} copy-done((bf16[12,64,128]{2,1,0:T(8,128)(2,1)S(1)}, bf16[12,64,128]{2,1,0:T(8,128)(2,1)}, u32[]{:S(2)}) %copy-start.2) | copy-done | bytes 196632
  3.3 0.8 prepare.1
  4.1 0.5 collective-permute-start
  4.7 2.6 %collective-permute-start.1 = (bf16[12,64,128]{2,1,0:T(8,128)(2,1)S(1)}, bf16[12,64,128]{2,1,0:T(8,128)(2,1)S(1)}, u32[]{:S(2)}, u32[]{:S(2)}) collective-permute-start(bf16[12,64,128]{2,1,0:T(8,128)(2,1)S(1)} %get-tuple-element.36.refs_0_.basis), channel_id=1, source_target_pairs={{0,2},{1,3},{2,0},{3,1},{4,6},{5,7},{6,4},{7,5},{8,10},{9,11},{10,... | collective-permute-start | bytes 589832 | tf_op jit(solution)/shard_map/ppermute | solution.py:29
  7.2 1.6 %collective-permute-start.3 = (bf16[4,64,128]{2,1,0:T(8,128)(2,1)S(1)}, bf16[4,64,128]{2,1,0:T(8,128)(2,1)S(1)}, u32[]{:S(2)}, u32[]{:S(2)}) collective-permute-start(bf16[4,64,128]{2,1,0:T(8,128)(2,1)S(1)} %get-tuple-element.38), channel_id=1, source_target_pairs={{0,8},{4,12},{16,24},{20,28},{8,0},{12,4},{24,16},{28,20},{1,9},{5... | collective-permute-start | bytes 196616 | tf_op jit(solution)/shard_map/ppermute | solution.py:41
  8.8 0.7 collective-permute-start.4
  9.5 2.0 %collective-permute-done.3.first.refs_0_ = bf16[4,64,128]{2,1,0:T(8,128)(2,1)S(1)} collective-permute-done((bf16[4,64,128]{2,1,0:T(8,128)(2,1)S(1)}, bf16[4,64,128]{2,1,0:T(8,128)(2,1)S(1)}, u32[]{:S(2)}, u32[]{:S(2)}) %collective-permute-start.3) | collective-permute-done | bytes 65568 | tf_op jit(solution)/shard_map/ppermute | solution.py:41
  11.5 1.6 %collective-permute-start.5 = (bf16[4,64,128]{2,1,0:T(8,128)(2,1)S(1)}, bf16[4,64,128]{2,1,0:T(8,128)(2,1)S(1)}, u32[]{:S(2)}, u32[]{:S(2)}) collective-permute-start(bf16[4,64,128]{2,1,0:T(8,128)(2,1)S(1)} %pass_on.2), channel_id=1, source_target_pairs={{0,4},{4,0},{8,12},{12,8},{16,20},{20,16},{24,28},{28,24},{1,5},{5... | collective-permute-start | bytes 196616 | tf_op jit(solution)/shard_map/ppermute | solution.py:29
  13.1 0.2 collective-permute-start.6
  13.3 1.9 %collective-permute-start.7 = (bf16[4,64,128]{2,1,0:T(8,128)(2,1)S(1)}, bf16[4,64,128]{2,1,0:T(8,128)(2,1)S(1)}, u32[]{:S(2)}, u32[]{:S(2)}) collective-permute-start(bf16[4,64,128]{2,1,0:T(8,128)(2,1)S(1)} %stack.12.refs_1_.refs_5_), channel_id=1, source_target_pairs={{0,2},{1,3},{2,0},{3,1},{4,6},{5,7},{6,4},{7,5},{8,10},{9,11},{10,... | collective-permute-start | bytes 196616 | tf_op jit(solution)/shard_map/ppermute | solution.py:29
  15.2 0.9 collective-permute-done.5.refs_0_.refs_4_
  16.1 2.3 %collective-permute-done.6.refs_2_.refs_6_ = bf16[4,64,128]{2,1,0:T(8,128)(2,1)S(1)} collective-permute-done((bf16[4,64,128]{2,1,0:T(8,128)(2,1)S(1)}, bf16[4,64,128]{2,1,0:T(8,128)(2,1)S(1)}, u32[]{:S(2)}, u32[]{:S(2)}) %collective-permute-start.6) | collective-permute-done | bytes 65568 | tf_op jit(solution)/shard_map/ppermute | solution.py:36
  18.4 0.1 collective-permute-start.8
  18.5 0.5 collective-permute-start.2
  19.0 1.3 %collective-permute-done.2.refs_3_ = bf16[12,64,128]{2,1,0:T(8,128)(2,1)S(1)} collective-permute-done((bf16[12,64,128]{2,1,0:T(8,128)(2,1)S(1)}, bf16[12,64,128]{2,1,0:T(8,128)(2,1)S(1)}, u32[]{:S(2)}, u32[]{:S(2)}) %collective-permute-start.2) | collective-permute-done | bytes 196640 | tf_op jit(solution)/shard_map/ppermute | solution.py:29
  20.3 5.9 %forward_adjoint.2 = (f32[40,64,128]{2,1,0:T(8,128)S(1)}, f32[40,64,128]{2,1,0:T(8,128)S(1)}, f32[64,128]{1,0:T(8,128)S(1)}) custom-call(s32[5,4]{1,0:T(8,128)S(1)} %pad_add_fusion.facts, s32[12,27]{1,0:T(8,128)S(1)} %copy-done, bf16[12,27,128,128]{3,2,1,0:T(8,128)(2,1)S(1)} %bitcast.8, f32[12,128]{1,0:T(8,128)S(1)} %copy-done.1, ...), custom_call_target="tpu_custom_call" | custom-call | flops 1358954496 | bytes 10616832 | tf_op jit(solution)/shard_map/forward_adjoint/pallas_call | solution.py:267
  26.2 2.4 %collective-permute-start.9 = (f32[40,64,128]{2,1,0:T(8,128)S(1)}, f32[40,64,128]{2,1,0:T(8,128)S(1)}, u32[]{:S(2)}, u32[]{:S(2)}) collective-permute-start(f32[40,64,128]{2,1,0:T(8,128)S(1)} %get-tuple-element.41), channel_id=1, source_target_pairs={{0,1},{1,0},{2,3},{3,2},{4,5},{5,4},{6,7},{7,6},{8,9},{9,8},{10,11... | collective-permute-start | bytes 3932168 | tf_op jit(solution)/shard_map/ppermute | solution.py:29
  28.6 5.2 %collective-permute-start.10 = (f32[64,128]{1,0:T(8,128)S(1)}, f32[64,128]{1,0:T(8,128)S(1)}, u32[]{:S(2)}, u32[]{:S(2)}) collective-permute-start(f32[64,128]{1,0:T(8,128)S(1)} %get-tuple-element.42), channel_id=1, source_target_pairs={{0,16},{4,20},{8,24},{12,28},{16,0},{20,4},{24,8},{28,12},{1,17},{... | collective-permute-start | bytes 98312 | tf_op jit(solution)/shard_map/ppermute | solution.py:29
  33.8 1.9 %collective-permute-done.10 = f32[64,128]{1,0:T(8,128)S(1)} collective-permute-done((f32[64,128]{1,0:T(8,128)S(1)}, f32[64,128]{1,0:T(8,128)S(1)}, u32[]{:S(2)}, u32[]{:S(2)}) %collective-permute-start.10) | collective-permute-done | bytes 32800 | tf_op jit(solution)/shard_map/ppermute | solution.py:29
  35.8 1.2 %collective-permute-done.11.there = f32[64,128]{1,0:T(8,128)S(1)} collective-permute-done((f32[64,128]{1,0:T(8,128)S(1)}, f32[64,128]{1,0:T(8,128)S(1)}, u32[]{:S(2)}, u32[]{:S(2)}) %collective-permute-start.11) | collective-permute-done | bytes 32800 | tf_op jit(solution)/shard_map/ppermute | solution.py:29
  37.0 0.9 collective-permute-start.14
  37.9 1.9 %collective-permute-start.12 = (bf16[6,64,128]{2,1,0:T(8,128)(2,1)S(1)}, bf16[6,64,128]{2,1,0:T(8,128)(2,1)S(1)}, u32[]{:S(2)}, u32[]{:S(2)}) collective-permute-start(bf16[6,64,128]{2,1,0:T(8,128)(2,1)S(1)} %get-tuple-element.43.sent), channel_id=1, source_target_pairs={{0,4},{4,0},{8,12},{12,8},{16,20},{20,16},{24,28},{28,24},{1,5},{5... | collective-permute-start | bytes 294920 | tf_op jit(solution)/shard_map/ppermute | solution.py:29
  39.9 0.7 collective-permute-start.13
  40.6 1.4 %collective-permute-done.14.far.refs_0_ = bf16[6,64,128]{2,1,0:T(8,128)(2,1)S(1)} collective-permute-done((bf16[6,64,128]{2,1,0:T(8,128)(2,1)S(1)}, bf16[6,64,128]{2,1,0:T(8,128)(2,1)S(1)}, u32[]{:S(2)}, u32[]{:S(2)}) %collective-permute-start.14) | collective-permute-done | bytes 98336 | tf_op jit(solution)/shard_map/ppermute | solution.py:29
  42.0 0.1 join.2
  42.0 0.9 collective-permute-start.15
  42.9 0.6 collective-permute-done.12.flip
  43.5 1.9 %collective-permute-done.13.flip_far = bf16[6,64,128]{2,1,0:T(8,128)(2,1)S(1)} collective-permute-done((bf16[6,64,128]{2,1,0:T(8,128)(2,1)S(1)}, bf16[6,64,128]{2,1,0:T(8,128)(2,1)S(1)}, u32[]{:S(2)}, u32[]{:S(2)}) %collective-permute-start.13) | collective-permute-done | bytes 98336 | tf_op jit(solution)/shard_map/ppermute | solution.py:36
  45.5 2.5 %collective-permute-start.16 = (bf16[6,64,128]{2,1,0:T(8,128)(2,1)S(1)}, bf16[6,64,128]{2,1,0:T(8,128)(2,1)S(1)}, u32[]{:S(2)}, u32[]{:S(2)}) collective-permute-start(bf16[6,64,128]{2,1,0:T(8,128)(2,1)S(1)} %get-tuple-element.47.passed), channel_id=1, source_target_pairs={{0,8},{4,12},{16,24},{20,28},{8,0},{12,4},{24,16},{28,20},{1,9},{5... | collective-permute-start | bytes 294920 | tf_op jit(solution)/shard_map/ppermute | solution.py:41
  48.0 0.7 collective-permute-start.17
  48.7 1.9 %collective-permute-done.16.refs_1_ = bf16[6,64,128]{2,1,0:T(8,128)(2,1)S(1)} collective-permute-done((bf16[6,64,128]{2,1,0:T(8,128)(2,1)S(1)}, bf16[6,64,128]{2,1,0:T(8,128)(2,1)S(1)}, u32[]{:S(2)}, u32[]{:S(2)}) %collective-permute-start.16) | collective-permute-done | bytes 98336 | tf_op jit(solution)/shard_map/ppermute | solution.py:41
  50.6 3.3 %project.2 = (bf16[12,64,128]{2,1,0:T(8,128)(2,1)S(1)}, bf16[2,64,128]{2,1,0:T(8,128)(2,1)S(1)}, bf16[4,64,128]{2,1,0:T(8,128)(2,1)S(1)}, bf16[4,64,128]{2,1,0:T(8,128)(2,1)S(1)}) custom-call(s32[5,4]{1,0:T(8,128)S(1)} %pad_add_fusion.facts, bf16[6,64,128]{2,1,0:T(8,128)(2,1)S(1)} %get-tuple-element.47.passed, ...), custom_call_target="tpu_custom_call" | custom-call | flops 37748736 | bytes 1966080 | tf_op jit(solution)/shard_map/project/pallas_call | solution.py:420
  54.0 0.6 collective-permute-start.19
  54.6 3.6 %collective-permute-start.21 = (bf16[4,64,128]{2,1,0:T(8,128)(2,1)S(1)}, bf16[4,64,128]{2,1,0:T(8,128)(2,1)S(1)}, u32[]{:S(2)}, u32[]{:S(2)}) collective-permute-start(bf16[4,64,128]{2,1,0:T(8,128)(2,1)S(1)} %get-tuple-element.54), channel_id=1, source_target_pairs={{0,8},{4,12},{16,24},{20,28},{8,0},{12,4},{24,16},{28,20},{1,9},{5... | collective-permute-start | bytes 196616 | tf_op jit(solution)/shard_map/ppermute | solution.py:41
  58.2 0.7 collective-permute-start.22
  58.8 1.8 %collective-permute-done.21.first.refs_0_ = bf16[4,64,128]{2,1,0:T(8,128)(2,1)S(1)} collective-permute-done((bf16[4,64,128]{2,1,0:T(8,128)(2,1)S(1)}, bf16[4,64,128]{2,1,0:T(8,128)(2,1)S(1)}, u32[]{:S(2)}, u32[]{:S(2)}) %collective-permute-start.21) | collective-permute-done | bytes 65568 | tf_op jit(solution)/shard_map/ppermute | solution.py:41
  60.6 1.8 %collective-permute-start.23 = (bf16[4,64,128]{2,1,0:T(8,128)(2,1)S(1)}, bf16[4,64,128]{2,1,0:T(8,128)(2,1)S(1)}, u32[]{:S(2)}, u32[]{:S(2)}) collective-permute-start(bf16[4,64,128]{2,1,0:T(8,128)(2,1)S(1)} %pass_on.3), channel_id=1, source_target_pairs={{0,4},{4,0},{8,12},{12,8},{16,20},{20,16},{24,28},{28,24},{1,5},{5... | collective-permute-start | bytes 196616 | tf_op jit(solution)/shard_map/ppermute | solution.py:29
  62.4 1.3 %collective-permute-start.24 = (bf16[4,64,128]{2,1,0:T(8,128)(2,1)S(1)}, bf16[4,64,128]{2,1,0:T(8,128)(2,1)S(1)}, u32[]{:S(2)}, u32[]{:S(2)}) collective-permute-start(bf16[4,64,128]{2,1,0:T(8,128)(2,1)S(1)} %pass_on.3), channel_id=1, source_target_pairs={{0,6},{1,7},{2,4},{3,5},{4,2},{5,3},{6,0},{7,1},{8,14},{9,15},{10,... | collective-permute-start | bytes 196616 | tf_op jit(solution)/shard_map/ppermute | solution.py:36
  63.7 0.5 collective-permute-start.25
  64.2 1.1 %collective-permute-done.23.refs_0_.refs_4_ = bf16[4,64,128]{2,1,0:T(8,128)(2,1)S(1)} collective-permute-done((bf16[4,64,128]{2,1,0:T(8,128)(2,1)S(1)}, bf16[4,64,128]{2,1,0:T(8,128)(2,1)S(1)}, u32[]{:S(2)}, u32[]{:S(2)}) %collective-permute-start.23) | collective-permute-done | bytes 65568 | tf_op jit(solution)/shard_map/ppermute | solution.py:29
  65.4 2.2 %collective-permute-done.24.refs_2_.refs_6_ = bf16[4,64,128]{2,1,0:T(8,128)(2,1)S(1)} collective-permute-done((bf16[4,64,128]{2,1,0:T(8,128)(2,1)S(1)}, bf16[4,64,128]{2,1,0:T(8,128)(2,1)S(1)}, u32[]{:S(2)}, u32[]{:S(2)}) %collective-permute-start.24) | collective-permute-done | bytes 65568 | tf_op jit(solution)/shard_map/ppermute | solution.py:36
  67.6 0.7 collective-permute-done.25.refs_3_.refs_7_
  68.3 0.1 collective-permute-start.26
  68.4 0.5 collective-permute-start.20
  68.9 1.3 %collective-permute-done.20.refs_3_ = bf16[12,64,128]{2,1,0:T(8,128)(2,1)S(1)} collective-permute-done((bf16[12,64,128]{2,1,0:T(8,128)(2,1)S(1)}, bf16[12,64,128]{2,1,0:T(8,128)(2,1)S(1)}, u32[]{:S(2)}, u32[]{:S(2)}) %collective-permute-start.20) | collective-permute-done | bytes 196640 | tf_op jit(solution)/shard_map/ppermute | solution.py:29
  70.2 5.9 %forward_adjoint.3 = (f32[40,64,128]{2,1,0:T(8,128)S(1)}, f32[40,64,128]{2,1,0:T(8,128)S(1)}, f32[64,128]{1,0:T(8,128)S(1)}) custom-call(s32[5,4]{1,0:T(8,128)S(1)} %pad_add_fusion.facts, s32[12,27]{1,0:T(8,128)S(1)} %copy-done, bf16[12,27,128,128]{3,2,1,0:T(8,128)(2,1)S(1)} %bitcast.8, f32[12,128]{1,0:T(8,128)S(1)} %copy-done.1, ...), custom_call_target="tpu_custom_call" | custom-call | flops 1358954496 | bytes 10616832 | tf_op jit(solution)/shard_map/forward_adjoint/pallas_call | solution.py:267
  76.1 2.4 %collective-permute-start.27 = (f32[40,64,128]{2,1,0:T(8,128)S(1)}, f32[40,64,128]{2,1,0:T(8,128)S(1)}, u32[]{:S(2)}, u32[]{:S(2)}) collective-permute-start(f32[40,64,128]{2,1,0:T(8,128)S(1)} %get-tuple-element.57), channel_id=1, source_target_pairs={{0,1},{1,0},{2,3},{3,2},{4,5},{5,4},{6,7},{7,6},{8,9},{9,8},{10,11... | collective-permute-start | bytes 3932168 | tf_op jit(solution)/shard_map/ppermute | solution.py:29
  78.5 3.1 %collective-permute-start.28 = (f32[64,128]{1,0:T(8,128)S(1)}, f32[64,128]{1,0:T(8,128)S(1)}, u32[]{:S(2)}, u32[]{:S(2)}) collective-permute-start(f32[64,128]{1,0:T(8,128)S(1)} %get-tuple-element.58), channel_id=1, source_target_pairs={{0,16},{4,20},{8,24},{12,28},{16,0},{20,4},{24,8},{28,12},{1,17},{... | collective-permute-start | bytes 98312 | tf_op jit(solution)/shard_map/ppermute | solution.py:29
  81.6 1.9 %collective-permute-done.28 = f32[64,128]{1,0:T(8,128)S(1)} collective-permute-done((f32[64,128]{1,0:T(8,128)S(1)}, f32[64,128]{1,0:T(8,128)S(1)}, u32[]{:S(2)}, u32[]{:S(2)}) %collective-permute-start.28) | collective-permute-done | bytes 32800 | tf_op jit(solution)/shard_map/ppermute | solution.py:29
  83.5 1.2 %collective-permute-done.29.there = f32[64,128]{1,0:T(8,128)S(1)} collective-permute-done((f32[64,128]{1,0:T(8,128)S(1)}, f32[64,128]{1,0:T(8,128)S(1)}, u32[]{:S(2)}, u32[]{:S(2)}) %collective-permute-start.29) | collective-permute-done | bytes 32800 | tf_op jit(solution)/shard_map/ppermute | solution.py:29
  84.8 1.1 %collective-permute-start.32 = (bf16[6,64,128]{2,1,0:T(8,128)(2,1)S(1)}, bf16[6,64,128]{2,1,0:T(8,128)(2,1)S(1)}, u32[]{:S(2)}, u32[]{:S(2)}) collective-permute-start(bf16[6,64,128]{2,1,0:T(8,128)(2,1)S(1)} %get-tuple-element.61), channel_id=1, source_target_pairs={{0,2},{1,3},{2,0},{3,1},{4,6},{5,7},{6,4},{7,5},{8,10},{9,11},{10,... | collective-permute-start | bytes 294920 | tf_op jit(solution)/shard_map/ppermute | solution.py:29
  85.9 0.9 collective-permute-start.30
  86.8 1.6 %collective-permute-start.31 = (bf16[6,64,128]{2,1,0:T(8,128)(2,1)S(1)}, bf16[6,64,128]{2,1,0:T(8,128)(2,1)S(1)}, u32[]{:S(2)}, u32[]{:S(2)}) collective-permute-start(bf16[6,64,128]{2,1,0:T(8,128)(2,1)S(1)} %get-tuple-element.60), channel_id=1, source_target_pairs={{0,6},{1,7},{2,4},{3,5},{4,2},{5,3},{6,0},{7,1},{8,14},{9,15},{10,... | collective-permute-start | bytes 294920 | tf_op jit(solution)/shard_map/ppermute | solution.py:36
  88.3 1.4 %collective-permute-done.32.far.refs_0_ = bf16[6,64,128]{2,1,0:T(8,128)(2,1)S(1)} collective-permute-done((bf16[6,64,128]{2,1,0:T(8,128)(2,1)S(1)}, bf16[6,64,128]{2,1,0:T(8,128)(2,1)S(1)}, u32[]{:S(2)}, u32[]{:S(2)}) %collective-permute-start.32) | collective-permute-done | bytes 98336 | tf_op jit(solution)/shard_map/ppermute | solution.py:29
  89.7 0.1 join.3
  89.8 1.1 %collective-permute-start.33 = (bf16[12,64,128]{2,1,0:T(8,128)(2,1)S(1)}, bf16[12,64,128]{2,1,0:T(8,128)(2,1)S(1)}, u32[]{:S(2)}, u32[]{:S(2)}) collective-permute-start(bf16[12,64,128]{2,1,0:T(8,128)(2,1)S(1)} %get-tuple-element.65), channel_id=1, source_target_pairs={{0,2},{1,3},{2,0},{3,1},{4,6},{5,7},{6,4},{7,5},{8,10},{9,11},{10,... | collective-permute-start | bytes 589832 | tf_op jit(solution)/shard_map/ppermute | solution.py:29
  90.9 0.6 collective-permute-done.30.flip
  91.5 1.6 %collective-permute-done.31.flip_far = bf16[6,64,128]{2,1,0:T(8,128)(2,1)S(1)} collective-permute-done((bf16[6,64,128]{2,1,0:T(8,128)(2,1)S(1)}, bf16[6,64,128]{2,1,0:T(8,128)(2,1)S(1)}, u32[]{:S(2)}, u32[]{:S(2)}) %collective-permute-start.31) | collective-permute-done | bytes 98336 | tf_op jit(solution)/shard_map/ppermute | solution.py:36
  93.2 3.6 %collective-permute-start.34 = (bf16[6,64,128]{2,1,0:T(8,128)(2,1)S(1)}, bf16[6,64,128]{2,1,0:T(8,128)(2,1)S(1)}, u32[]{:S(2)}, u32[]{:S(2)}) collective-permute-start(bf16[6,64,128]{2,1,0:T(8,128)(2,1)S(1)} %get-tuple-element.63.passed), channel_id=1, source_target_pairs={{0,8},{4,12},{16,24},{20,28},{8,0},{12,4},{24,16},{28,20},{1,9},{5... | collective-permute-start | bytes 294920 | tf_op jit(solution)/shard_map/ppermute | solution.py:41
  96.8 0.7 collective-permute-start.35
  97.4 1.9 %collective-permute-done.34.refs_1_ = bf16[6,64,128]{2,1,0:T(8,128)(2,1)S(1)} collective-permute-done((bf16[6,64,128]{2,1,0:T(8,128)(2,1)S(1)}, bf16[6,64,128]{2,1,0:T(8,128)(2,1)S(1)}, u32[]{:S(2)}, u32[]{:S(2)}) %collective-permute-start.34) | collective-permute-done | bytes 98336 | tf_op jit(solution)/shard_map/ppermute | solution.py:41
  99.4 4.0 %project.3 = (f32[12,64,128]{2,1,0:T(8,128)}, f32[64,64]{1,0:T(8,128)}) custom-call(s32[5,4]{1,0:T(8,128)S(1)} %pad_add_fusion.facts, bf16[6,64,128]{2,1,0:T(8,128)(2,1)S(1)} %get-tuple-element.63.passed, bf16[12,64,128]{2,1,0:T(8,128)(2,1)S(1)} %get-tuple-element.52.refs_0_.basis, f32[12,64,128]{2,1,0:T(8,128)S(1)} %get-tuple-element.64.near_own, ...), custom_call_target="tpu_custom_call" | custom-call | flops 37748736 | bytes 1966080 | tf_op jit(solution)/shard_map/project/pallas_call | solution.py:420
  (43 shorter events, 0.5 us)
Async XLA Ops:
  1.4 18.9 %slice-start = ((s8[10616832]{0:T(1024)(128)(4,1)}), s8[4194304]{0:T(1024)(128)(4,1)S(1)}, s32[]{:S(2)}) async-start(s8[10616832]{0:T(1024)(128)(4,1)} %bitcast.7), calls=%async_computation | async-start | bytes 8388608
  2.2 1.1 %copy-start.2 = (bf16[12,64,128]{2,1,0:T(8,128)(2,1)S(1)}, bf16[12,64,128]{2,1,0:T(8,128)(2,1)}, u32[]{:S(2)}) copy-start(bf16[12,64,128]{2,1,0:T(8,128)(2,1)} %directions.1) | copy-start | bytes 589828
  3.3 16.9 %slice-start.1 = ((s8[10616832]{0:T(1024)(128)(4,1)}), s8[4194304]{0:T(1024)(128)(4,1)S(1)}, s32[]{:S(2)}) async-start(s8[10616832]{0:T(1024)(128)(4,1)} %bitcast.7), calls=%async_computation.1 | async-start | bytes 8388608
  3.3 16.9 %slice-start.2 = ((s8[10616832]{0:T(1024)(128)(4,1)}), s8[2228224]{0:T(1024)(128)(4,1)S(1)}, s32[]{:S(2)}) async-start(s8[10616832]{0:T(1024)(128)(4,1)} %bitcast.7), calls=%async_computation.2 | async-start | bytes 4456448
  4.1 16.2 %copy-start = (s32[12,27]{1,0:T(8,128)S(1)}, s32[12,27]{1,0:T(8,128)}, u32[]{:S(2)}) copy-start(s32[12,27]{1,0:T(8,128)} %cols.3) | copy-start | bytes 3892
  4.1 16.2 %copy-start.1 = (f32[12,128]{1,0:T(8,128)S(1)}, f32[12,128]{1,0:T(8,128)}, u32[]{:S(2)}) copy-start(f32[12,128]{1,0:T(8,128)} %friction.3) | copy-start | bytes 18436
  4.1 9.2 %collective-permute-start = (bf16[12,64,128]{2,1,0:T(8,128)(2,1)S(1)}, bf16[12,64,128]{2,1,0:T(8,128)(2,1)S(1)}, u32[]{:S(2)}, u32[]{:S(2)}) collective-permute-start(bf16[12,64,128]{2,1,0:T(8,128)(2,1)S(1)} %get-tuple-element.36.refs_0_.basis), channel_id=1, source_target_pairs={{0,1},{1,0},{2,3},{3,2},{4,5},{5,4},{6,7},{7,6},{8,9},{9,8},{10,11... | collective-permute-start | bytes 589832 | tf_op jit(solution)/shard_map/ppermute | solution.py:29
  4.7 8.7 %collective-permute-start.1 = (bf16[12,64,128]{2,1,0:T(8,128)(2,1)S(1)}, bf16[12,64,128]{2,1,0:T(8,128)(2,1)S(1)}, u32[]{:S(2)}, u32[]{:S(2)}) collective-permute-start(bf16[12,64,128]{2,1,0:T(8,128)(2,1)S(1)} %get-tuple-element.36.refs_0_.basis), channel_id=1, source_target_pairs={{0,2},{1,3},{2,0},{3,1},{4,6},{5,7},{6,4},{7,5},{8,10},{9,11},{10,... | collective-permute-start | bytes 589832 | tf_op jit(solution)/shard_map/ppermute | solution.py:29
  7.2 4.3 %collective-permute-start.3 = (bf16[4,64,128]{2,1,0:T(8,128)(2,1)S(1)}, bf16[4,64,128]{2,1,0:T(8,128)(2,1)S(1)}, u32[]{:S(2)}, u32[]{:S(2)}) collective-permute-start(bf16[4,64,128]{2,1,0:T(8,128)(2,1)S(1)} %get-tuple-element.38), channel_id=1, source_target_pairs={{0,8},{4,12},{16,24},{20,28},{8,0},{12,4},{24,16},{28,20},{1,9},{5... | collective-permute-start | bytes 196616 | tf_op jit(solution)/shard_map/ppermute | solution.py:41
  8.8 2.7 %collective-permute-start.4 = (bf16[4,64,128]{2,1,0:T(8,128)(2,1)S(1)}, bf16[4,64,128]{2,1,0:T(8,128)(2,1)S(1)}, u32[]{:S(2)}, u32[]{:S(2)}) collective-permute-start(bf16[4,64,128]{2,1,0:T(8,128)(2,1)S(1)} %get-tuple-element.39), channel_id=1, source_target_pairs={{8,16},{12,20},{16,8},{20,12},{9,17},{13,21},{17,9},{21,13},{10,18... | collective-permute-start | bytes 196616 | tf_op jit(solution)/shard_map/ppermute | solution.py:41
  11.5 4.5 %collective-permute-start.5 = (bf16[4,64,128]{2,1,0:T(8,128)(2,1)S(1)}, bf16[4,64,128]{2,1,0:T(8,128)(2,1)S(1)}, u32[]{:S(2)}, u32[]{:S(2)}) collective-permute-start(bf16[4,64,128]{2,1,0:T(8,128)(2,1)S(1)} %pass_on.2), channel_id=1, source_target_pairs={{0,4},{4,0},{8,12},{12,8},{16,20},{20,16},{24,28},{28,24},{1,5},{5... | collective-permute-start | bytes 196616 | tf_op jit(solution)/shard_map/ppermute | solution.py:29
  13.1 5.3 %collective-permute-start.6 = (bf16[4,64,128]{2,1,0:T(8,128)(2,1)S(1)}, bf16[4,64,128]{2,1,0:T(8,128)(2,1)S(1)}, u32[]{:S(2)}, u32[]{:S(2)}) collective-permute-start(bf16[4,64,128]{2,1,0:T(8,128)(2,1)S(1)} %pass_on.2), channel_id=1, source_target_pairs={{0,6},{1,7},{2,4},{3,5},{4,2},{5,3},{6,0},{7,1},{8,14},{9,15},{10,... | collective-permute-start | bytes 196616 | tf_op jit(solution)/shard_map/ppermute | solution.py:36
  13.3 5.0 %collective-permute-start.7 = (bf16[4,64,128]{2,1,0:T(8,128)(2,1)S(1)}, bf16[4,64,128]{2,1,0:T(8,128)(2,1)S(1)}, u32[]{:S(2)}, u32[]{:S(2)}) collective-permute-start(bf16[4,64,128]{2,1,0:T(8,128)(2,1)S(1)} %stack.12.refs_1_.refs_5_), channel_id=1, source_target_pairs={{0,2},{1,3},{2,0},{3,1},{4,6},{5,7},{6,4},{7,5},{8,10},{9,11},{10,... | collective-permute-start | bytes 196616 | tf_op jit(solution)/shard_map/ppermute | solution.py:29
  18.4 1.9 %collective-permute-start.8 = (bf16[16,64,128]{2,1,0:T(8,128)(2,1)S(1)}, bf16[16,64,128]{2,1,0:T(8,128)(2,1)S(1)}, u32[]{:S(2)}, u32[]{:S(2)}) collective-permute-start(bf16[16,64,128]{2,1,0:T(8,128)(2,1)S(1)} %stack.13), channel_id=1, source_target_pairs={{0,1},{1,0},{2,3},{3,2},{4,5},{5,4},{6,7},{7,6},{8,9},{9,8},{10,11... | collective-permute-start | bytes 786440 | tf_op jit(solution)/shard_map/ppermute | solution.py:29
  18.5 1.8 %collective-permute-start.2 = (bf16[12,64,128]{2,1,0:T(8,128)(2,1)S(1)}, bf16[12,64,128]{2,1,0:T(8,128)(2,1)S(1)}, u32[]{:S(2)}, u32[]{:S(2)}) collective-permute-start(bf16[12,64,128]{2,1,0:T(8,128)(2,1)S(1)} %collective-permute-done.1.refs_3_.refs_2_), channel_id=1, source_target_pairs={{0,1},{1,0},{2,3},{3,2},{4,5},{5,4},{6,7},{7,6},{8,9},{9,8},{10,11... | collective-permute-start | bytes 589832 | tf_op jit(solution)/shard_map/ppermute | solution.py:29
  26.2 10.7 %collective-permute-start.9 = (f32[40,64,128]{2,1,0:T(8,128)S(1)}, f32[40,64,128]{2,1,0:T(8,128)S(1)}, u32[]{:S(2)}, u32[]{:S(2)}) collective-permute-start(f32[40,64,128]{2,1,0:T(8,128)S(1)} %get-tuple-element.41), channel_id=1, source_target_pairs={{0,1},{1,0},{2,3},{3,2},{4,5},{5,4},{6,7},{7,6},{8,9},{9,8},{10,11... | collective-permute-start | bytes 3932168 | tf_op jit(solution)/shard_map/ppermute | solution.py:29
  28.6 7.1 %collective-permute-start.10 = (f32[64,128]{1,0:T(8,128)S(1)}, f32[64,128]{1,0:T(8,128)S(1)}, u32[]{:S(2)}, u32[]{:S(2)}) collective-permute-start(f32[64,128]{1,0:T(8,128)S(1)} %get-tuple-element.42), channel_id=1, source_target_pairs={{0,16},{4,20},{8,24},{12,28},{16,0},{20,4},{24,8},{28,12},{1,17},{... | collective-permute-start | bytes 98312 | tf_op jit(solution)/shard_map/ppermute | solution.py:29
  35.8 1.2 %collective-permute-start.11 = (f32[64,128]{1,0:T(8,128)S(1)}, f32[64,128]{1,0:T(8,128)S(1)}, u32[]{:S(2)}, u32[]{:S(2)}) collective-permute-start(f32[64,128]{1,0:T(8,128)S(1)} %add.8.here), channel_id=1, source_target_pairs={{0,1},{1,0},{2,3},{3,2},{4,5},{5,4},{6,7},{7,6},{8,9},{9,8},{10,11... | collective-permute-start | bytes 98312 | tf_op jit(solution)/shard_map/ppermute | solution.py:29
  37.0 4.9 %collective-permute-start.14 = (bf16[6,64,128]{2,1,0:T(8,128)(2,1)S(1)}, bf16[6,64,128]{2,1,0:T(8,128)(2,1)S(1)}, u32[]{:S(2)}, u32[]{:S(2)}) collective-permute-start(bf16[6,64,128]{2,1,0:T(8,128)(2,1)S(1)} %get-tuple-element.45), channel_id=1, source_target_pairs={{0,2},{1,3},{2,0},{3,1},{4,6},{5,7},{6,4},{7,5},{8,10},{9,11},{10,... | collective-permute-start | bytes 294920 | tf_op jit(solution)/shard_map/ppermute | solution.py:29
  37.9 5.6 %collective-permute-start.12 = (bf16[6,64,128]{2,1,0:T(8,128)(2,1)S(1)}, bf16[6,64,128]{2,1,0:T(8,128)(2,1)S(1)}, u32[]{:S(2)}, u32[]{:S(2)}) collective-permute-start(bf16[6,64,128]{2,1,0:T(8,128)(2,1)S(1)} %get-tuple-element.43.sent), channel_id=1, source_target_pairs={{0,4},{4,0},{8,12},{12,8},{16,20},{20,16},{24,28},{28,24},{1,5},{5... | collective-permute-start | bytes 294920 | tf_op jit(solution)/shard_map/ppermute | solution.py:29
  39.9 5.6 %collective-permute-start.13 = (bf16[6,64,128]{2,1,0:T(8,128)(2,1)S(1)}, bf16[6,64,128]{2,1,0:T(8,128)(2,1)S(1)}, u32[]{:S(2)}, u32[]{:S(2)}) collective-permute-start(bf16[6,64,128]{2,1,0:T(8,128)(2,1)S(1)} %get-tuple-element.44), channel_id=1, source_target_pairs={{0,6},{1,7},{2,4},{3,5},{4,2},{5,3},{6,0},{7,1},{8,14},{9,15},{10,... | collective-permute-start | bytes 294920 | tf_op jit(solution)/shard_map/ppermute | solution.py:36
  42.0 8.6 %collective-permute-start.15 = (bf16[12,64,128]{2,1,0:T(8,128)(2,1)S(1)}, bf16[12,64,128]{2,1,0:T(8,128)(2,1)S(1)}, u32[]{:S(2)}, u32[]{:S(2)}) collective-permute-start(bf16[12,64,128]{2,1,0:T(8,128)(2,1)S(1)} %get-tuple-element.49), channel_id=1, source_target_pairs={{0,2},{1,3},{2,0},{3,1},{4,6},{5,7},{6,4},{7,5},{8,10},{9,11},{10,... | collective-permute-start | bytes 589832 | tf_op jit(solution)/shard_map/ppermute | solution.py:29
  45.5 5.1 %collective-permute-start.16 = (bf16[6,64,128]{2,1,0:T(8,128)(2,1)S(1)}, bf16[6,64,128]{2,1,0:T(8,128)(2,1)S(1)}, u32[]{:S(2)}, u32[]{:S(2)}) collective-permute-start(bf16[6,64,128]{2,1,0:T(8,128)(2,1)S(1)} %get-tuple-element.47.passed), channel_id=1, source_target_pairs={{0,8},{4,12},{16,24},{20,28},{8,0},{12,4},{24,16},{28,20},{1,9},{5... | collective-permute-start | bytes 294920 | tf_op jit(solution)/shard_map/ppermute | solution.py:41
  48.0 0.7 collective-permute-start.17
  54.0 9.7 %collective-permute-start.18 = (bf16[12,64,128]{2,1,0:T(8,128)(2,1)S(1)}, bf16[12,64,128]{2,1,0:T(8,128)(2,1)S(1)}, u32[]{:S(2)}, u32[]{:S(2)}) collective-permute-start(bf16[12,64,128]{2,1,0:T(8,128)(2,1)S(1)} %get-tuple-element.52.refs_0_.basis), channel_id=1, source_target_pairs={{0,1},{1,0},{2,3},{3,2},{4,5},{5,4},{6,7},{7,6},{8,9},{9,8},{10,11... | collective-permute-start | bytes 589832 | tf_op jit(solution)/shard_map/ppermute | solution.py:29
  54.0 9.7 %collective-permute-start.19 = (bf16[12,64,128]{2,1,0:T(8,128)(2,1)S(1)}, bf16[12,64,128]{2,1,0:T(8,128)(2,1)S(1)}, u32[]{:S(2)}, u32[]{:S(2)}) collective-permute-start(bf16[12,64,128]{2,1,0:T(8,128)(2,1)S(1)} %get-tuple-element.52.refs_0_.basis), channel_id=1, source_target_pairs={{0,2},{1,3},{2,0},{3,1},{4,6},{5,7},{6,4},{7,5},{8,10},{9,11},{10,... | collective-permute-start | bytes 589832 | tf_op jit(solution)/shard_map/ppermute | solution.py:29
  54.6 6.0 %collective-permute-start.21 = (bf16[4,64,128]{2,1,0:T(8,128)(2,1)S(1)}, bf16[4,64,128]{2,1,0:T(8,128)(2,1)S(1)}, u32[]{:S(2)}, u32[]{:S(2)}) collective-permute-start(bf16[4,64,128]{2,1,0:T(8,128)(2,1)S(1)} %get-tuple-element.54), channel_id=1, source_target_pairs={{0,8},{4,12},{16,24},{20,28},{8,0},{12,4},{24,16},{28,20},{1,9},{5... | collective-permute-start | bytes 196616 | tf_op jit(solution)/shard_map/ppermute | solution.py:41
  58.2 2.4 %collective-permute-start.22 = (bf16[4,64,128]{2,1,0:T(8,128)(2,1)S(1)}, bf16[4,64,128]{2,1,0:T(8,128)(2,1)S(1)}, u32[]{:S(2)}, u32[]{:S(2)}) collective-permute-start(bf16[4,64,128]{2,1,0:T(8,128)(2,1)S(1)} %get-tuple-element.55), channel_id=1, source_target_pairs={{8,16},{12,20},{16,8},{20,12},{9,17},{13,21},{17,9},{21,13},{10,18... | collective-permute-start | bytes 196616 | tf_op jit(solution)/shard_map/ppermute | solution.py:41
  60.6 4.8 %collective-permute-start.23 = (bf16[4,64,128]{2,1,0:T(8,128)(2,1)S(1)}, bf16[4,64,128]{2,1,0:T(8,128)(2,1)S(1)}, u32[]{:S(2)}, u32[]{:S(2)}) collective-permute-start(bf16[4,64,128]{2,1,0:T(8,128)(2,1)S(1)} %pass_on.3), channel_id=1, source_target_pairs={{0,4},{4,0},{8,12},{12,8},{16,20},{20,16},{24,28},{28,24},{1,5},{5... | collective-permute-start | bytes 196616 | tf_op jit(solution)/shard_map/ppermute | solution.py:29
  62.4 5.2 %collective-permute-start.24 = (bf16[4,64,128]{2,1,0:T(8,128)(2,1)S(1)}, bf16[4,64,128]{2,1,0:T(8,128)(2,1)S(1)}, u32[]{:S(2)}, u32[]{:S(2)}) collective-permute-start(bf16[4,64,128]{2,1,0:T(8,128)(2,1)S(1)} %pass_on.3), channel_id=1, source_target_pairs={{0,6},{1,7},{2,4},{3,5},{4,2},{5,3},{6,0},{7,1},{8,14},{9,15},{10,... | collective-permute-start | bytes 196616 | tf_op jit(solution)/shard_map/ppermute | solution.py:36
  63.7 4.6 %collective-permute-start.25 = (bf16[4,64,128]{2,1,0:T(8,128)(2,1)S(1)}, bf16[4,64,128]{2,1,0:T(8,128)(2,1)S(1)}, u32[]{:S(2)}, u32[]{:S(2)}) collective-permute-start(bf16[4,64,128]{2,1,0:T(8,128)(2,1)S(1)} %stack.14.refs_1_.refs_5_), channel_id=1, source_target_pairs={{0,2},{1,3},{2,0},{3,1},{4,6},{5,7},{6,4},{7,5},{8,10},{9,11},{10,... | collective-permute-start | bytes 196616 | tf_op jit(solution)/shard_map/ppermute | solution.py:29
  68.3 1.9 %collective-permute-start.26 = (bf16[16,64,128]{2,1,0:T(8,128)(2,1)S(1)}, bf16[16,64,128]{2,1,0:T(8,128)(2,1)S(1)}, u32[]{:S(2)}, u32[]{:S(2)}) collective-permute-start(bf16[16,64,128]{2,1,0:T(8,128)(2,1)S(1)} %stack.15), channel_id=1, source_target_pairs={{0,1},{1,0},{2,3},{3,2},{4,5},{5,4},{6,7},{7,6},{8,9},{9,8},{10,11... | collective-permute-start | bytes 786440 | tf_op jit(solution)/shard_map/ppermute | solution.py:29
  68.4 1.8 %collective-permute-start.20 = (bf16[12,64,128]{2,1,0:T(8,128)(2,1)S(1)}, bf16[12,64,128]{2,1,0:T(8,128)(2,1)S(1)}, u32[]{:S(2)}, u32[]{:S(2)}) collective-permute-start(bf16[12,64,128]{2,1,0:T(8,128)(2,1)S(1)} %collective-permute-done.19.refs_3_.refs_2_), channel_id=1, source_target_pairs={{0,1},{1,0},{2,3},{3,2},{4,5},{5,4},{6,7},{7,6},{8,9},{9,8},{10,11... | collective-permute-start | bytes 589832 | tf_op jit(solution)/shard_map/ppermute | solution.py:29
  76.1 8.6 %collective-permute-start.27 = (f32[40,64,128]{2,1,0:T(8,128)S(1)}, f32[40,64,128]{2,1,0:T(8,128)S(1)}, u32[]{:S(2)}, u32[]{:S(2)}) collective-permute-start(f32[40,64,128]{2,1,0:T(8,128)S(1)} %get-tuple-element.57), channel_id=1, source_target_pairs={{0,1},{1,0},{2,3},{3,2},{4,5},{5,4},{6,7},{7,6},{8,9},{9,8},{10,11... | collective-permute-start | bytes 3932168 | tf_op jit(solution)/shard_map/ppermute | solution.py:29
  78.5 5.0 %collective-permute-start.28 = (f32[64,128]{1,0:T(8,128)S(1)}, f32[64,128]{1,0:T(8,128)S(1)}, u32[]{:S(2)}, u32[]{:S(2)}) collective-permute-start(f32[64,128]{1,0:T(8,128)S(1)} %get-tuple-element.58), channel_id=1, source_target_pairs={{0,16},{4,20},{8,24},{12,28},{16,0},{20,4},{24,8},{28,12},{1,17},{... | collective-permute-start | bytes 98312 | tf_op jit(solution)/shard_map/ppermute | solution.py:29
  83.5 1.2 %collective-permute-start.29 = (f32[64,128]{1,0:T(8,128)S(1)}, f32[64,128]{1,0:T(8,128)S(1)}, u32[]{:S(2)}, u32[]{:S(2)}) collective-permute-start(f32[64,128]{1,0:T(8,128)S(1)} %add.9.here), channel_id=1, source_target_pairs={{0,1},{1,0},{2,3},{3,2},{4,5},{5,4},{6,7},{7,6},{8,9},{9,8},{10,11... | collective-permute-start | bytes 98312 | tf_op jit(solution)/shard_map/ppermute | solution.py:29
  84.8 4.9 %collective-permute-start.32 = (bf16[6,64,128]{2,1,0:T(8,128)(2,1)S(1)}, bf16[6,64,128]{2,1,0:T(8,128)(2,1)S(1)}, u32[]{:S(2)}, u32[]{:S(2)}) collective-permute-start(bf16[6,64,128]{2,1,0:T(8,128)(2,1)S(1)} %get-tuple-element.61), channel_id=1, source_target_pairs={{0,2},{1,3},{2,0},{3,1},{4,6},{5,7},{6,4},{7,5},{8,10},{9,11},{10,... | collective-permute-start | bytes 294920 | tf_op jit(solution)/shard_map/ppermute | solution.py:29
  85.9 5.6 %collective-permute-start.30 = (bf16[6,64,128]{2,1,0:T(8,128)(2,1)S(1)}, bf16[6,64,128]{2,1,0:T(8,128)(2,1)S(1)}, u32[]{:S(2)}, u32[]{:S(2)}) collective-permute-start(bf16[6,64,128]{2,1,0:T(8,128)(2,1)S(1)} %get-tuple-element.59.sent), channel_id=1, source_target_pairs={{0,4},{4,0},{8,12},{12,8},{16,20},{20,16},{24,28},{28,24},{1,5},{5... | collective-permute-start | bytes 294920 | tf_op jit(solution)/shard_map/ppermute | solution.py:29
  86.8 6.4 %collective-permute-start.31 = (bf16[6,64,128]{2,1,0:T(8,128)(2,1)S(1)}, bf16[6,64,128]{2,1,0:T(8,128)(2,1)S(1)}, u32[]{:S(2)}, u32[]{:S(2)}) collective-permute-start(bf16[6,64,128]{2,1,0:T(8,128)(2,1)S(1)} %get-tuple-element.60), channel_id=1, source_target_pairs={{0,6},{1,7},{2,4},{3,5},{4,2},{5,3},{6,0},{7,1},{8,14},{9,15},{10,... | collective-permute-start | bytes 294920 | tf_op jit(solution)/shard_map/ppermute | solution.py:36
  89.8 9.6 %collective-permute-start.33 = (bf16[12,64,128]{2,1,0:T(8,128)(2,1)S(1)}, bf16[12,64,128]{2,1,0:T(8,128)(2,1)S(1)}, u32[]{:S(2)}, u32[]{:S(2)}) collective-permute-start(bf16[12,64,128]{2,1,0:T(8,128)(2,1)S(1)} %get-tuple-element.65), channel_id=1, source_target_pairs={{0,2},{1,3},{2,0},{3,1},{4,6},{5,7},{6,4},{7,5},{8,10},{9,11},{10,... | collective-permute-start | bytes 589832 | tf_op jit(solution)/shard_map/ppermute | solution.py:29
  93.2 6.2 %collective-permute-start.34 = (bf16[6,64,128]{2,1,0:T(8,128)(2,1)S(1)}, bf16[6,64,128]{2,1,0:T(8,128)(2,1)S(1)}, u32[]{:S(2)}, u32[]{:S(2)}) collective-permute-start(bf16[6,64,128]{2,1,0:T(8,128)(2,1)S(1)} %get-tuple-element.63.passed), channel_id=1, source_target_pairs={{0,8},{4,12},{16,24},{20,28},{8,0},{12,4},{24,16},{28,20},{1,9},{5... | collective-permute-start | bytes 294920 | tf_op jit(solution)/shard_map/ppermute | solution.py:41
  96.8 0.7 collective-permute-start.35

commit v5 on v4

--- a/solution.py
+++ b/solution.py
@@ -441,12 +441,13 @@
     facts = pack_facts(neighbours, send_idx, send_count, row_counts)
     basis, ways, *outgoing = call_prepare(shape, facts, directions)
     for step in range(ITERS):
-        own_far, own_near = swap(basis, "sub", far), swap(basis, "sub", near)
+        own_near = swap(basis, "sub", near)
         pairs = [pair_up(x, i) for i, x in enumerate(outgoing[1:])]
         pair = 2 * slots
+        own_far = swap(call_stack([basis], (blocks,), [pairs[0]]), "sub", far)
         onward = call_pass_on(slots, ways, outgoing[0], *pairs)
         flip, far01 = swap(onward, "dom", dom_bits[0]), swap_both(onward, dom_bits[0], far)
-        halo23 = call_stack(pairs, (slots, slots), [own_near, own_far])
+        halo23 = call_stack(pairs, (slots, slots), [own_near])
         far23 = swap(halo23, "sub", far)
         rest = swap(call_stack([flip, halo23, far01, far23], (pair,) * 4), "sub", near)
         parts = [basis, own_near, own_far, swap(own_far, "sub", near)]

time: 105 us -> 104 us (level)
  starting transfers between devices: 48.2 us -> 36.7 us
  waiting for transfers between devices: 31.2 us -> 38.1 us
  Pallas kernels: 20.5 us -> 24.9 us
    ppermute x24, starting transfers between devices: 30.5 us -> 19.9 us  [swap(): return lax.ppermute(x, axis, [(i, i ^ bit) for i in range(peers)])]
    pallas_call x2, Pallas kernels: 11.8 us -> 16.2 us  [call_forward_adjoint(): pl.pallas_call(functools.partial(forward_adjoint, shape, relatives, sourc...]
    ppermute x24, waiting for transfers between devices: 15.5 us -> 19.5 us  [swap(): return lax.ppermute(x, axis, [(i, i ^ bit) for i in range(peers)])]
    ppermute x4, waiting for transfers between devices: 8.02 us -> 9.73 us  [swap_both(): return lax.ppermute(x, ('dom', 'sub'), pairs)]
    ppermute x8, waiting for transfers between devices: 7.65 us -> 8.95 us  [pair_up(): lax.ppermute(x, 'dom', [(p, p + 2) for p in low] + [(p + 2, p) for p in l...]
  transfers between devices with their start and end apart: 36 -> 36, of which waited for: 21 -> 22; matrix products, arithmetic and copies ran while one was open for 0% -> 0% of each run, Pallas kernels for 0% -> 0%
where the time goes in v5:
time: 104 us; the launch traced here: 103 us
  waiting for transfers between devices  38.1 us (37%)
  starting transfers between devices  36.7 us (35%)
  Pallas kernels  24.9 us (24%)
  between operations  1.56 us (2%)
  local copies, waits for them, and re-layouts  1.13 us (1%)
    ppermute x24, starting transfers between devices, swap(): return lax.ppermute(x, axis, [(i, i ^ bit) for i in range(peers)])  19.9 us
    ppermute x24, waiting for transfers between devices, swap(): return lax.ppermute(x, axis, [(i, i ^ bit) for i in range(peers)])  19.5 us
    pallas_call x2, Pallas kernels, call_forward_adjoint(): pl.pallas_call(functools.partial(forward_adjoint, shape, relatives, sourc...  16.2 us
    ppermute x8, starting transfers between devices, pair_up(): lax.ppermute(x, 'dom', [(p, p + 2) for p in low] + [(p + 2, p) for p in l...  12.9 us
    ppermute x4, waiting for transfers between devices, swap_both(): return lax.ppermute(x, ('dom', 'sub'), pairs)  9.73 us
    ppermute x8, waiting for transfers between devices, pair_up(): lax.ppermute(x, 'dom', [(p, p + 2) for p in low] + [(p + 2, p) for p in l...  8.95 us
    pallas_call x2, Pallas kernels, call_project(): pl.pallas_call(functools.partial(project, shape, last), in_specs=[SMEM] +...  7.37 us
    ppermute x4, starting transfers between devices, swap_both(): return lax.ppermute(x, ('dom', 'sub'), pairs)  3.86 us
  transfers between devices with their start and end apart: 36, of which 22 were waited for; matrix products, arithmetic and copies ran while one was open for 0% of the time, Pallas kernels for 0%

profile of v5, /device:TPU:0, one launch (start us, length us, event | category | flops | bytes accessed | tf_op | source)
XLA Modules:
  0.0 103.4 jit_solution(4294066697590111817)
XLA Ops:
  1.3 0.1 pad_add_fusion.1
  1.4 0.9 pad_add_fusion.facts
  2.2 1.1 %copy-done.2 = bf16[12,64,128]{2,1,0:T(8,128)(2,1)S(1)} copy-done((bf16[12,64,128]{2,1,0:T(8,128)(2,1)S(1)}, bf16[12,64,128]{2,1,0:T(8,128)(2,1)}, u32[]{:S(2)}) %copy-start.2) | copy-done | bytes 196632
  3.3 0.8 prepare.1
  4.1 0.5 collective-permute-start
  4.7 2.6 %collective-permute-start.1 = (bf16[4,64,128]{2,1,0:T(8,128)(2,1)S(1)}, bf16[4,64,128]{2,1,0:T(8,128)(2,1)S(1)}, u32[]{:S(2)}, u32[]{:S(2)}) collective-permute-start(bf16[4,64,128]{2,1,0:T(8,128)(2,1)S(1)} %get-tuple-element.37), channel_id=1, source_target_pairs={{0,8},{4,12},{16,24},{20,28},{8,0},{12,4},{24,16},{28,20},{1,9},{5... | collective-permute-start | bytes 196616 | tf_op jit(solution)/shard_map/ppermute | solution.py:41
  7.3 0.7 collective-permute-start.4
  8.0 2.0 %collective-permute-done.1.refs_1_.first.refs_0_ = bf16[4,64,128]{2,1,0:T(8,128)(2,1)S(1)} collective-permute-done((bf16[4,64,128]{2,1,0:T(8,128)(2,1)S(1)}, bf16[4,64,128]{2,1,0:T(8,128)(2,1)S(1)}, u32[]{:S(2)}, u32[]{:S(2)}) %collective-permute-start.1) | collective-permute-done | bytes 65568 | tf_op jit(solution)/shard_map/ppermute | solution.py:41
  10.0 1.8 %collective-permute-start.2 = (bf16[12,64,128]{2,1,0:T(8,128)(2,1)S(1)}, bf16[12,64,128]{2,1,0:T(8,128)(2,1)S(1)}, u32[]{:S(2)}, u32[]{:S(2)}) collective-permute-start(bf16[12,64,128]{2,1,0:T(8,128)(2,1)S(1)} %stack.14), channel_id=1, source_target_pairs={{0,2},{1,3},{2,0},{3,1},{4,6},{5,7},{6,4},{7,5},{8,10},{9,11},{10,... | collective-permute-start | bytes 589832 | tf_op jit(solution)/shard_map/ppermute | solution.py:29
  11.8 1.6 %collective-permute-start.5 = (bf16[4,64,128]{2,1,0:T(8,128)(2,1)S(1)}, bf16[4,64,128]{2,1,0:T(8,128)(2,1)S(1)}, u32[]{:S(2)}, u32[]{:S(2)}) collective-permute-start(bf16[4,64,128]{2,1,0:T(8,128)(2,1)S(1)} %pass_on.2), channel_id=1, source_target_pairs={{0,4},{4,0},{8,12},{12,8},{16,20},{20,16},{24,28},{28,24},{1,5},{5... | collective-permute-start | bytes 196616 | tf_op jit(solution)/shard_map/ppermute | solution.py:29
  13.4 0.3 collective-permute-start.6
  13.7 1.8 %collective-permute-start.7 = (bf16[4,64,128]{2,1,0:T(8,128)(2,1)S(1)}, bf16[4,64,128]{2,1,0:T(8,128)(2,1)S(1)}, u32[]{:S(2)}, u32[]{:S(2)}) collective-permute-start(bf16[4,64,128]{2,1,0:T(8,128)(2,1)S(1)} %stack.15.refs_1_.refs_5_), channel_id=1, source_target_pairs={{0,2},{1,3},{2,0},{3,1},{4,6},{5,7},{6,4},{7,5},{8,10},{9,11},{10,... | collective-permute-start | bytes 196616 | tf_op jit(solution)/shard_map/ppermute | solution.py:29
  15.4 1.0 collective-permute-done.5.refs_0_.refs_4_
  16.4 2.2 %collective-permute-done.6.refs_2_.refs_6_ = bf16[4,64,128]{2,1,0:T(8,128)(2,1)S(1)} collective-permute-done((bf16[4,64,128]{2,1,0:T(8,128)(2,1)S(1)}, bf16[4,64,128]{2,1,0:T(8,128)(2,1)S(1)}, u32[]{:S(2)}, u32[]{:S(2)}) %collective-permute-start.6) | collective-permute-done | bytes 65568 | tf_op jit(solution)/shard_map/ppermute | solution.py:36
  18.6 0.9 collective-permute-done.7.refs_3_.refs_7_
  19.6 0.1 collective-permute-start.8
  19.7 0.5 collective-permute-start.3
  20.1 1.3 %collective-permute-done.3.refs_3_ = bf16[12,64,128]{2,1,0:T(8,128)(2,1)S(1)} collective-permute-done((bf16[12,64,128]{2,1,0:T(8,128)(2,1)S(1)}, bf16[12,64,128]{2,1,0:T(8,128)(2,1)S(1)}, u32[]{:S(2)}, u32[]{:S(2)}) %collective-permute-start.3) | collective-permute-done | bytes 196640 | tf_op jit(solution)/shard_map/ppermute | solution.py:29
  21.5 8.1 %forward_adjoint.2 = (f32[40,64,128]{2,1,0:T(8,128)S(1)}, f32[40,64,128]{2,1,0:T(8,128)S(1)}, f32[64,128]{1,0:T(8,128)S(1)}) custom-call(s32[5,4]{1,0:T(8,128)S(1)} %pad_add_fusion.facts, s32[12,27]{1,0:T(8,128)S(1)} %copy-done, bf16[12,27,128,128]{3,2,1,0:T(8,128)(2,1)S(1)} %bitcast.8, f32[12,128]{1,0:T(8,128)S(1)} %copy-done.1, ...), custom_call_target="tpu_custom_call" | custom-call | flops 1358954496 | bytes 10616832 | tf_op jit(solution)/shard_map/forward_adjoint/pallas_call | solution.py:267
  29.7 2.4 %collective-permute-start.10 = (f32[64,128]{1,0:T(8,128)S(1)}, f32[64,128]{1,0:T(8,128)S(1)}, u32[]{:S(2)}, u32[]{:S(2)}) collective-permute-start(f32[64,128]{1,0:T(8,128)S(1)} %get-tuple-element.42), channel_id=1, source_target_pairs={{0,16},{4,20},{8,24},{12,28},{16,0},{20,4},{24,8},{28,12},{1,17},{... | collective-permute-start | bytes 98312 | tf_op jit(solution)/shard_map/ppermute | solution.py:29
  32.1 2.5 %collective-permute-done.10 = f32[64,128]{1,0:T(8,128)S(1)} collective-permute-done((f32[64,128]{1,0:T(8,128)S(1)}, f32[64,128]{1,0:T(8,128)S(1)}, u32[]{:S(2)}, u32[]{:S(2)}) %collective-permute-start.10) | collective-permute-done | bytes 32800 | tf_op jit(solution)/shard_map/ppermute | solution.py:29
  34.6 1.2 %collective-permute-done.11.there = f32[64,128]{1,0:T(8,128)S(1)} collective-permute-done((f32[64,128]{1,0:T(8,128)S(1)}, f32[64,128]{1,0:T(8,128)S(1)}, u32[]{:S(2)}, u32[]{:S(2)}) %collective-permute-start.11) | collective-permute-done | bytes 32800 | tf_op jit(solution)/shard_map/ppermute | solution.py:29
  35.9 0.7 collective-permute-start.14
  36.6 1.9 %collective-permute-start.12 = (bf16[6,64,128]{2,1,0:T(8,128)(2,1)S(1)}, bf16[6,64,128]{2,1,0:T(8,128)(2,1)S(1)}, u32[]{:S(2)}, u32[]{:S(2)}) collective-permute-start(bf16[6,64,128]{2,1,0:T(8,128)(2,1)S(1)} %get-tuple-element.43.sent), channel_id=1, source_target_pairs={{0,4},{4,0},{8,12},{12,8},{16,20},{20,16},{24,28},{28,24},{1,5},{5... | collective-permute-start | bytes 294920 | tf_op jit(solution)/shard_map/ppermute | solution.py:29
  38.5 0.9 collective-permute-start.13
  39.4 1.4 %collective-permute-done.14.far.refs_0_ = bf16[6,64,128]{2,1,0:T(8,128)(2,1)S(1)} collective-permute-done((bf16[6,64,128]{2,1,0:T(8,128)(2,1)S(1)}, bf16[6,64,128]{2,1,0:T(8,128)(2,1)S(1)}, u32[]{:S(2)}, u32[]{:S(2)}) %collective-permute-start.14) | collective-permute-done | bytes 98336 | tf_op jit(solution)/shard_map/ppermute | solution.py:29
  40.8 0.1 join.2
  40.9 0.7 collective-permute-start.15
  41.6 0.1 collective-permute-done.12.flip
  41.7 2.8 %collective-permute-done.13.flip_far = bf16[6,64,128]{2,1,0:T(8,128)(2,1)S(1)} collective-permute-done((bf16[6,64,128]{2,1,0:T(8,128)(2,1)S(1)}, bf16[6,64,128]{2,1,0:T(8,128)(2,1)S(1)}, u32[]{:S(2)}, u32[]{:S(2)}) %collective-permute-start.13) | collective-permute-done | bytes 98336 | tf_op jit(solution)/shard_map/ppermute | solution.py:36
  44.5 2.6 %collective-permute-start.16 = (bf16[6,64,128]{2,1,0:T(8,128)(2,1)S(1)}, bf16[6,64,128]{2,1,0:T(8,128)(2,1)S(1)}, u32[]{:S(2)}, u32[]{:S(2)}) collective-permute-start(bf16[6,64,128]{2,1,0:T(8,128)(2,1)S(1)} %get-tuple-element.47.passed), channel_id=1, source_target_pairs={{0,8},{4,12},{16,24},{20,28},{8,0},{12,4},{24,16},{28,20},{1,9},{5... | collective-permute-start | bytes 294920 | tf_op jit(solution)/shard_map/ppermute | solution.py:41
  47.1 0.7 collective-permute-start.17
  47.8 1.9 %collective-permute-done.16.refs_1_ = bf16[6,64,128]{2,1,0:T(8,128)(2,1)S(1)} collective-permute-done((bf16[6,64,128]{2,1,0:T(8,128)(2,1)S(1)}, bf16[6,64,128]{2,1,0:T(8,128)(2,1)S(1)}, u32[]{:S(2)}, u32[]{:S(2)}) %collective-permute-start.16) | collective-permute-done | bytes 98336 | tf_op jit(solution)/shard_map/ppermute | solution.py:41
  49.7 3.3 %project.2 = (bf16[12,64,128]{2,1,0:T(8,128)(2,1)S(1)}, bf16[2,64,128]{2,1,0:T(8,128)(2,1)S(1)}, bf16[4,64,128]{2,1,0:T(8,128)(2,1)S(1)}, bf16[4,64,128]{2,1,0:T(8,128)(2,1)S(1)}) custom-call(s32[5,4]{1,0:T(8,128)S(1)} %pad_add_fusion.facts, bf16[6,64,128]{2,1,0:T(8,128)(2,1)S(1)} %get-tuple-element.47.passed, ...), custom_call_target="tpu_custom_call" | custom-call | flops 37748736 | bytes 1966080 | tf_op jit(solution)/shard_map/project/pallas_call | solution.py:420
  53.0 0.1 collective-permute-start.18
  53.1 4.0 %collective-permute-start.19 = (bf16[4,64,128]{2,1,0:T(8,128)(2,1)S(1)}, bf16[4,64,128]{2,1,0:T(8,128)(2,1)S(1)}, u32[]{:S(2)}, u32[]{:S(2)}) collective-permute-start(bf16[4,64,128]{2,1,0:T(8,128)(2,1)S(1)} %get-tuple-element.53), channel_id=1, source_target_pairs={{0,8},{4,12},{16,24},{20,28},{8,0},{12,4},{24,16},{28,20},{1,9},{5... | collective-permute-start | bytes 196616 | tf_op jit(solution)/shard_map/ppermute | solution.py:41
  57.1 0.7 collective-permute-start.22
  57.8 2.0 %collective-permute-done.19.refs_1_.first.refs_0_ = bf16[4,64,128]{2,1,0:T(8,128)(2,1)S(1)} collective-permute-done((bf16[4,64,128]{2,1,0:T(8,128)(2,1)S(1)}, bf16[4,64,128]{2,1,0:T(8,128)(2,1)S(1)}, u32[]{:S(2)}, u32[]{:S(2)}) %collective-permute-start.19) | collective-permute-done | bytes 65568 | tf_op jit(solution)/shard_map/ppermute | solution.py:41
  59.8 1.0 collective-permute-start.20
  60.8 1.8 %collective-permute-start.23 = (bf16[4,64,128]{2,1,0:T(8,128)(2,1)S(1)}, bf16[4,64,128]{2,1,0:T(8,128)(2,1)S(1)}, u32[]{:S(2)}, u32[]{:S(2)}) collective-permute-start(bf16[4,64,128]{2,1,0:T(8,128)(2,1)S(1)} %pass_on.3), channel_id=1, source_target_pairs={{0,4},{4,0},{8,12},{12,8},{16,20},{20,16},{24,28},{28,24},{1,5},{5... | collective-permute-start | bytes 196616 | tf_op jit(solution)/shard_map/ppermute | solution.py:29
  62.7 0.8 collective-permute-start.24
  63.5 1.0 collective-permute-start.25
  64.5 1.3 %collective-permute-done.23.refs_0_.refs_4_ = bf16[4,64,128]{2,1,0:T(8,128)(2,1)S(1)} collective-permute-done((bf16[4,64,128]{2,1,0:T(8,128)(2,1)S(1)}, bf16[4,64,128]{2,1,0:T(8,128)(2,1)S(1)}, u32[]{:S(2)}, u32[]{:S(2)}) %collective-permute-start.23) | collective-permute-done | bytes 65568 | tf_op jit(solution)/shard_map/ppermute | solution.py:29
  65.8 2.2 %collective-permute-done.24.refs_2_.refs_6_ = bf16[4,64,128]{2,1,0:T(8,128)(2,1)S(1)} collective-permute-done((bf16[4,64,128]{2,1,0:T(8,128)(2,1)S(1)}, bf16[4,64,128]{2,1,0:T(8,128)(2,1)S(1)}, u32[]{:S(2)}, u32[]{:S(2)}) %collective-permute-start.24) | collective-permute-done | bytes 65568 | tf_op jit(solution)/shard_map/ppermute | solution.py:36
  67.9 1.4 %collective-permute-done.25.refs_3_.refs_7_ = bf16[4,64,128]{2,1,0:T(8,128)(2,1)S(1)} collective-permute-done((bf16[4,64,128]{2,1,0:T(8,128)(2,1)S(1)}, bf16[4,64,128]{2,1,0:T(8,128)(2,1)S(1)}, u32[]{:S(2)}, u32[]{:S(2)}) %collective-permute-start.25) | collective-permute-done | bytes 65568 | tf_op jit(solution)/shard_map/ppermute | solution.py:29
  69.4 0.1 collective-permute-start.26
  69.5 0.5 collective-permute-start.21
  70.0 1.3 %collective-permute-done.21.refs_3_ = bf16[12,64,128]{2,1,0:T(8,128)(2,1)S(1)} collective-permute-done((bf16[12,64,128]{2,1,0:T(8,128)(2,1)S(1)}, bf16[12,64,128]{2,1,0:T(8,128)(2,1)S(1)}, u32[]{:S(2)}, u32[]{:S(2)}) %collective-permute-start.21) | collective-permute-done | bytes 196640 | tf_op jit(solution)/shard_map/ppermute | solution.py:29
  71.3 8.1 %forward_adjoint.3 = (f32[40,64,128]{2,1,0:T(8,128)S(1)}, f32[40,64,128]{2,1,0:T(8,128)S(1)}, f32[64,128]{1,0:T(8,128)S(1)}) custom-call(s32[5,4]{1,0:T(8,128)S(1)} %pad_add_fusion.facts, s32[12,27]{1,0:T(8,128)S(1)} %copy-done, bf16[12,27,128,128]{3,2,1,0:T(8,128)(2,1)S(1)} %bitcast.8, f32[12,128]{1,0:T(8,128)S(1)} %copy-done.1, ...), custom_call_target="tpu_custom_call" | custom-call | flops 1358954496 | bytes 10616832 | tf_op jit(solution)/shard_map/forward_adjoint/pallas_call | solution.py:267
  79.5 1.4 %collective-permute-start.28 = (f32[64,128]{1,0:T(8,128)S(1)}, f32[64,128]{1,0:T(8,128)S(1)}, u32[]{:S(2)}, u32[]{:S(2)}) collective-permute-start(f32[64,128]{1,0:T(8,128)S(1)} %get-tuple-element.58), channel_id=1, source_target_pairs={{0,16},{4,20},{8,24},{12,28},{16,0},{20,4},{24,8},{28,12},{1,17},{... | collective-permute-start | bytes 98312 | tf_op jit(solution)/shard_map/ppermute | solution.py:29
  80.9 4.1 %collective-permute-done.28 = f32[64,128]{1,0:T(8,128)S(1)} collective-permute-done((f32[64,128]{1,0:T(8,128)S(1)}, f32[64,128]{1,0:T(8,128)S(1)}, u32[]{:S(2)}, u32[]{:S(2)}) %collective-permute-start.28) | collective-permute-done | bytes 32800 | tf_op jit(solution)/shard_map/ppermute | solution.py:29
  85.0 1.2 %collective-permute-done.29.there = f32[64,128]{1,0:T(8,128)S(1)} collective-permute-done((f32[64,128]{1,0:T(8,128)S(1)}, f32[64,128]{1,0:T(8,128)S(1)}, u32[]{:S(2)}, u32[]{:S(2)}) %collective-permute-start.29) | collective-permute-done | bytes 32800 | tf_op jit(solution)/shard_map/ppermute | solution.py:29
  86.3 0.1 collective-permute-start.32
  86.3 1.6 %collective-permute-start.30 = (bf16[6,64,128]{2,1,0:T(8,128)(2,1)S(1)}, bf16[6,64,128]{2,1,0:T(8,128)(2,1)S(1)}, u32[]{:S(2)}, u32[]{:S(2)}) collective-permute-start(bf16[6,64,128]{2,1,0:T(8,128)(2,1)S(1)} %get-tuple-element.59.sent), channel_id=1, source_target_pairs={{0,4},{4,0},{8,12},{12,8},{16,20},{20,16},{24,28},{28,24},{1,5},{5... | collective-permute-start | bytes 294920 | tf_op jit(solution)/shard_map/ppermute | solution.py:29
  88.0 1.8 %collective-permute-start.31 = (bf16[6,64,128]{2,1,0:T(8,128)(2,1)S(1)}, bf16[6,64,128]{2,1,0:T(8,128)(2,1)S(1)}, u32[]{:S(2)}, u32[]{:S(2)}) collective-permute-start(bf16[6,64,128]{2,1,0:T(8,128)(2,1)S(1)} %get-tuple-element.60), channel_id=1, source_target_pairs={{0,6},{1,7},{2,4},{3,5},{4,2},{5,3},{6,0},{7,1},{8,14},{9,15},{10,... | collective-permute-start | bytes 294920 | tf_op jit(solution)/shard_map/ppermute | solution.py:36
  89.8 1.4 %collective-permute-done.32.far.refs_0_ = bf16[6,64,128]{2,1,0:T(8,128)(2,1)S(1)} collective-permute-done((bf16[6,64,128]{2,1,0:T(8,128)(2,1)S(1)}, bf16[6,64,128]{2,1,0:T(8,128)(2,1)S(1)}, u32[]{:S(2)}, u32[]{:S(2)}) %collective-permute-start.32) | collective-permute-done | bytes 98336 | tf_op jit(solution)/shard_map/ppermute | solution.py:29
  91.2 0.1 join.3
  91.3 0.4 collective-permute-start.33
  91.6 0.4 collective-permute-done.30.flip
  92.0 2.5 %collective-permute-done.31.flip_far = bf16[6,64,128]{2,1,0:T(8,128)(2,1)S(1)} collective-permute-done((bf16[6,64,128]{2,1,0:T(8,128)(2,1)S(1)}, bf16[6,64,128]{2,1,0:T(8,128)(2,1)S(1)}, u32[]{:S(2)}, u32[]{:S(2)}) %collective-permute-start.31) | collective-permute-done | bytes 98336 | tf_op jit(solution)/shard_map/ppermute | solution.py:36
  94.6 1.1 %collective-permute-start.34 = (bf16[6,64,128]{2,1,0:T(8,128)(2,1)S(1)}, bf16[6,64,128]{2,1,0:T(8,128)(2,1)S(1)}, u32[]{:S(2)}, u32[]{:S(2)}) collective-permute-start(bf16[6,64,128]{2,1,0:T(8,128)(2,1)S(1)} %get-tuple-element.63.passed), channel_id=1, source_target_pairs={{0,8},{4,12},{16,24},{20,28},{8,0},{12,4},{24,16},{28,20},{1,9},{5... | collective-permute-start | bytes 294920 | tf_op jit(solution)/shard_map/ppermute | solution.py:41
  95.7 0.7 collective-permute-start.35
  96.4 3.0 %collective-permute-done.34.refs_1_ = bf16[6,64,128]{2,1,0:T(8,128)(2,1)S(1)} collective-permute-done((bf16[6,64,128]{2,1,0:T(8,128)(2,1)S(1)}, bf16[6,64,128]{2,1,0:T(8,128)(2,1)S(1)}, u32[]{:S(2)}, u32[]{:S(2)}) %collective-permute-start.34) | collective-permute-done | bytes 98336 | tf_op jit(solution)/shard_map/ppermute | solution.py:41
  99.3 4.0 %project.3 = (f32[12,64,128]{2,1,0:T(8,128)}, f32[64,64]{1,0:T(8,128)}) custom-call(s32[5,4]{1,0:T(8,128)S(1)} %pad_add_fusion.facts, bf16[6,64,128]{2,1,0:T(8,128)(2,1)S(1)} %get-tuple-element.63.passed, bf16[12,64,128]{2,1,0:T(8,128)(2,1)S(1)} %get-tuple-element.52.refs_0_.basis, f32[12,64,128]{2,1,0:T(8,128)S(1)} %get-tuple-element.64.near_own, ...), custom_call_target="tpu_custom_call" | custom-call | flops 37748736 | bytes 1966080 | tf_op jit(solution)/shard_map/project/pallas_call | solution.py:420
  (45 shorter events, 0.5 us)
Async XLA Ops:
  1.4 20.1 %slice-start = ((s8[10616832]{0:T(1024)(128)(4,1)}), s8[4194304]{0:T(1024)(128)(4,1)S(1)}, s32[]{:S(2)}) async-start(s8[10616832]{0:T(1024)(128)(4,1)} %bitcast.7), calls=%async_computation | async-start | bytes 8388608
  2.2 1.1 %copy-start.2 = (bf16[12,64,128]{2,1,0:T(8,128)(2,1)S(1)}, bf16[12,64,128]{2,1,0:T(8,128)(2,1)}, u32[]{:S(2)}) copy-start(bf16[12,64,128]{2,1,0:T(8,128)(2,1)} %directions.1) | copy-start | bytes 589828
  3.3 18.1 %slice-start.1 = ((s8[10616832]{0:T(1024)(128)(4,1)}), s8[4194304]{0:T(1024)(128)(4,1)S(1)}, s32[]{:S(2)}) async-start(s8[10616832]{0:T(1024)(128)(4,1)} %bitcast.7), calls=%async_computation.1 | async-start | bytes 8388608
  3.3 18.1 %slice-start.2 = ((s8[10616832]{0:T(1024)(128)(4,1)}), s8[2228224]{0:T(1024)(128)(4,1)S(1)}, s32[]{:S(2)}) async-start(s8[10616832]{0:T(1024)(128)(4,1)} %bitcast.7), calls=%async_computation.2 | async-start | bytes 4456448
  4.1 17.4 %copy-start = (s32[12,27]{1,0:T(8,128)S(1)}, s32[12,27]{1,0:T(8,128)}, u32[]{:S(2)}) copy-start(s32[12,27]{1,0:T(8,128)} %cols.3) | copy-start | bytes 3892
  4.1 17.4 %copy-start.1 = (f32[12,128]{1,0:T(8,128)S(1)}, f32[12,128]{1,0:T(8,128)}, u32[]{:S(2)}) copy-start(f32[12,128]{1,0:T(8,128)} %friction.3) | copy-start | bytes 18436
  4.1 9.5 %collective-permute-start = (bf16[12,64,128]{2,1,0:T(8,128)(2,1)S(1)}, bf16[12,64,128]{2,1,0:T(8,128)(2,1)S(1)}, u32[]{:S(2)}, u32[]{:S(2)}) collective-permute-start(bf16[12,64,128]{2,1,0:T(8,128)(2,1)S(1)} %get-tuple-element.36.refs_0_.basis), channel_id=1, source_target_pairs={{0,1},{1,0},{2,3},{3,2},{4,5},{5,4},{6,7},{7,6},{8,9},{9,8},{10,11... | collective-permute-start | bytes 589832 | tf_op jit(solution)/shard_map/ppermute | solution.py:29
  4.7 5.3 %collective-permute-start.1 = (bf16[4,64,128]{2,1,0:T(8,128)(2,1)S(1)}, bf16[4,64,128]{2,1,0:T(8,128)(2,1)S(1)}, u32[]{:S(2)}, u32[]{:S(2)}) collective-permute-start(bf16[4,64,128]{2,1,0:T(8,128)(2,1)S(1)} %get-tuple-element.37), channel_id=1, source_target_pairs={{0,8},{4,12},{16,24},{20,28},{8,0},{12,4},{24,16},{28,20},{1,9},{5... | collective-permute-start | bytes 196616 | tf_op jit(solution)/shard_map/ppermute | solution.py:41
  7.3 4.5 %collective-permute-start.4 = (bf16[4,64,128]{2,1,0:T(8,128)(2,1)S(1)}, bf16[4,64,128]{2,1,0:T(8,128)(2,1)S(1)}, u32[]{:S(2)}, u32[]{:S(2)}) collective-permute-start(bf16[4,64,128]{2,1,0:T(8,128)(2,1)S(1)} %get-tuple-element.39), channel_id=1, source_target_pairs={{8,16},{12,20},{16,8},{20,12},{9,17},{13,21},{17,9},{21,13},{10,18... | collective-permute-start | bytes 196616 | tf_op jit(solution)/shard_map/ppermute | solution.py:41
  10.0 9.6 %collective-permute-start.2 = (bf16[12,64,128]{2,1,0:T(8,128)(2,1)S(1)}, bf16[12,64,128]{2,1,0:T(8,128)(2,1)S(1)}, u32[]{:S(2)}, u32[]{:S(2)}) collective-permute-start(bf16[12,64,128]{2,1,0:T(8,128)(2,1)S(1)} %stack.14), channel_id=1, source_target_pairs={{0,2},{1,3},{2,0},{3,1},{4,6},{5,7},{6,4},{7,5},{8,10},{9,11},{10,... | collective-permute-start | bytes 589832 | tf_op jit(solution)/shard_map/ppermute | solution.py:29
  11.8 4.6 %collective-permute-start.5 = (bf16[4,64,128]{2,1,0:T(8,128)(2,1)S(1)}, bf16[4,64,128]{2,1,0:T(8,128)(2,1)S(1)}, u32[]{:S(2)}, u32[]{:S(2)}) collective-permute-start(bf16[4,64,128]{2,1,0:T(8,128)(2,1)S(1)} %pass_on.2), channel_id=1, source_target_pairs={{0,4},{4,0},{8,12},{12,8},{16,20},{20,16},{24,28},{28,24},{1,5},{5... | collective-permute-start | bytes 196616 | tf_op jit(solution)/shard_map/ppermute | solution.py:29
  13.4 5.3 %collective-permute-start.6 = (bf16[4,64,128]{2,1,0:T(8,128)(2,1)S(1)}, bf16[4,64,128]{2,1,0:T(8,128)(2,1)S(1)}, u32[]{:S(2)}, u32[]{:S(2)}) collective-permute-start(bf16[4,64,128]{2,1,0:T(8,128)(2,1)S(1)} %pass_on.2), channel_id=1, source_target_pairs={{0,6},{1,7},{2,4},{3,5},{4,2},{5,3},{6,0},{7,1},{8,14},{9,15},{10,... | collective-permute-start | bytes 196616 | tf_op jit(solution)/shard_map/ppermute | solution.py:36
  13.7 5.9 %collective-permute-start.7 = (bf16[4,64,128]{2,1,0:T(8,128)(2,1)S(1)}, bf16[4,64,128]{2,1,0:T(8,128)(2,1)S(1)}, u32[]{:S(2)}, u32[]{:S(2)}) collective-permute-start(bf16[4,64,128]{2,1,0:T(8,128)(2,1)S(1)} %stack.15.refs_1_.refs_5_), channel_id=1, source_target_pairs={{0,2},{1,3},{2,0},{3,1},{4,6},{5,7},{6,4},{7,5},{8,10},{9,11},{10,... | collective-permute-start | bytes 196616 | tf_op jit(solution)/shard_map/ppermute | solution.py:29
  19.6 1.9 %collective-permute-start.8 = (bf16[16,64,128]{2,1,0:T(8,128)(2,1)S(1)}, bf16[16,64,128]{2,1,0:T(8,128)(2,1)S(1)}, u32[]{:S(2)}, u32[]{:S(2)}) collective-permute-start(bf16[16,64,128]{2,1,0:T(8,128)(2,1)S(1)} %stack.16), channel_id=1, source_target_pairs={{0,1},{1,0},{2,3},{3,2},{4,5},{5,4},{6,7},{7,6},{8,9},{9,8},{10,11... | collective-permute-start | bytes 786440 | tf_op jit(solution)/shard_map/ppermute | solution.py:29
  19.7 1.8 %collective-permute-start.3 = (bf16[12,64,128]{2,1,0:T(8,128)(2,1)S(1)}, bf16[12,64,128]{2,1,0:T(8,128)(2,1)S(1)}, u32[]{:S(2)}, u32[]{:S(2)}) collective-permute-start(bf16[12,64,128]{2,1,0:T(8,128)(2,1)S(1)} %collective-permute-done.2.refs_2_), channel_id=1, source_target_pairs={{0,1},{1,0},{2,3},{3,2},{4,5},{5,4},{6,7},{7,6},{8,9},{9,8},{10,11... | collective-permute-start | bytes 589832 | tf_op jit(solution)/shard_map/ppermute | solution.py:29
  29.6 6.2 %collective-permute-start.9 = (f32[40,64,128]{2,1,0:T(8,128)S(1)}, f32[40,64,128]{2,1,0:T(8,128)S(1)}, u32[]{:S(2)}, u32[]{:S(2)}) collective-permute-start(f32[40,64,128]{2,1,0:T(8,128)S(1)} %get-tuple-element.41), channel_id=1, source_target_pairs={{0,1},{1,0},{2,3},{3,2},{4,5},{5,4},{6,7},{7,6},{8,9},{9,8},{10,11... | collective-permute-start | bytes 3932168 | tf_op jit(solution)/shard_map/ppermute | solution.py:29
  29.7 4.9 %collective-permute-start.10 = (f32[64,128]{1,0:T(8,128)S(1)}, f32[64,128]{1,0:T(8,128)S(1)}, u32[]{:S(2)}, u32[]{:S(2)}) collective-permute-start(f32[64,128]{1,0:T(8,128)S(1)} %get-tuple-element.42), channel_id=1, source_target_pairs={{0,16},{4,20},{8,24},{12,28},{16,0},{20,4},{24,8},{28,12},{1,17},{... | collective-permute-start | bytes 98312 | tf_op jit(solution)/shard_map/ppermute | solution.py:29
  34.6 1.2 %collective-permute-start.11 = (f32[64,128]{1,0:T(8,128)S(1)}, f32[64,128]{1,0:T(8,128)S(1)}, u32[]{:S(2)}, u32[]{:S(2)}) collective-permute-start(f32[64,128]{1,0:T(8,128)S(1)} %add.8.here), channel_id=1, source_target_pairs={{0,1},{1,0},{2,3},{3,2},{4,5},{5,4},{6,7},{7,6},{8,9},{9,8},{10,11... | collective-permute-start | bytes 98312 | tf_op jit(solution)/shard_map/ppermute | solution.py:29
  35.9 4.9 %collective-permute-start.14 = (bf16[6,64,128]{2,1,0:T(8,128)(2,1)S(1)}, bf16[6,64,128]{2,1,0:T(8,128)(2,1)S(1)}, u32[]{:S(2)}, u32[]{:S(2)}) collective-permute-start(bf16[6,64,128]{2,1,0:T(8,128)(2,1)S(1)} %get-tuple-element.45), channel_id=1, source_target_pairs={{0,2},{1,3},{2,0},{3,1},{4,6},{5,7},{6,4},{7,5},{8,10},{9,11},{10,... | collective-permute-start | bytes 294920 | tf_op jit(solution)/shard_map/ppermute | solution.py:29
  36.6 5.1 %collective-permute-start.12 = (bf16[6,64,128]{2,1,0:T(8,128)(2,1)S(1)}, bf16[6,64,128]{2,1,0:T(8,128)(2,1)S(1)}, u32[]{:S(2)}, u32[]{:S(2)}) collective-permute-start(bf16[6,64,128]{2,1,0:T(8,128)(2,1)S(1)} %get-tuple-element.43.sent), channel_id=1, source_target_pairs={{0,4},{4,0},{8,12},{12,8},{16,20},{20,16},{24,28},{28,24},{1,5},{5... | collective-permute-start | bytes 294920 | tf_op jit(solution)/shard_map/ppermute | solution.py:29
  38.5 6.0 %collective-permute-start.13 = (bf16[6,64,128]{2,1,0:T(8,128)(2,1)S(1)}, bf16[6,64,128]{2,1,0:T(8,128)(2,1)S(1)}, u32[]{:S(2)}, u32[]{:S(2)}) collective-permute-start(bf16[6,64,128]{2,1,0:T(8,128)(2,1)S(1)} %get-tuple-element.44), channel_id=1, source_target_pairs={{0,6},{1,7},{2,4},{3,5},{4,2},{5,3},{6,0},{7,1},{8,14},{9,15},{10,... | collective-permute-start | bytes 294920 | tf_op jit(solution)/shard_map/ppermute | solution.py:36
  40.9 8.8 %collective-permute-start.15 = (bf16[12,64,128]{2,1,0:T(8,128)(2,1)S(1)}, bf16[12,64,128]{2,1,0:T(8,128)(2,1)S(1)}, u32[]{:S(2)}, u32[]{:S(2)}) collective-permute-start(bf16[12,64,128]{2,1,0:T(8,128)(2,1)S(1)} %get-tuple-element.49), channel_id=1, source_target_pairs={{0,2},{1,3},{2,0},{3,1},{4,6},{5,7},{6,4},{7,5},{8,10},{9,11},{10,... | collective-permute-start | bytes 589832 | tf_op jit(solution)/shard_map/ppermute | solution.py:29
  44.5 5.2 %collective-permute-start.16 = (bf16[6,64,128]{2,1,0:T(8,128)(2,1)S(1)}, bf16[6,64,128]{2,1,0:T(8,128)(2,1)S(1)}, u32[]{:S(2)}, u32[]{:S(2)}) collective-permute-start(bf16[6,64,128]{2,1,0:T(8,128)(2,1)S(1)} %get-tuple-element.47.passed), channel_id=1, source_target_pairs={{0,8},{4,12},{16,24},{20,28},{8,0},{12,4},{24,16},{28,20},{1,9},{5... | collective-permute-start | bytes 294920 | tf_op jit(solution)/shard_map/ppermute | solution.py:41
  47.1 0.7 collective-permute-start.17
  53.0 10.4 %collective-permute-start.18 = (bf16[12,64,128]{2,1,0:T(8,128)(2,1)S(1)}, bf16[12,64,128]{2,1,0:T(8,128)(2,1)S(1)}, u32[]{:S(2)}, u32[]{:S(2)}) collective-permute-start(bf16[12,64,128]{2,1,0:T(8,128)(2,1)S(1)} %get-tuple-element.52.refs_0_.basis), channel_id=1, source_target_pairs={{0,1},{1,0},{2,3},{3,2},{4,5},{5,4},{6,7},{7,6},{8,9},{9,8},{10,11... | collective-permute-start | bytes 589832 | tf_op jit(solution)/shard_map/ppermute | solution.py:29
  53.1 6.7 %collective-permute-start.19 = (bf16[4,64,128]{2,1,0:T(8,128)(2,1)S(1)}, bf16[4,64,128]{2,1,0:T(8,128)(2,1)S(1)}, u32[]{:S(2)}, u32[]{:S(2)}) collective-permute-start(bf16[4,64,128]{2,1,0:T(8,128)(2,1)S(1)} %get-tuple-element.53), channel_id=1, source_target_pairs={{0,8},{4,12},{16,24},{20,28},{8,0},{12,4},{24,16},{28,20},{1,9},{5... | collective-permute-start | bytes 196616 | tf_op jit(solution)/shard_map/ppermute | solution.py:41
  57.1 3.7 %collective-permute-start.22 = (bf16[4,64,128]{2,1,0:T(8,128)(2,1)S(1)}, bf16[4,64,128]{2,1,0:T(8,128)(2,1)S(1)}, u32[]{:S(2)}, u32[]{:S(2)}) collective-permute-start(bf16[4,64,128]{2,1,0:T(8,128)(2,1)S(1)} %get-tuple-element.55), channel_id=1, source_target_pairs={{8,16},{12,20},{16,8},{20,12},{9,17},{13,21},{17,9},{21,13},{10,18... | collective-permute-start | bytes 196616 | tf_op jit(solution)/shard_map/ppermute | solution.py:41
  59.8 9.6 %collective-permute-start.20 = (bf16[12,64,128]{2,1,0:T(8,128)(2,1)S(1)}, bf16[12,64,128]{2,1,0:T(8,128)(2,1)S(1)}, u32[]{:S(2)}, u32[]{:S(2)}) collective-permute-start(bf16[12,64,128]{2,1,0:T(8,128)(2,1)S(1)} %stack.17), channel_id=1, source_target_pairs={{0,2},{1,3},{2,0},{3,1},{4,6},{5,7},{6,4},{7,5},{8,10},{9,11},{10,... | collective-permute-start | bytes 589832 | tf_op jit(solution)/shard_map/ppermute | solution.py:29
  60.8 4.9 %collective-permute-start.23 = (bf16[4,64,128]{2,1,0:T(8,128)(2,1)S(1)}, bf16[4,64,128]{2,1,0:T(8,128)(2,1)S(1)}, u32[]{:S(2)}, u32[]{:S(2)}) collective-permute-start(bf16[4,64,128]{2,1,0:T(8,128)(2,1)S(1)} %pass_on.3), channel_id=1, source_target_pairs={{0,4},{4,0},{8,12},{12,8},{16,20},{20,16},{24,28},{28,24},{1,5},{5... | collective-permute-start | bytes 196616 | tf_op jit(solution)/shard_map/ppermute | solution.py:29
  62.7 5.3 %collective-permute-start.24 = (bf16[4,64,128]{2,1,0:T(8,128)(2,1)S(1)}, bf16[4,64,128]{2,1,0:T(8,128)(2,1)S(1)}, u32[]{:S(2)}, u32[]{:S(2)}) collective-permute-start(bf16[4,64,128]{2,1,0:T(8,128)(2,1)S(1)} %pass_on.3), channel_id=1, source_target_pairs={{0,6},{1,7},{2,4},{3,5},{4,2},{5,3},{6,0},{7,1},{8,14},{9,15},{10,... | collective-permute-start | bytes 196616 | tf_op jit(solution)/shard_map/ppermute | solution.py:36
  63.5 5.9 %collective-permute-start.25 = (bf16[4,64,128]{2,1,0:T(8,128)(2,1)S(1)}, bf16[4,64,128]{2,1,0:T(8,128)(2,1)S(1)}, u32[]{:S(2)}, u32[]{:S(2)}) collective-permute-start(bf16[4,64,128]{2,1,0:T(8,128)(2,1)S(1)} %stack.18.refs_1_.refs_5_), channel_id=1, source_target_pairs={{0,2},{1,3},{2,0},{3,1},{4,6},{5,7},{6,4},{7,5},{8,10},{9,11},{10,... | collective-permute-start | bytes 196616 | tf_op jit(solution)/shard_map/ppermute | solution.py:29
  69.4 1.9 %collective-permute-start.26 = (bf16[16,64,128]{2,1,0:T(8,128)(2,1)S(1)}, bf16[16,64,128]{2,1,0:T(8,128)(2,1)S(1)}, u32[]{:S(2)}, u32[]{:S(2)}) collective-permute-start(bf16[16,64,128]{2,1,0:T(8,128)(2,1)S(1)} %stack.19), channel_id=1, source_target_pairs={{0,1},{1,0},{2,3},{3,2},{4,5},{5,4},{6,7},{7,6},{8,9},{9,8},{10,11... | collective-permute-start | bytes 786440 | tf_op jit(solution)/shard_map/ppermute | solution.py:29
  69.5 1.8 %collective-permute-start.21 = (bf16[12,64,128]{2,1,0:T(8,128)(2,1)S(1)}, bf16[12,64,128]{2,1,0:T(8,128)(2,1)S(1)}, u32[]{:S(2)}, u32[]{:S(2)}) collective-permute-start(bf16[12,64,128]{2,1,0:T(8,128)(2,1)S(1)} %collective-permute-done.20.refs_2_), channel_id=1, source_target_pairs={{0,1},{1,0},{2,3},{3,2},{4,5},{5,4},{6,7},{7,6},{8,9},{9,8},{10,11... | collective-permute-start | bytes 589832 | tf_op jit(solution)/shard_map/ppermute | solution.py:29
  79.4 6.8 %collective-permute-start.27 = (f32[40,64,128]{2,1,0:T(8,128)S(1)}, f32[40,64,128]{2,1,0:T(8,128)S(1)}, u32[]{:S(2)}, u32[]{:S(2)}) collective-permute-start(f32[40,64,128]{2,1,0:T(8,128)S(1)} %get-tuple-element.57), channel_id=1, source_target_pairs={{0,1},{1,0},{2,3},{3,2},{4,5},{5,4},{6,7},{7,6},{8,9},{9,8},{10,11... | collective-permute-start | bytes 3932168 | tf_op jit(solution)/shard_map/ppermute | solution.py:29
  79.5 5.5 %collective-permute-start.28 = (f32[64,128]{1,0:T(8,128)S(1)}, f32[64,128]{1,0:T(8,128)S(1)}, u32[]{:S(2)}, u32[]{:S(2)}) collective-permute-start(f32[64,128]{1,0:T(8,128)S(1)} %get-tuple-element.58), channel_id=1, source_target_pairs={{0,16},{4,20},{8,24},{12,28},{16,0},{20,4},{24,8},{28,12},{1,17},{... | collective-permute-start | bytes 98312 | tf_op jit(solution)/shard_map/ppermute | solution.py:29
  85.0 1.2 %collective-permute-start.29 = (f32[64,128]{1,0:T(8,128)S(1)}, f32[64,128]{1,0:T(8,128)S(1)}, u32[]{:S(2)}, u32[]{:S(2)}) collective-permute-start(f32[64,128]{1,0:T(8,128)S(1)} %add.9.here), channel_id=1, source_target_pairs={{0,1},{1,0},{2,3},{3,2},{4,5},{5,4},{6,7},{7,6},{8,9},{9,8},{10,11... | collective-permute-start | bytes 98312 | tf_op jit(solution)/shard_map/ppermute | solution.py:29
  86.3 4.9 %collective-permute-start.32 = (bf16[6,64,128]{2,1,0:T(8,128)(2,1)S(1)}, bf16[6,64,128]{2,1,0:T(8,128)(2,1)S(1)}, u32[]{:S(2)}, u32[]{:S(2)}) collective-permute-start(bf16[6,64,128]{2,1,0:T(8,128)(2,1)S(1)} %get-tuple-element.61), channel_id=1, source_target_pairs={{0,2},{1,3},{2,0},{3,1},{4,6},{5,7},{6,4},{7,5},{8,10},{9,11},{10,... | collective-permute-start | bytes 294920 | tf_op jit(solution)/shard_map/ppermute | solution.py:29
  86.3 5.7 %collective-permute-start.30 = (bf16[6,64,128]{2,1,0:T(8,128)(2,1)S(1)}, bf16[6,64,128]{2,1,0:T(8,128)(2,1)S(1)}, u32[]{:S(2)}, u32[]{:S(2)}) collective-permute-start(bf16[6,64,128]{2,1,0:T(8,128)(2,1)S(1)} %get-tuple-element.59.sent), channel_id=1, source_target_pairs={{0,4},{4,0},{8,12},{12,8},{16,20},{20,16},{24,28},{28,24},{1,5},{5... | collective-permute-start | bytes 294920 | tf_op jit(solution)/shard_map/ppermute | solution.py:29
  88.0 6.6 %collective-permute-start.31 = (bf16[6,64,128]{2,1,0:T(8,128)(2,1)S(1)}, bf16[6,64,128]{2,1,0:T(8,128)(2,1)S(1)}, u32[]{:S(2)}, u32[]{:S(2)}) collective-permute-start(bf16[6,64,128]{2,1,0:T(8,128)(2,1)S(1)} %get-tuple-element.60), channel_id=1, source_target_pairs={{0,6},{1,7},{2,4},{3,5},{4,2},{5,3},{6,0},{7,1},{8,14},{9,15},{10,... | collective-permute-start | bytes 294920 | tf_op jit(solution)/shard_map/ppermute | solution.py:36
  91.3 8.1 %collective-permute-start.33 = (bf16[12,64,128]{2,1,0:T(8,128)(2,1)S(1)}, bf16[12,64,128]{2,1,0:T(8,128)(2,1)S(1)}, u32[]{:S(2)}, u32[]{:S(2)}) collective-permute-start(bf16[12,64,128]{2,1,0:T(8,128)(2,1)S(1)} %get-tuple-element.65), channel_id=1, source_target_pairs={{0,2},{1,3},{2,0},{3,1},{4,6},{5,7},{6,4},{7,5},{8,10},{9,11},{10,... | collective-permute-start | bytes 589832 | tf_op jit(solution)/shard_map/ppermute | solution.py:29
  94.6 4.7 %collective-permute-start.34 = (bf16[6,64,128]{2,1,0:T(8,128)(2,1)S(1)}, bf16[6,64,128]{2,1,0:T(8,128)(2,1)S(1)}, u32[]{:S(2)}, u32[]{:S(2)}) collective-permute-start(bf16[6,64,128]{2,1,0:T(8,128)(2,1)S(1)} %get-tuple-element.63.passed), channel_id=1, source_target_pairs={{0,8},{4,12},{16,24},{20,28},{8,0},{12,4},{24,16},{28,20},{1,9},{5... | collective-permute-start | bytes 294920 | tf_op jit(solution)/shard_map/ppermute | solution.py:41
  95.7 0.7 collective-permute-start.35

commit v6 on v5

--- a/solution.py
+++ b/solution.py
@@ -383,11 +383,31 @@
     return jnp.concatenate(panels, axis=0)[:, dirs:]
 
 
-def project(shape, last, facts, passed, basis, near_own, far_own, *refs):
+def solve(start, sent, got, coupling, cross):
+    grams = joined(sent, start) + joined(got, start)
+    dirs = grams.shape[0]
+    coupling[...] = jnp.concatenate(split_bf16(eliminate(grams, dirs).T, 3), axis=1)
+    cross[...] = grams[:, dirs:]
+
+
+def call_solve(start, sent, got):
+    dirs = sent.shape[1]
+    return pl.pallas_call(
+        functools.partial(solve, start),
+        in_specs=[VMEM] * 2,
+        out_specs=[VMEM] * 2,
+        out_shape=[jax.ShapeDtypeStruct((dirs, 3 * dirs), BF16), jax.ShapeDtypeStruct((dirs, dirs), F32)],
+        compiler_params=SMALL,
+        cost_estimate=pl.CostEstimate(flops=4 * dirs**3, bytes_accessed=16 * dirs * dirs, transcendentals=dirs),
+        name="solve",
+    )(sent, got)
+
+
+def project(shape, last, facts, coupling, basis, near_own, far_own, *refs):
     slots = shape[1]
     facts = Facts(facts, *shape)
     flip, pairs, outs, image = refs[0], refs[1:3], refs[3:-1], refs[-1]
-    blocks, dirs = basis.shape[0], basis.shape[1]
+    blocks = basis.shape[0]
     for b in range(blocks):
         image[b] = near_own[b] + far_own[b].astype(F32)
     for s in range(slots):
@@ -395,25 +415,20 @@
         for role, back in enumerate((flip[s], relayed, pairs[0][s], pairs[1][s])):
             block, sent = facts.send(role, s)
             image[block] += back.astype(F32) * sent
-    grams = joined(passed, 2 * slots) + joined(pairs[0], 2 * slots)
-    coupling = eliminate(grams, dirs)
-    turned = jnp.concatenate(split_bf16(coupling.T, 3), axis=1)
-    if last:
-        outs[1][...] = grams[:, dirs:]
     for b in range(blocks):
         block = basis[b]
         wanted = facts.live(b) * (image[b] + 1.0 * block.astype(F32))
         tall = jnp.concatenate([block] * 3, axis=0)
-        rest = wanted - jnp.dot(turned, tall, preferred_element_type=F32)
+        rest = wanted - jnp.dot(coupling[...], tall, preferred_element_type=F32)
         outs[0][b] = rest.astype(outs[0].dtype)
     if not last:
         write_outgoing(facts, outs[0], *outs[1:])
 
 
-def call_project(shape, last, facts, sent, basis, near_own, far_own, returned):
+def call_project(shape, last, facts, coupling, basis, near_own, far_own, returned):
     blocks, dirs, width = basis.shape
     if last:
-        out_shape = [jax.ShapeDtypeStruct(basis.shape, F32), jax.ShapeDtypeStruct((dirs, dirs), F32)]
+        out_shape = [jax.ShapeDtypeStruct(basis.shape, F32)]
     else:
         out_shape = [jax.ShapeDtypeStruct(basis.shape, BF16)]
         out_shape += outgoing_shapes(shape[1], dirs, width)
@@ -428,7 +443,7 @@
         ),
         compiler_params=SMALL,
         name="project",
-    )(facts, sent, basis, near_own, far_own, *returned)
+    )(facts, coupling, basis, near_own, far_own, *returned)
 
 
 def on_device(directions, tiles, tile_cols, friction, neighbours, send_idx, send_count, row_counts):
@@ -471,12 +486,12 @@
         far_own_got = swap(far_own, "sub", far)
         *back, flip = call_pass_back(slots, ways, near_flip, flip, flip_far, pairs_got, near_pairs)
         returned = [flip] + [pair_up(x, i) for i, x in enumerate(back)]
+        coupling, cross = call_solve(2 * slots, back[0], returned[1])
         last = step == ITERS - 1
         basis, *outgoing = call_project(
-            shape, last, facts, back[0], basis, near_own, far_own_got, returned
+            shape, last, facts, coupling, basis, near_own, far_own_got, returned
         )
-    remainder, cross = basis, outgoing[0]
-    return (remainder, cross)
+    return (basis, cross)
 
 
 def solution(mesh):

time: 104 us -> 101 us (0.971)
  waiting for transfers between devices: 38.1 us -> 32.7 us
  starting transfers between devices: 36.7 us -> 40.2 us
  Pallas kernels: 24.9 us -> 23.6 us
    pallas_call x2, Pallas kernels: 7.37 us -> 2.7 us  [call_project(): pl.pallas_call(functools.partial(project, shape, last), in_specs=[SMEM] +...]
    pallas_call x0 -> x2, Pallas kernels: none -> 4.54 us  [call_solve(): pl.pallas_call(functools.partial(solve, start), in_specs=[VMEM] * 2, out_...]
    ppermute x24, starting transfers between devices: 19.9 us -> 24.4 us  [swap(): return lax.ppermute(x, axis, [(i, i ^ bit) for i in range(peers)])]
    ppermute x4, waiting for transfers between devices: 9.73 us -> 6.12 us  [swap_both(): return lax.ppermute(x, ('dom', 'sub'), pairs)]
    pallas_call x2, Pallas kernels: 16.2 us -> 15.1 us  [call_forward_adjoint(): pl.pallas_call(functools.partial(forward_adjoint, shape, relatives, sourc...]
  transfers between devices with their start and end apart: 36 -> 36, of which waited for: 22 -> 22; matrix products, arithmetic and copies ran while one was open for 0% -> 0% of each run, Pallas kernels for 0% -> 5%
where the time goes in v6:
time: 101 us; the launch traced here: 100 us
  starting transfers between devices  40.2 us (40%)
  waiting for transfers between devices  32.7 us (32%)
  Pallas kernels  23.6 us (23%)
  between operations  1.54 us (2%)
  local copies, waits for them, and re-layouts  1.13 us (1%)
    ppermute x24, starting transfers between devices, swap(): return lax.ppermute(x, axis, [(i, i ^ bit) for i in range(peers)])  24.4 us
    ppermute x24, waiting for transfers between devices, swap(): return lax.ppermute(x, axis, [(i, i ^ bit) for i in range(peers)])  18.7 us
    pallas_call x2, Pallas kernels, call_forward_adjoint(): pl.pallas_call(functools.partial(forward_adjoint, shape, relatives, sourc...  15.1 us
    ppermute x8, starting transfers between devices, pair_up(): lax.ppermute(x, 'dom', [(p, p + 2) for p in low] + [(p + 2, p) for p in l...  12.2 us
    ppermute x8, waiting for transfers between devices, pair_up(): lax.ppermute(x, 'dom', [(p, p + 2) for p in low] + [(p + 2, p) for p in l...  7.93 us
    ppermute x4, waiting for transfers between devices, swap_both(): return lax.ppermute(x, ('dom', 'sub'), pairs)  6.12 us
    pallas_call x2, Pallas kernels, call_solve(): pl.pallas_call(functools.partial(solve, start), in_specs=[VMEM] * 2, out_...  4.54 us
    ppermute x4, starting transfers between devices, swap_both(): return lax.ppermute(x, ('dom', 'sub'), pairs)  3.61 us
  transfers between devices with their start and end apart: 36, of which 22 were waited for; matrix products, arithmetic and copies ran while one was open for 0% of the time, Pallas kernels for 5%

profile of v6, /device:TPU:0, one launch (start us, length us, event | category | flops | bytes accessed | tf_op | source)
XLA Modules:
  0.0 100.2 jit_solution(2530599832225082672)
XLA Ops:
  1.3 0.1 pad_add_fusion.1
  1.4 0.9 pad_add_fusion.facts
  2.2 1.1 %copy-done.2 = bf16[12,64,128]{2,1,0:T(8,128)(2,1)S(1)} copy-done((bf16[12,64,128]{2,1,0:T(8,128)(2,1)S(1)}, bf16[12,64,128]{2,1,0:T(8,128)(2,1)}, u32[]{:S(2)}) %copy-start.2) | copy-done | bytes 196632
  3.3 0.8 prepare.1
  4.1 0.5 collective-permute-start
  4.7 2.6 %collective-permute-start.1 = (bf16[4,64,128]{2,1,0:T(8,128)(2,1)S(1)}, bf16[4,64,128]{2,1,0:T(8,128)(2,1)S(1)}, u32[]{:S(2)}, u32[]{:S(2)}) collective-permute-start(bf16[4,64,128]{2,1,0:T(8,128)(2,1)S(1)} %get-tuple-element.40), channel_id=1, source_target_pairs={{0,8},{4,12},{16,24},{20,28},{8,0},{12,4},{24,16},{28,20},{1,9},{5... | collective-permute-start | bytes 196616 | tf_op jit(solution)/shard_map/ppermute | solution.py:41
  7.3 0.7 collective-permute-start.4
  8.0 2.0 %collective-permute-done.1.refs_1_.first.refs_0_ = bf16[4,64,128]{2,1,0:T(8,128)(2,1)S(1)} collective-permute-done((bf16[4,64,128]{2,1,0:T(8,128)(2,1)S(1)}, bf16[4,64,128]{2,1,0:T(8,128)(2,1)S(1)}, u32[]{:S(2)}, u32[]{:S(2)}) %collective-permute-start.1) | collective-permute-done | bytes 65568 | tf_op jit(solution)/shard_map/ppermute | solution.py:41
  10.0 1.8 %collective-permute-start.2 = (bf16[12,64,128]{2,1,0:T(8,128)(2,1)S(1)}, bf16[12,64,128]{2,1,0:T(8,128)(2,1)S(1)}, u32[]{:S(2)}, u32[]{:S(2)}) collective-permute-start(bf16[12,64,128]{2,1,0:T(8,128)(2,1)S(1)} %stack.14), channel_id=1, source_target_pairs={{0,2},{1,3},{2,0},{3,1},{4,6},{5,7},{6,4},{7,5},{8,10},{9,11},{10,... | collective-permute-start | bytes 589832 | tf_op jit(solution)/shard_map/ppermute | solution.py:29
  11.8 1.6 %collective-permute-start.5 = (bf16[4,64,128]{2,1,0:T(8,128)(2,1)S(1)}, bf16[4,64,128]{2,1,0:T(8,128)(2,1)S(1)}, u32[]{:S(2)}, u32[]{:S(2)}) collective-permute-start(bf16[4,64,128]{2,1,0:T(8,128)(2,1)S(1)} %pass_on.2), channel_id=1, source_target_pairs={{0,4},{4,0},{8,12},{12,8},{16,20},{20,16},{24,28},{28,24},{1,5},{5... | collective-permute-start | bytes 196616 | tf_op jit(solution)/shard_map/ppermute | solution.py:29
  13.4 0.3 collective-permute-start.6
  13.7 1.8 %collective-permute-start.7 = (bf16[4,64,128]{2,1,0:T(8,128)(2,1)S(1)}, bf16[4,64,128]{2,1,0:T(8,128)(2,1)S(1)}, u32[]{:S(2)}, u32[]{:S(2)}) collective-permute-start(bf16[4,64,128]{2,1,0:T(8,128)(2,1)S(1)} %stack.15.refs_1_.refs_5_), channel_id=1, source_target_pairs={{0,2},{1,3},{2,0},{3,1},{4,6},{5,7},{6,4},{7,5},{8,10},{9,11},{10,... | collective-permute-start | bytes 196616 | tf_op jit(solution)/shard_map/ppermute | solution.py:29
  15.4 1.0 collective-permute-done.5.refs_0_.refs_4_
  16.4 2.2 %collective-permute-done.6.refs_2_.refs_6_ = bf16[4,64,128]{2,1,0:T(8,128)(2,1)S(1)} collective-permute-done((bf16[4,64,128]{2,1,0:T(8,128)(2,1)S(1)}, bf16[4,64,128]{2,1,0:T(8,128)(2,1)S(1)}, u32[]{:S(2)}, u32[]{:S(2)}) %collective-permute-start.6) | collective-permute-done | bytes 65568 | tf_op jit(solution)/shard_map/ppermute | solution.py:36
  18.6 0.9 collective-permute-done.7.refs_3_.refs_7_
  19.7 0.5 collective-permute-start.3
  20.1 1.3 %collective-permute-done.3.refs_3_ = bf16[12,64,128]{2,1,0:T(8,128)(2,1)S(1)} collective-permute-done((bf16[12,64,128]{2,1,0:T(8,128)(2,1)S(1)}, bf16[12,64,128]{2,1,0:T(8,128)(2,1)S(1)}, u32[]{:S(2)}, u32[]{:S(2)}) %collective-permute-start.3) | collective-permute-done | bytes 196640 | tf_op jit(solution)/shard_map/ppermute | solution.py:29
  21.5 7.6 %forward_adjoint.2 = (f32[40,64,128]{2,1,0:T(8,128)S(1)}, f32[40,64,128]{2,1,0:T(8,128)S(1)}, f32[64,128]{1,0:T(8,128)S(1)}) custom-call(s32[5,4]{1,0:T(8,128)S(1)} %pad_add_fusion.facts, s32[12,27]{1,0:T(8,128)S(1)} %copy-done, bf16[12,27,128,128]{3,2,1,0:T(8,128)(2,1)S(1)} %bitcast.8, f32[12,128]{1,0:T(8,128)S(1)} %copy-done.1, ...), custom_call_target="tpu_custom_call" | custom-call | flops 1358954496 | bytes 10616832 | tf_op jit(solution)/shard_map/forward_adjoint/pallas_call | solution.py:267
  29.1 3.5 %collective-permute-start.10 = (f32[64,128]{1,0:T(8,128)S(1)}, f32[64,128]{1,0:T(8,128)S(1)}, u32[]{:S(2)}, u32[]{:S(2)}) collective-permute-start(f32[64,128]{1,0:T(8,128)S(1)} %get-tuple-element.45), channel_id=1, source_target_pairs={{0,16},{4,20},{8,24},{12,28},{16,0},{20,4},{24,8},{28,12},{1,17},{... | collective-permute-start | bytes 98312 | tf_op jit(solution)/shard_map/ppermute | solution.py:29
  32.6 2.0 %collective-permute-done.10 = f32[64,128]{1,0:T(8,128)S(1)} collective-permute-done((f32[64,128]{1,0:T(8,128)S(1)}, f32[64,128]{1,0:T(8,128)S(1)}, u32[]{:S(2)}, u32[]{:S(2)}) %collective-permute-start.10) | collective-permute-done | bytes 32800 | tf_op jit(solution)/shard_map/ppermute | solution.py:29
  34.6 1.2 %collective-permute-done.11.there = f32[64,128]{1,0:T(8,128)S(1)} collective-permute-done((f32[64,128]{1,0:T(8,128)S(1)}, f32[64,128]{1,0:T(8,128)S(1)}, u32[]{:S(2)}, u32[]{:S(2)}) %collective-permute-start.11) | collective-permute-done | bytes 32800 | tf_op jit(solution)/shard_map/ppermute | solution.py:29
  35.9 1.8 %collective-permute-start.14 = (bf16[6,64,128]{2,1,0:T(8,128)(2,1)S(1)}, bf16[6,64,128]{2,1,0:T(8,128)(2,1)S(1)}, u32[]{:S(2)}, u32[]{:S(2)}) collective-permute-start(bf16[6,64,128]{2,1,0:T(8,128)(2,1)S(1)} %get-tuple-element.48), channel_id=1, source_target_pairs={{0,2},{1,3},{2,0},{3,1},{4,6},{5,7},{6,4},{7,5},{8,10},{9,11},{10,... | collective-permute-start | bytes 294920 | tf_op jit(solution)/shard_map/ppermute | solution.py:29
  37.7 0.6 collective-permute-start.12
  38.4 1.1 %collective-permute-start.13 = (bf16[6,64,128]{2,1,0:T(8,128)(2,1)S(1)}, bf16[6,64,128]{2,1,0:T(8,128)(2,1)S(1)}, u32[]{:S(2)}, u32[]{:S(2)}) collective-permute-start(bf16[6,64,128]{2,1,0:T(8,128)(2,1)S(1)} %get-tuple-element.47), channel_id=1, source_target_pairs={{0,6},{1,7},{2,4},{3,5},{4,2},{5,3},{6,0},{7,1},{8,14},{9,15},{10,... | collective-permute-start | bytes 294920 | tf_op jit(solution)/shard_map/ppermute | solution.py:36
  39.4 1.4 %collective-permute-done.14.far.refs_0_ = bf16[6,64,128]{2,1,0:T(8,128)(2,1)S(1)} collective-permute-done((bf16[6,64,128]{2,1,0:T(8,128)(2,1)S(1)}, bf16[6,64,128]{2,1,0:T(8,128)(2,1)S(1)}, u32[]{:S(2)}, u32[]{:S(2)}) %collective-permute-start.14) | collective-permute-done | bytes 98336 | tf_op jit(solution)/shard_map/ppermute | solution.py:29
  40.8 0.1 join.2
  40.9 1.8 %collective-permute-start.16 = (bf16[12,64,128]{2,1,0:T(8,128)(2,1)S(1)}, bf16[12,64,128]{2,1,0:T(8,128)(2,1)S(1)}, u32[]{:S(2)}, u32[]{:S(2)}) collective-permute-start(bf16[12,64,128]{2,1,0:T(8,128)(2,1)S(1)} %get-tuple-element.53), channel_id=1, source_target_pairs={{0,2},{1,3},{2,0},{3,1},{4,6},{5,7},{6,4},{7,5},{8,10},{9,11},{10,... | collective-permute-start | bytes 589832 | tf_op jit(solution)/shard_map/ppermute | solution.py:29
  42.7 0.6 collective-permute-done.12.flip
  43.4 1.0 collective-permute-done.13.flip_far
  44.4 2.6 %collective-permute-start.15 = (bf16[6,64,128]{2,1,0:T(8,128)(2,1)S(1)}, bf16[6,64,128]{2,1,0:T(8,128)(2,1)S(1)}, u32[]{:S(2)}, u32[]{:S(2)}) collective-permute-start(bf16[6,64,128]{2,1,0:T(8,128)(2,1)S(1)} %get-tuple-element.50.sent), channel_id=1, source_target_pairs={{0,8},{4,12},{16,24},{20,28},{8,0},{12,4},{24,16},{28,20},{1,9},{5... | collective-permute-start | bytes 294920 | tf_op jit(solution)/shard_map/ppermute | solution.py:41
  47.0 0.7 collective-permute-start.17
  47.6 1.9 %collective-permute-done.15.got.refs_1_ = bf16[6,64,128]{2,1,0:T(8,128)(2,1)S(1)} collective-permute-done((bf16[6,64,128]{2,1,0:T(8,128)(2,1)S(1)}, bf16[6,64,128]{2,1,0:T(8,128)(2,1)S(1)}, u32[]{:S(2)}, u32[]{:S(2)}) %collective-permute-start.15) | collective-permute-done | bytes 98336 | tf_op jit(solution)/shard_map/ppermute | solution.py:41
  49.6 2.3 %solve.2 = (bf16[64,192]{1,0:T(8,128)(2,1)S(1)}, f32[64,64]{1,0:T(8,128)}) custom-call(bf16[6,64,128]{2,1,0:T(8,128)(2,1)S(1)} %get-tuple-element.50.sent, bf16[6,64,128]{2,1,0:T(8,128)(2,1)S(1)} %collective-permute-done.15.got.refs_1_), custom_call_target="tpu_custom_call" | custom-call | flops 1048576 | bytes 65536 | tf_op jit(solution)/shard_map/solve/pallas_call | solution.py:395
  51.8 1.0 project.2
  52.8 0.1 collective-permute-start.18
  52.9 2.1 %collective-permute-start.19 = (bf16[4,64,128]{2,1,0:T(8,128)(2,1)S(1)}, bf16[4,64,128]{2,1,0:T(8,128)(2,1)S(1)}, u32[]{:S(2)}, u32[]{:S(2)}) collective-permute-start(bf16[4,64,128]{2,1,0:T(8,128)(2,1)S(1)} %get-tuple-element.57), channel_id=1, source_target_pairs={{0,8},{4,12},{16,24},{20,28},{8,0},{12,4},{24,16},{28,20},{1,9},{5... | collective-permute-start | bytes 196616 | tf_op jit(solution)/shard_map/ppermute | solution.py:41
  55.0 0.7 collective-permute-start.22
  55.7 2.0 %collective-permute-done.19.refs_1_.first.refs_0_ = bf16[4,64,128]{2,1,0:T(8,128)(2,1)S(1)} collective-permute-done((bf16[4,64,128]{2,1,0:T(8,128)(2,1)S(1)}, bf16[4,64,128]{2,1,0:T(8,128)(2,1)S(1)}, u32[]{:S(2)}, u32[]{:S(2)}) %collective-permute-start.19) | collective-permute-done | bytes 65568 | tf_op jit(solution)/shard_map/ppermute | solution.py:41
  57.7 1.0 collective-permute-start.20
  58.7 1.5 %collective-permute-start.23 = (bf16[4,64,128]{2,1,0:T(8,128)(2,1)S(1)}, bf16[4,64,128]{2,1,0:T(8,128)(2,1)S(1)}, u32[]{:S(2)}, u32[]{:S(2)}) collective-permute-start(bf16[4,64,128]{2,1,0:T(8,128)(2,1)S(1)} %pass_on.3), channel_id=1, source_target_pairs={{0,4},{4,0},{8,12},{12,8},{16,20},{20,16},{24,28},{28,24},{1,5},{5... | collective-permute-start | bytes 196616 | tf_op jit(solution)/shard_map/ppermute | solution.py:29
  60.2 1.1 %collective-permute-start.24 = (bf16[4,64,128]{2,1,0:T(8,128)(2,1)S(1)}, bf16[4,64,128]{2,1,0:T(8,128)(2,1)S(1)}, u32[]{:S(2)}, u32[]{:S(2)}) collective-permute-start(bf16[4,64,128]{2,1,0:T(8,128)(2,1)S(1)} %pass_on.3), channel_id=1, source_target_pairs={{0,6},{1,7},{2,4},{3,5},{4,2},{5,3},{6,0},{7,1},{8,14},{9,15},{10,... | collective-permute-start | bytes 196616 | tf_op jit(solution)/shard_map/ppermute | solution.py:36
  61.4 1.0 collective-permute-start.25
  62.3 1.3 %collective-permute-done.23.refs_0_.refs_4_ = bf16[4,64,128]{2,1,0:T(8,128)(2,1)S(1)} collective-permute-done((bf16[4,64,128]{2,1,0:T(8,128)(2,1)S(1)}, bf16[4,64,128]{2,1,0:T(8,128)(2,1)S(1)}, u32[]{:S(2)}, u32[]{:S(2)}) %collective-permute-start.23) | collective-permute-done | bytes 65568 | tf_op jit(solution)/shard_map/ppermute | solution.py:29
  63.6 1.9 %collective-permute-done.24.refs_2_.refs_6_ = bf16[4,64,128]{2,1,0:T(8,128)(2,1)S(1)} collective-permute-done((bf16[4,64,128]{2,1,0:T(8,128)(2,1)S(1)}, bf16[4,64,128]{2,1,0:T(8,128)(2,1)S(1)}, u32[]{:S(2)}, u32[]{:S(2)}) %collective-permute-start.24) | collective-permute-done | bytes 65568 | tf_op jit(solution)/shard_map/ppermute | solution.py:36
  65.4 1.8 %collective-permute-done.25.refs_3_.refs_7_ = bf16[4,64,128]{2,1,0:T(8,128)(2,1)S(1)} collective-permute-done((bf16[4,64,128]{2,1,0:T(8,128)(2,1)S(1)}, bf16[4,64,128]{2,1,0:T(8,128)(2,1)S(1)}, u32[]{:S(2)}, u32[]{:S(2)}) %collective-permute-start.25) | collective-permute-done | bytes 65568 | tf_op jit(solution)/shard_map/ppermute | solution.py:29
  67.4 0.5 collective-permute-start.21
  67.8 1.3 %collective-permute-done.21.refs_3_ = bf16[12,64,128]{2,1,0:T(8,128)(2,1)S(1)} collective-permute-done((bf16[12,64,128]{2,1,0:T(8,128)(2,1)S(1)}, bf16[12,64,128]{2,1,0:T(8,128)(2,1)S(1)}, u32[]{:S(2)}, u32[]{:S(2)}) %collective-permute-start.21) | collective-permute-done | bytes 196640 | tf_op jit(solution)/shard_map/ppermute | solution.py:29
  69.2 7.6 %forward_adjoint.3 = (f32[40,64,128]{2,1,0:T(8,128)S(1)}, f32[40,64,128]{2,1,0:T(8,128)S(1)}, f32[64,128]{1,0:T(8,128)S(1)}) custom-call(s32[5,4]{1,0:T(8,128)S(1)} %pad_add_fusion.facts, s32[12,27]{1,0:T(8,128)S(1)} %copy-done, bf16[12,27,128,128]{3,2,1,0:T(8,128)(2,1)S(1)} %bitcast.8, f32[12,128]{1,0:T(8,128)S(1)} %copy-done.1, ...), custom_call_target="tpu_custom_call" | custom-call | flops 1358954496 | bytes 10616832 | tf_op jit(solution)/shard_map/forward_adjoint/pallas_call | solution.py:267
  76.8 2.2 %collective-permute-start.28 = (f32[64,128]{1,0:T(8,128)S(1)}, f32[64,128]{1,0:T(8,128)S(1)}, u32[]{:S(2)}, u32[]{:S(2)}) collective-permute-start(f32[64,128]{1,0:T(8,128)S(1)} %get-tuple-element.62), channel_id=1, source_target_pairs={{0,16},{4,20},{8,24},{12,28},{16,0},{20,4},{24,8},{28,12},{1,17},{... | collective-permute-start | bytes 98312 | tf_op jit(solution)/shard_map/ppermute | solution.py:29
  79.0 2.7 %collective-permute-done.28 = f32[64,128]{1,0:T(8,128)S(1)} collective-permute-done((f32[64,128]{1,0:T(8,128)S(1)}, f32[64,128]{1,0:T(8,128)S(1)}, u32[]{:S(2)}, u32[]{:S(2)}) %collective-permute-start.28) | collective-permute-done | bytes 32800 | tf_op jit(solution)/shard_map/ppermute | solution.py:29
  81.7 1.2 %collective-permute-done.29.there = f32[64,128]{1,0:T(8,128)S(1)} collective-permute-done((f32[64,128]{1,0:T(8,128)S(1)}, f32[64,128]{1,0:T(8,128)S(1)}, u32[]{:S(2)}, u32[]{:S(2)}) %collective-permute-start.29) | collective-permute-done | bytes 32800 | tf_op jit(solution)/shard_map/ppermute | solution.py:29
  82.9 1.6 %collective-permute-start.32 = (bf16[6,64,128]{2,1,0:T(8,128)(2,1)S(1)}, bf16[6,64,128]{2,1,0:T(8,128)(2,1)S(1)}, u32[]{:S(2)}, u32[]{:S(2)}) collective-permute-start(bf16[6,64,128]{2,1,0:T(8,128)(2,1)S(1)} %get-tuple-element.65), channel_id=1, source_target_pairs={{0,2},{1,3},{2,0},{3,1},{4,6},{5,7},{6,4},{7,5},{8,10},{9,11},{10,... | collective-permute-start | bytes 294920 | tf_op jit(solution)/shard_map/ppermute | solution.py:29
  84.6 0.8 collective-permute-start.30
  85.4 1.1 %collective-permute-start.31 = (bf16[6,64,128]{2,1,0:T(8,128)(2,1)S(1)}, bf16[6,64,128]{2,1,0:T(8,128)(2,1)S(1)}, u32[]{:S(2)}, u32[]{:S(2)}) collective-permute-start(bf16[6,64,128]{2,1,0:T(8,128)(2,1)S(1)} %get-tuple-element.64), channel_id=1, source_target_pairs={{0,6},{1,7},{2,4},{3,5},{4,2},{5,3},{6,0},{7,1},{8,14},{9,15},{10,... | collective-permute-start | bytes 294920 | tf_op jit(solution)/shard_map/ppermute | solution.py:36
  86.5 1.4 %collective-permute-done.32.far.refs_0_ = bf16[6,64,128]{2,1,0:T(8,128)(2,1)S(1)} collective-permute-done((bf16[6,64,128]{2,1,0:T(8,128)(2,1)S(1)}, bf16[6,64,128]{2,1,0:T(8,128)(2,1)S(1)}, u32[]{:S(2)}, u32[]{:S(2)}) %collective-permute-start.32) | collective-permute-done | bytes 98336 | tf_op jit(solution)/shard_map/ppermute | solution.py:29
  87.9 0.1 join.3
  88.0 1.6 %collective-permute-start.34 = (bf16[12,64,128]{2,1,0:T(8,128)(2,1)S(1)}, bf16[12,64,128]{2,1,0:T(8,128)(2,1)S(1)}, u32[]{:S(2)}, u32[]{:S(2)}) collective-permute-start(bf16[12,64,128]{2,1,0:T(8,128)(2,1)S(1)} %get-tuple-element.70), channel_id=1, source_target_pairs={{0,2},{1,3},{2,0},{3,1},{4,6},{5,7},{6,4},{7,5},{8,10},{9,11},{10,... | collective-permute-start | bytes 589832 | tf_op jit(solution)/shard_map/ppermute | solution.py:29
  89.6 0.6 collective-permute-done.30.flip
  90.2 1.1 %collective-permute-done.31.flip_far = bf16[6,64,128]{2,1,0:T(8,128)(2,1)S(1)} collective-permute-done((bf16[6,64,128]{2,1,0:T(8,128)(2,1)S(1)}, bf16[6,64,128]{2,1,0:T(8,128)(2,1)S(1)}, u32[]{:S(2)}, u32[]{:S(2)}) %collective-permute-start.31) | collective-permute-done | bytes 98336 | tf_op jit(solution)/shard_map/ppermute | solution.py:36
  91.4 2.2 %collective-permute-start.33 = (bf16[6,64,128]{2,1,0:T(8,128)(2,1)S(1)}, bf16[6,64,128]{2,1,0:T(8,128)(2,1)S(1)}, u32[]{:S(2)}, u32[]{:S(2)}) collective-permute-start(bf16[6,64,128]{2,1,0:T(8,128)(2,1)S(1)} %get-tuple-element.67.sent), channel_id=1, source_target_pairs={{0,8},{4,12},{16,24},{20,28},{8,0},{12,4},{24,16},{28,20},{1,9},{5... | collective-permute-start | bytes 294920 | tf_op jit(solution)/shard_map/ppermute | solution.py:41
  93.6 0.7 collective-permute-start.35
  94.3 1.9 %collective-permute-done.33.got.refs_1_ = bf16[6,64,128]{2,1,0:T(8,128)(2,1)S(1)} collective-permute-done((bf16[6,64,128]{2,1,0:T(8,128)(2,1)S(1)}, bf16[6,64,128]{2,1,0:T(8,128)(2,1)S(1)}, u32[]{:S(2)}, u32[]{:S(2)}) %collective-permute-start.33) | collective-permute-done | bytes 98336 | tf_op jit(solution)/shard_map/ppermute | solution.py:41
  96.2 2.3 %solve.3 = (bf16[64,192]{1,0:T(8,128)(2,1)S(1)}, f32[64,64]{1,0:T(8,128)}) custom-call(bf16[6,64,128]{2,1,0:T(8,128)(2,1)S(1)} %get-tuple-element.67.sent, bf16[6,64,128]{2,1,0:T(8,128)(2,1)S(1)} %collective-permute-done.33.got.refs_1_), custom_call_target="tpu_custom_call" | custom-call | flops 1048576 | bytes 65536 | tf_op jit(solution)/shard_map/solve/pallas_call | solution.py:395
  98.5 1.7 %project.3 = f32[12,64,128]{2,1,0:T(8,128)} custom-call(s32[5,4]{1,0:T(8,128)S(1)} %pad_add_fusion.facts, bf16[64,192]{1,0:T(8,128)(2,1)S(1)} %get-tuple-element.68.coupling, bf16[12,64,128]{2,1,0:T(8,128)(2,1)S(1)} %get-tuple-element.56.refs_0_.basis, f32[12,64,128]{2,1,0:T(8,128)S(1)} %get-tuple-element.69.near_own, ...), custom_call_target="tpu_custom_call" | custom-call | flops 37748736 | bytes 1966080 | tf_op jit(solution)/shard_map/project/pallas_call | solution.py:435
  (47 shorter events, 0.7 us)
Async XLA Ops:
  1.4 20.1 %slice-start = ((s8[10616832]{0:T(1024)(128)(4,1)}), s8[4194304]{0:T(1024)(128)(4,1)S(1)}, s32[]{:S(2)}) async-start(s8[10616832]{0:T(1024)(128)(4,1)} %bitcast.7), calls=%async_computation | async-start | bytes 8388608
  2.2 1.1 %copy-start.2 = (bf16[12,64,128]{2,1,0:T(8,128)(2,1)S(1)}, bf16[12,64,128]{2,1,0:T(8,128)(2,1)}, u32[]{:S(2)}) copy-start(bf16[12,64,128]{2,1,0:T(8,128)(2,1)} %directions.1) | copy-start | bytes 589828
  3.3 18.1 %slice-start.1 = ((s8[10616832]{0:T(1024)(128)(4,1)}), s8[4194304]{0:T(1024)(128)(4,1)S(1)}, s32[]{:S(2)}) async-start(s8[10616832]{0:T(1024)(128)(4,1)} %bitcast.7), calls=%async_computation.1 | async-start | bytes 8388608
  3.3 18.1 %slice-start.2 = ((s8[10616832]{0:T(1024)(128)(4,1)}), s8[2228224]{0:T(1024)(128)(4,1)S(1)}, s32[]{:S(2)}) async-start(s8[10616832]{0:T(1024)(128)(4,1)} %bitcast.7), calls=%async_computation.2 | async-start | bytes 4456448
  4.1 17.4 %copy-start = (s32[12,27]{1,0:T(8,128)S(1)}, s32[12,27]{1,0:T(8,128)}, u32[]{:S(2)}) copy-start(s32[12,27]{1,0:T(8,128)} %cols.3) | copy-start | bytes 3892
  4.1 17.4 %copy-start.1 = (f32[12,128]{1,0:T(8,128)S(1)}, f32[12,128]{1,0:T(8,128)}, u32[]{:S(2)}) copy-start(f32[12,128]{1,0:T(8,128)} %friction.3) | copy-start | bytes 18436
  4.1 9.5 %collective-permute-start = (bf16[12,64,128]{2,1,0:T(8,128)(2,1)S(1)}, bf16[12,64,128]{2,1,0:T(8,128)(2,1)S(1)}, u32[]{:S(2)}, u32[]{:S(2)}) collective-permute-start(bf16[12,64,128]{2,1,0:T(8,128)(2,1)S(1)} %get-tuple-element.39.refs_0_.basis), channel_id=1, source_target_pairs={{0,1},{1,0},{2,3},{3,2},{4,5},{5,4},{6,7},{7,6},{8,9},{9,8},{10,11... | collective-permute-start | bytes 589832 | tf_op jit(solution)/shard_map/ppermute | solution.py:29
  4.7 5.3 %collective-permute-start.1 = (bf16[4,64,128]{2,1,0:T(8,128)(2,1)S(1)}, bf16[4,64,128]{2,1,0:T(8,128)(2,1)S(1)}, u32[]{:S(2)}, u32[]{:S(2)}) collective-permute-start(bf16[4,64,128]{2,1,0:T(8,128)(2,1)S(1)} %get-tuple-element.40), channel_id=1, source_target_pairs={{0,8},{4,12},{16,24},{20,28},{8,0},{12,4},{24,16},{28,20},{1,9},{5... | collective-permute-start | bytes 196616 | tf_op jit(solution)/shard_map/ppermute | solution.py:41
  7.3 4.5 %collective-permute-start.4 = (bf16[4,64,128]{2,1,0:T(8,128)(2,1)S(1)}, bf16[4,64,128]{2,1,0:T(8,128)(2,1)S(1)}, u32[]{:S(2)}, u32[]{:S(2)}) collective-permute-start(bf16[4,64,128]{2,1,0:T(8,128)(2,1)S(1)} %get-tuple-element.42), channel_id=1, source_target_pairs={{8,16},{12,20},{16,8},{20,12},{9,17},{13,21},{17,9},{21,13},{10,18... | collective-permute-start | bytes 196616 | tf_op jit(solution)/shard_map/ppermute | solution.py:41
  10.0 9.6 %collective-permute-start.2 = (bf16[12,64,128]{2,1,0:T(8,128)(2,1)S(1)}, bf16[12,64,128]{2,1,0:T(8,128)(2,1)S(1)}, u32[]{:S(2)}, u32[]{:S(2)}) collective-permute-start(bf16[12,64,128]{2,1,0:T(8,128)(2,1)S(1)} %stack.14), channel_id=1, source_target_pairs={{0,2},{1,3},{2,0},{3,1},{4,6},{5,7},{6,4},{7,5},{8,10},{9,11},{10,... | collective-permute-start | bytes 589832 | tf_op jit(solution)/shard_map/ppermute | solution.py:29
  11.8 4.6 %collective-permute-start.5 = (bf16[4,64,128]{2,1,0:T(8,128)(2,1)S(1)}, bf16[4,64,128]{2,1,0:T(8,128)(2,1)S(1)}, u32[]{:S(2)}, u32[]{:S(2)}) collective-permute-start(bf16[4,64,128]{2,1,0:T(8,128)(2,1)S(1)} %pass_on.2), channel_id=1, source_target_pairs={{0,4},{4,0},{8,12},{12,8},{16,20},{20,16},{24,28},{28,24},{1,5},{5... | collective-permute-start | bytes 196616 | tf_op jit(solution)/shard_map/ppermute | solution.py:29
  13.4 5.3 %collective-permute-start.6 = (bf16[4,64,128]{2,1,0:T(8,128)(2,1)S(1)}, bf16[4,64,128]{2,1,0:T(8,128)(2,1)S(1)}, u32[]{:S(2)}, u32[]{:S(2)}) collective-permute-start(bf16[4,64,128]{2,1,0:T(8,128)(2,1)S(1)} %pass_on.2), channel_id=1, source_target_pairs={{0,6},{1,7},{2,4},{3,5},{4,2},{5,3},{6,0},{7,1},{8,14},{9,15},{10,... | collective-permute-start | bytes 196616 | tf_op jit(solution)/shard_map/ppermute | solution.py:36
  13.7 5.9 %collective-permute-start.7 = (bf16[4,64,128]{2,1,0:T(8,128)(2,1)S(1)}, bf16[4,64,128]{2,1,0:T(8,128)(2,1)S(1)}, u32[]{:S(2)}, u32[]{:S(2)}) collective-permute-start(bf16[4,64,128]{2,1,0:T(8,128)(2,1)S(1)} %stack.15.refs_1_.refs_5_), channel_id=1, source_target_pairs={{0,2},{1,3},{2,0},{3,1},{4,6},{5,7},{6,4},{7,5},{8,10},{9,11},{10,... | collective-permute-start | bytes 196616 | tf_op jit(solution)/shard_map/ppermute | solution.py:29
  19.6 1.9 %collective-permute-start.8 = (bf16[16,64,128]{2,1,0:T(8,128)(2,1)S(1)}, bf16[16,64,128]{2,1,0:T(8,128)(2,1)S(1)}, u32[]{:S(2)}, u32[]{:S(2)}) collective-permute-start(bf16[16,64,128]{2,1,0:T(8,128)(2,1)S(1)} %stack.16), channel_id=1, source_target_pairs={{0,1},{1,0},{2,3},{3,2},{4,5},{5,4},{6,7},{7,6},{8,9},{9,8},{10,11... | collective-permute-start | bytes 786440 | tf_op jit(solution)/shard_map/ppermute | solution.py:29
  19.7 1.8 %collective-permute-start.3 = (bf16[12,64,128]{2,1,0:T(8,128)(2,1)S(1)}, bf16[12,64,128]{2,1,0:T(8,128)(2,1)S(1)}, u32[]{:S(2)}, u32[]{:S(2)}) collective-permute-start(bf16[12,64,128]{2,1,0:T(8,128)(2,1)S(1)} %collective-permute-done.2.refs_2_), channel_id=1, source_target_pairs={{0,1},{1,0},{2,3},{3,2},{4,5},{5,4},{6,7},{7,6},{8,9},{9,8},{10,11... | collective-permute-start | bytes 589832 | tf_op jit(solution)/shard_map/ppermute | solution.py:29
  29.1 6.7 %collective-permute-start.9 = (f32[40,64,128]{2,1,0:T(8,128)S(1)}, f32[40,64,128]{2,1,0:T(8,128)S(1)}, u32[]{:S(2)}, u32[]{:S(2)}) collective-permute-start(f32[40,64,128]{2,1,0:T(8,128)S(1)} %get-tuple-element.44), channel_id=1, source_target_pairs={{0,1},{1,0},{2,3},{3,2},{4,5},{5,4},{6,7},{7,6},{8,9},{9,8},{10,11... | collective-permute-start | bytes 3932168 | tf_op jit(solution)/shard_map/ppermute | solution.py:29
  29.1 5.4 %collective-permute-start.10 = (f32[64,128]{1,0:T(8,128)S(1)}, f32[64,128]{1,0:T(8,128)S(1)}, u32[]{:S(2)}, u32[]{:S(2)}) collective-permute-start(f32[64,128]{1,0:T(8,128)S(1)} %get-tuple-element.45), channel_id=1, source_target_pairs={{0,16},{4,20},{8,24},{12,28},{16,0},{20,4},{24,8},{28,12},{1,17},{... | collective-permute-start | bytes 98312 | tf_op jit(solution)/shard_map/ppermute | solution.py:29
  34.6 1.2 %collective-permute-start.11 = (f32[64,128]{1,0:T(8,128)S(1)}, f32[64,128]{1,0:T(8,128)S(1)}, u32[]{:S(2)}, u32[]{:S(2)}) collective-permute-start(f32[64,128]{1,0:T(8,128)S(1)} %add.8.here), channel_id=1, source_target_pairs={{0,1},{1,0},{2,3},{3,2},{4,5},{5,4},{6,7},{7,6},{8,9},{9,8},{10,11... | collective-permute-start | bytes 98312 | tf_op jit(solution)/shard_map/ppermute | solution.py:29
  35.9 5.0 %collective-permute-start.14 = (bf16[6,64,128]{2,1,0:T(8,128)(2,1)S(1)}, bf16[6,64,128]{2,1,0:T(8,128)(2,1)S(1)}, u32[]{:S(2)}, u32[]{:S(2)}) collective-permute-start(bf16[6,64,128]{2,1,0:T(8,128)(2,1)S(1)} %get-tuple-element.48), channel_id=1, source_target_pairs={{0,2},{1,3},{2,0},{3,1},{4,6},{5,7},{6,4},{7,5},{8,10},{9,11},{10,... | collective-permute-start | bytes 294920 | tf_op jit(solution)/shard_map/ppermute | solution.py:29
  37.7 5.6 %collective-permute-start.12 = (bf16[6,64,128]{2,1,0:T(8,128)(2,1)S(1)}, bf16[6,64,128]{2,1,0:T(8,128)(2,1)S(1)}, u32[]{:S(2)}, u32[]{:S(2)}) collective-permute-start(bf16[6,64,128]{2,1,0:T(8,128)(2,1)S(1)} %get-tuple-element.46.sent), channel_id=1, source_target_pairs={{0,4},{4,0},{8,12},{12,8},{16,20},{20,16},{24,28},{28,24},{1,5},{5... | collective-permute-start | bytes 294920 | tf_op jit(solution)/shard_map/ppermute | solution.py:29
  38.4 5.9 %collective-permute-start.13 = (bf16[6,64,128]{2,1,0:T(8,128)(2,1)S(1)}, bf16[6,64,128]{2,1,0:T(8,128)(2,1)S(1)}, u32[]{:S(2)}, u32[]{:S(2)}) collective-permute-start(bf16[6,64,128]{2,1,0:T(8,128)(2,1)S(1)} %get-tuple-element.47), channel_id=1, source_target_pairs={{0,6},{1,7},{2,4},{3,5},{4,2},{5,3},{6,0},{7,1},{8,14},{9,15},{10,... | collective-permute-start | bytes 294920 | tf_op jit(solution)/shard_map/ppermute | solution.py:36
  40.9 10.9 %collective-permute-start.16 = (bf16[12,64,128]{2,1,0:T(8,128)(2,1)S(1)}, bf16[12,64,128]{2,1,0:T(8,128)(2,1)S(1)}, u32[]{:S(2)}, u32[]{:S(2)}) collective-permute-start(bf16[12,64,128]{2,1,0:T(8,128)(2,1)S(1)} %get-tuple-element.53), channel_id=1, source_target_pairs={{0,2},{1,3},{2,0},{3,1},{4,6},{5,7},{6,4},{7,5},{8,10},{9,11},{10,... | collective-permute-start | bytes 589832 | tf_op jit(solution)/shard_map/ppermute | solution.py:29
  44.4 5.2 %collective-permute-start.15 = (bf16[6,64,128]{2,1,0:T(8,128)(2,1)S(1)}, bf16[6,64,128]{2,1,0:T(8,128)(2,1)S(1)}, u32[]{:S(2)}, u32[]{:S(2)}) collective-permute-start(bf16[6,64,128]{2,1,0:T(8,128)(2,1)S(1)} %get-tuple-element.50.sent), channel_id=1, source_target_pairs={{0,8},{4,12},{16,24},{20,28},{8,0},{12,4},{24,16},{28,20},{1,9},{5... | collective-permute-start | bytes 294920 | tf_op jit(solution)/shard_map/ppermute | solution.py:41
  47.0 4.9 %collective-permute-start.17 = (bf16[4,64,128]{2,1,0:T(8,128)(2,1)S(1)}, bf16[4,64,128]{2,1,0:T(8,128)(2,1)S(1)}, u32[]{:S(2)}, u32[]{:S(2)}) collective-permute-start(bf16[4,64,128]{2,1,0:T(8,128)(2,1)S(1)} %get-tuple-element.55), channel_id=1, source_target_pairs={{8,16},{12,20},{16,8},{20,12},{9,17},{13,21},{17,9},{21,13},{10,18... | collective-permute-start | bytes 196616 | tf_op jit(solution)/shard_map/ppermute | solution.py:41
  52.8 8.5 %collective-permute-start.18 = (bf16[12,64,128]{2,1,0:T(8,128)(2,1)S(1)}, bf16[12,64,128]{2,1,0:T(8,128)(2,1)S(1)}, u32[]{:S(2)}, u32[]{:S(2)}) collective-permute-start(bf16[12,64,128]{2,1,0:T(8,128)(2,1)S(1)} %get-tuple-element.56.refs_0_.basis), channel_id=1, source_target_pairs={{0,1},{1,0},{2,3},{3,2},{4,5},{5,4},{6,7},{7,6},{8,9},{9,8},{10,11... | collective-permute-start | bytes 589832 | tf_op jit(solution)/shard_map/ppermute | solution.py:29
  52.9 4.8 %collective-permute-start.19 = (bf16[4,64,128]{2,1,0:T(8,128)(2,1)S(1)}, bf16[4,64,128]{2,1,0:T(8,128)(2,1)S(1)}, u32[]{:S(2)}, u32[]{:S(2)}) collective-permute-start(bf16[4,64,128]{2,1,0:T(8,128)(2,1)S(1)} %get-tuple-element.57), channel_id=1, source_target_pairs={{0,8},{4,12},{16,24},{20,28},{8,0},{12,4},{24,16},{28,20},{1,9},{5... | collective-permute-start | bytes 196616 | tf_op jit(solution)/shard_map/ppermute | solution.py:41
  55.0 3.7 %collective-permute-start.22 = (bf16[4,64,128]{2,1,0:T(8,128)(2,1)S(1)}, bf16[4,64,128]{2,1,0:T(8,128)(2,1)S(1)}, u32[]{:S(2)}, u32[]{:S(2)}) collective-permute-start(bf16[4,64,128]{2,1,0:T(8,128)(2,1)S(1)} %get-tuple-element.59), channel_id=1, source_target_pairs={{8,16},{12,20},{16,8},{20,12},{9,17},{13,21},{17,9},{21,13},{10,18... | collective-permute-start | bytes 196616 | tf_op jit(solution)/shard_map/ppermute | solution.py:41
  57.7 9.6 %collective-permute-start.20 = (bf16[12,64,128]{2,1,0:T(8,128)(2,1)S(1)}, bf16[12,64,128]{2,1,0:T(8,128)(2,1)S(1)}, u32[]{:S(2)}, u32[]{:S(2)}) collective-permute-start(bf16[12,64,128]{2,1,0:T(8,128)(2,1)S(1)} %stack.17), channel_id=1, source_target_pairs={{0,2},{1,3},{2,0},{3,1},{4,6},{5,7},{6,4},{7,5},{8,10},{9,11},{10,... | collective-permute-start | bytes 589832 | tf_op jit(solution)/shard_map/ppermute | solution.py:29
  58.7 4.9 %collective-permute-start.23 = (bf16[4,64,128]{2,1,0:T(8,128)(2,1)S(1)}, bf16[4,64,128]{2,1,0:T(8,128)(2,1)S(1)}, u32[]{:S(2)}, u32[]{:S(2)}) collective-permute-start(bf16[4,64,128]{2,1,0:T(8,128)(2,1)S(1)} %pass_on.3), channel_id=1, source_target_pairs={{0,4},{4,0},{8,12},{12,8},{16,20},{20,16},{24,28},{28,24},{1,5},{5... | collective-permute-start | bytes 196616 | tf_op jit(solution)/shard_map/ppermute | solution.py:29
  60.2 5.2 %collective-permute-start.24 = (bf16[4,64,128]{2,1,0:T(8,128)(2,1)S(1)}, bf16[4,64,128]{2,1,0:T(8,128)(2,1)S(1)}, u32[]{:S(2)}, u32[]{:S(2)}) collective-permute-start(bf16[4,64,128]{2,1,0:T(8,128)(2,1)S(1)} %pass_on.3), channel_id=1, source_target_pairs={{0,6},{1,7},{2,4},{3,5},{4,2},{5,3},{6,0},{7,1},{8,14},{9,15},{10,... | collective-permute-start | bytes 196616 | tf_op jit(solution)/shard_map/ppermute | solution.py:36
  61.4 5.9 %collective-permute-start.25 = (bf16[4,64,128]{2,1,0:T(8,128)(2,1)S(1)}, bf16[4,64,128]{2,1,0:T(8,128)(2,1)S(1)}, u32[]{:S(2)}, u32[]{:S(2)}) collective-permute-start(bf16[4,64,128]{2,1,0:T(8,128)(2,1)S(1)} %stack.18.refs_1_.refs_5_), channel_id=1, source_target_pairs={{0,2},{1,3},{2,0},{3,1},{4,6},{5,7},{6,4},{7,5},{8,10},{9,11},{10,... | collective-permute-start | bytes 196616 | tf_op jit(solution)/shard_map/ppermute | solution.py:29
  67.3 1.9 %collective-permute-start.26 = (bf16[16,64,128]{2,1,0:T(8,128)(2,1)S(1)}, bf16[16,64,128]{2,1,0:T(8,128)(2,1)S(1)}, u32[]{:S(2)}, u32[]{:S(2)}) collective-permute-start(bf16[16,64,128]{2,1,0:T(8,128)(2,1)S(1)} %stack.19), channel_id=1, source_target_pairs={{0,1},{1,0},{2,3},{3,2},{4,5},{5,4},{6,7},{7,6},{8,9},{9,8},{10,11... | collective-permute-start | bytes 786440 | tf_op jit(solution)/shard_map/ppermute | solution.py:29
  67.4 1.8 %collective-permute-start.21 = (bf16[12,64,128]{2,1,0:T(8,128)(2,1)S(1)}, bf16[12,64,128]{2,1,0:T(8,128)(2,1)S(1)}, u32[]{:S(2)}, u32[]{:S(2)}) collective-permute-start(bf16[12,64,128]{2,1,0:T(8,128)(2,1)S(1)} %collective-permute-done.20.refs_2_), channel_id=1, source_target_pairs={{0,1},{1,0},{2,3},{3,2},{4,5},{5,4},{6,7},{7,6},{8,9},{9,8},{10,11... | collective-permute-start | bytes 589832 | tf_op jit(solution)/shard_map/ppermute | solution.py:29
  76.7 6.2 %collective-permute-start.27 = (f32[40,64,128]{2,1,0:T(8,128)S(1)}, f32[40,64,128]{2,1,0:T(8,128)S(1)}, u32[]{:S(2)}, u32[]{:S(2)}) collective-permute-start(f32[40,64,128]{2,1,0:T(8,128)S(1)} %get-tuple-element.61), channel_id=1, source_target_pairs={{0,1},{1,0},{2,3},{3,2},{4,5},{5,4},{6,7},{7,6},{8,9},{9,8},{10,11... | collective-permute-start | bytes 3932168 | tf_op jit(solution)/shard_map/ppermute | solution.py:29
  76.8 4.9 %collective-permute-start.28 = (f32[64,128]{1,0:T(8,128)S(1)}, f32[64,128]{1,0:T(8,128)S(1)}, u32[]{:S(2)}, u32[]{:S(2)}) collective-permute-start(f32[64,128]{1,0:T(8,128)S(1)} %get-tuple-element.62), channel_id=1, source_target_pairs={{0,16},{4,20},{8,24},{12,28},{16,0},{20,4},{24,8},{28,12},{1,17},{... | collective-permute-start | bytes 98312 | tf_op jit(solution)/shard_map/ppermute | solution.py:29
  81.7 1.2 %collective-permute-start.29 = (f32[64,128]{1,0:T(8,128)S(1)}, f32[64,128]{1,0:T(8,128)S(1)}, u32[]{:S(2)}, u32[]{:S(2)}) collective-permute-start(f32[64,128]{1,0:T(8,128)S(1)} %add.9.here), channel_id=1, source_target_pairs={{0,1},{1,0},{2,3},{3,2},{4,5},{5,4},{6,7},{7,6},{8,9},{9,8},{10,11... | collective-permute-start | bytes 98312 | tf_op jit(solution)/shard_map/ppermute | solution.py:29
  82.9 4.9 %collective-permute-start.32 = (bf16[6,64,128]{2,1,0:T(8,128)(2,1)S(1)}, bf16[6,64,128]{2,1,0:T(8,128)(2,1)S(1)}, u32[]{:S(2)}, u32[]{:S(2)}) collective-permute-start(bf16[6,64,128]{2,1,0:T(8,128)(2,1)S(1)} %get-tuple-element.65), channel_id=1, source_target_pairs={{0,2},{1,3},{2,0},{3,1},{4,6},{5,7},{6,4},{7,5},{8,10},{9,11},{10,... | collective-permute-start | bytes 294920 | tf_op jit(solution)/shard_map/ppermute | solution.py:29
  84.6 5.6 %collective-permute-start.30 = (bf16[6,64,128]{2,1,0:T(8,128)(2,1)S(1)}, bf16[6,64,128]{2,1,0:T(8,128)(2,1)S(1)}, u32[]{:S(2)}, u32[]{:S(2)}) collective-permute-start(bf16[6,64,128]{2,1,0:T(8,128)(2,1)S(1)} %get-tuple-element.63.sent), channel_id=1, source_target_pairs={{0,4},{4,0},{8,12},{12,8},{16,20},{20,16},{24,28},{28,24},{1,5},{5... | collective-permute-start | bytes 294920 | tf_op jit(solution)/shard_map/ppermute | solution.py:29
  85.4 5.9 %collective-permute-start.31 = (bf16[6,64,128]{2,1,0:T(8,128)(2,1)S(1)}, bf16[6,64,128]{2,1,0:T(8,128)(2,1)S(1)}, u32[]{:S(2)}, u32[]{:S(2)}) collective-permute-start(bf16[6,64,128]{2,1,0:T(8,128)(2,1)S(1)} %get-tuple-element.64), channel_id=1, source_target_pairs={{0,6},{1,7},{2,4},{3,5},{4,2},{5,3},{6,0},{7,1},{8,14},{9,15},{10,... | collective-permute-start | bytes 294920 | tf_op jit(solution)/shard_map/ppermute | solution.py:36
  88.0 10.5 %collective-permute-start.34 = (bf16[12,64,128]{2,1,0:T(8,128)(2,1)S(1)}, bf16[12,64,128]{2,1,0:T(8,128)(2,1)S(1)}, u32[]{:S(2)}, u32[]{:S(2)}) collective-permute-start(bf16[12,64,128]{2,1,0:T(8,128)(2,1)S(1)} %get-tuple-element.70), channel_id=1, source_target_pairs={{0,2},{1,3},{2,0},{3,1},{4,6},{5,7},{6,4},{7,5},{8,10},{9,11},{10,... | collective-permute-start | bytes 589832 | tf_op jit(solution)/shard_map/ppermute | solution.py:29
  91.4 4.8 %collective-permute-start.33 = (bf16[6,64,128]{2,1,0:T(8,128)(2,1)S(1)}, bf16[6,64,128]{2,1,0:T(8,128)(2,1)S(1)}, u32[]{:S(2)}, u32[]{:S(2)}) collective-permute-start(bf16[6,64,128]{2,1,0:T(8,128)(2,1)S(1)} %get-tuple-element.67.sent), channel_id=1, source_target_pairs={{0,8},{4,12},{16,24},{20,28},{8,0},{12,4},{24,16},{28,20},{1,9},{5... | collective-permute-start | bytes 294920 | tf_op jit(solution)/shard_map/ppermute | solution.py:41
  93.6 4.9 %collective-permute-start.35 = (bf16[4,64,128]{2,1,0:T(8,128)(2,1)S(1)}, bf16[4,64,128]{2,1,0:T(8,128)(2,1)S(1)}, u32[]{:S(2)}, u32[]{:S(2)}) collective-permute-start(bf16[4,64,128]{2,1,0:T(8,128)(2,1)S(1)} %get-tuple-element.72), channel_id=1, source_target_pairs={{8,16},{12,20},{16,8},{20,12},{9,17},{13,21},{17,9},{21,13},{10,18... | collective-permute-start | bytes 196616 | tf_op jit(solution)/shard_map/ppermute | solution.py:41

commit v7 on v6

--- a/solution.py
+++ b/solution.py
@@ -123,7 +123,7 @@
         out_specs=[VMEM] * 5,
         out_shape=[
             jax.ShapeDtypeStruct(directions.shape, BF16),
-            jax.ShapeDtypeStruct((2, 16, directions.shape[2]), BF16),
+            jax.ShapeDtypeStruct((2,) + directions.shape[1:], BF16),
         ]
         + outgoing_shapes(shape[1], *directions.shape[1:]),
         compiler_params=SMALL,
@@ -135,7 +135,7 @@
 def pass_on(slots, ways, flip, first, second, out):
     for s in range(slots):
         out[s] = flip[s]
-        out[slots + s] = first[slots + s] * ways[0, :1] + second[slots + s] * ways[1, :1]
+        out[slots + s] = first[slots + s] * ways[0] + second[slots + s] * ways[1]
 
 
 def call_pass_on(slots, ways, flip, first, second):
@@ -300,7 +300,7 @@
     )(keep, got, *after)
 
 
-def hand_back(slots, blocks, keep, got, here, there, near_flip, far_flip, far_pairs, near_pairs):
+def hand_back(slots, blocks, keep, got, grams, near_flip, far_flip, far_pairs, near_pairs):
     pair = 2 * slots
     near = [keep[2 * blocks + i] + got[2 * blocks + i] for i in range(2 * pair)]
     far = [keep[2 * blocks + 2 * pair + i] + got[2 * blocks + 2 * pair + i] for i in range(2 * pair)]
@@ -309,22 +309,22 @@
         far_flip[i] = far[i].astype(BF16)
         far_pairs[i] = far[pair + i].astype(BF16)
         near_pairs[i] = near[pair + i]
-    for i, piece in enumerate(split_bf16(here[...] + there[...], 2)):
+    for i, piece in enumerate(split_bf16(grams[...], 2)):
         for out in (near_flip, far_flip, far_pairs):
             out[pair + i] = piece
 
 
-def call_hand_back(slots, blocks, keep, got, here, there):
+def call_hand_back(slots, blocks, keep, got, grams):
     pair, tail = 2 * slots, keep.shape[1:]
     out = jax.ShapeDtypeStruct((pair + 2,) + tail, BF16)
     return pl.pallas_call(
         functools.partial(hand_back, slots, blocks),
-        in_specs=[VMEM] * 4,
+        in_specs=[VMEM] * 3,
         out_specs=[VMEM] * 4,
         out_shape=[out, out, out, jax.ShapeDtypeStruct((pair,) + tail, F32)],
         compiler_params=SMALL,
         name="hand_back",
-    )(keep, got, here, there)
+    )(keep, got, grams)
 
 
 def pass_back(slots, ways, sent, flip, flip_far, far, near_pairs, first, second, own):
@@ -335,7 +335,7 @@
         for pairing, out in enumerate((first, second)):
             i = pairing * slots + s
             out[s] = (near_pairs[i] + far[i].astype(F32)).astype(BF16)
-            out[slots + s] = relayed * ways[pairing, :1]
+            out[slots + s] = relayed * ways[pairing]
     grams = (joined(sent, pair) + joined(far, pair)) + (joined(flip, pair) + joined(flip_far, pair))
     for i, piece in enumerate(split_bf16(grams, 2)):
         first[pair + i] = piece
@@ -383,24 +383,43 @@
     return jnp.concatenate(panels, axis=0)[:, dirs:]
 
 
-def solve(start, sent, got, coupling, cross):
-    grams = joined(sent, start) + joined(got, start)
+def sum_grams(start, sent, got, out):
+    out[...] = joined(sent, start) + joined(got, start)
+
+
+def call_sum_grams(start, sent, got):
+    return pl.pallas_call(
+        functools.partial(sum_grams, start),
+        in_specs=[VMEM] * 2,
+        out_specs=VMEM,
+        out_shape=jax.ShapeDtypeStruct(sent.shape[1:], F32),
+        compiler_params=SMALL,
+        name="sum_grams",
+    )(sent, got)
+
+
+def solve(here, there, coupling, *cross):
+    grams = here[...] + there[...]
     dirs = grams.shape[0]
     coupling[...] = jnp.concatenate(split_bf16(eliminate(grams, dirs).T, 3), axis=1)
-    cross[...] = grams[:, dirs:]
-
-
-def call_solve(start, sent, got):
-    dirs = sent.shape[1]
-    return pl.pallas_call(
-        functools.partial(solve, start),
+    for out in cross:
+        out[...] = grams[:, dirs:]
+
+
+def call_solve(last, here, there):
+    dirs = here.shape[0]
+    out_shape = [jax.ShapeDtypeStruct((dirs, 3 * dirs), BF16)]
+    if last:
+        out_shape.append(jax.ShapeDtypeStruct((dirs, dirs), F32))
+    return pl.pallas_call(
+        solve,
         in_specs=[VMEM] * 2,
-        out_specs=[VMEM] * 2,
-        out_shape=[jax.ShapeDtypeStruct((dirs, 3 * dirs), BF16), jax.ShapeDtypeStruct((dirs, dirs), F32)],
+        out_specs=[VMEM] * len(out_shape),
+        out_shape=out_shape,
         compiler_params=SMALL,
         cost_estimate=pl.CostEstimate(flops=4 * dirs**3, bytes_accessed=16 * dirs * dirs, transcendentals=dirs),
         name="solve",
-    )(sent, got)
+    )(here, there)
 
 
 def project(shape, last, facts, coupling, basis, near_own, far_own, *refs):
@@ -478,20 +497,21 @@
         )
         for bit in dom_bits[2:]:
             grams = grams + swap(grams, "dom", bit)
-        got, grams_got = swap(send, "sub", near), swap(grams, "sub", near)
-        near_flip, far_flip, far_pairs, near_pairs = call_hand_back(slots, blocks, keep, got, grams, grams_got)
+        got = swap(send, "sub", near)
+        near_flip, far_flip, far_pairs, near_pairs = call_hand_back(slots, blocks, keep, got, grams)
         flip, flip_far = swap(near_flip, "dom", dom_bits[0]), swap_both(far_flip, dom_bits[0], far)
         pairs_got = swap(far_pairs, "sub", far)
         near_own, far_own = call_join(0, blocks, keep, got, [pairs_got])
         far_own_got = swap(far_own, "sub", far)
         *back, flip = call_pass_back(slots, ways, near_flip, flip, flip_far, pairs_got, near_pairs)
         returned = [flip] + [pair_up(x, i) for i, x in enumerate(back)]
-        coupling, cross = call_solve(2 * slots, back[0], returned[1])
+        grams = call_sum_grams(2 * slots, back[0], returned[1])
         last = step == ITERS - 1
+        coupling, *cross = call_solve(last, grams, swap(grams, "sub", near))
         basis, *outgoing = call_project(
             shape, last, facts, coupling, basis, near_own, far_own_got, returned
         )
-    return (basis, cross)
+    return (basis, cross[0])
 
 
 def solution(mesh):

time: 101 us -> 99.1 us (0.981); the launches traced: 100 us -> 99.4 us
  waiting for transfers between devices: 32.7 us -> 38.8 us
  Pallas kernels: 23.6 us -> 18.7 us
  starting transfers between devices: 40.2 us -> 38.3 us
    ppermute x4, starting transfers between devices: 3.61 us -> 9.26 us  [swap_both(): return lax.ppermute(x, ('dom', 'sub'), pairs)]
    ppermute x8, starting transfers between devices: 12.2 us -> 7.34 us  [pair_up(): lax.ppermute(x, 'dom', [(p, p + 2) for p in low] + [(p + 2, p) for p in l...]
    pallas_call x2, Pallas kernels: 15.1 us -> 10.8 us  [call_forward_adjoint(): pl.pallas_call(functools.partial(forward_adjoint, shape, relatives, sourc...]
    ppermute x24, waiting for transfers between devices: 18.7 us -> 22.6 us  [swap(): return lax.ppermute(x, axis, [(i, i ^ bit) for i in range(peers)])]
    ppermute x8, waiting for transfers between devices: 7.93 us -> 11.7 us  [pair_up(): lax.ppermute(x, 'dom', [(p, p + 2) for p in low] + [(p + 2, p) for p in l...]
    ppermute x24, starting transfers between devices: 24.4 us -> 21.7 us  [swap(): return lax.ppermute(x, axis, [(i, i ^ bit) for i in range(peers)])]
    ppermute x4, waiting for transfers between devices: 6.12 us -> 4.54 us  [swap_both(): return lax.ppermute(x, ('dom', 'sub'), pairs)]
    pallas_call x2 -> x4, Pallas kernels: 4.54 us -> 3.95 us  [the longest x2 3.93 us: call_solve(): pl.pallas_call(solve, in_specs=[VMEM] * 2, out_specs=[VMEM] * len(out_sha...]
  transfers between devices with their start and end apart: 36 -> 36, of which waited for: 22 -> 21; matrix products, arithmetic and copies ran while one was open for 0% -> 0% of each run, Pallas kernels for 5% -> 4%
where the time goes in v7:
time: 99.1 us; the launch traced here: 99.4 us
  waiting for transfers between devices  38.8 us (39%)
  starting transfers between devices  38.3 us (39%)
  Pallas kernels  18.7 us (19%)
  between operations  1.56 us (2%)
  local copies, waits for them, and re-layouts  1.13 us (1%)
    ppermute x24, waiting for transfers between devices, swap(): return lax.ppermute(x, axis, [(i, i ^ bit) for i in range(peers)])  22.6 us
    ppermute x24, starting transfers between devices, swap(): return lax.ppermute(x, axis, [(i, i ^ bit) for i in range(peers)])  21.7 us
    ppermute x8, waiting for transfers between devices, pair_up(): lax.ppermute(x, 'dom', [(p, p + 2) for p in low] + [(p + 2, p) for p in l...  11.7 us
    pallas_call x2, Pallas kernels, call_forward_adjoint(): pl.pallas_call(functools.partial(forward_adjoint, shape, relatives, sourc...  10.8 us
    ppermute x4, starting transfers between devices, swap_both(): return lax.ppermute(x, ('dom', 'sub'), pairs)  9.26 us
    ppermute x8, starting transfers between devices, pair_up(): lax.ppermute(x, 'dom', [(p, p + 2) for p in low] + [(p + 2, p) for p in l...  7.34 us
    ppermute x4, waiting for transfers between devices, swap_both(): return lax.ppermute(x, ('dom', 'sub'), pairs)  4.54 us
    pallas_call x2, Pallas kernels, call_solve(): pl.pallas_call(solve, in_specs=[VMEM] * 2, out_specs=[VMEM] * len(out_sha...  3.93 us
  transfers between devices with their start and end apart: 36, of which 21 were waited for; matrix products, arithmetic and copies ran while one was open for 0% of the time, Pallas kernels for 4%

profile of v7, /device:TPU:0, one launch (start us, length us, event | category | flops | bytes accessed | tf_op | source)
XLA Modules:
  0.0 99.4 jit_solution(16417724390161566556)
XLA Ops:
  1.3 0.1 pad_add_fusion.1
  1.4 0.9 pad_add_fusion.facts
  2.2 1.1 %copy-done.2 = bf16[12,64,128]{2,1,0:T(8,128)(2,1)S(1)} copy-done((bf16[12,64,128]{2,1,0:T(8,128)(2,1)S(1)}, bf16[12,64,128]{2,1,0:T(8,128)(2,1)}, u32[]{:S(2)}) %copy-start.2) | copy-done | bytes 196632
  3.3 0.8 prepare.1
  4.1 0.5 collective-permute-start
  4.7 2.6 %collective-permute-start.1 = (bf16[4,64,128]{2,1,0:T(8,128)(2,1)S(1)}, bf16[4,64,128]{2,1,0:T(8,128)(2,1)S(1)}, u32[]{:S(2)}, u32[]{:S(2)}) collective-permute-start(bf16[4,64,128]{2,1,0:T(8,128)(2,1)S(1)} %get-tuple-element.39), channel_id=1, source_target_pairs={{0,8},{4,12},{16,24},{20,28},{8,0},{12,4},{24,16},{28,20},{1,9},{5... | collective-permute-start | bytes 196616 | tf_op jit(solution)/shard_map/ppermute | solution.py:41
  7.3 0.7 collective-permute-start.4
  8.0 2.0 %collective-permute-done.1.refs_1_.first.refs_0_ = bf16[4,64,128]{2,1,0:T(8,128)(2,1)S(1)} collective-permute-done((bf16[4,64,128]{2,1,0:T(8,128)(2,1)S(1)}, bf16[4,64,128]{2,1,0:T(8,128)(2,1)S(1)}, u32[]{:S(2)}, u32[]{:S(2)}) %collective-permute-start.1) | collective-permute-done | bytes 65568 | tf_op jit(solution)/shard_map/ppermute | solution.py:41
  10.0 1.8 %collective-permute-start.2 = (bf16[12,64,128]{2,1,0:T(8,128)(2,1)S(1)}, bf16[12,64,128]{2,1,0:T(8,128)(2,1)S(1)}, u32[]{:S(2)}, u32[]{:S(2)}) collective-permute-start(bf16[12,64,128]{2,1,0:T(8,128)(2,1)S(1)} %stack.14), channel_id=1, source_target_pairs={{0,2},{1,3},{2,0},{3,1},{4,6},{5,7},{6,4},{7,5},{8,10},{9,11},{10,... | collective-permute-start | bytes 589832 | tf_op jit(solution)/shard_map/ppermute | solution.py:29
  11.8 1.5 %collective-permute-start.6 = (bf16[4,64,128]{2,1,0:T(8,128)(2,1)S(1)}, bf16[4,64,128]{2,1,0:T(8,128)(2,1)S(1)}, u32[]{:S(2)}, u32[]{:S(2)}) collective-permute-start(bf16[4,64,128]{2,1,0:T(8,128)(2,1)S(1)} %pass_on.2), channel_id=1, source_target_pairs={{0,6},{1,7},{2,4},{3,5},{4,2},{5,3},{6,0},{7,1},{8,14},{9,15},{10,... | collective-permute-start | bytes 196616 | tf_op jit(solution)/shard_map/ppermute | solution.py:36
  13.3 0.4 collective-permute-start.5
  13.7 1.8 %collective-permute-start.7 = (bf16[4,64,128]{2,1,0:T(8,128)(2,1)S(1)}, bf16[4,64,128]{2,1,0:T(8,128)(2,1)S(1)}, u32[]{:S(2)}, u32[]{:S(2)}) collective-permute-start(bf16[4,64,128]{2,1,0:T(8,128)(2,1)S(1)} %stack.15.refs_1_.refs_5_), channel_id=1, source_target_pairs={{0,2},{1,3},{2,0},{3,1},{4,6},{5,7},{6,4},{7,5},{8,10},{9,11},{10,... | collective-permute-start | bytes 196616 | tf_op jit(solution)/shard_map/ppermute | solution.py:29
  15.4 2.0 %collective-permute-done.6.refs_2_.refs_6_ = bf16[4,64,128]{2,1,0:T(8,128)(2,1)S(1)} collective-permute-done((bf16[4,64,128]{2,1,0:T(8,128)(2,1)S(1)}, bf16[4,64,128]{2,1,0:T(8,128)(2,1)S(1)}, u32[]{:S(2)}, u32[]{:S(2)}) %collective-permute-start.6) | collective-permute-done | bytes 65568 | tf_op jit(solution)/shard_map/ppermute | solution.py:36
  17.4 0.2 collective-permute-done.5.refs_0_.refs_4_
  17.6 2.0 %collective-permute-done.7.refs_3_.refs_7_ = bf16[4,64,128]{2,1,0:T(8,128)(2,1)S(1)} collective-permute-done((bf16[4,64,128]{2,1,0:T(8,128)(2,1)S(1)}, bf16[4,64,128]{2,1,0:T(8,128)(2,1)S(1)}, u32[]{:S(2)}, u32[]{:S(2)}) %collective-permute-start.7) | collective-permute-done | bytes 65568 | tf_op jit(solution)/shard_map/ppermute | solution.py:29
  19.6 0.1 collective-permute-start.8
  19.7 0.5 collective-permute-start.3
  20.1 1.3 %collective-permute-done.3.refs_3_ = bf16[12,64,128]{2,1,0:T(8,128)(2,1)S(1)} collective-permute-done((bf16[12,64,128]{2,1,0:T(8,128)(2,1)S(1)}, bf16[12,64,128]{2,1,0:T(8,128)(2,1)S(1)}, u32[]{:S(2)}, u32[]{:S(2)}) %collective-permute-start.3) | collective-permute-done | bytes 196640 | tf_op jit(solution)/shard_map/ppermute | solution.py:29
  21.5 5.4 %forward_adjoint.2 = (f32[40,64,128]{2,1,0:T(8,128)S(1)}, f32[40,64,128]{2,1,0:T(8,128)S(1)}, f32[64,128]{1,0:T(8,128)S(1)}) custom-call(s32[5,4]{1,0:T(8,128)S(1)} %pad_add_fusion.facts, s32[12,27]{1,0:T(8,128)S(1)} %copy-done, bf16[12,27,128,128]{3,2,1,0:T(8,128)(2,1)S(1)} %bitcast.8, f32[12,128]{1,0:T(8,128)S(1)} %copy-done.1, ...), custom_call_target="tpu_custom_call" | custom-call | flops 1358954496 | bytes 10616832 | tf_op jit(solution)/shard_map/forward_adjoint/pallas_call | solution.py:267
  26.9 2.9 %collective-permute-start.9 = (f32[40,64,128]{2,1,0:T(8,128)S(1)}, f32[40,64,128]{2,1,0:T(8,128)S(1)}, u32[]{:S(2)}, u32[]{:S(2)}) collective-permute-start(f32[40,64,128]{2,1,0:T(8,128)S(1)} %get-tuple-element.43), channel_id=1, source_target_pairs={{0,1},{1,0},{2,3},{3,2},{4,5},{5,4},{6,7},{7,6},{8,9},{9,8},{10,11... | collective-permute-start | bytes 3932168 | tf_op jit(solution)/shard_map/ppermute | solution.py:29
  29.8 2.3 %collective-permute-start.10 = (f32[64,128]{1,0:T(8,128)S(1)}, f32[64,128]{1,0:T(8,128)S(1)}, u32[]{:S(2)}, u32[]{:S(2)}) collective-permute-start(f32[64,128]{1,0:T(8,128)S(1)} %get-tuple-element.44), channel_id=1, source_target_pairs={{0,16},{4,20},{8,24},{12,28},{16,0},{20,4},{24,8},{28,12},{1,17},{... | collective-permute-start | bytes 98312 | tf_op jit(solution)/shard_map/ppermute | solution.py:29
  32.1 2.5 %collective-permute-done.10 = f32[64,128]{1,0:T(8,128)S(1)} collective-permute-done((f32[64,128]{1,0:T(8,128)S(1)}, f32[64,128]{1,0:T(8,128)S(1)}, u32[]{:S(2)}, u32[]{:S(2)}) %collective-permute-start.10) | collective-permute-done | bytes 32800 | tf_op jit(solution)/shard_map/ppermute | solution.py:29
  34.7 1.0 %collective-permute-start.13 = (bf16[6,64,128]{2,1,0:T(8,128)(2,1)S(1)}, bf16[6,64,128]{2,1,0:T(8,128)(2,1)S(1)}, u32[]{:S(2)}, u32[]{:S(2)}) collective-permute-start(bf16[6,64,128]{2,1,0:T(8,128)(2,1)S(1)} %get-tuple-element.47), channel_id=1, source_target_pairs={{0,2},{1,3},{2,0},{3,1},{4,6},{5,7},{6,4},{7,5},{8,10},{9,11},{10,... | collective-permute-start | bytes 294920 | tf_op jit(solution)/shard_map/ppermute | solution.py:29
  35.7 3.6 %collective-permute-start.12 = (bf16[6,64,128]{2,1,0:T(8,128)(2,1)S(1)}, bf16[6,64,128]{2,1,0:T(8,128)(2,1)S(1)}, u32[]{:S(2)}, u32[]{:S(2)}) collective-permute-start(bf16[6,64,128]{2,1,0:T(8,128)(2,1)S(1)} %get-tuple-element.46), channel_id=1, source_target_pairs={{0,6},{1,7},{2,4},{3,5},{4,2},{5,3},{6,0},{7,1},{8,14},{9,15},{10,... | collective-permute-start | bytes 294920 | tf_op jit(solution)/shard_map/ppermute | solution.py:36
  39.4 1.3 %collective-permute-done.13.far.refs_0_ = bf16[6,64,128]{2,1,0:T(8,128)(2,1)S(1)} collective-permute-done((bf16[6,64,128]{2,1,0:T(8,128)(2,1)S(1)}, bf16[6,64,128]{2,1,0:T(8,128)(2,1)S(1)}, u32[]{:S(2)}, u32[]{:S(2)}) %collective-permute-start.13) | collective-permute-done | bytes 98336 | tf_op jit(solution)/shard_map/ppermute | solution.py:29
  40.7 0.1 join.2
  40.8 0.5 collective-permute-start.16
  41.3 0.8 collective-permute-done.12.flip_far
  42.1 1.9 %collective-permute-done.11.flip = bf16[6,64,128]{2,1,0:T(8,128)(2,1)S(1)} collective-permute-done((bf16[6,64,128]{2,1,0:T(8,128)(2,1)S(1)}, bf16[6,64,128]{2,1,0:T(8,128)(2,1)S(1)}, u32[]{:S(2)}, u32[]{:S(2)}) %collective-permute-start.11) | collective-permute-done | bytes 98336 | tf_op jit(solution)/shard_map/ppermute | solution.py:29
  44.0 0.8 collective-permute-start.14
  44.8 0.7 collective-permute-start.17
  45.5 3.3 %collective-permute-done.14.got.refs_1_ = bf16[6,64,128]{2,1,0:T(8,128)(2,1)S(1)} collective-permute-done((bf16[6,64,128]{2,1,0:T(8,128)(2,1)S(1)}, bf16[6,64,128]{2,1,0:T(8,128)(2,1)S(1)}, u32[]{:S(2)}, u32[]{:S(2)}) %collective-permute-start.14) | collective-permute-done | bytes 98336 | tf_op jit(solution)/shard_map/ppermute | solution.py:41
  48.8 1.2 %collective-permute-done.15.there = f32[64,128]{1,0:T(8,128)S(1)} collective-permute-done((f32[64,128]{1,0:T(8,128)S(1)}, f32[64,128]{1,0:T(8,128)S(1)}, u32[]{:S(2)}, u32[]{:S(2)}) %collective-permute-start.15) | collective-permute-done | bytes 32800 | tf_op jit(solution)/shard_map/ppermute | solution.py:29
  50.0 1.7 %solve.2.coupling = bf16[64,192]{1,0:T(8,128)(2,1)S(1)} custom-call(f32[64,128]{1,0:T(8,128)S(1)} %sum_grams.2.here, f32[64,128]{1,0:T(8,128)S(1)} %collective-permute-done.15.there), custom_call_target="tpu_custom_call" | custom-call | flops 1048576 | bytes 65536 | tf_op jit(solution)/shard_map/solve/pallas_call | solution.py:414
  51.7 1.0 project.2
  52.7 0.2 collective-permute-start.18
  52.9 0.7 collective-permute-start.19
  53.6 0.7 collective-permute-start.22
  54.3 3.0 %collective-permute-done.19.refs_1_.first.refs_0_ = bf16[4,64,128]{2,1,0:T(8,128)(2,1)S(1)} collective-permute-done((bf16[4,64,128]{2,1,0:T(8,128)(2,1)S(1)}, bf16[4,64,128]{2,1,0:T(8,128)(2,1)S(1)}, u32[]{:S(2)}, u32[]{:S(2)}) %collective-permute-start.19) | collective-permute-done | bytes 65568 | tf_op jit(solution)/shard_map/ppermute | solution.py:41
  57.3 0.6 collective-permute-start.20
  57.9 2.1 %collective-permute-start.24 = (bf16[4,64,128]{2,1,0:T(8,128)(2,1)S(1)}, bf16[4,64,128]{2,1,0:T(8,128)(2,1)S(1)}, u32[]{:S(2)}, u32[]{:S(2)}) collective-permute-start(bf16[4,64,128]{2,1,0:T(8,128)(2,1)S(1)} %pass_on.3), channel_id=1, source_target_pairs={{0,6},{1,7},{2,4},{3,5},{4,2},{5,3},{6,0},{7,1},{8,14},{9,15},{10,... | collective-permute-start | bytes 196616 | tf_op jit(solution)/shard_map/ppermute | solution.py:36
  60.0 0.9 collective-permute-start.23
  60.9 0.6 collective-permute-start.25
  61.5 1.8 %collective-permute-done.24.refs_2_.refs_6_ = bf16[4,64,128]{2,1,0:T(8,128)(2,1)S(1)} collective-permute-done((bf16[4,64,128]{2,1,0:T(8,128)(2,1)S(1)}, bf16[4,64,128]{2,1,0:T(8,128)(2,1)S(1)}, u32[]{:S(2)}, u32[]{:S(2)}) %collective-permute-start.24) | collective-permute-done | bytes 65568 | tf_op jit(solution)/shard_map/ppermute | solution.py:36
  63.3 0.9 collective-permute-done.23.refs_0_.refs_4_
  64.3 2.2 %collective-permute-done.25.refs_3_.refs_7_ = bf16[4,64,128]{2,1,0:T(8,128)(2,1)S(1)} collective-permute-done((bf16[4,64,128]{2,1,0:T(8,128)(2,1)S(1)}, bf16[4,64,128]{2,1,0:T(8,128)(2,1)S(1)}, u32[]{:S(2)}, u32[]{:S(2)}) %collective-permute-start.25) | collective-permute-done | bytes 65568 | tf_op jit(solution)/shard_map/ppermute | solution.py:29
  66.6 0.5 collective-permute-start.21
  67.1 1.3 %collective-permute-done.21.refs_3_ = bf16[12,64,128]{2,1,0:T(8,128)(2,1)S(1)} collective-permute-done((bf16[12,64,128]{2,1,0:T(8,128)(2,1)S(1)}, bf16[12,64,128]{2,1,0:T(8,128)(2,1)S(1)}, u32[]{:S(2)}, u32[]{:S(2)}) %collective-permute-start.21) | collective-permute-done | bytes 196640 | tf_op jit(solution)/shard_map/ppermute | solution.py:29
  68.4 5.4 %forward_adjoint.3 = (f32[40,64,128]{2,1,0:T(8,128)S(1)}, f32[40,64,128]{2,1,0:T(8,128)S(1)}, f32[64,128]{1,0:T(8,128)S(1)}) custom-call(s32[5,4]{1,0:T(8,128)S(1)} %pad_add_fusion.facts, s32[12,27]{1,0:T(8,128)S(1)} %copy-done, bf16[12,27,128,128]{3,2,1,0:T(8,128)(2,1)S(1)} %bitcast.8, f32[12,128]{1,0:T(8,128)S(1)} %copy-done.1, ...), custom_call_target="tpu_custom_call" | custom-call | flops 1358954496 | bytes 10616832 | tf_op jit(solution)/shard_map/forward_adjoint/pallas_call | solution.py:267
  73.8 2.9 %collective-permute-start.27 = (f32[40,64,128]{2,1,0:T(8,128)S(1)}, f32[40,64,128]{2,1,0:T(8,128)S(1)}, u32[]{:S(2)}, u32[]{:S(2)}) collective-permute-start(f32[40,64,128]{2,1,0:T(8,128)S(1)} %get-tuple-element.59), channel_id=1, source_target_pairs={{0,1},{1,0},{2,3},{3,2},{4,5},{5,4},{6,7},{7,6},{8,9},{9,8},{10,11... | collective-permute-start | bytes 3932168 | tf_op jit(solution)/shard_map/ppermute | solution.py:29
  76.7 0.6 collective-permute-start.28
  77.4 4.7 %collective-permute-done.28 = f32[64,128]{1,0:T(8,128)S(1)} collective-permute-done((f32[64,128]{1,0:T(8,128)S(1)}, f32[64,128]{1,0:T(8,128)S(1)}, u32[]{:S(2)}, u32[]{:S(2)}) %collective-permute-start.28) | collective-permute-done | bytes 32800 | tf_op jit(solution)/shard_map/ppermute | solution.py:29
  82.2 2.0 %collective-permute-start.30 = (bf16[6,64,128]{2,1,0:T(8,128)(2,1)S(1)}, bf16[6,64,128]{2,1,0:T(8,128)(2,1)S(1)}, u32[]{:S(2)}, u32[]{:S(2)}) collective-permute-start(bf16[6,64,128]{2,1,0:T(8,128)(2,1)S(1)} %get-tuple-element.62), channel_id=1, source_target_pairs={{0,6},{1,7},{2,4},{3,5},{4,2},{5,3},{6,0},{7,1},{8,14},{9,15},{10,... | collective-permute-start | bytes 294920 | tf_op jit(solution)/shard_map/ppermute | solution.py:36
  84.2 1.5 %collective-permute-start.29 = (bf16[6,64,128]{2,1,0:T(8,128)(2,1)S(1)}, bf16[6,64,128]{2,1,0:T(8,128)(2,1)S(1)}, u32[]{:S(2)}, u32[]{:S(2)}) collective-permute-start(bf16[6,64,128]{2,1,0:T(8,128)(2,1)S(1)} %get-tuple-element.61.sent), channel_id=1, source_target_pairs={{0,4},{4,0},{8,12},{12,8},{16,20},{20,16},{24,28},{28,24},{1,5},{5... | collective-permute-start | bytes 294920 | tf_op jit(solution)/shard_map/ppermute | solution.py:29
  85.7 1.1 %collective-permute-done.31.far.refs_0_ = bf16[6,64,128]{2,1,0:T(8,128)(2,1)S(1)} collective-permute-done((bf16[6,64,128]{2,1,0:T(8,128)(2,1)S(1)}, bf16[6,64,128]{2,1,0:T(8,128)(2,1)S(1)}, u32[]{:S(2)}, u32[]{:S(2)}) %collective-permute-start.31) | collective-permute-done | bytes 98336 | tf_op jit(solution)/shard_map/ppermute | solution.py:29
  86.8 0.1 join.3
  86.9 1.8 %collective-permute-start.34 = (bf16[12,64,128]{2,1,0:T(8,128)(2,1)S(1)}, bf16[12,64,128]{2,1,0:T(8,128)(2,1)S(1)}, u32[]{:S(2)}, u32[]{:S(2)}) collective-permute-start(bf16[12,64,128]{2,1,0:T(8,128)(2,1)S(1)} %get-tuple-element.68), channel_id=1, source_target_pairs={{0,2},{1,3},{2,0},{3,1},{4,6},{5,7},{6,4},{7,5},{8,10},{9,11},{10,... | collective-permute-start | bytes 589832 | tf_op jit(solution)/shard_map/ppermute | solution.py:29
  88.7 0.6 collective-permute-done.29.flip
  89.4 0.6 collective-permute-start.32
  90.0 0.7 collective-permute-start.35
  90.7 3.4 %collective-permute-done.32.got.refs_1_ = bf16[6,64,128]{2,1,0:T(8,128)(2,1)S(1)} collective-permute-done((bf16[6,64,128]{2,1,0:T(8,128)(2,1)S(1)}, bf16[6,64,128]{2,1,0:T(8,128)(2,1)S(1)}, u32[]{:S(2)}, u32[]{:S(2)}) %collective-permute-start.32) | collective-permute-done | bytes 98336 | tf_op jit(solution)/shard_map/ppermute | solution.py:41
  94.2 1.2 %collective-permute-done.33.there = f32[64,128]{1,0:T(8,128)S(1)} collective-permute-done((f32[64,128]{1,0:T(8,128)S(1)}, f32[64,128]{1,0:T(8,128)S(1)}, u32[]{:S(2)}, u32[]{:S(2)}) %collective-permute-start.33) | collective-permute-done | bytes 32800 | tf_op jit(solution)/shard_map/ppermute | solution.py:29
  95.4 2.3 %solve.3 = (bf16[64,192]{1,0:T(8,128)(2,1)S(1)}, f32[64,64]{1,0:T(8,128)}) custom-call(f32[64,128]{1,0:T(8,128)S(1)} %sum_grams.3.here, f32[64,128]{1,0:T(8,128)S(1)} %collective-permute-done.33.there), custom_call_target="tpu_custom_call" | custom-call | flops 1048576 | bytes 65536 | tf_op jit(solution)/shard_map/solve/pallas_call | solution.py:414
  97.7 1.7 %project.3 = f32[12,64,128]{2,1,0:T(8,128)} custom-call(s32[5,4]{1,0:T(8,128)S(1)} %pad_add_fusion.facts, bf16[64,192]{1,0:T(8,128)(2,1)S(1)} %get-tuple-element.66.coupling, bf16[12,64,128]{2,1,0:T(8,128)(2,1)S(1)} %get-tuple-element.54.refs_0_.basis, f32[12,64,128]{2,1,0:T(8,128)S(1)} %get-tuple-element.67.near_own, ...), custom_call_target="tpu_custom_call" | custom-call | flops 37748736 | bytes 1966080 | tf_op jit(solution)/shard_map/project/pallas_call | solution.py:454
  (49 shorter events, 0.7 us)
Async XLA Ops:
  1.4 20.1 %slice-start = ((s8[10616832]{0:T(1024)(128)(4,1)}), s8[4194304]{0:T(1024)(128)(4,1)S(1)}, s32[]{:S(2)}) async-start(s8[10616832]{0:T(1024)(128)(4,1)} %bitcast.7), calls=%async_computation | async-start | bytes 8388608
  2.2 1.1 %copy-start.2 = (bf16[12,64,128]{2,1,0:T(8,128)(2,1)S(1)}, bf16[12,64,128]{2,1,0:T(8,128)(2,1)}, u32[]{:S(2)}) copy-start(bf16[12,64,128]{2,1,0:T(8,128)(2,1)} %directions.1) | copy-start | bytes 589828
  3.3 18.1 %slice-start.1 = ((s8[10616832]{0:T(1024)(128)(4,1)}), s8[4194304]{0:T(1024)(128)(4,1)S(1)}, s32[]{:S(2)}) async-start(s8[10616832]{0:T(1024)(128)(4,1)} %bitcast.7), calls=%async_computation.1 | async-start | bytes 8388608
  3.3 18.1 %slice-start.2 = ((s8[10616832]{0:T(1024)(128)(4,1)}), s8[2228224]{0:T(1024)(128)(4,1)S(1)}, s32[]{:S(2)}) async-start(s8[10616832]{0:T(1024)(128)(4,1)} %bitcast.7), calls=%async_computation.2 | async-start | bytes 4456448
  4.1 17.4 %copy-start = (s32[12,27]{1,0:T(8,128)S(1)}, s32[12,27]{1,0:T(8,128)}, u32[]{:S(2)}) copy-start(s32[12,27]{1,0:T(8,128)} %cols.3) | copy-start | bytes 3892
  4.1 17.4 %copy-start.1 = (f32[12,128]{1,0:T(8,128)S(1)}, f32[12,128]{1,0:T(8,128)}, u32[]{:S(2)}) copy-start(f32[12,128]{1,0:T(8,128)} %friction.3) | copy-start | bytes 18436
  4.1 9.5 %collective-permute-start = (bf16[12,64,128]{2,1,0:T(8,128)(2,1)S(1)}, bf16[12,64,128]{2,1,0:T(8,128)(2,1)S(1)}, u32[]{:S(2)}, u32[]{:S(2)}) collective-permute-start(bf16[12,64,128]{2,1,0:T(8,128)(2,1)S(1)} %get-tuple-element.38.refs_0_.basis), channel_id=1, source_target_pairs={{0,1},{1,0},{2,3},{3,2},{4,5},{5,4},{6,7},{7,6},{8,9},{9,8},{10,11... | collective-permute-start | bytes 589832 | tf_op jit(solution)/shard_map/ppermute | solution.py:29
  4.7 5.3 %collective-permute-start.1 = (bf16[4,64,128]{2,1,0:T(8,128)(2,1)S(1)}, bf16[4,64,128]{2,1,0:T(8,128)(2,1)S(1)}, u32[]{:S(2)}, u32[]{:S(2)}) collective-permute-start(bf16[4,64,128]{2,1,0:T(8,128)(2,1)S(1)} %get-tuple-element.39), channel_id=1, source_target_pairs={{0,8},{4,12},{16,24},{20,28},{8,0},{12,4},{24,16},{28,20},{1,9},{5... | collective-permute-start | bytes 196616 | tf_op jit(solution)/shard_map/ppermute | solution.py:41
  7.3 4.5 %collective-permute-start.4 = (bf16[4,64,128]{2,1,0:T(8,128)(2,1)S(1)}, bf16[4,64,128]{2,1,0:T(8,128)(2,1)S(1)}, u32[]{:S(2)}, u32[]{:S(2)}) collective-permute-start(bf16[4,64,128]{2,1,0:T(8,128)(2,1)S(1)} %get-tuple-element.41), channel_id=1, source_target_pairs={{8,16},{12,20},{16,8},{20,12},{9,17},{13,21},{17,9},{21,13},{10,18... | collective-permute-start | bytes 196616 | tf_op jit(solution)/shard_map/ppermute | solution.py:41
  10.0 9.6 %collective-permute-start.2 = (bf16[12,64,128]{2,1,0:T(8,128)(2,1)S(1)}, bf16[12,64,128]{2,1,0:T(8,128)(2,1)S(1)}, u32[]{:S(2)}, u32[]{:S(2)}) collective-permute-start(bf16[12,64,128]{2,1,0:T(8,128)(2,1)S(1)} %stack.14), channel_id=1, source_target_pairs={{0,2},{1,3},{2,0},{3,1},{4,6},{5,7},{6,4},{7,5},{8,10},{9,11},{10,... | collective-permute-start | bytes 589832 | tf_op jit(solution)/shard_map/ppermute | solution.py:29
  11.8 5.6 %collective-permute-start.6 = (bf16[4,64,128]{2,1,0:T(8,128)(2,1)S(1)}, bf16[4,64,128]{2,1,0:T(8,128)(2,1)S(1)}, u32[]{:S(2)}, u32[]{:S(2)}) collective-permute-start(bf16[4,64,128]{2,1,0:T(8,128)(2,1)S(1)} %pass_on.2), channel_id=1, source_target_pairs={{0,6},{1,7},{2,4},{3,5},{4,2},{5,3},{6,0},{7,1},{8,14},{9,15},{10,... | collective-permute-start | bytes 196616 | tf_op jit(solution)/shard_map/ppermute | solution.py:36
  13.3 4.3 %collective-permute-start.5 = (bf16[4,64,128]{2,1,0:T(8,128)(2,1)S(1)}, bf16[4,64,128]{2,1,0:T(8,128)(2,1)S(1)}, u32[]{:S(2)}, u32[]{:S(2)}) collective-permute-start(bf16[4,64,128]{2,1,0:T(8,128)(2,1)S(1)} %pass_on.2), channel_id=1, source_target_pairs={{0,4},{4,0},{8,12},{12,8},{16,20},{20,16},{24,28},{28,24},{1,5},{5... | collective-permute-start | bytes 196616 | tf_op jit(solution)/shard_map/ppermute | solution.py:29
  13.7 5.9 %collective-permute-start.7 = (bf16[4,64,128]{2,1,0:T(8,128)(2,1)S(1)}, bf16[4,64,128]{2,1,0:T(8,128)(2,1)S(1)}, u32[]{:S(2)}, u32[]{:S(2)}) collective-permute-start(bf16[4,64,128]{2,1,0:T(8,128)(2,1)S(1)} %stack.15.refs_1_.refs_5_), channel_id=1, source_target_pairs={{0,2},{1,3},{2,0},{3,1},{4,6},{5,7},{6,4},{7,5},{8,10},{9,11},{10,... | collective-permute-start | bytes 196616 | tf_op jit(solution)/shard_map/ppermute | solution.py:29
  19.6 1.9 %collective-permute-start.8 = (bf16[16,64,128]{2,1,0:T(8,128)(2,1)S(1)}, bf16[16,64,128]{2,1,0:T(8,128)(2,1)S(1)}, u32[]{:S(2)}, u32[]{:S(2)}) collective-permute-start(bf16[16,64,128]{2,1,0:T(8,128)(2,1)S(1)} %stack.16), channel_id=1, source_target_pairs={{0,1},{1,0},{2,3},{3,2},{4,5},{5,4},{6,7},{7,6},{8,9},{9,8},{10,11... | collective-permute-start | bytes 786440 | tf_op jit(solution)/shard_map/ppermute | solution.py:29
  19.7 1.8 %collective-permute-start.3 = (bf16[12,64,128]{2,1,0:T(8,128)(2,1)S(1)}, bf16[12,64,128]{2,1,0:T(8,128)(2,1)S(1)}, u32[]{:S(2)}, u32[]{:S(2)}) collective-permute-start(bf16[12,64,128]{2,1,0:T(8,128)(2,1)S(1)} %collective-permute-done.2.refs_2_), channel_id=1, source_target_pairs={{0,1},{1,0},{2,3},{3,2},{4,5},{5,4},{6,7},{7,6},{8,9},{9,8},{10,11... | collective-permute-start | bytes 589832 | tf_op jit(solution)/shard_map/ppermute | solution.py:29
  26.9 7.8 %collective-permute-start.9 = (f32[40,64,128]{2,1,0:T(8,128)S(1)}, f32[40,64,128]{2,1,0:T(8,128)S(1)}, u32[]{:S(2)}, u32[]{:S(2)}) collective-permute-start(f32[40,64,128]{2,1,0:T(8,128)S(1)} %get-tuple-element.43), channel_id=1, source_target_pairs={{0,1},{1,0},{2,3},{3,2},{4,5},{5,4},{6,7},{7,6},{8,9},{9,8},{10,11... | collective-permute-start | bytes 3932168 | tf_op jit(solution)/shard_map/ppermute | solution.py:29
  29.8 4.8 %collective-permute-start.10 = (f32[64,128]{1,0:T(8,128)S(1)}, f32[64,128]{1,0:T(8,128)S(1)}, u32[]{:S(2)}, u32[]{:S(2)}) collective-permute-start(f32[64,128]{1,0:T(8,128)S(1)} %get-tuple-element.44), channel_id=1, source_target_pairs={{0,16},{4,20},{8,24},{12,28},{16,0},{20,4},{24,8},{28,12},{1,17},{... | collective-permute-start | bytes 98312 | tf_op jit(solution)/shard_map/ppermute | solution.py:29
  34.7 6.0 %collective-permute-start.13 = (bf16[6,64,128]{2,1,0:T(8,128)(2,1)S(1)}, bf16[6,64,128]{2,1,0:T(8,128)(2,1)S(1)}, u32[]{:S(2)}, u32[]{:S(2)}) collective-permute-start(bf16[6,64,128]{2,1,0:T(8,128)(2,1)S(1)} %get-tuple-element.47), channel_id=1, source_target_pairs={{0,2},{1,3},{2,0},{3,1},{4,6},{5,7},{6,4},{7,5},{8,10},{9,11},{10,... | collective-permute-start | bytes 294920 | tf_op jit(solution)/shard_map/ppermute | solution.py:29
  35.7 6.3 %collective-permute-start.12 = (bf16[6,64,128]{2,1,0:T(8,128)(2,1)S(1)}, bf16[6,64,128]{2,1,0:T(8,128)(2,1)S(1)}, u32[]{:S(2)}, u32[]{:S(2)}) collective-permute-start(bf16[6,64,128]{2,1,0:T(8,128)(2,1)S(1)} %get-tuple-element.46), channel_id=1, source_target_pairs={{0,6},{1,7},{2,4},{3,5},{4,2},{5,3},{6,0},{7,1},{8,14},{9,15},{10,... | collective-permute-start | bytes 294920 | tf_op jit(solution)/shard_map/ppermute | solution.py:36
  39.4 4.6 %collective-permute-start.11 = (bf16[6,64,128]{2,1,0:T(8,128)(2,1)S(1)}, bf16[6,64,128]{2,1,0:T(8,128)(2,1)S(1)}, u32[]{:S(2)}, u32[]{:S(2)}) collective-permute-start(bf16[6,64,128]{2,1,0:T(8,128)(2,1)S(1)} %get-tuple-element.45.sent), channel_id=1, source_target_pairs={{0,4},{4,0},{8,12},{12,8},{16,20},{20,16},{24,28},{28,24},{1,5},{5... | collective-permute-start | bytes 294920 | tf_op jit(solution)/shard_map/ppermute | solution.py:29
  40.8 10.9 %collective-permute-start.16 = (bf16[12,64,128]{2,1,0:T(8,128)(2,1)S(1)}, bf16[12,64,128]{2,1,0:T(8,128)(2,1)S(1)}, u32[]{:S(2)}, u32[]{:S(2)}) collective-permute-start(bf16[12,64,128]{2,1,0:T(8,128)(2,1)S(1)} %get-tuple-element.51), channel_id=1, source_target_pairs={{0,2},{1,3},{2,0},{3,1},{4,6},{5,7},{6,4},{7,5},{8,10},{9,11},{10,... | collective-permute-start | bytes 589832 | tf_op jit(solution)/shard_map/ppermute | solution.py:29
  44.0 4.7 %collective-permute-start.14 = (bf16[6,64,128]{2,1,0:T(8,128)(2,1)S(1)}, bf16[6,64,128]{2,1,0:T(8,128)(2,1)S(1)}, u32[]{:S(2)}, u32[]{:S(2)}) collective-permute-start(bf16[6,64,128]{2,1,0:T(8,128)(2,1)S(1)} %get-tuple-element.49.sent), channel_id=1, source_target_pairs={{0,8},{4,12},{16,24},{20,28},{8,0},{12,4},{24,16},{28,20},{1,9},{5... | collective-permute-start | bytes 294920 | tf_op jit(solution)/shard_map/ppermute | solution.py:41
  44.8 6.9 %collective-permute-start.17 = (bf16[4,64,128]{2,1,0:T(8,128)(2,1)S(1)}, bf16[4,64,128]{2,1,0:T(8,128)(2,1)S(1)}, u32[]{:S(2)}, u32[]{:S(2)}) collective-permute-start(bf16[4,64,128]{2,1,0:T(8,128)(2,1)S(1)} %get-tuple-element.53), channel_id=1, source_target_pairs={{8,16},{12,20},{16,8},{20,12},{9,17},{13,21},{17,9},{21,13},{10,18... | collective-permute-start | bytes 196616 | tf_op jit(solution)/shard_map/ppermute | solution.py:41
  48.7 1.3 %collective-permute-start.15 = (f32[64,128]{1,0:T(8,128)S(1)}, f32[64,128]{1,0:T(8,128)S(1)}, u32[]{:S(2)}, u32[]{:S(2)}) collective-permute-start(f32[64,128]{1,0:T(8,128)S(1)} %sum_grams.2.here), channel_id=1, source_target_pairs={{0,1},{1,0},{2,3},{3,2},{4,5},{5,4},{6,7},{7,6},{8,9},{9,8},{10,11... | collective-permute-start | bytes 98312 | tf_op jit(solution)/shard_map/ppermute | solution.py:29
  52.7 8.2 %collective-permute-start.18 = (bf16[12,64,128]{2,1,0:T(8,128)(2,1)S(1)}, bf16[12,64,128]{2,1,0:T(8,128)(2,1)S(1)}, u32[]{:S(2)}, u32[]{:S(2)}) collective-permute-start(bf16[12,64,128]{2,1,0:T(8,128)(2,1)S(1)} %get-tuple-element.54.refs_0_.basis), channel_id=1, source_target_pairs={{0,1},{1,0},{2,3},{3,2},{4,5},{5,4},{6,7},{7,6},{8,9},{9,8},{10,11... | collective-permute-start | bytes 589832 | tf_op jit(solution)/shard_map/ppermute | solution.py:29
  52.9 4.3 %collective-permute-start.19 = (bf16[4,64,128]{2,1,0:T(8,128)(2,1)S(1)}, bf16[4,64,128]{2,1,0:T(8,128)(2,1)S(1)}, u32[]{:S(2)}, u32[]{:S(2)}) collective-permute-start(bf16[4,64,128]{2,1,0:T(8,128)(2,1)S(1)} %get-tuple-element.55), channel_id=1, source_target_pairs={{0,8},{4,12},{16,24},{20,28},{8,0},{12,4},{24,16},{28,20},{1,9},{5... | collective-permute-start | bytes 196616 | tf_op jit(solution)/shard_map/ppermute | solution.py:41
  53.6 4.2 %collective-permute-start.22 = (bf16[4,64,128]{2,1,0:T(8,128)(2,1)S(1)}, bf16[4,64,128]{2,1,0:T(8,128)(2,1)S(1)}, u32[]{:S(2)}, u32[]{:S(2)}) collective-permute-start(bf16[4,64,128]{2,1,0:T(8,128)(2,1)S(1)} %get-tuple-element.57), channel_id=1, source_target_pairs={{8,16},{12,20},{16,8},{20,12},{9,17},{13,21},{17,9},{21,13},{10,18... | collective-permute-start | bytes 196616 | tf_op jit(solution)/shard_map/ppermute | solution.py:41
  57.3 9.3 %collective-permute-start.20 = (bf16[12,64,128]{2,1,0:T(8,128)(2,1)S(1)}, bf16[12,64,128]{2,1,0:T(8,128)(2,1)S(1)}, u32[]{:S(2)}, u32[]{:S(2)}) collective-permute-start(bf16[12,64,128]{2,1,0:T(8,128)(2,1)S(1)} %stack.17), channel_id=1, source_target_pairs={{0,2},{1,3},{2,0},{3,1},{4,6},{5,7},{6,4},{7,5},{8,10},{9,11},{10,... | collective-permute-start | bytes 589832 | tf_op jit(solution)/shard_map/ppermute | solution.py:29
  57.9 5.5 %collective-permute-start.24 = (bf16[4,64,128]{2,1,0:T(8,128)(2,1)S(1)}, bf16[4,64,128]{2,1,0:T(8,128)(2,1)S(1)}, u32[]{:S(2)}, u32[]{:S(2)}) collective-permute-start(bf16[4,64,128]{2,1,0:T(8,128)(2,1)S(1)} %pass_on.3), channel_id=1, source_target_pairs={{0,6},{1,7},{2,4},{3,5},{4,2},{5,3},{6,0},{7,1},{8,14},{9,15},{10,... | collective-permute-start | bytes 196616 | tf_op jit(solution)/shard_map/ppermute | solution.py:36
  60.0 4.3 %collective-permute-start.23 = (bf16[4,64,128]{2,1,0:T(8,128)(2,1)S(1)}, bf16[4,64,128]{2,1,0:T(8,128)(2,1)S(1)}, u32[]{:S(2)}, u32[]{:S(2)}) collective-permute-start(bf16[4,64,128]{2,1,0:T(8,128)(2,1)S(1)} %pass_on.3), channel_id=1, source_target_pairs={{0,4},{4,0},{8,12},{12,8},{16,20},{20,16},{24,28},{28,24},{1,5},{5... | collective-permute-start | bytes 196616 | tf_op jit(solution)/shard_map/ppermute | solution.py:29
  60.9 5.6 %collective-permute-start.25 = (bf16[4,64,128]{2,1,0:T(8,128)(2,1)S(1)}, bf16[4,64,128]{2,1,0:T(8,128)(2,1)S(1)}, u32[]{:S(2)}, u32[]{:S(2)}) collective-permute-start(bf16[4,64,128]{2,1,0:T(8,128)(2,1)S(1)} %stack.18.refs_1_.refs_5_), channel_id=1, source_target_pairs={{0,2},{1,3},{2,0},{3,1},{4,6},{5,7},{6,4},{7,5},{8,10},{9,11},{10,... | collective-permute-start | bytes 196616 | tf_op jit(solution)/shard_map/ppermute | solution.py:29
  66.5 1.9 %collective-permute-start.26 = (bf16[16,64,128]{2,1,0:T(8,128)(2,1)S(1)}, bf16[16,64,128]{2,1,0:T(8,128)(2,1)S(1)}, u32[]{:S(2)}, u32[]{:S(2)}) collective-permute-start(bf16[16,64,128]{2,1,0:T(8,128)(2,1)S(1)} %stack.19), channel_id=1, source_target_pairs={{0,1},{1,0},{2,3},{3,2},{4,5},{5,4},{6,7},{7,6},{8,9},{9,8},{10,11... | collective-permute-start | bytes 786440 | tf_op jit(solution)/shard_map/ppermute | solution.py:29
  66.6 1.8 %collective-permute-start.21 = (bf16[12,64,128]{2,1,0:T(8,128)(2,1)S(1)}, bf16[12,64,128]{2,1,0:T(8,128)(2,1)S(1)}, u32[]{:S(2)}, u32[]{:S(2)}) collective-permute-start(bf16[12,64,128]{2,1,0:T(8,128)(2,1)S(1)} %collective-permute-done.20.refs_2_), channel_id=1, source_target_pairs={{0,1},{1,0},{2,3},{3,2},{4,5},{5,4},{6,7},{7,6},{8,9},{9,8},{10,11... | collective-permute-start | bytes 589832 | tf_op jit(solution)/shard_map/ppermute | solution.py:29
  73.8 8.3 %collective-permute-start.27 = (f32[40,64,128]{2,1,0:T(8,128)S(1)}, f32[40,64,128]{2,1,0:T(8,128)S(1)}, u32[]{:S(2)}, u32[]{:S(2)}) collective-permute-start(f32[40,64,128]{2,1,0:T(8,128)S(1)} %get-tuple-element.59), channel_id=1, source_target_pairs={{0,1},{1,0},{2,3},{3,2},{4,5},{5,4},{6,7},{7,6},{8,9},{9,8},{10,11... | collective-permute-start | bytes 3932168 | tf_op jit(solution)/shard_map/ppermute | solution.py:29
  76.7 5.3 %collective-permute-start.28 = (f32[64,128]{1,0:T(8,128)S(1)}, f32[64,128]{1,0:T(8,128)S(1)}, u32[]{:S(2)}, u32[]{:S(2)}) collective-permute-start(f32[64,128]{1,0:T(8,128)S(1)} %get-tuple-element.60), channel_id=1, source_target_pairs={{0,16},{4,20},{8,24},{12,28},{16,0},{20,4},{24,8},{28,12},{1,17},{... | collective-permute-start | bytes 98312 | tf_op jit(solution)/shard_map/ppermute | solution.py:29
  82.1 4.7 %collective-permute-start.31 = (bf16[6,64,128]{2,1,0:T(8,128)(2,1)S(1)}, bf16[6,64,128]{2,1,0:T(8,128)(2,1)S(1)}, u32[]{:S(2)}, u32[]{:S(2)}) collective-permute-start(bf16[6,64,128]{2,1,0:T(8,128)(2,1)S(1)} %get-tuple-element.63), channel_id=1, source_target_pairs={{0,2},{1,3},{2,0},{3,1},{4,6},{5,7},{6,4},{7,5},{8,10},{9,11},{10,... | collective-permute-start | bytes 294920 | tf_op jit(solution)/shard_map/ppermute | solution.py:29
  82.2 6.5 %collective-permute-start.30 = (bf16[6,64,128]{2,1,0:T(8,128)(2,1)S(1)}, bf16[6,64,128]{2,1,0:T(8,128)(2,1)S(1)}, u32[]{:S(2)}, u32[]{:S(2)}) collective-permute-start(bf16[6,64,128]{2,1,0:T(8,128)(2,1)S(1)} %get-tuple-element.62), channel_id=1, source_target_pairs={{0,6},{1,7},{2,4},{3,5},{4,2},{5,3},{6,0},{7,1},{8,14},{9,15},{10,... | collective-permute-start | bytes 294920 | tf_op jit(solution)/shard_map/ppermute | solution.py:36
  84.2 5.2 %collective-permute-start.29 = (bf16[6,64,128]{2,1,0:T(8,128)(2,1)S(1)}, bf16[6,64,128]{2,1,0:T(8,128)(2,1)S(1)}, u32[]{:S(2)}, u32[]{:S(2)}) collective-permute-start(bf16[6,64,128]{2,1,0:T(8,128)(2,1)S(1)} %get-tuple-element.61.sent), channel_id=1, source_target_pairs={{0,4},{4,0},{8,12},{12,8},{16,20},{20,16},{24,28},{28,24},{1,5},{5... | collective-permute-start | bytes 294920 | tf_op jit(solution)/shard_map/ppermute | solution.py:29
  86.9 10.8 %collective-permute-start.34 = (bf16[12,64,128]{2,1,0:T(8,128)(2,1)S(1)}, bf16[12,64,128]{2,1,0:T(8,128)(2,1)S(1)}, u32[]{:S(2)}, u32[]{:S(2)}) collective-permute-start(bf16[12,64,128]{2,1,0:T(8,128)(2,1)S(1)} %get-tuple-element.68), channel_id=1, source_target_pairs={{0,2},{1,3},{2,0},{3,1},{4,6},{5,7},{6,4},{7,5},{8,10},{9,11},{10,... | collective-permute-start | bytes 589832 | tf_op jit(solution)/shard_map/ppermute | solution.py:29
  89.4 4.7 %collective-permute-start.32 = (bf16[6,64,128]{2,1,0:T(8,128)(2,1)S(1)}, bf16[6,64,128]{2,1,0:T(8,128)(2,1)S(1)}, u32[]{:S(2)}, u32[]{:S(2)}) collective-permute-start(bf16[6,64,128]{2,1,0:T(8,128)(2,1)S(1)} %get-tuple-element.65.sent), channel_id=1, source_target_pairs={{0,8},{4,12},{16,24},{20,28},{8,0},{12,4},{24,16},{28,20},{1,9},{5... | collective-permute-start | bytes 294920 | tf_op jit(solution)/shard_map/ppermute | solution.py:41
  90.0 7.6 %collective-permute-start.35 = (bf16[4,64,128]{2,1,0:T(8,128)(2,1)S(1)}, bf16[4,64,128]{2,1,0:T(8,128)(2,1)S(1)}, u32[]{:S(2)}, u32[]{:S(2)}) collective-permute-start(bf16[4,64,128]{2,1,0:T(8,128)(2,1)S(1)} %get-tuple-element.70), channel_id=1, source_target_pairs={{8,16},{12,20},{16,8},{20,12},{9,17},{13,21},{17,9},{21,13},{10,18... | collective-permute-start | bytes 196616 | tf_op jit(solution)/shard_map/ppermute | solution.py:41
  94.1 1.3 %collective-permute-start.33 = (f32[64,128]{1,0:T(8,128)S(1)}, f32[64,128]{1,0:T(8,128)S(1)}, u32[]{:S(2)}, u32[]{:S(2)}) collective-permute-start(f32[64,128]{1,0:T(8,128)S(1)} %sum_grams.3.here), channel_id=1, source_target_pairs={{0,1},{1,0},{2,3},{3,2},{4,5},{5,4},{6,7},{7,6},{8,9},{9,8},{10,11... | collective-permute-start | bytes 98312 | tf_op jit(solution)/shard_map/ppermute | solution.py:29
